TPU v7x, 32 devices: a whole 2x2x4 slice. The times are simulated.
32 devices in a mesh: ctx: 16 (over z, x, core), shard: 2 (over y).
Axes of the slice: x: 2, y: 2, z: 4, core: 2. Of those that a mesh axis runs over, the one named last changes fastest.
Arguments:
- tokens: bfloat16 [2, 2048, 768], P('shard', 'ctx'), may hold values from -6 to 6
- gain_one: bfloat16 [768], P('shard'), may hold values from 0.099609375 to 1.8984375
- w_qkv: bfloat16 [768, 2304], P('shard'), may hold values from -0.21875 to 0.21875
- w_out: bfloat16 [768, 768], P('shard'), may hold values from -6 to 6
- gain_two: bfloat16 [768], P('shard'), may hold values from 0.099609375 to 1.8984375
- w_in: bfloat16 [768, 2304], P('shard'), may hold values from -0.21875 to 0.21875
- w_down: bfloat16 [1152, 768], P('shard'), may hold values from -0.1875 to 0.1875
- cotangent: bfloat16 [2, 2048, 768], P('shard', 'ctx'), may hold values from -6 to 6
Outputs:
- result: float32 [2, 2048, 768], P('shard', 'ctx')
- grad_tokens: float32 [2, 2048, 768], P('shard', 'ctx')
- grad_gain_one: float32 [768], P('shard')
- grad_w_qkv: float32 [768, 2304], P('shard')
- grad_w_out: float32 [768, 768], P('shard')
- grad_gain_two: float32 [768], P('shard')
- grad_w_in: float32 [768, 2304], P('shard')
- grad_w_down: float32 [1152, 768], P('shard')
All inputs are finite; a program needn't handle non-finite values.
Results may differ from a plain program's by a relative error of at most 0.024.
Values may be sent and summed in bfloat16 or wider, within the bound.
No kernel may reach another device: no remote copies, remote signals or barrier semaphores. Data moves between devices by JAX's collectives and lax.ppermute only.
A program may use at most 192 MiB of HBM per device.

v0:
```python
import jax
import jax.numpy as jnp
from jax import lax
from jax.sharding import PartitionSpec as P

D = 768
HEADS = 12
HEAD_DIM = 64
FF = 1152


EPS = 1e-05
THETA = 160000.0


def layer_norm(values, gain):
    mean = jnp.mean(values, axis=-1, keepdims=True)
    centred = values - mean
    spread = jnp.mean(centred * centred, axis=-1, keepdims=True)
    return centred * lax.rsqrt(spread + EPS) * gain


def rotary(length, start):
    half = HEAD_DIM // 2
    freq = THETA ** (-jnp.arange(half, dtype=jnp.float32) * (2.0 / HEAD_DIM))
    places = (start + jnp.arange(length, dtype=jnp.int32)).astype(jnp.float32)
    angle = places[:, None] * freq[None, :]
    angle = jnp.concatenate([angle, angle], axis=1)
    return (jnp.cos(angle), jnp.sin(angle))


def rotate(values, cosine, sine):
    half = HEAD_DIM // 2
    turned = jnp.concatenate([-values[..., half:], values[..., :half]], axis=-1)
    return values * cosine[:, None, :] + turned * sine[:, None, :]


def gelu_mix(gate_up):
    return jax.nn.gelu(gate_up[:, :FF], approximate=False) * gate_up[:, FF:]


def head_forward(parts):
    query_h, keys_h, values_h = parts
    factor = HEAD_DIM ** (-0.5)
    scores = (
        lax.dot_general(
            query_h, keys_h, (((1,), (1,)), ((), ())), preferred_element_type=jnp.float32
        )
        * factor
    )
    highest = jnp.max(scores, axis=-1, keepdims=True)
    log_total = highest + jnp.log(jnp.sum(jnp.exp(scores - highest), axis=-1, keepdims=True))
    probs = jnp.exp(scores - log_total).astype(jnp.bfloat16)
    attended = jnp.dot(probs, values_h, preferred_element_type=jnp.float32)
    return (attended, log_total)


def score_grads(query_h, keys_h, values_h, log_total, grad_att_h, inner=None):
    factor = HEAD_DIM ** (-0.5)
    scores = (
        lax.dot_general(
            query_h, keys_h, (((1,), (1,)), ((), ())), preferred_element_type=jnp.float32
        )
        * factor
    )
    probs_full = jnp.exp(scores - log_total)
    grad_probs = lax.dot_general(
        grad_att_h, values_h, (((1,), (1,)), ((), ())), preferred_element_type=jnp.float32
    )
    inner = jnp.sum(probs_full * grad_probs, axis=-1, keepdims=True)
    grad_scores = (probs_full * (grad_probs - inner)).astype(jnp.bfloat16)
    return (probs_full, grad_scores, inner)


def head_backward(parts):
    query_h, keys_h, values_h, log_total, grad_att_h = parts
    factor = HEAD_DIM ** (-0.5)
    probs_full, grad_scores, inner = score_grads(query_h, keys_h, values_h, log_total, grad_att_h)
    probs_low = probs_full.astype(jnp.bfloat16)
    grad_query = jnp.dot(grad_scores, keys_h, preferred_element_type=jnp.float32) * factor
    grad_key = (
        lax.dot_general(
            grad_scores, query_h, (((0,), (0,)), ((), ())), preferred_element_type=jnp.float32
        )
        * factor
    )
    grad_value = lax.dot_general(
        probs_low, grad_att_h, (((0,), (0,)), ((), ())), preferred_element_type=jnp.float32
    )
    return (grad_query, grad_key, grad_value)


def per_device(tokens, gain_one, w_qkv, w_out, gain_two, w_in, w_down, cotangent):
    inputs = tokens[0].astype(jnp.float32)
    rows = inputs.shape[0]
    attn_full = (
        lax.all_gather(gain_one, "shard", axis=0, tiled=True),
        lax.all_gather(w_qkv, "shard", axis=0, tiled=True),
        lax.all_gather(w_out, "shard", axis=0, tiled=True),
    )
    norm_one, norm_one_back = jax.vjp(layer_norm, inputs, attn_full[0].astype(jnp.float32))
    h_one = norm_one.astype(jnp.bfloat16)
    qkv = jnp.dot(h_one, attn_full[1], preferred_element_type=jnp.float32).reshape(
        rows, 3, HEADS, HEAD_DIM
    )
    cosine, sine = rotary(rows, lax.axis_index("ctx") * rows)
    query = rotate(qkv[:, 0], cosine, sine).astype(jnp.bfloat16).transpose(1, 0, 2)
    own_keys = rotate(qkv[:, 1], cosine, sine).astype(jnp.bfloat16).transpose(1, 0, 2)
    own_values = qkv[:, 2].astype(jnp.bfloat16).transpose(1, 0, 2)
    keys, values = (
        lax.all_gather(own_keys, "ctx", axis=1, tiled=True),
        lax.all_gather(own_values, "ctx", axis=1, tiled=True),
    )
    attended, log_total = lax.map(head_forward, (query, keys, values))
    att_low = attended.transpose(1, 0, 2).reshape(rows, D).astype(jnp.bfloat16)
    middle = inputs + jnp.dot(att_low, attn_full[2], preferred_element_type=jnp.float32)
    ffn_full = (
        lax.all_gather(gain_two, "shard", axis=0, tiled=True),
        lax.all_gather(w_in, "shard", axis=0, tiled=True),
        lax.all_gather(w_down, "shard", axis=0, tiled=True),
    )
    norm_two, norm_two_back = jax.vjp(layer_norm, middle, ffn_full[0].astype(jnp.float32))
    h_two = norm_two.astype(jnp.bfloat16)
    gate_up = jnp.dot(h_two, ffn_full[1], preferred_element_type=jnp.float32)
    mixed, mix_back = jax.vjp(gelu_mix, gate_up)
    mixed_low = mixed.astype(jnp.bfloat16)
    result = middle + jnp.dot(mixed_low, ffn_full[2], preferred_element_type=jnp.float32)
    ffn_back = (
        lax.all_gather(gain_two, "shard", axis=0, tiled=True),
        lax.all_gather(w_in, "shard", axis=0, tiled=True),
        lax.all_gather(w_down, "shard", axis=0, tiled=True),
    )
    grad_out = cotangent[0]
    grad_down = jnp.dot(mixed_low.T, grad_out, preferred_element_type=jnp.float32)
    grad_mixed = jnp.dot(grad_out, ffn_back[2].T, preferred_element_type=jnp.float32)
    grad_gate_up = mix_back(grad_mixed)[0].astype(jnp.bfloat16)
    grad_in = jnp.dot(h_two.T, grad_gate_up, preferred_element_type=jnp.float32)
    grad_h_two = jnp.dot(grad_gate_up, ffn_back[1].T, preferred_element_type=jnp.float32)
    grad_middle_norm, grad_gain_two = norm_two_back(grad_h_two)
    grad_middle = grad_out.astype(jnp.float32) + grad_middle_norm
    ffn_sums = (
        lax.psum_scatter(
            grad_gain_two.astype(jnp.bfloat16), "shard", scatter_dimension=0, tiled=True
        ).astype(jnp.float32),
        lax.psum_scatter(
            grad_in.astype(jnp.bfloat16), "shard", scatter_dimension=0, tiled=True
        ).astype(jnp.float32),
        lax.psum_scatter(
            grad_down.astype(jnp.bfloat16), "shard", scatter_dimension=0, tiled=True
        ).astype(jnp.float32),
    )
    ffn_sums = (
        lax.psum(ffn_sums[0].astype(jnp.bfloat16), "ctx").astype(jnp.float32),
        lax.psum(ffn_sums[1].astype(jnp.bfloat16), "ctx").astype(jnp.float32),
        lax.psum(ffn_sums[2].astype(jnp.bfloat16), "ctx").astype(jnp.float32),
    )
    attn_back = (
        lax.all_gather(gain_one, "shard", axis=0, tiled=True),
        lax.all_gather(w_qkv, "shard", axis=0, tiled=True),
        lax.all_gather(w_out, "shard", axis=0, tiled=True),
    )
    grad_branch = grad_middle.astype(jnp.bfloat16)
    grad_wo = jnp.dot(att_low.T, grad_branch, preferred_element_type=jnp.float32)
    grad_att = jnp.dot(grad_branch, attn_back[2].T, preferred_element_type=jnp.float32)
    grad_att = grad_att.astype(jnp.bfloat16).reshape(rows, HEADS, HEAD_DIM).transpose(1, 0, 2)
    grad_query, grad_key, grad_value = lax.map(
        head_backward, (query, keys, values, log_total, grad_att)
    )
    mine_key, mine_value = (
        lax.psum_scatter(
            grad_key.astype(jnp.bfloat16), "ctx", scatter_dimension=1, tiled=True
        ).astype(jnp.float32),
        lax.psum_scatter(
            grad_value.astype(jnp.bfloat16), "ctx", scatter_dimension=1, tiled=True
        ).astype(jnp.float32),
    )
    plain_query = rotate(grad_query.transpose(1, 0, 2), cosine, -sine).reshape(rows, D)
    plain_key = rotate(mine_key.transpose(1, 0, 2), cosine, -sine).reshape(rows, D)
    plain_value = mine_value.transpose(1, 0, 2).reshape(rows, D)
    grad_qkv = jnp.concatenate([plain_query, plain_key, plain_value], axis=1).astype(jnp.bfloat16)
    grad_wqkv = jnp.dot(h_one.T, grad_qkv, preferred_element_type=jnp.float32)
    grad_h_one = jnp.dot(grad_qkv, attn_back[1].T, preferred_element_type=jnp.float32)
    grad_input_norm, grad_gain_one = norm_one_back(grad_h_one)
    grad_inputs = grad_middle + grad_input_norm
    attn_sums = (
        lax.psum_scatter(
            grad_gain_one.astype(jnp.bfloat16), "shard", scatter_dimension=0, tiled=True
        ).astype(jnp.float32),
        lax.psum_scatter(
            grad_wqkv.astype(jnp.bfloat16), "shard", scatter_dimension=0, tiled=True
        ).astype(jnp.float32),
        lax.psum_scatter(
            grad_wo.astype(jnp.bfloat16), "shard", scatter_dimension=0, tiled=True
        ).astype(jnp.float32),
    )
    attn_sums = (
        lax.psum(attn_sums[0].astype(jnp.bfloat16), "ctx").astype(jnp.float32),
        lax.psum(attn_sums[1].astype(jnp.bfloat16), "ctx").astype(jnp.float32),
        lax.psum(attn_sums[2].astype(jnp.bfloat16), "ctx").astype(jnp.float32),
    )
    return (
        result[None],
        grad_inputs[None],
        attn_sums[0],
        attn_sums[1],
        attn_sums[2],
        ffn_sums[0],
        ffn_sums[1],
        ffn_sums[2],
    )


def solution(mesh):
    return jax.shard_map(
        per_device,
        mesh=mesh,
        in_specs=(
            P("shard", "ctx", None),
            P("shard"),
            P("shard", None),
            P("shard", None),
            P("shard"),
            P("shard", None),
            P("shard", None),
            P("shard", "ctx", None),
        ),
        out_specs=(
            P("shard", "ctx", None),
            P("shard", "ctx", None),
            P("shard"),
            P("shard", None),
            P("shard", None),
            P("shard"),
            P("shard", None),
            P("shard", None),
        ),
        check_vma=False,
    )
```

profile of v0, /device:TPU:0, one launch (start us, length us, event | category | flops | bytes accessed | tf_op | source)
XLA Modules:
  0.0 827.2 jit_solution(10667967576008692830)
XLA Ops:
  8.6 5.2 all-gather
  16.9 44.7 %all-gather.9.cloned.1.call-done = bf16[768,2304]{1,0:T(8,128)(2,1)} async-done(((bf16[384,2304]{1,0:T(8,128)(2,1)}), bf16[768,2304]{1,0:T(8,128)(2,1)}) %all-gather.9.cloned.1.call-update) | async-done | bytes 3538960 | tf_op jit(solution)/shard_map/all_gather | solution.py:98
  61.6 4.5 copy.33
  66.2 2.1 fusion.75
  73.9 4.3 all-gather.1
  78.5 39.1 %all-gather.11.cloned.1.call-done = bf16[12,2048,64]{1,2,0:T(8,128)(2,1)} async-done(((bf16[12,128,64]{1,2,0:T(8,128)(2,1)}), bf16[12,2048,64]{1,2,0:T(8,128)(2,1)}) %all-gather.11.cloned.1.call-update) | async-done | bytes 3145744 | tf_op jit(solution)/shard_map/all_gather | solution.py:111
  117.6 6.6 copy.35
  124.2 41.6 %all-gather.13.cloned.1.call-done = bf16[12,2048,64]{1,2,0:T(8,128)(2,1)} async-done(((bf16[12,128,64]{1,2,0:T(8,128)(2,1)}), bf16[12,2048,64]{1,2,0:T(8,128)(2,1)}) %all-gather.13.cloned.1.call-update) | async-done | bytes 3145744 | tf_op jit(solution)/shard_map/all_gather | solution.py:112
  165.7 6.6 copy.36
  172.3 38.7 %while.28 = (s32[]{:T(128)}, bf16[12,128,64]{1,2,0:T(8,128)(2,1)S(1)}, f32[12,128,1]{1,2,0:T(1,128)S(1)}, bf16[12,128,64]{2,1,0:T(8,128)(2,1)S(1)}, bf16[12,2048...) while((s32[]{:T(128)}, bf16[12,128,64]{1,2,0:T(8,128)(2,1)S(1)}, f32[12,128,1]{1,2,0:T(1,128)S(1)}, ...), condition=%wide.region_5.6_spmd.clone, body=%wide.region_2.5_spmd.sunk.clone | while | flops 68681600 | bytes 4266065 | solution.py:114
  213.8 25.1 %all-gather.17.cloned.1.call-done = bf16[768,2304]{1,0:T(8,128)(2,1)} async-done(((bf16[384,2304]{1,0:T(8,128)(2,1)}), bf16[768,2304]{1,0:T(8,128)(2,1)}) %all-gather.17.cloned.1.call-update) | async-done | bytes 3538960 | tf_op jit(solution)/shard_map/all_gather | solution.py:119
  238.9 2.7 fusion.99
  241.6 28.2 %all-gather.19.cloned.1.call-done = bf16[1152,768]{1,0:T(8,128)(2,1)} async-done(((bf16[576,768]{1,0:T(8,128)(2,1)}), bf16[1152,768]{1,0:T(8,128)(2,1)}) %all-gather.19.cloned.1.call-update) | async-done | bytes 1769488 | tf_op jit(solution)/shard_map/all_gather | solution.py:120
  269.8 3.2 fusion.87
  276.4 1.7 copy.37
  278.1 94.8 %while.29 = (s32[]{:T(128)}, f32[12,128,64]{1,2,0:T(8,128)S(1)}, bf16[12,2048,64]{1,2,0:T(8,128)(2,1)}, bf16[12,2048,64]{1,2,0:T(8,128)(2,1)}, bf16[12,128,64]{2...) while((s32[]{:T(128)}, f32[12,128,64]{1,2,0:T(8,128)S(1)}, ...), condition=%wide.region_12.13_spmd.clone, body=%wide.region_10.12_spmd.sunk.clone | while | flops 170008448 | bytes 10624617 | solution.py:166
  282.6 1.7 fusion.166
  290.5 1.7 fusion.166
  298.4 1.7 fusion.166
  306.3 1.7 fusion.166
  314.2 1.7 fusion.166
  322.1 1.7 fusion.166
  330.0 1.7 fusion.166
  337.9 1.7 fusion.166
  345.8 1.7 fusion.166
  353.7 1.7 fusion.166
  361.6 1.7 fusion.166
  369.5 1.7 fusion.166
  372.9 10.5 %copy.45 = bf16[12,2048,64]{2,0,1:T(8,128)(2,1)} copy(bf16[12,2048,64]{1,2,0:T(8,128)(2,1)} %get-tuple-element.94) | data formatting | bytes 6291456
  383.4 11.2 %reshape.224 = bf16[2048,768]{1,0:T(8,128)(2,1)} reshape(bf16[2048,12,64]{2,1,0:T(8,128)(2,1)} %bitcast.222) | data formatting | bytes 6291456
  394.8 10.5 %copy.43 = bf16[12,2048,64]{2,0,1:T(8,128)(2,1)} copy(bf16[12,2048,64]{1,2,0:T(8,128)(2,1)} %get-tuple-element.93) | data formatting | bytes 6291456
  405.3 11.3 %reshape.222 = bf16[2048,768]{1,0:T(8,128)(2,1)} reshape(bf16[2048,12,64]{2,1,0:T(8,128)(2,1)} %bitcast.223) | data formatting | bytes 6291456
  418.2 1.9 convolution_convert_fusion.2
  420.1 3.0 convolution_convert_fusion
  423.3 37.7 %reduce-scatter.21.cloned.1.call-done = bf16[128,768]{1,0:T(8,128)(2,1)} async-done(((bf16[2048,768]{1,0:T(8,128)(2,1)}), bf16[128,768]{1,0:T(8,128)(2,1)}) %reduce-scatter.21.cloned.1.call-update) | async-done | bytes 196624
  462.6 67.9 %reduce-scatter.19.cloned.1.call-done = bf16[128,768]{1,0:T(8,128)(2,1)} async-done(((bf16[2048,768]{1,0:T(8,128)(2,1)}), bf16[128,768]{1,0:T(8,128)(2,1)}) %reduce-scatter.19.cloned.1.call-update) | async-done | bytes 196624
  532.4 3.0 convolution_convert_fusion.1
  535.5 18.6 %reduce-scatter.13.cloned.1.call-done = bf16[384,768]{1,0:T(8,128)(2,1)} async-done(((bf16[768,768]{1,0:T(8,128)(2,1)}), bf16[384,768]{1,0:T(8,128)(2,1)}) %reduce-scatter.13.cloned.1.call-update) | async-done | bytes 589840 | tf_op jit(solution)/shard_map/reduce_scatter | solution.py:192
  554.1 31.1 %reduce-scatter.17.cloned.1.call-done = bf16[576,768]{1,0:T(8,128)(2,1)} async-done(((bf16[1152,768]{1,0:T(8,128)(2,1)}), bf16[576,768]{1,0:T(8,128)(2,1)}) %reduce-scatter.17.cloned.1.call-update) | async-done | bytes 884752 | tf_op jit(solution)/shard_map/reduce_scatter | solution.py:148
  585.2 50.5 %reduce-scatter.15.cloned.1.call-done = bf16[384,2304]{1,0:T(8,128)(2,1)} async-done(((bf16[768,2304]{1,0:T(8,128)(2,1)}), bf16[384,2304]{1,0:T(8,128)(2,1)}) %reduce-scatter.15.cloned.1.call-update) | async-done | bytes 1769488 | tf_op jit(solution)/shard_map/reduce_scatter | solution.py:145
  635.7 50.5 %reduce-scatter.11.cloned.1.call-done = bf16[384,2304]{1,0:T(8,128)(2,1)} async-done(((bf16[768,2304]{1,0:T(8,128)(2,1)}), bf16[384,2304]{1,0:T(8,128)(2,1)}) %reduce-scatter.11.cloned.1.call-update) | async-done | bytes 1769488 | tf_op jit(solution)/shard_map/reduce_scatter | solution.py:189
  687.4 2.7 fusion.39
  690.1 3.4 fusion.57
  693.8 4.9 all-reduce.6
  698.9 33.9 %all-reduce.4 = (bf16[384]{0:T(512)(128)(2,1)S(1)}, bf16[384]{0:T(512)(128)(2,1)S(1)}) all-reduce(bf16[384]{0:T(512)(128)(2,1)S(1)} %dynamic-slice.1, bf16[384]{0:T(512)(128)(2,1)S(1)} %dynamic-slice.3), channel_id=1, replica_groups=mesh['ctx'=16,'shard'=2] {'ctx'}, use_global_device_ids=true, to_apply=%region_19.20 | all-reduce | flops 768 | bytes 3072 | tf_op jit(solution)/shard_map/psum | solution.py:197
  734.9 77.7 %all-reduce.9.cloned.1.call-done = (bf16[384,2304]{1,0:T(8,128)(2,1)}, bf16[384,768]{1,0:T(8,128)(2,1)}, bf16[384,2304]{1,0:T(8,128)(2,1)}, bf16[576,768]{1,0:T(8,128)(2,1)}) async-done(((bf16[384,2304]{1,0:T(8,128)(2,1)}, bf16[384,768]{1,0:T(8,128)(2,1)}, bf16[384,2304]{1,0:T(8,128)(2,1)}, bf16[576,768]{1,0:T(8,128)(2,1)}), (bf16[384,2304]{1,0:T(8,128)(2,1)}, bf16[384,768]{1,0:T(8,128)(2,1)}, ...) | async-done | bytes 5013520 | tf_op jit(solution)/shard_map/psum | solution.py:198
  812.6 3.6 convert_element_type.156
  817.3 2.0 convert_element_type.162
  (236 shorter events, 139.2 us)
Async XLA Ops:
  7.2 54.5 %all-gather.9.cloned.1.call-start = ((), (), s32[]{:S(2)}) async-start(), calls=%async_computation.6 | async-start | bytes 5308416 | tf_op jit(solution)/shard_map/all_gather | solution.py:98
  7.9 109.7 %all-gather.11.cloned.1.call-start = ((), (), s32[]{:S(2)}) async-start(), calls=%async_computation.7 | async-start | bytes 3342336 | tf_op jit(solution)/shard_map/all_gather | solution.py:111
  66.2 3.2 copy-start.11
  66.2 3.2 copy-start.14
  68.3 1.0 copy-start.2
  68.5 5.4 copy-start.15
  70.2 95.5 %all-gather.13.cloned.1.call-start = ((), (), s32[]{:S(2)}) async-start(), calls=%async_computation.8 | async-start | bytes 3342336 | tf_op jit(solution)/shard_map/all_gather | solution.py:112
  72.0 139.1 %all-gather.15.cloned.1.call-start = ((), (), s32[]{:S(2)}) async-start(), calls=%async_computation.9 | async-start | bytes 1769472 | tf_op jit(solution)/shard_map/all_gather | solution.py:99
  72.6 166.3 %all-gather.17.cloned.1.call-start = ((), (), s32[]{:S(2)}) async-start(), calls=%async_computation.10 | async-start | bytes 5308416 | tf_op jit(solution)/shard_map/all_gather | solution.py:119
  73.2 196.6 %all-gather.19.cloned.1.call-start = ((), (), s32[]{:S(2)}) async-start(), calls=%async_computation.11 | async-start | bytes 2654208 | tf_op jit(solution)/shard_map/all_gather | solution.py:120
  73.7 387.2 %reduce-scatter.21.cloned.1.call-start = ((), (), s32[]{:S(2)}) async-start(), calls=%async_computation.17 | async-start | bytes 3342336
  172.3 39.5 %copy-start.1 = (bf16[1,128,768]{2,1,0:T(8,128)(2,1)S(1)}, bf16[1,128,768]{2,1,0:T(8,128)(2,1)}, u32[]{:S(2)}) copy-start(bf16[1,128,768]{2,1,0:T(8,128)(2,1)} %param.12) | copy-start | bytes 589828
  211.1 0.7 copy-start.4
  213.5 56.2 %copy-start.5 = (bf16[1,128,768]{2,1,0:T(8,128)(2,1)S(1)}, bf16[1,128,768]{2,1,0:T(8,128)(2,1)}, u32[]{:S(2)}) copy-start(bf16[1,128,768]{2,1,0:T(8,128)(2,1)} %param.19) | copy-start | bytes 589828
  269.8 3.5 copy-start
  273.3 1.7 copy-start.6
  273.3 1.8 copy-start.3
  274.7 3.4 copy-start.8
  394.5 136.0 %reduce-scatter.19.cloned.1.call-start = ((), (), s32[]{:S(2)}) async-start(), calls=%async_computation.16 | async-start | bytes 3342336
  416.6 137.5 %reduce-scatter.13.cloned.1.call-start = ((), (), s32[]{:S(2)}) async-start(), calls=%async_computation.13 | async-start | bytes 1769472 | tf_op jit(solution)/shard_map/reduce_scatter | solution.py:192
  418.1 167.0 %reduce-scatter.17.cloned.1.call-start = ((), (), s32[]{:S(2)}) async-start(), calls=%async_computation.15 | async-start | bytes 2654208 | tf_op jit(solution)/shard_map/reduce_scatter | solution.py:148
  420.1 215.6 %reduce-scatter.15.cloned.1.call-start = ((), (), s32[]{:S(2)}) async-start(), calls=%async_computation.14 | async-start | bytes 5308416 | tf_op jit(solution)/shard_map/reduce_scatter | solution.py:145
  423.1 109.1 %copy-start.12 = (f32[128,64]{0,1:T(8,128)S(1)}, f32[128,64]{0,1:T(8,128)}, u32[]{:S(2)}) copy-start(f32[128,64]{0,1:T(8,128)} %get-tuple-element.210) | copy-start | bytes 98308
  423.2 109.1 %copy-start.13 = (f32[128,64]{0,1:T(8,128)S(1)}, f32[128,64]{0,1:T(8,128)}, u32[]{:S(2)}) copy-start(f32[128,64]{0,1:T(8,128)} %get-tuple-element.208) | copy-start | bytes 98308
  423.2 263.0 %reduce-scatter.11.cloned.1.call-start = ((), (), s32[]{:S(2)}) async-start(), calls=%async_computation.12 | async-start | bytes 5308416 | tf_op jit(solution)/shard_map/reduce_scatter | solution.py:189
  535.4 150.8 %copy-start.16 = (u32[32]{0:T(128)S(1)}, u32[32]{0:T(128)}, u32[]{:S(2)}) copy-start(u32[32]{0:T(128)} %constant.143) | copy-start | bytes 388
  535.4 277.1 %all-reduce.9.cloned.1.call-start = ((), (), s32[]{:S(2)}) async-start(), calls=%async_computation.18 | async-start | bytes 10027008 | tf_op jit(solution)/shard_map/psum | solution.py:198
  812.6 3.7 copy-start.10
  812.6 4.7 copy-start.7
  816.2 3.1 copy-start.9
Sparse Core Ops, SparseCore 0:
  9.5 52.0 all-gather.8
  70.3 47.1 all-gather.10
  120.3 45.3 all-gather.12
  167.1 20.9 all-gather.14
  189.5 49.3 all-gather.16
  240.3 29.4 all-gather.18
  394.7 66.2 reduce-scatter.20
  465.3 65.1 reduce-scatter.18
  533.3 20.7 reduce-scatter.12
  556.9 28.2 reduce-scatter.16
  588.0 47.6 reduce-scatter.14
  638.5 47.6 reduce-scatter.10
  690.2 122.3 all-reduce.8
where the time goes:
time: 833 us; the launch traced here: 827 us
  waiting for transfers between devices  515 us (62%)
  matrix products  155 us (19%)
  local copies, waits for them, and re-layouts  71.3 us (9%)
  blocking collectives  48.4 us (6%)
  other arithmetic  21.4 us (3%)
  between operations  15 us (2%)
    unnamed x15, waiting for transfers between devices  108 us
    psum x1, waiting for transfers between devices, per_device(): lax.psum(attn_sums[1].astype(jnp.bfloat16), 'ctx').astype(jnp.float32)  77.7 us
    reduce_scatter x1, waiting for transfers between devices, per_device(): lax.psum_scatter(grad_in.astype(jnp.bfloat16), 'shard', scatter_dimension...  50.5 us
    reduce_scatter x1, waiting for transfers between devices, per_device(): lax.psum_scatter(grad_wqkv.astype(jnp.bfloat16), 'shard', scatter_dimensi...  50.5 us
    unnamed x47, local copies, waits for them, and re-layouts  49.8 us
    all_gather x1, waiting for transfers between devices, per_device(): lax.all_gather(w_qkv, 'shard', axis=0, tiled=True)  44.7 us
    all_gather x1, waiting for transfers between devices, per_device(): lax.all_gather(own_values, 'ctx', axis=1, tiled=True)  41.6 us
    all_gather x1, waiting for transfers between devices, per_device(): lax.all_gather(own_keys, 'ctx', axis=1, tiled=True)  39.1 us
  transfers between devices with their start and end apart: 13, of which 12 were waited for; matrix products, arithmetic and copies ran while one was open for 13% of the time, Pallas kernels for 0%

commit v1 on v0

v1 whole, which is shorter than its diff:
```python
import functools
import math

import jax
import jax.numpy as jnp
from jax import lax
from jax.experimental import pallas as pl
from jax.experimental.pallas import tpu as pltpu
from jax.sharding import Mesh, PartitionSpec as P

D = 768
HEADS = 12
HEAD_DIM = 64
FF = 1152
EPS = 1e-05
THETA = 160000.0

TP = 4
GH = HEADS // TP
GW = GH * HEAD_DIM
WC = 640
CTX = ("zo", "z", "x", "core")
BF = jnp.bfloat16
F32 = jnp.float32
VMEM_LIMIT = 56 * 1024 * 1024

KEY_AT = ((0, 0), (0, 1), (1, 0))
VALUE_AT = ((1, 1), (2, 0), (2, 1))


def dot(a, b):
    return jnp.dot(a, b, preferred_element_type=F32)


def dot_nt(a, b):
    return lax.dot_general(a, b, (((1,), (1,)), ((), ())), preferred_element_type=F32)


def dot_tn(a, b):
    return lax.dot_general(a, b, (((0,), (0,)), ((), ())), preferred_element_type=F32)


def call(body, outs, n_smem, ins, scratch=(), any_ins=(), flops=0, bytes_accessed=0, name=None):
    specs = []
    for i in range(len(ins)):
        if i < n_smem:
            specs.append(pl.BlockSpec(memory_space=pltpu.SMEM))
        elif i in any_ins:
            specs.append(pl.BlockSpec(memory_space=pl.ANY))
        else:
            specs.append(pl.BlockSpec(memory_space=pltpu.VMEM))
    return pl.pallas_call(
        body,
        out_shape=[jax.ShapeDtypeStruct(s, t) for s, t in outs],
        in_specs=specs,
        out_specs=[pl.BlockSpec(memory_space=pltpu.VMEM)] * len(outs),
        scratch_shapes=list(scratch),
        compiler_params=pltpu.CompilerParams(vmem_limit_bytes=VMEM_LIMIT),
        cost_estimate=pl.CostEstimate(
            flops=flops, bytes_accessed=bytes_accessed, transcendentals=0
        ),
        name=name,
    )(*ins)


def normalise(values):
    mean = jnp.mean(values, axis=-1, keepdims=True)
    centred = values - mean
    spread = jnp.mean(centred * centred, axis=-1, keepdims=True)
    scale = lax.rsqrt(spread + EPS)
    return centred * scale, scale


def normalise_back(grad_unit, unit, scale):
    return scale * (
        grad_unit
        - jnp.mean(grad_unit, axis=-1, keepdims=True)
        - unit * jnp.mean(grad_unit * unit, axis=-1, keepdims=True)
    )


def turn(tile, cosine, signed_sine, first_half):
    swapped = jnp.where(first_half, pltpu.roll(tile, 96, 1), pltpu.roll(tile, 32, 1))
    return tile * cosine + swapped * signed_sine


def lane_masks(rows):
    lane = lax.broadcasted_iota(jnp.int32, (rows, 128), 1)
    return lax.rem(lane, 64) < 32, lane < 64


def front_kernel(n_w, offs, *refs):
    toks = refs[:TP]
    ws = refs[TP : TP + n_w]
    cos_ref, sin_ref, q_ref, kv_ref, h_ref, w_ref, gains_ref = refs[TP + n_w :]
    rows = toks[0].shape[0]
    part = ws[0].shape[0]
    for i, block in enumerate(ws):
        w_ref[pl.ds(pl.multiple_of(offs[i], part), part), :] = block[...]
    gains = w_ref[:, 512:640].astype(F32).T[64:72]
    gains_ref[...] = gains
    gain = gains[0:1]
    first, low = lane_masks(rows)
    for j in range(TP):
        at = slice(j * rows, (j + 1) * rows)
        unit, _ = normalise(toks[j][...].astype(F32))
        h = (unit * gain).astype(BF)
        h_ref[at, :] = h
        out = dot(h, w_ref[...])
        cosine, sine = cos_ref[at, :], sin_ref[at, :]
        key_a = turn(out[:, 0:128], cosine, sine, first)
        mixed = out[:, 128:256]
        key_b = jnp.where(low, turn(mixed, cosine, sine, first), mixed)
        kv_ref[at, 0:128] = key_a.astype(BF)
        kv_ref[at, 128:256] = key_b.astype(BF)
        kv_ref[at, 256:384] = out[:, 256:384].astype(BF)
        query_a = turn(out[:, 384:512], cosine, sine, first)
        query_b = jnp.where(low, turn(out[:, 512:640], cosine, sine, first), 0.0)
        factor = HEAD_DIM ** (-0.5)
        q_ref[at, 0:128] = (query_a * factor).astype(BF)
        q_ref[at, 128:256] = (query_b * factor).astype(BF)


def half_rows(values_t, head):
    at = head * HEAD_DIM
    rows = values_t[at : at + HEAD_DIM]
    zeros = jnp.zeros_like(rows)
    return jnp.concatenate([rows, zeros] if head % 2 == 0 else [zeros, rows], axis=0)


def forward_kernel(n_kv, q_ref, *refs):
    kvs = refs[:n_kv]
    att_ref, att_t_ref, lse_ref, kv_s, v_t, q_t = refs[n_kv:]
    rows = kvs[0].shape[0]
    block = math.gcd(rows, 256)
    for i, kv in enumerate(kvs):
        kv_s[i * rows : (i + 1) * rows, :] = kv[...]
        v_t[:, i * rows : (i + 1) * rows] = kv[:, 128:384].T
    q_t[...] = q_ref[...].T
    lse_ref[...] = jnp.zeros_like(lse_ref)
    for i in range(rows // block):
        at = slice(i * block, (i + 1) * block)
        for h in range(GH):
            tile = KEY_AT[h][0]
            keys = kv_s[:, tile * 128 : tile * 128 + 128]
            scores = dot(keys, half_rows(q_t[:, at], h))
            top = jnp.max(scores, axis=0, keepdims=True)
            weights = jnp.exp(scores - top)
            total = jnp.sum(weights, axis=0, keepdims=True)
            tile, half = VALUE_AT[h]
            values_t = v_t[(tile - 1) * 128 : tile * 128, :]
            out = dot(values_t, weights.astype(BF))[half * 64 : half * 64 + 64]
            att_t_ref[h * 64 : h * 64 + 64, at] = out / total
            lse_ref[h : h + 1, at] = top + jnp.log(total)
    att_ref[...] = att_t_ref[...].T.astype(BF)


def backward_kernel(n_kv, q_ref, *refs):
    kvs = refs[:n_kv]
    gas = refs[n_kv : n_kv + TP]
    att_t_ref, lse_ref, dkv_ref, dq_ref = refs[n_kv + TP : n_kv + TP + 4]
    kv_s, k_t, q_t, g_t, q_m, g_m, acc, dq_t = refs[n_kv + TP + 4 :]
    rows = kvs[0].shape[0]
    small = gas[0].shape[0]
    block = math.gcd(rows, 256)
    for i, kv in enumerate(kvs):
        kv_s[i * rows : (i + 1) * rows, :] = kv[...]
        k_t[:, i * rows : (i + 1) * rows] = kv[:, 0:256].T
    q_t[...] = q_ref[...].T
    _, low = lane_masks(small)
    for j in range(TP):
        at = slice(j * small, (j + 1) * small)
        g_t[:, at] = gas[j][...].T
        first, second = gas[j][:, 0:128], gas[j][:, 128:256].astype(F32)
        g_m[at, 0:128] = first
        g_m[at, 128:256] = jnp.where(low, second, 0.0).astype(BF)
        g_m[at, 256:384] = jnp.where(low, 0.0, second).astype(BF)
        both = q_ref[at, 0:128].astype(F32)
        q_m[at, 0:128] = jnp.where(low, both, 0.0).astype(BF)
        q_m[at, 128:256] = jnp.where(low, 0.0, both).astype(BF)
        q_m[at, 256:384] = q_ref[at, 128:256]
    dq_t[...] = jnp.zeros_like(dq_t)
    acc[...] = jnp.zeros_like(acc)
    for i in range(rows // block):
        at = slice(i * block, (i + 1) * block)
        for h in range(GH):
            ktile, khalf = KEY_AT[h]
            vtile = VALUE_AT[h][0]
            klanes = slice(ktile * 128, ktile * 128 + 128)
            vlanes = slice(vtile * 128, vtile * 128 + 128)
            scores = dot(kv_s[:, klanes], half_rows(q_t[:, at], h))
            probs = jnp.exp(scores - lse_ref[h : h + 1, at])
            grad_t = half_rows(g_t[:, at], h + 1)
            grad_probs = dot(kv_s[:, vlanes], grad_t)
            own = g_t[(h + 1) * 64 : (h + 2) * 64, at].astype(F32)
            inner = jnp.sum(
                own * att_t_ref[h * 64 : h * 64 + 64, at], axis=0, keepdims=True
            )
            grad_scores = (probs * (grad_probs - inner)).astype(BF)
            lanes = slice(h * 128, h * 128 + 128)
            acc[:, vlanes] += dot(probs.astype(BF), g_m[at, lanes])
            acc[:, klanes] += dot(grad_scores, q_m[at, lanes])
            part = dot(k_t[klanes, :], grad_scores)[khalf * 64 : khalf * 64 + 64]
            dq_t[h * 64 : h * 64 + 64, at] = part * HEAD_DIM ** (-0.5)
    dq_ref[...] = dq_t[...].T
    for i in range(n_kv):
        dkv_ref[i] = acc[i * rows : (i + 1) * rows, :].astype(BF)


def middle_kernel(n_out, n_in, n_down, offs, *refs):
    n_w = n_out + n_in + n_down
    atts = refs[:TP]
    tok_ref, cot_ref, gains_ref = refs[TP : TP + 3]
    ws = refs[TP + 3 : TP + 3 + n_w]
    rest = refs[TP + 3 + n_w :]
    result_ref, gmid_ref, gb_ref, h_ref, mixed_ref, ggu_ref, gain_ref = rest[:7]
    gatts = rest[7 : 7 + TP]
    w_out, w_in, w_down, sems = rest[7 + TP :]
    copies = []
    for i, block in enumerate(ws):
        target = w_out if i < n_out else (w_in if i < n_out + n_in else w_down)
        height = block.shape[0]
        at = pl.ds(pl.multiple_of(offs[i], math.gcd(height, 1024 * 9)), height)
        copies.append(pltpu.make_async_copy(block, target.at[at, :], sems.at[i]))
    for copy in copies:
        copy.start()
    starts = [pl.multiple_of(offs[n_w + j], GW) for j in range(TP)]
    for copy in copies[:n_out]:
        copy.wait()
    middle = tok_ref[...].astype(F32)
    for j in range(TP):
        middle += dot(atts[j][...], w_out[pl.ds(starts[j], GW), :])
    gain = gains_ref[1:2, :]
    unit, scale = normalise(middle)
    h = (unit * gain).astype(BF)
    h_ref[...] = h
    for copy in copies[n_out : n_out + n_in]:
        copy.wait()
    gate = dot(h, w_in[:, :FF])
    up = dot(h, w_in[:, FF:])
    phi = 0.5 * (1.0 + lax.erf(gate * math.sqrt(0.5)))
    active = gate * phi
    mixed = (active * up).astype(BF)
    mixed_ref[...] = mixed
    for copy in copies[n_out + n_in :]:
        copy.wait()
    grad_mixed = dot_nt(cot_ref[...], w_down[...])
    slope = phi + gate * (jnp.exp(-0.5 * gate * gate) * (1.0 / math.sqrt(2.0 * math.pi)))
    grad_gate = (grad_mixed * up * slope).astype(BF)
    grad_up = (grad_mixed * active).astype(BF)
    ggu_ref[:, :FF] = grad_gate
    ggu_ref[:, FF:] = grad_up
    grad_h = dot_nt(grad_gate, w_in[:, :FF]) + dot_nt(grad_up, w_in[:, FF:])
    gain_ref[...] = jnp.broadcast_to(
        jnp.sum(grad_h * unit, axis=0, keepdims=True), gain_ref.shape
    )
    grad_middle = cot_ref[...].astype(F32) + normalise_back(grad_h * gain, unit, scale)
    gmid_ref[...] = grad_middle
    gb = grad_middle.astype(BF)
    gb_ref[...] = gb
    for j in range(TP):
        part = dot_nt(gb, w_out[pl.ds(starts[j], GW), :])
        pad = jnp.zeros((part.shape[0], 256 - GW), F32)
        gatts[j][...] = jnp.concatenate([pad, part], axis=1).astype(BF)
    result_ref[...] = middle + dot(mixed, w_down[...])


def plan(shards):
    pieces = 4 * shards
    up16 = lambda n: -(-n // 16) * 16
    rows_d, rows_f = D // pieces, FF // pieces
    starts = [0, up16(rows_d), 2 * up16(rows_d), 3 * up16(rows_d)]
    starts.append(starts[-1] + up16(rows_f))
    starts.append(starts[-1] + up16(rows_d))
    total = -(-(starts[-1] + 16) // 64) * 64
    return pieces, rows_d, rows_f, starts, total


def ffn_grads_kernel(shards, groups, *refs):
    atts = refs[:TP]
    h_ref, ggu_ref, mixed_ref, cot_ref, gb_ref, gain_ref, out_ref = refs[TP:]
    pieces, rows_d, rows_f, starts, total = plan(shards)
    cot = cot_ref[...]
    h_t = h_ref[...].T
    for b in range(3):
        grad = dot(h_t, ggu_ref[:, b * D : (b + 1) * D]).astype(BF)
        for m in range(pieces):
            out_ref[m, starts[b] : starts[b] + rows_d, :] = grad[m * rows_d : (m + 1) * rows_d]
    grad = dot(mixed_ref[...].T, cot).astype(BF)
    for m in range(pieces):
        out_ref[m, starts[3] : starts[3] + rows_f, :] = grad[m * rows_f : (m + 1) * rows_f]
    gb = gb_ref[...]
    per = GW // rows_d
    for j in range(TP):
        grad = dot(atts[j][...].T, gb).astype(BF)
        for i in range(per):
            out_ref[groups[j] * per + i, starts[4] : starts[4] + rows_d, :] = grad[
                i * rows_d : (i + 1) * rows_d
            ]
    row = jnp.broadcast_to(gain_ref[0:1, :], (total - starts[5], D)).astype(BF)
    for m in range(pieces):
        out_ref[m, starts[5] :, :] = row


def qkv_grads_kernel(pieces, n_sum, *refs):
    parts = refs[:n_sum]
    dq_ref, cos_ref, sin_ref, h_ref, w_ref, grad_w_ref = refs[n_sum : n_sum + 6]
    outs = refs[n_sum + 6 : n_sum + 6 + TP]
    full = refs[n_sum + 6 + TP]
    rows = outs[0].shape[0]
    first, low = lane_masks(rows)
    for j in range(TP):
        at = slice(j * rows, (j + 1) * rows)
        cosine, sine = cos_ref[at, :], -sin_ref[at, :]
        tiles = []
        for t in range(3):
            total = parts[0][at, t * 128 : t * 128 + 128].astype(F32)
            for part in parts[1:]:
                total += part[at, t * 128 : t * 128 + 128].astype(F32)
            if t == 0:
                total = turn(total, cosine, sine, first)
            if t == 1:
                total = jnp.where(low, turn(total, cosine, sine, first), total)
            tiles.append(total)
        for t in range(2):
            tiles.append(turn(dq_ref[at, t * 128 : t * 128 + 128], cosine, sine, first))
        for t, tile in enumerate(tiles):
            tile = tile.astype(BF)
            full[at, t * 128 : t * 128 + 128] = tile
            outs[j][:, t * 128 : t * 128 + 128] = tile
    grad = dot(h_ref[...].T, full[...])
    w = w_ref[...].astype(F32)
    gain = w[:, 576:577]
    lane = lax.broadcasted_iota(jnp.int32, grad.shape, 1)
    by_gain = jnp.sum(grad * w, axis=1, keepdims=True) / gain
    grad = jnp.where(lane < 3 * GW, grad, by_gain).astype(BF)
    height = D // pieces
    for m in range(pieces):
        grad_w_ref[m] = grad[m * height : (m + 1) * height]


def tail_kernel(n_w, offs, *refs):
    grads = refs[:TP]
    tok_ref, gmid_ref, gains_ref = refs[TP : TP + 3]
    ws = refs[TP + 3 : TP + 3 + n_w]
    out_ref, w_all, sems = refs[TP + 3 + n_w :]
    copies = []
    for i, block in enumerate(ws):
        count, height = block.shape[:2]
        at = pl.ds(pl.multiple_of(offs[2 * i + 1], height), height)
        target = w_all.at[pl.ds(offs[2 * i], count), at, :]
        copies.append(pltpu.make_async_copy(block, target, sems.at[i]))
    for copy in copies:
        copy.start()
    unit, scale = normalise(tok_ref[...].astype(F32))
    for copy in copies:
        copy.wait()
    total = jnp.zeros(out_ref.shape, F32)
    for j in range(TP):
        total += dot_nt(grads[j][...], w_all[offs[2 * n_w + j]])
    grad_unit = total * gains_ref[0:1, :]
    out_ref[...] = gmid_ref[...] + normalise_back(grad_unit, unit, scale)


def ffn_unpack_kernel(shards, idx, *refs):
    blocks = refs[:4]
    in_ref, out_ref, down_ref, gain_ref, held = refs[4:]
    _, rows_d, rows_f, starts, total = plan(shards)
    quarter = total // TP
    z, x, c = idx[0], idx[1], idx[2]
    for cr in range(2):
        for xr in range(2):
            block = blocks[2 * cr + xr]
            for k in range(TP):
                at = pl.multiple_of(lax.rem(z - k + TP, TP) * quarter, quarter)
                held[pl.ds(at, quarter), :] = block[k].astype(F32)
            cc, xx = lax.rem(c + cr, 2), lax.rem(x + xr, 2)
            for b in range(3):
                in_ref[cc, xx, :, b * D : (b + 1) * D] = held[starts[b] : starts[b] + rows_d, :]
            down_ref[cc, xx] = held[starts[3] : starts[3] + rows_f, :]
            out_ref[cc, xx] = held[starts[4] : starts[4] + rows_d, :]
            if cr == 0 and xr == 0:
                gain_ref[...] = held[starts[5] : starts[5] + 8, :]


def qkv_unpack_kernel(idx, *refs):
    blocks = refs[:4]
    out_ref, gain_ref = refs[4:]
    z, x, c = idx[0], idx[1], idx[2]
    for cr in range(2):
        for xr in range(2):
            cc, xx = lax.rem(c + cr, 2), lax.rem(x + xr, 2)
            gain = None
            for g in range(TP):
                block = blocks[2 * cr + xr][lax.rem(z - g + TP, TP)].astype(F32)
                for source, place in ((0, 1), (1, 2), (2, 0)):
                    out_ref[cc, xx, :, place * D + g * GW : place * D + (g + 1) * GW] = block[
                        :, source * GW : (source + 1) * GW
                    ]
                tail = block[:, 512:640]
                gain = tail if gain is None else gain + tail
            gain_ref[cc, xx] = gain


def shift(value, axis, k):
    n = lax.axis_size(axis)
    return lax.ppermute(value, axis, [(i, (i + k) % n) for i in range(n)])


def gather(value, axis):
    return [value] + [shift(value, axis, k) for k in range(1, lax.axis_size(axis))]


def pick(value, index, dim):
    return lax.dynamic_index_in_dim(value, index, dim, keepdims=False)


def reduce_scatter(value, axis, dim):
    n, i = lax.axis_size(axis), lax.axis_index(axis)
    total = None
    for k in range(1, n):
        got = shift(pick(value, lax.rem(i + k, n), dim), axis, k).astype(F32)
        total = got if total is None else total + got
    own = pick(value, i, dim).astype(F32)
    return (own if total is None else own + total).astype(BF)


def sum_over(value, axis):
    total = value.astype(F32)
    for k in range(1, lax.axis_size(axis)):
        total = total + shift(value, axis, k).astype(F32)
    return total.astype(BF)


def fetch(weight):
    n, y, c = lax.axis_size("shard"), lax.axis_index("shard"), lax.axis_index("core")
    height = weight.shape[0]
    half = height // 2
    blocks = [(weight, y * height)]
    for k in range(1, n):
        start = lax.rem(y - k + n, n) * height
        if half % 16:
            blocks.append((shift(weight, "shard", k), start))
            continue
        mine = lax.dynamic_slice_in_dim(weight, c * half, half, 0)
        mine = shift(mine, "shard", k)
        blocks.append((mine, start + c * half))
        blocks.append((shift(mine, "core", 1), start + (1 - c) * half))
    return blocks


def per_device(tokens, gain_one, w_qkv, w_out, gain_two, w_in, w_down, cotangent):
    tok, cot = tokens[0], cotangent[0]
    rows = tok.shape[0]
    many = TP * rows
    zo, z = lax.axis_index("zo"), lax.axis_index("z")
    x, c, y = lax.axis_index("x"), lax.axis_index("core"), lax.axis_index("shard")
    shards = lax.axis_size("shard")
    part = w_qkv.shape[0]
    i32 = jnp.int32

    toks = gather(tok, "z")
    w_groups = w_qkv.reshape(part, 3, TP, GW).transpose(2, 0, 1, 3)
    gains_col = jnp.stack([gain_one, gain_two], axis=1)
    gains_col = jnp.broadcast_to(gains_col[None], (TP, part, 2))
    w_groups = jnp.concatenate(
        [
            w_groups[:, :, 1],
            w_groups[:, :, 2],
            w_groups[:, :, 0],
            gains_col,
            jnp.zeros((TP, part, WC - 3 * GW - 2), BF),
        ],
        axis=2,
    )
    w_own = pick(w_groups, z, 0)
    w_slices = gather(w_own, "shard")
    w_offs = jnp.stack([lax.rem(y - k + shards, shards) * part for k in range(shards)]).astype(i32)

    freq = THETA ** (-jnp.arange(HEAD_DIM // 2, dtype=F32) * (2.0 / HEAD_DIM))
    owners = lax.rem(z - jnp.arange(TP, dtype=i32) + TP, TP)
    first_places = (((zo * TP + owners) * 2 + x) * 2 + c) * rows
    places = (first_places[:, None] + jnp.arange(rows, dtype=i32)).reshape(many)
    angle = places.astype(F32)[:, None] * jnp.tile(freq, 4)[None, :]
    sign = jnp.where(jnp.arange(128) % 64 < 32, -1.0, 1.0).astype(F32)
    cosine, sine = jnp.cos(angle), jnp.sin(angle) * sign[None, :]

    query, kv, h_one, w_full, gains = call(
        functools.partial(front_kernel, shards),
        [
            ((many, 256), BF),
            ((many, 2 * GW), BF),
            ((many, D), BF),
            ((D, WC), BF),
            ((8, D), F32),
        ],
        1,
        [w_offs, *toks, *w_slices, cosine, sine],
        flops=2 * many * D * WC,
        bytes_accessed=5_000_000,
        name="front",
    )

    kvs = gather(kv, "zo")
    kvs = [b for k in range(2) for b in (kvs if k == 0 else [shift(v, "x", 1) for v in kvs])]
    kvs = kvs + [shift(v, "core", 1) for v in kvs]
    n_kv = len(kvs)
    keys = n_kv * many

    out_blocks = fetch(w_out)
    in_blocks = fetch(w_in)
    down_blocks = fetch(w_down)

    attended, attended_t, lse = call(
        functools.partial(forward_kernel, n_kv),
        [((many, GW), BF), ((GW, many), F32), ((8, many), F32)],
        0,
        [query, *kvs],
        scratch=[
            pltpu.VMEM((keys, 2 * GW), BF),
            pltpu.VMEM((256, keys), BF),
            pltpu.VMEM((256, many), BF),
        ],
        flops=4 * keys * many * 256 * GH,
        bytes_accessed=4_000_000,
        name="attention_forward",
    )
    att_blocks = attended.reshape(TP, rows, GW)
    atts = [att_blocks[0]] + [shift(att_blocks[k], "z", -k) for k in range(1, TP)]
    groups = lax.rem(z + jnp.arange(TP, dtype=i32), TP)

    blocks = out_blocks + in_blocks + down_blocks
    offs = jnp.concatenate(
        [jnp.stack([o for _, o in blocks]).astype(i32), groups * GW]
    )
    mid = call(
        functools.partial(middle_kernel, len(out_blocks), len(in_blocks), len(down_blocks)),
        [
            ((rows, D), F32),
            ((rows, D), F32),
            ((rows, D), BF),
            ((rows, D), BF),
            ((rows, FF), BF),
            ((rows, 2 * FF), BF),
            ((8, D), F32),
        ]
        + [((rows, 256), BF)] * TP,
        1,
        [offs, *atts, tok, cot, gains, *[b for b, _ in blocks]],
        scratch=[
            pltpu.VMEM((D, D), BF),
            pltpu.VMEM((D, 2 * FF), BF),
            pltpu.VMEM((FF, D), BF),
            pltpu.SemaphoreType.DMA((len(blocks),)),
        ],
        any_ins=range(1 + TP + 3, 1 + TP + 3 + len(blocks)),
        flops=2 * rows * (2 * D * D + 2 * D * 2 * FF + 2 * FF * D),
        bytes_accessed=14_000_000,
        name="feed_forward",
    )
    result, grad_middle, grad_branch, h_two, mixed, grad_gate_up, gain_two_row = mid[:7]
    gatts = mid[7:]
    gas = [gatts[0]] + [shift(gatts[k], "z", k) for k in range(1, TP)]

    pieces, rows_d, rows_f, _, total = plan(shards)
    (packed,) = call(
        functools.partial(ffn_grads_kernel, shards),
        [((pieces, total, D), BF)],
        1,
        [groups, *atts, h_two, grad_gate_up, mixed, cot, grad_branch, gain_two_row],
        flops=2 * rows * (D * 2 * FF + FF * D + D * D),
        bytes_accessed=10_000_000,
        name="ffn_weight_grads",
    )
    ffn = packed.reshape(shards, 2, 2, total, D)
    ffn = reduce_scatter(ffn, "core", 1)
    ffn = reduce_scatter(ffn, "shard", 0)
    ffn = reduce_scatter(ffn, "x", 0)
    ffn = reduce_scatter(ffn.reshape(TP, total // TP, D), "z", 0)
    ffn = sum_over(ffn, "zo")

    dkv, dq = call(
        functools.partial(backward_kernel, n_kv),
        [((n_kv, many, 2 * GW), BF), ((many, 256), F32)],
        0,
        [query, *kvs, *gas, attended_t, lse],
        scratch=[
            pltpu.VMEM((keys, 2 * GW), BF),
            pltpu.VMEM((256, keys), BF),
            pltpu.VMEM((256, many), BF),
            pltpu.VMEM((256, many), BF),
            pltpu.VMEM((many, 2 * GW), BF),
            pltpu.VMEM((many, 2 * GW), BF),
            pltpu.VMEM((keys, 2 * GW), F32),
            pltpu.VMEM((256, many), F32),
        ],
        flops=10 * keys * many * 256 * GH,
        bytes_accessed=8_000_000,
        name="attention_backward",
    )
    half = n_kv // 2
    got = shift(dkv[half:], "core", 1)
    summed = (dkv[:half].astype(F32) + got.astype(F32)).astype(BF)
    outer = half // 2
    keep, got = summed[:outer], shift(summed[outer:], "x", 1)
    if outer > 1:
        both = (keep.astype(F32) + got.astype(F32)).astype(BF)
        sums = [both[0]] + [shift(both[k], "zo", -k) for k in range(1, outer)]
    else:
        sums = [keep[0], got[0]]

    grads = call(
        functools.partial(qkv_grads_kernel, pieces, len(sums)),
        [((pieces, D // pieces, WC), BF)] + [((rows, WC), BF)] * TP,
        0,
        [*sums, dq, cosine, sine, h_one, w_full],
        scratch=[pltpu.VMEM((many, WC), BF)],
        flops=2 * many * D * WC,
        bytes_accessed=5_000_000,
        name="qkv_weight_grads",
    )
    gqkv = [grads[1]] + [shift(grads[1 + k], "z", -k) for k in range(1, TP)]

    wq = grads[0].reshape(shards, 2, 2, D // pieces, WC)
    wq = reduce_scatter(wq, "core", 1)
    wq = reduce_scatter(wq, "shard", 0)
    wq = reduce_scatter(wq, "x", 0)
    wq = sum_over(wq, "zo")

    w_parts = [(w_groups, 0, y * part)]
    for k in range(1, shards):
        start = lax.rem(y - k + shards, shards) * part
        mine = shift(lax.dynamic_slice_in_dim(w_groups, 2 * c, 2, 0), "shard", k)
        w_parts.append((mine, 2 * c, start))
        w_parts.append((shift(mine, "core", 1), 2 * (1 - c), start))
    tail_offs = jnp.concatenate(
        [jnp.stack([jnp.asarray(v, i32) for _, a, b in w_parts for v in (a, b)]), groups]
    )
    (grad_tokens,) = call(
        functools.partial(tail_kernel, len(w_parts)),
        [((rows, D), F32)],
        1,
        [tail_offs, *gqkv, tok, grad_middle, gains, *[w for w, _, _ in w_parts]],
        scratch=[
            pltpu.VMEM((TP, D, WC), BF),
            pltpu.SemaphoreType.DMA((len(w_parts),)),
        ],
        any_ins=range(1 + TP + 3, 1 + TP + 3 + len(w_parts)),
        flops=2 * rows * D * WC * TP,
        bytes_accessed=6_000_000,
        name="token_grads",
    )

    idx = jnp.stack([z, x, c]).astype(i32)
    ffn = jnp.stack(gather(ffn, "z"))
    ffn = gather(ffn, "x")
    ffn = ffn + [shift(v, "core", 1) for v in ffn]
    g_in, g_out, g_down, g_gain = call(
        functools.partial(ffn_unpack_kernel, shards),
        [
            ((2, 2, rows_d, 2 * FF), F32),
            ((2, 2, rows_d, D), F32),
            ((2, 2, rows_f, D), F32),
            ((8, D), F32),
        ],
        1,
        [idx, *ffn],
        scratch=[pltpu.VMEM((total, D), F32)],
        bytes_accessed=12_000_000,
        name="ffn_unpack",
    )
    grad_gain_two = lax.dynamic_slice_in_dim(g_gain[0], y * part, part, 0)

    wq = gather(wq, "x")
    wq = gather(jnp.stack(wq), "z")
    wq = jnp.stack(wq, axis=1)
    other = shift(wq, "core", 1)
    g_qkv, g_one = call(
        qkv_unpack_kernel,
        [((2, 2, rows_d, 3 * D), F32), ((2, 2, rows_d, 128), F32)],
        1,
        [idx, wq[0], wq[1], other[0], other[1]],
        bytes_accessed=6_000_000,
        name="qkv_unpack",
    )
    grad_gain_one = g_one[..., 64].reshape(part)

    return (
        result[None],
        grad_tokens[None],
        grad_gain_one,
        g_qkv.reshape(part, 3 * D),
        g_out.reshape(part, D),
        grad_gain_two,
        g_in.reshape(part, 2 * FF),
        g_down.reshape(w_down.shape[0], D),
    )


def solution(mesh):
    blocks = mesh.shape["ctx"]
    fine = Mesh(
        mesh.devices.reshape(blocks // (TP * 4), TP, 2, 2, mesh.shape["shard"]), CTX + ("shard",)
    )
    rows, split = P("shard", CTX, None), P("shard", None)
    return jax.shard_map(
        per_device,
        mesh=fine,
        in_specs=(rows, P("shard"), split, split, P("shard"), split, split, rows),
        out_specs=(rows, rows, P("shard"), split, split, P("shard"), split, split),
        check_vma=False,
    )
```

time: 833 us -> 295 us (0.35)
  waiting for transfers between devices: 515 us -> 125 us
  matrix products: 155 us -> 0 us
  Pallas kernels: 0 us -> 57.9 us
  starting transfers between devices: 0.7 us -> 54.3 us
  blocking collectives: 48.4 us -> 0 us
  local copies, waits for them, and re-layouts: 71.3 us -> 42.2 us
  between operations: 15 us -> 1.12 us
    all_gather x6 -> x0, waiting for transfers between devices: 179 us -> none  [the longest x1 44.7 us: per_device(): lax.all_gather(w_qkv, 'shard', axis=0, tiled=True)]
    dot_general x96 -> x0, matrix products: 155 us -> none  [the longest x12 21 us: head_backward(): lax.dot_general(grad_scores, query_h, (((0,), (0,)), ((), ())), preferred...]
    reduce_scatter x4 -> x0, waiting for transfers between devices: 151 us -> none  [the longest x1 50.5 us: per_device(): lax.psum_scatter(grad_in.astype(jnp.bfloat16), 'shard', scatter_dimension...]
    ppermute x0 -> x46, waiting for transfers between devices: none -> 125 us  [shift(): return lax.ppermute(value, axis, [(i, (i + k) % n) for i in range(n)])]
    unnamed x15 -> x0, waiting for transfers between devices: 108 us -> none
    psum x1 -> x0, waiting for transfers between devices: 77.7 us -> none  [per_device(): lax.psum(attn_sums[1].astype(jnp.bfloat16), 'ctx').astype(jnp.float32)]
    pallas_call x0 -> x9, Pallas kernels: none -> 57.9 us  [call(): pl.pallas_call(body, out_shape=[jax.ShapeDtypeStruct(s, t) for s, t in ou...]
    ppermute x0 -> x46, starting transfers between devices: none -> 54.3 us  [shift(): return lax.ppermute(value, axis, [(i, (i + k) % n) for i in range(n)])]
  transfers between devices with their start and end apart: 13 -> 46, of which waited for: 12 -> 20; matrix products, arithmetic and copies ran while one was open for 13% -> 15% of each run, Pallas kernels for 0% -> 13%
where the time goes in v1:
time: 295 us; the launch traced here: 294 us
  waiting for transfers between devices  125 us (42%)
  Pallas kernels  57.9 us (20%)
  starting transfers between devices  54.3 us (18%)
  local copies, waits for them, and re-layouts  42.2 us (14%)
  other arithmetic  13.4 us (5%)
    ppermute x46, waiting for transfers between devices, shift(): return lax.ppermute(value, axis, [(i, (i + k) % n) for i in range(n)])  125 us
    pallas_call x9, Pallas kernels, call(): pl.pallas_call(body, out_shape=[jax.ShapeDtypeStruct(s, t) for s, t in ou...  57.9 us
    ppermute x46, starting transfers between devices, shift(): return lax.ppermute(value, axis, [(i, (i + k) % n) for i in range(n)])  54.3 us
    unnamed x69, local copies, waits for them, and re-layouts  10.8 us
    convert_element_type x7, other arithmetic, reduce_scatter(): return (own if total is None else own + total).astype(BF)  8.69 us
    squeeze x8, local copies, waits for them, and re-layouts, pick(): return lax.dynamic_index_in_dim(value, index, dim, keepdims=False)  6.56 us
  transfers between devices with their start and end apart: 46, of which 20 were waited for; matrix products, arithmetic and copies ran while one was open for 15% of the time, Pallas kernels for 13%

profile of v1, /device:TPU:0, one launch (start us, length us, event | category | flops | bytes accessed | tf_op | source)
XLA Modules:
  0.0 294.0 jit_solution(2921699336975189527)
XLA Ops:
  0.6 3.1 %collective-permute-start = (bf16[128,768]{1,0:T(8,128)(2,1)}, bf16[128,768]{1,0:T(8,128)(2,1)}, u32[]{:S(2)}, u32[]{:S(2)}) collective-permute-start(bf16[128,768]{1,0:T(8,128)(2,1)} %bitcast.113), channel_id=1, source_target_pairs={{0,8},{8,16},{16,24},{24,0},{1,9},{9,17},{17,25},{25,1},{2,10},{10... | collective-permute-start | bytes 589832 | tf_op jit(solution)/shard_map/ppermute | solution.py:407
  3.7 2.6 collective-permute-start.1
  7.6 3.9 %copy.20 = bf16[384,2304]{0,1:T(8,128)(2,1)} copy(bf16[384,2304]{1,0:T(8,128)(2,1)} %param.10) | data formatting | bytes 3538944 | tf_op args[2]
  11.5 2.7 copy.21
  15.9 4.1 %concatenate.10.refs_7_ = bf16[4,384,640]{2,1,0:T(8,128)(2,1)S(1)} concatenate(bf16[4,384,192]{2,1,0:T(8,128)(2,1)} %get-tuple-element.74, bf16[4,384,192]{2,1,0:T(8,128)(2,1)} %get-tuple-element.73, bf16[4,384,192]{2,1,0:T(8,128)(2,1)S(1)} %get-tuple-element.72, bf16[4,384,2]{2,1,0:T(8,128)(2,1)S(1)} %broadcast_in_dim.27, bf16[4,384,62]{2,1,0:T(8,128)(2,1)S(1)} %broadcast_in_dim.28), dimensions={2} | concatenate | bytes 3932160 | tf_op jit(solution)/shard_map/concatenate | solution.py:466
  21.6 2.2 constant_dynamic-slice_fusion.3
  25.3 1.8 fusion.6
  27.1 7.3 %collective-permute-done.3.refs_5_ = bf16[384,640]{1,0:T(8,128)(2,1)} collective-permute-done((bf16[384,640]{1,0:T(8,128)(2,1)S(1)}, bf16[384,640]{1,0:T(8,128)(2,1)}, u32[]{:S(2)}, u32[]{:S(2)}) %collective-permute-start.3) | collective-permute-done | bytes 491552 | tf_op jit(solution)/shard_map/ppermute | solution.py:407
  34.4 4.1 %front.1 = (bf16[512,256]{1,0:T(8,128)(2,1)}, bf16[512,384]{1,0:T(8,128)(2,1)}, bf16[512,768]{1,0:T(8,128)(2,1)}, bf16[768,640]{1,0:T(8,128)(2,1)}, f32[8,768]{1,0:T(8,128)}) custom-call(s32[2]{0:T(128)} %pad_add_fusion.offs, bf16[128,768]{1,0:T(8,128)(2,1)} %bitcast.116, bf16[128,768]{1,0:T(8,128)(2,1)} %collective-permute-done.refs_1_, ...), custom_call_target="tpu_custom_call" | custom-call | flops 503316480 | bytes 5000000 | tf_op jit(solution)/shard_map/front/pallas_call | solution.py:52
  40.0 1.6 collective-permute-start.14
  41.6 5.0 %collective-permute-done.4.refs_1_ = bf16[512,384]{1,0:T(8,128)(2,1)} collective-permute-done((bf16[512,384]{1,0:T(8,128)(2,1)}, bf16[512,384]{1,0:T(8,128)(2,1)}, u32[]{:S(2)}, u32[]{:S(2)}) %collective-permute-start.4) | collective-permute-done | bytes 393248 | tf_op jit(solution)/shard_map/ppermute | solution.py:407
  49.1 4.2 %collective-permute-done.12.refs_11_ = bf16[192,2304]{1,0:T(8,128)(2,1)} collective-permute-done((bf16[192,2304]{1,0:T(8,128)(2,1)}, bf16[192,2304]{1,0:T(8,128)(2,1)}, u32[]{:S(2)}, u32[]{:S(2)}) %collective-permute-start.12) | collective-permute-done | bytes 884768 | tf_op jit(solution)/shard_map/ppermute | solution.py:407
  53.9 13.1 %collective-permute-done.10.refs_8_ = bf16[192,768]{1,0:T(8,128)(2,1)S(1)} collective-permute-done((bf16[192,768]{1,0:T(8,128)(2,1)S(1)}, bf16[192,768]{1,0:T(8,128)(2,1)S(1)}, u32[]{:S(2)}, u32[]{:S(2)}) %collective-permute-start.10) | collective-permute-done | bytes 294944 | tf_op jit(solution)/shard_map/ppermute | solution.py:407
  68.4 9.5 %attention_forward.1 = (bf16[512,192]{1,0:T(8,128)(2,1)}, f32[192,512]{1,0:T(8,128)}, f32[8,512]{1,0:T(8,128)}) custom-call(bf16[512,256]{1,0:T(8,128)(2,1)} %get-tuple-element.40.q_ref, bf16[512,384]{1,0:T(8,128)(2,1)} %get-tuple-element.41.refs_0_, bf16[512,384]{1,0:T(8,128)(2,1)} %collective-permute-done.4.refs_1_, bf16[512,384]{1,0:T(8,128)(2,1)} %copy-done.24, ...), custom_call_target="tpu_custom_call" | custom-call | flops 3221225472 | bytes 4000000 | tf_op jit(solution)/shard_map/attention_forward/pallas_call | solution.py:52
  77.9 1.6 fusion.18
  80.0 1.7 collective-permute-start.8
  84.5 3.1 %collective-permute-done.8.refs_2_ = bf16[128,192]{1,0:T(8,128)(2,1)S(1)} collective-permute-done((bf16[128,192]{1,0:T(8,128)(2,1)}, bf16[128,192]{1,0:T(8,128)(2,1)S(1)}, u32[]{:S(2)}, u32[]{:S(2)}) %collective-permute-start.8) | collective-permute-done | bytes 49184 | tf_op jit(solution)/shard_map/ppermute | solution.py:407
  89.4 8.1 %feed_forward.1 = (f32[128,768]{1,0:T(8,128)}, f32[128,768]{1,0:T(8,128)}, bf16[128,768]{1,0:T(8,128)(2,1)}, bf16[128,768]{1,0:T(8,128)(2,1)}, bf16[128,1152]{1,...) custom-call(s32[13]{0:T(128)} %concatenate.9.offs, ...), custom_call_target="tpu_custom_call" | custom-call | flops 1660944384 | bytes 14000000 | tf_op jit(solution)/shard_map/feed_forward/pallas_call | solution.py:52
  97.4 6.2 %ffn_weight_grads.1 = bf16[8,576,768]{2,1,0:T(8,128)(2,1)} custom-call(s32[4]{0:T(128)} %compare_select_fusion.2.groups, bf16[128,192]{1,0:T(8,128)(2,1)} %get-tuple-element.87.refs_0_, bf16[128,192]{1,0:T(8,128)(2,1)} %copy-done.15, bf16[128,192]{1,0:T(8,128)(2,1)} %copy-done.16, bf16[128,192]{1,0:T(8,128)(2,1)} %copy-done.17, ...), custom_call_target="tpu_custom_call" | custom-call | flops 830472192 | bytes 10000000 | tf_op jit(solution)/shard_map/ffn_weight_grads/pallas_call | solution.py:52
  103.6 4.1 %dynamic-slice_bitcast_fusion = bf16[2,2,576,768]{3,2,1,0:T(8,128)(2,1)} fusion(bf16[2,2,2,576,768]{4,3,2,1,0:T(8,128)(2,1)} %bitcast.107, s32[]{:T(128)S(6)} %select_n.84), kind=kLoop, calls=%fused_computation.4 | loop fusion | bytes 7077892 | tf_op jit(solution)/shard_map/jit(dynamic_index_in_dim)/squeeze | solution.py:415
  109.3 2.3 collective-permute-start.18
  111.7 2.6 collective-permute-done.34
  114.3 3.9 %fusion = bf16[2,2,576,768]{3,2,1,0:T(8,128)(2,1)S(1)} fusion(bf16[2,2,576,768]{3,2,1,0:T(8,128)(2,1)} %collective-permute-done.34, bf16[2,2,2,576,768]{4,3,2,1,0:T(8,128)(2,1)} %bitcast.108, s32[]{:T(128)S(6)} %select_n.83), kind=kLoop, calls=%fused_computation.1 | loop fusion | flops 7077888 | bytes 10616836 | tf_op jit(solution)/shard_map/convert_element_type | solution.py:425
  118.2 1.8 copy-done.1
  123.5 10.7 %attention_backward.1 = (bf16[4,512,384]{2,1,0:T(8,128)(2,1)}, f32[512,256]{1,0:T(8,128)}) custom-call(bf16[512,256]{1,0:T(8,128)(2,1)} %get-tuple-element.40.q_ref, bf16[512,384]{1,0:T(8,128)(2,1)} %get-tuple-element.41.refs_0_, bf16[512,384]{1,0:T(8,128)(2,1)} %collective-permute-done.4.refs_1_, bf16[512,384]{1,0:T(8,128)(2,1)} %copy-done.24, ...), custom_call_target="tpu_custom_call" | custom-call | flops 8053063680 | bytes 8000000 | tf_op jit(solution)/shard_map/attention_backward/pallas_call | solution.py:52
  135.6 2.3 collective-permute-done.19
  142.1 8.4 %collective-permute-done.20 = bf16[1,512,384]{2,1,0:T(8,128)(2,1)} collective-permute-done((bf16[1,512,384]{2,1,0:T(8,128)(2,1)}, bf16[1,512,384]{2,1,0:T(8,128)(2,1)}, u32[]{:S(2)}, u32[]{:S(2)}) %collective-permute-start.20) | collective-permute-done | bytes 393248 | tf_op jit(solution)/shard_map/ppermute | solution.py:407
  150.5 4.5 %qkv_weight_grads.1 = (bf16[8,96,640]{2,1,0:T(8,128)(2,1)}, bf16[128,640]{1,0:T(8,128)(2,1)}, bf16[128,640]{1,0:T(8,128)(2,1)}, bf16[128,640]{1,0:T(8,128)(2,1)}, bf16[128,640]{1,0:T(8,128)(2,1)}) custom-call(bf16[512,384]{1,0:T(8,128)(2,1)} %get-tuple-element.83.refs_0_, bf16[512,384]{1,0:T(8,128)(2,1)} %bitcast.21.refs_1_, ...), custom_call_target="tpu_custom_call" | custom-call | flops 503316480 | bytes 5000000 | tf_op jit(solution)/shard_map/qkv_weight_grads/pallas_call | solution.py:52
  155.0 8.0 %collective-permute-done.35 = bf16[2,576,768]{2,1,0:T(8,128)(2,1)} collective-permute-done((bf16[2,576,768]{2,1,0:T(8,128)(2,1)}, bf16[2,576,768]{2,1,0:T(8,128)(2,1)}, u32[]{:S(2)}, u32[]{:S(2)}) %collective-permute-start.35) | collective-permute-done | bytes 1769504 | tf_op jit(solution)/shard_map/ppermute | solution.py:407
  163.1 1.9 fusion.1
  168.8 14.5 %collective-permute-done.24.refs_8_ = bf16[2,384,640]{2,1,0:T(8,128)(2,1)} collective-permute-done((bf16[2,384,640]{2,1,0:T(8,128)(2,1)}, bf16[2,384,640]{2,1,0:T(8,128)(2,1)}, u32[]{:S(2)}, u32[]{:S(2)}) %collective-permute-start.24) | collective-permute-done | bytes 983072 | tf_op jit(solution)/shard_map/ppermute | solution.py:407
  184.7 1.8 collective-permute-start.27
  190.1 1.9 collective-permute-start.37
  195.0 1.6 collective-permute-done.39
  196.6 12.4 %collective-permute-done.38 = bf16[144,768]{1,0:T(8,128)(2,1)S(1)} collective-permute-done((bf16[144,768]{1,0:T(8,128)(2,1)S(1)}, bf16[144,768]{1,0:T(8,128)(2,1)S(1)}, u32[]{:S(2)}, u32[]{:S(2)}) %collective-permute-start.38) | collective-permute-done | bytes 221216 | tf_op jit(solution)/shard_map/ppermute | solution.py:407
  209.2 9.9 %collective-permute-start.41 = (bf16[144,768]{1,0:T(8,128)(2,1)S(1)}, bf16[144,768]{1,0:T(8,128)(2,1)S(1)}, u32[]{:S(2)}, u32[]{:S(2)}) collective-permute-start(bf16[144,768]{1,0:T(8,128)(2,1)S(1)} %fusion.5), channel_id=1, source_target_pairs={{0,16},{8,24},{16,0},{24,8},{1,17},{9,25},{17,1},{25,9},{2,18},{10... | collective-permute-start | bytes 663560 | tf_op jit(solution)/shard_map/ppermute | solution.py:407
  219.1 1.9 collective-permute-start.40
  222.6 16.9 %collective-permute-done.41 = bf16[144,768]{1,0:T(8,128)(2,1)S(1)} collective-permute-done((bf16[144,768]{1,0:T(8,128)(2,1)S(1)}, bf16[144,768]{1,0:T(8,128)(2,1)S(1)}, u32[]{:S(2)}, u32[]{:S(2)}) %collective-permute-start.41) | collective-permute-done | bytes 221216 | tf_op jit(solution)/shard_map/ppermute | solution.py:407
  241.5 1.9 collective-permute-start.30
  243.4 5.6 %collective-permute-done.32 = bf16[2,96,640]{2,1,0:T(8,128)(2,1)S(1)} collective-permute-done((bf16[2,96,640]{2,1,0:T(8,128)(2,1)S(1)}, bf16[2,96,640]{2,1,0:T(8,128)(2,1)S(1)}, u32[]{:S(2)}, u32[]{:S(2)}) %collective-permute-start.32) | collective-permute-done | bytes 245792 | tf_op jit(solution)/shard_map/ppermute | solution.py:407
  249.0 4.9 %collective-permute-done.31 = bf16[2,96,640]{2,1,0:T(8,128)(2,1)S(1)} collective-permute-done((bf16[2,96,640]{2,1,0:T(8,128)(2,1)S(1)}, bf16[2,96,640]{2,1,0:T(8,128)(2,1)S(1)}, u32[]{:S(2)}, u32[]{:S(2)}) %collective-permute-start.31) | collective-permute-done | bytes 245792 | tf_op jit(solution)/shard_map/ppermute | solution.py:407
  255.4 1.8 collective-permute-start.22
  257.3 3.4 %collective-permute-done.21.refs_1_ = bf16[128,640]{1,0:T(8,128)(2,1)S(1)} collective-permute-done((bf16[128,640]{1,0:T(8,128)(2,1)S(1)}, bf16[128,640]{1,0:T(8,128)(2,1)S(1)}, u32[]{:S(2)}, u32[]{:S(2)}) %collective-permute-start.21) | collective-permute-done | bytes 163872 | tf_op jit(solution)/shard_map/ppermute | solution.py:407
  263.5 8.5 %collective-permute-done.22.refs_2_ = bf16[128,640]{1,0:T(8,128)(2,1)S(1)} collective-permute-done((bf16[128,640]{1,0:T(8,128)(2,1)}, bf16[128,640]{1,0:T(8,128)(2,1)S(1)}, u32[]{:S(2)}, u32[]{:S(2)}) %collective-permute-start.22) | collective-permute-done | bytes 163872 | tf_op jit(solution)/shard_map/ppermute | solution.py:407
  272.7 5.6 %token_grads.1 = f32[128,768]{1,0:T(8,128)} custom-call(s32[10]{0:T(128)} %concatenate.11.offs, bf16[128,640]{1,0:T(8,128)(2,1)} %get-tuple-element.55.refs_0_, bf16[128,640]{1,0:T(8,128)(2,1)} %copy-done.18, bf16[128,640]{1,0:T(8,128)(2,1)} %copy-done.19, bf16[128,640]{1,0:T(8,128)(2,1)} %copy-done.20, bf16[128,768]{1,0:T(8,128)(2,1)} %bitcast.118, ...), custom_call_target="tpu_custom_call" | custom-call | flops 503316480 | bytes 6000000 | tf_op jit(solution)/shard_map/token_grads/pallas_call | solution.py:52
  279.4 2.2 slice_bitcast_fusion.3
  281.6 3.8 %qkv_unpack.1 = (f32[2,2,96,2304]{3,2,1,0:T(8,128)}, f32[2,2,96,128]{3,2,1,0:T(8,128)}) custom-call(s32[3]{0:T(128)} %pad_add_fusion.1.idx, bf16[4,96,640]{2,1,0:T(8,128)(2,1)} %get-tuple-element.78.refs_0_, bf16[4,96,640]{2,1,0:T(8,128)(2,1)} %get-tuple-element.77.refs_1_, bf16[4,96,640]{2,1,0:T(8,128)(2,1)} %get-tuple-element.76.refs_2_, ...), custom_call_target="tpu_custom_call" | custom-call | bytes 6000000 | tf_op jit(solution)/shard_map/qkv_unpack/pallas_call | solution.py:52
  287.2 5.5 %ffn_unpack.1 = (f32[2,2,96,2304]{3,2,1,0:T(8,128)}, f32[2,2,96,768]{3,2,1,0:T(8,128)}, f32[2,2,144,768]{3,2,1,0:T(8,128)}, f32[8,768]{1,0:T(8,128)}) custom-call(s32[3]{0:T(128)} %pad_add_fusion.1.idx, bf16[4,144,768]{2,1,0:T(8,128)(2,1)} %copy-done.5, bf16[4,144,768]{2,1,0:T(8,128)(2,1)} %collective-permute-done.43.refs_1_, ...), custom_call_target="tpu_custom_call" | custom-call | bytes 12000000 | tf_op jit(solution)/shard_map/ffn_unpack/pallas_call | solution.py:52
  (176 shorter events, 52.5 us)
Async XLA Ops:
  0.6 26.4 %collective-permute-start = (bf16[128,768]{1,0:T(8,128)(2,1)}, bf16[128,768]{1,0:T(8,128)(2,1)}, u32[]{:S(2)}, u32[]{:S(2)}) collective-permute-start(bf16[128,768]{1,0:T(8,128)(2,1)} %bitcast.113), channel_id=1, source_target_pairs={{0,8},{8,16},{16,24},{24,0},{1,9},{9,17},{17,25},{25,1},{2,10},{10... | collective-permute-start | bytes 589832 | tf_op jit(solution)/shard_map/ppermute | solution.py:407
  3.7 23.4 %collective-permute-start.1 = (bf16[128,768]{1,0:T(8,128)(2,1)}, bf16[128,768]{1,0:T(8,128)(2,1)}, u32[]{:S(2)}, u32[]{:S(2)}) collective-permute-start(bf16[128,768]{1,0:T(8,128)(2,1)} %bitcast.114), channel_id=1, source_target_pairs={{0,16},{8,24},{16,0},{24,8},{1,17},{9,25},{17,1},{25,9},{2,18},{10... | collective-permute-start | bytes 589832 | tf_op jit(solution)/shard_map/ppermute | solution.py:407
  6.3 20.8 %collective-permute-start.2 = (bf16[128,768]{1,0:T(8,128)(2,1)}, bf16[128,768]{1,0:T(8,128)(2,1)}, u32[]{:S(2)}, u32[]{:S(2)}) collective-permute-start(bf16[128,768]{1,0:T(8,128)(2,1)} %bitcast.115), channel_id=1, source_target_pairs={{0,24},{8,0},{16,8},{24,16},{1,25},{9,1},{17,9},{25,17},{2,26},{10... | collective-permute-start | bytes 589832 | tf_op jit(solution)/shard_map/ppermute | solution.py:407
  19.9 120.6 %copy-start = (bf16[4,384,640]{2,1,0:T(8,128)(2,1)}, bf16[4,384,640]{2,1,0:T(8,128)(2,1)S(1)}, u32[]{:S(2)}) copy-start(bf16[4,384,640]{2,1,0:T(8,128)(2,1)S(1)} %concatenate.10.refs_7_) | copy-start | bytes 5898244
  20.0 14.3 %collective-permute-start.3 = (bf16[384,640]{1,0:T(8,128)(2,1)S(1)}, bf16[384,640]{1,0:T(8,128)(2,1)}, u32[]{:S(2)}, u32[]{:S(2)}) collective-permute-start(bf16[384,640]{1,0:T(8,128)(2,1)S(1)} %dynamic-slice_bitcast_fusion.4.refs_4_), channel_id=1, source_target_pairs={{0,1},{1,0},{2,3},{3,2},{4,5},{5,4},{6,7},{7,6},{8,9},{9,8},{10,11... | collective-permute-start | bytes 1474568 | tf_op jit(solution)/shard_map/ppermute | solution.py:407
  23.8 29.5 %collective-permute-start.12 = (bf16[192,2304]{1,0:T(8,128)(2,1)}, bf16[192,2304]{1,0:T(8,128)(2,1)}, u32[]{:S(2)}, u32[]{:S(2)}) collective-permute-start(bf16[192,2304]{1,0:T(8,128)(2,1)} %constant_dynamic-slice_fusion.3), channel_id=1, source_target_pairs={{0,1},{1,0},{2,3},{3,2},{4,5},{5,4},{6,7},{7,6},{8,9},{9,8},{10,11... | collective-permute-start | bytes 2654216 | tf_op jit(solution)/shard_map/ppermute | solution.py:407
  38.4 8.1 %collective-permute-start.4 = (bf16[512,384]{1,0:T(8,128)(2,1)}, bf16[512,384]{1,0:T(8,128)(2,1)}, u32[]{:S(2)}, u32[]{:S(2)}) collective-permute-start(bf16[512,384]{1,0:T(8,128)(2,1)} %get-tuple-element.41.refs_0_), channel_id=1, source_target_pairs={{0,4},{4,0},{1,5},{5,1},{2,6},{6,2},{3,7},{7,3},{8,12},{12,8},{9,1... | collective-permute-start | bytes 1179656 | tf_op jit(solution)/shard_map/ppermute | solution.py:407
  40.0 27.0 %collective-permute-start.14 = (bf16[288,768]{1,0:T(8,128)(2,1)S(1)}, bf16[288,768]{1,0:T(8,128)(2,1)S(1)}, u32[]{:S(2)}, u32[]{:S(2)}) collective-permute-start(bf16[288,768]{1,0:T(8,128)(2,1)S(1)} %constant_dynamic-slice_fusion.2), channel_id=1, source_target_pairs={{0,1},{1,0},{2,3},{3,2},{4,5},{5,4},{6,7},{7,6},{8,9},{9,8},{10,11... | collective-permute-start | bytes 1327112 | tf_op jit(solution)/shard_map/ppermute | solution.py:407
  41.6 25.9 %collective-permute-start.5 = (bf16[512,384]{1,0:T(8,128)(2,1)}, bf16[512,384]{1,0:T(8,128)(2,1)S(1)}, u32[]{:S(2)}, u32[]{:S(2)}) collective-permute-start(bf16[512,384]{1,0:T(8,128)(2,1)} %get-tuple-element.41.refs_0_), channel_id=1, source_target_pairs={{0,2},{2,0},{1,3},{3,1},{4,6},{6,4},{5,7},{7,5},{8,10},{10,8},{9,1... | collective-permute-start | bytes 1179656 | tf_op jit(solution)/shard_map/ppermute | solution.py:407
  46.5 21.0 %collective-permute-start.6 = (bf16[512,384]{1,0:T(8,128)(2,1)}, bf16[512,384]{1,0:T(8,128)(2,1)S(1)}, u32[]{:S(2)}, u32[]{:S(2)}) collective-permute-start(bf16[512,384]{1,0:T(8,128)(2,1)} %collective-permute-done.4.refs_1_), channel_id=1, source_target_pairs={{0,2},{2,0},{1,3},{3,1},{4,6},{6,4},{5,7},{7,5},{8,10},{10,8},{9,1... | collective-permute-start | bytes 1179656 | tf_op jit(solution)/shard_map/ppermute | solution.py:407
  47.5 19.5 %collective-permute-start.10 = (bf16[192,768]{1,0:T(8,128)(2,1)S(1)}, bf16[192,768]{1,0:T(8,128)(2,1)S(1)}, u32[]{:S(2)}, u32[]{:S(2)}) collective-permute-start(bf16[192,768]{1,0:T(8,128)(2,1)S(1)} %constant_dynamic-slice_fusion.4), channel_id=1, source_target_pairs={{0,1},{1,0},{2,3},{3,2},{4,5},{5,4},{6,7},{7,6},{8,9},{9,8},{10,11... | collective-permute-start | bytes 884744 | tf_op jit(solution)/shard_map/ppermute | solution.py:407
  53.3 35.1 %collective-permute-start.13 = (bf16[192,2304]{1,0:T(8,128)(2,1)}, bf16[192,2304]{1,0:T(8,128)(2,1)S(1)}, u32[]{:S(2)}, u32[]{:S(2)}) collective-permute-start(bf16[192,2304]{1,0:T(8,128)(2,1)} %collective-permute-done.12.refs_11_), channel_id=1, source_target_pairs={{0,2},{2,0},{1,3},{3,1},{4,6},{6,4},{5,7},{7,5},{8,10},{10,8},{9,1... | collective-permute-start | bytes 2654216 | tf_op jit(solution)/shard_map/ppermute | solution.py:407
  67.0 14.7 %collective-permute-start.11 = (bf16[192,768]{1,0:T(8,128)(2,1)S(1)}, bf16[192,768]{1,0:T(8,128)(2,1)S(1)}, u32[]{:S(2)}, u32[]{:S(2)}) collective-permute-start(bf16[192,768]{1,0:T(8,128)(2,1)S(1)} %collective-permute-done.10.refs_8_), channel_id=1, source_target_pairs={{0,2},{2,0},{1,3},{3,1},{4,6},{6,4},{5,7},{7,5},{8,10},{10,8},{9,1... | collective-permute-start | bytes 884744 | tf_op jit(solution)/shard_map/ppermute | solution.py:407
  67.0 17.5 %collective-permute-start.15 = (bf16[288,768]{1,0:T(8,128)(2,1)S(1)}, bf16[288,768]{1,0:T(8,128)(2,1)}, u32[]{:S(2)}, u32[]{:S(2)}) collective-permute-start(bf16[288,768]{1,0:T(8,128)(2,1)S(1)} %collective-permute-done.14.refs_14_), channel_id=1, source_target_pairs={{0,2},{2,0},{1,3},{3,1},{4,6},{6,4},{5,7},{7,5},{8,10},{10,8},{9,1... | collective-permute-start | bytes 1327112 | tf_op jit(solution)/shard_map/ppermute | solution.py:407
  79.5 5.0 %collective-permute-start.7 = (bf16[128,192]{1,0:T(8,128)(2,1)}, bf16[128,192]{1,0:T(8,128)(2,1)S(1)}, u32[]{:S(2)}, u32[]{:S(2)}) collective-permute-start(bf16[128,192]{1,0:T(8,128)(2,1)} %get-tuple-element.86), channel_id=1, source_target_pairs={{0,24},{8,0},{16,8},{24,16},{1,25},{9,1},{17,9},{25,17},{2,26},{10... | collective-permute-start | bytes 147464 | tf_op jit(solution)/shard_map/ppermute | solution.py:407
  80.0 7.6 %collective-permute-start.8 = (bf16[128,192]{1,0:T(8,128)(2,1)}, bf16[128,192]{1,0:T(8,128)(2,1)S(1)}, u32[]{:S(2)}, u32[]{:S(2)}) collective-permute-start(bf16[128,192]{1,0:T(8,128)(2,1)} %get-tuple-element.85), channel_id=1, source_target_pairs={{0,16},{8,24},{16,0},{24,8},{1,17},{9,25},{17,1},{25,9},{2,18},{10... | collective-permute-start | bytes 147464 | tf_op jit(solution)/shard_map/ppermute | solution.py:407
  82.4 6.1 %collective-permute-start.9 = (bf16[128,192]{1,0:T(8,128)(2,1)S(1)}, bf16[128,192]{1,0:T(8,128)(2,1)S(1)}, u32[]{:S(2)}, u32[]{:S(2)}) collective-permute-start(bf16[128,192]{1,0:T(8,128)(2,1)S(1)} %get-tuple-element.84), channel_id=1, source_target_pairs={{0,8},{8,16},{16,24},{24,0},{1,9},{9,17},{17,25},{25,1},{2,10},{10... | collective-permute-start | bytes 147464 | tf_op jit(solution)/shard_map/ppermute | solution.py:407
  107.7 6.6 %collective-permute-start.34 = (bf16[2,2,576,768]{3,2,1,0:T(8,128)(2,1)}, bf16[2,2,576,768]{3,2,1,0:T(8,128)(2,1)}, u32[]{:S(2)}, u32[]{:S(2)}) collective-permute-start(bf16[2,2,576,768]{3,2,1,0:T(8,128)(2,1)} %dynamic-slice_bitcast_fusion), channel_id=1, source_target_pairs={{0,2},{2,0},{1,3},{3,1},{4,6},{6,4},{5,7},{7,5},{8,10},{10,8},{9,1... | collective-permute-start | bytes 10616840 | tf_op jit(solution)/shard_map/ppermute | solution.py:407
  107.7 15.1 %collective-permute-start.16 = (bf16[128,256]{1,0:T(8,128)(2,1)S(1)}, bf16[128,256]{1,0:T(8,128)(2,1)S(1)}, u32[]{:S(2)}, u32[]{:S(2)}) collective-permute-start(bf16[128,256]{1,0:T(8,128)(2,1)S(1)} %copy-done.30), channel_id=1, source_target_pairs={{0,8},{8,16},{16,24},{24,0},{1,9},{9,17},{17,25},{25,1},{2,10},{10... | collective-permute-start | bytes 196616 | tf_op jit(solution)/shard_map/ppermute | solution.py:407
  107.7 15.1 %collective-permute-start.17 = (bf16[128,256]{1,0:T(8,128)(2,1)S(1)}, bf16[128,256]{1,0:T(8,128)(2,1)S(1)}, u32[]{:S(2)}, u32[]{:S(2)}) collective-permute-start(bf16[128,256]{1,0:T(8,128)(2,1)S(1)} %copy-done.29), channel_id=1, source_target_pairs={{0,16},{8,24},{16,0},{24,8},{1,17},{9,25},{17,1},{25,9},{2,18},{10... | collective-permute-start | bytes 196616 | tf_op jit(solution)/shard_map/ppermute | solution.py:407
  109.3 13.5 %collective-permute-start.18 = (bf16[128,256]{1,0:T(8,128)(2,1)S(1)}, bf16[128,256]{1,0:T(8,128)(2,1)S(1)}, u32[]{:S(2)}, u32[]{:S(2)}) collective-permute-start(bf16[128,256]{1,0:T(8,128)(2,1)S(1)} %copy-done.28), channel_id=1, source_target_pairs={{0,24},{8,0},{16,8},{24,16},{1,25},{9,1},{17,9},{25,17},{2,26},{10... | collective-permute-start | bytes 196616 | tf_op jit(solution)/shard_map/ppermute | solution.py:407
  121.3 41.8 %collective-permute-start.35 = (bf16[2,576,768]{2,1,0:T(8,128)(2,1)}, bf16[2,576,768]{2,1,0:T(8,128)(2,1)}, u32[]{:S(2)}, u32[]{:S(2)}) collective-permute-start(bf16[2,576,768]{2,1,0:T(8,128)(2,1)} %dynamic-slice_bitcast_fusion.1), channel_id=1, source_target_pairs={{0,1},{1,0},{2,3},{3,2},{4,5},{5,4},{6,7},{7,6},{8,9},{9,8},{10,11... | collective-permute-start | bytes 5308424 | tf_op jit(solution)/shard_map/ppermute | solution.py:407
  135.5 2.4 collective-permute-start.19
  139.1 11.5 %collective-permute-start.20 = (bf16[1,512,384]{2,1,0:T(8,128)(2,1)}, bf16[1,512,384]{2,1,0:T(8,128)(2,1)}, u32[]{:S(2)}, u32[]{:S(2)}) collective-permute-start(bf16[1,512,384]{2,1,0:T(8,128)(2,1)} %get-tuple-element.82), channel_id=1, source_target_pairs={{0,4},{4,0},{1,5},{5,1},{2,6},{6,2},{3,7},{7,3},{8,12},{12,8},{9,1... | collective-permute-start | bytes 1179656 | tf_op jit(solution)/shard_map/ppermute | solution.py:407
  141.6 41.7 %collective-permute-start.24 = (bf16[2,384,640]{2,1,0:T(8,128)(2,1)}, bf16[2,384,640]{2,1,0:T(8,128)(2,1)}, u32[]{:S(2)}, u32[]{:S(2)}) collective-permute-start(bf16[2,384,640]{2,1,0:T(8,128)(2,1)} %constant_dynamic-slice_fusion.1), channel_id=1, source_target_pairs={{0,1},{1,0},{2,3},{3,2},{4,5},{5,4},{6,7},{7,6},{8,9},{9,8},{10,11... | collective-permute-start | bytes 2949128 | tf_op jit(solution)/shard_map/ppermute | solution.py:407
  167.1 20.4 %collective-permute-start.36 = (bf16[576,768]{1,0:T(8,128)(2,1)}, bf16[576,768]{1,0:T(8,128)(2,1)}, u32[]{:S(2)}, u32[]{:S(2)}) collective-permute-start(bf16[576,768]{1,0:T(8,128)(2,1)} %dynamic-slice_bitcast_fusion.2), channel_id=1, source_target_pairs={{0,4},{4,0},{1,5},{5,1},{2,6},{6,2},{3,7},{7,3},{8,12},{12,8},{9,1... | collective-permute-start | bytes 2654216 | tf_op jit(solution)/shard_map/ppermute | solution.py:407
  168.7 14.6 %collective-permute-start.26 = (bf16[2,2,96,640]{3,2,1,0:T(8,128)(2,1)S(1)}, bf16[2,2,96,640]{3,2,1,0:T(8,128)(2,1)}, u32[]{:S(2)}, u32[]{:S(2)}) collective-permute-start(bf16[2,2,96,640]{3,2,1,0:T(8,128)(2,1)S(1)} %dynamic-slice_bitcast_fusion.3), channel_id=1, source_target_pairs={{0,2},{2,0},{1,3},{3,1},{4,6},{6,4},{5,7},{7,5},{8,10},{10,8},{9,1... | collective-permute-start | bytes 1474568 | tf_op jit(solution)/shard_map/ppermute | solution.py:407
  183.3 72.1 %collective-permute-start.25 = (bf16[2,384,640]{2,1,0:T(8,128)(2,1)}, bf16[2,384,640]{2,1,0:T(8,128)(2,1)S(1)}, u32[]{:S(2)}, u32[]{:S(2)}) collective-permute-start(bf16[2,384,640]{2,1,0:T(8,128)(2,1)} %collective-permute-done.24.refs_8_), channel_id=1, source_target_pairs={{0,2},{2,0},{1,3},{3,1},{4,6},{6,4},{5,7},{7,5},{8,10},{10,8},{9,1... | collective-permute-start | bytes 2949128 | tf_op jit(solution)/shard_map/ppermute | solution.py:407
  184.7 8.7 %collective-permute-start.27 = (bf16[2,96,640]{2,1,0:T(8,128)(2,1)S(1)}, bf16[2,96,640]{2,1,0:T(8,128)(2,1)S(1)}, u32[]{:S(2)}, u32[]{:S(2)}) collective-permute-start(bf16[2,96,640]{2,1,0:T(8,128)(2,1)S(1)} %dynamic-slice_bitcast_fusion.5), channel_id=1, source_target_pairs={{0,1},{1,0},{2,3},{3,2},{4,5},{5,4},{6,7},{7,6},{8,9},{9,8},{10,11... | collective-permute-start | bytes 737288 | tf_op jit(solution)/shard_map/ppermute | solution.py:407
  189.0 7.6 %collective-permute-start.39 = (bf16[144,768]{1,0:T(8,128)(2,1)S(1)}, bf16[144,768]{1,0:T(8,128)(2,1)S(1)}, u32[]{:S(2)}, u32[]{:S(2)}) collective-permute-start(bf16[144,768]{1,0:T(8,128)(2,1)S(1)} %get-tuple-element.80), channel_id=1, source_target_pairs={{0,24},{8,0},{16,8},{24,16},{1,25},{9,1},{17,9},{25,17},{2,26},{10... | collective-permute-start | bytes 663560 | tf_op jit(solution)/shard_map/ppermute | solution.py:407
  190.1 19.0 %collective-permute-start.38 = (bf16[144,768]{1,0:T(8,128)(2,1)S(1)}, bf16[144,768]{1,0:T(8,128)(2,1)S(1)}, u32[]{:S(2)}, u32[]{:S(2)}) collective-permute-start(bf16[144,768]{1,0:T(8,128)(2,1)S(1)} %get-tuple-element.81), channel_id=1, source_target_pairs={{0,16},{8,24},{16,0},{24,8},{1,17},{9,25},{17,1},{25,9},{2,18},{10... | collective-permute-start | bytes 663560 | tf_op jit(solution)/shard_map/ppermute | solution.py:407
  190.1 18.9 %collective-permute-start.37 = (bf16[144,768]{1,0:T(8,128)(2,1)S(1)}, bf16[144,768]{1,0:T(8,128)(2,1)S(1)}, u32[]{:S(2)}, u32[]{:S(2)}) collective-permute-start(bf16[144,768]{1,0:T(8,128)(2,1)S(1)} %get-tuple-element.79), channel_id=1, source_target_pairs={{0,8},{8,16},{16,24},{24,0},{1,9},{9,17},{17,25},{25,1},{2,10},{10... | collective-permute-start | bytes 663560 | tf_op jit(solution)/shard_map/ppermute | solution.py:407
  193.4 27.6 %collective-permute-start.28 = (bf16[96,640]{1,0:T(8,128)(2,1)S(1)}, bf16[96,640]{1,0:T(8,128)(2,1)S(1)}, u32[]{:S(2)}, u32[]{:S(2)}) collective-permute-start(bf16[96,640]{1,0:T(8,128)(2,1)S(1)} %dynamic-slice_bitcast_fusion.9), channel_id=1, source_target_pairs={{0,4},{4,0},{1,5},{5,1},{2,6},{6,2},{3,7},{7,3},{8,12},{12,8},{9,1... | collective-permute-start | bytes 368648 | tf_op jit(solution)/shard_map/ppermute | solution.py:407
  209.2 13.5 %collective-permute-start.42 = (bf16[144,768]{1,0:T(8,128)(2,1)S(1)}, bf16[144,768]{1,0:T(8,128)(2,1)S(1)}, u32[]{:S(2)}, u32[]{:S(2)}) collective-permute-start(bf16[144,768]{1,0:T(8,128)(2,1)S(1)} %fusion.5), channel_id=1, source_target_pairs={{0,24},{8,0},{16,8},{24,16},{1,25},{9,1},{17,9},{25,17},{2,26},{10... | collective-permute-start | bytes 663560 | tf_op jit(solution)/shard_map/ppermute | solution.py:407
  209.2 30.3 %collective-permute-start.41 = (bf16[144,768]{1,0:T(8,128)(2,1)S(1)}, bf16[144,768]{1,0:T(8,128)(2,1)S(1)}, u32[]{:S(2)}, u32[]{:S(2)}) collective-permute-start(bf16[144,768]{1,0:T(8,128)(2,1)S(1)} %fusion.5), channel_id=1, source_target_pairs={{0,16},{8,24},{16,0},{24,8},{1,17},{9,25},{17,1},{25,9},{2,18},{10... | collective-permute-start | bytes 663560 | tf_op jit(solution)/shard_map/ppermute | solution.py:407
  219.1 20.5 %collective-permute-start.40 = (bf16[144,768]{1,0:T(8,128)(2,1)S(1)}, bf16[144,768]{1,0:T(8,128)(2,1)S(1)}, u32[]{:S(2)}, u32[]{:S(2)}) collective-permute-start(bf16[144,768]{1,0:T(8,128)(2,1)S(1)} %fusion.5), channel_id=1, source_target_pairs={{0,8},{8,16},{16,24},{24,0},{1,9},{9,17},{17,25},{25,1},{2,10},{10... | collective-permute-start | bytes 663560 | tf_op jit(solution)/shard_map/ppermute | solution.py:407
  221.1 20.2 %collective-permute-start.29 = (bf16[96,640]{1,0:T(8,128)(2,1)S(1)}, bf16[96,640]{1,0:T(8,128)(2,1)S(1)}, u32[]{:S(2)}, u32[]{:S(2)}) collective-permute-start(bf16[96,640]{1,0:T(8,128)(2,1)S(1)} %fusion.7), channel_id=1, source_target_pairs={{0,4},{4,0},{1,5},{5,1},{2,6},{6,2},{3,7},{7,3},{8,12},{12,8},{9,1... | collective-permute-start | bytes 368648 | tf_op jit(solution)/shard_map/ppermute | solution.py:407
  239.7 38.6 %copy-start.5 = (bf16[4,144,768]{2,1,0:T(8,128)(2,1)}, bf16[4,144,768]{2,1,0:T(8,128)(2,1)S(1)}, u32[]{:S(2)}) copy-start(bf16[4,144,768]{2,1,0:T(8,128)(2,1)S(1)} %pad_maximum_fusion.1.refs_0_) | copy-start | bytes 2654212
  239.7 15.4 %collective-permute-start.43 = (bf16[4,144,768]{2,1,0:T(8,128)(2,1)S(1)}, bf16[4,144,768]{2,1,0:T(8,128)(2,1)}, u32[]{:S(2)}, u32[]{:S(2)}) collective-permute-start(bf16[4,144,768]{2,1,0:T(8,128)(2,1)S(1)} %pad_maximum_fusion.1.refs_0_), channel_id=1, source_target_pairs={{0,4},{4,0},{1,5},{5,1},{2,6},{6,2},{3,7},{7,3},{8,12},{12,8},{9,1... | collective-permute-start | bytes 2654216 | tf_op jit(solution)/shard_map/ppermute | solution.py:407
  241.3 7.7 %collective-permute-start.32 = (bf16[2,96,640]{2,1,0:T(8,128)(2,1)S(1)}, bf16[2,96,640]{2,1,0:T(8,128)(2,1)S(1)}, u32[]{:S(2)}, u32[]{:S(2)}) collective-permute-start(bf16[2,96,640]{2,1,0:T(8,128)(2,1)S(1)} %get-tuple-element.89), channel_id=1, source_target_pairs={{0,24},{8,0},{16,8},{24,16},{1,25},{9,1},{17,9},{25,17},{2,26},{10... | collective-permute-start | bytes 737288 | tf_op jit(solution)/shard_map/ppermute | solution.py:407
  241.4 12.5 %collective-permute-start.31 = (bf16[2,96,640]{2,1,0:T(8,128)(2,1)S(1)}, bf16[2,96,640]{2,1,0:T(8,128)(2,1)S(1)}, u32[]{:S(2)}, u32[]{:S(2)}) collective-permute-start(bf16[2,96,640]{2,1,0:T(8,128)(2,1)S(1)} %get-tuple-element.89), channel_id=1, source_target_pairs={{0,16},{8,24},{16,0},{24,8},{1,17},{9,25},{17,1},{25,9},{2,18},{10... | collective-permute-start | bytes 737288 | tf_op jit(solution)/shard_map/ppermute | solution.py:407
  241.5 12.4 %collective-permute-start.30 = (bf16[2,96,640]{2,1,0:T(8,128)(2,1)S(1)}, bf16[2,96,640]{2,1,0:T(8,128)(2,1)S(1)}, u32[]{:S(2)}, u32[]{:S(2)}) collective-permute-start(bf16[2,96,640]{2,1,0:T(8,128)(2,1)S(1)} %get-tuple-element.89), channel_id=1, source_target_pairs={{0,8},{8,16},{16,24},{24,0},{1,9},{9,17},{17,25},{25,1},{2,10},{10... | collective-permute-start | bytes 737288 | tf_op jit(solution)/shard_map/ppermute | solution.py:407
  254.0 25.3 %collective-permute-start.33 = (bf16[2,4,96,640]{3,2,1,0:T(8,128)(2,1)S(1)}, bf16[2,4,96,640]{3,2,1,0:T(8,128)(2,1)}, u32[]{:S(2)}, u32[]{:S(2)}) collective-permute-start(bf16[2,4,96,640]{3,2,1,0:T(8,128)(2,1)S(1)} %pad_maximum_fusion), channel_id=1, source_target_pairs={{0,2},{2,0},{1,3},{3,1},{4,6},{6,4},{5,7},{7,5},{8,10},{10,8},{9,1... | collective-permute-start | bytes 2949128 | tf_op jit(solution)/shard_map/ppermute | solution.py:407
  254.1 6.6 %collective-permute-start.21 = (bf16[128,640]{1,0:T(8,128)(2,1)S(1)}, bf16[128,640]{1,0:T(8,128)(2,1)S(1)}, u32[]{:S(2)}, u32[]{:S(2)}) collective-permute-start(bf16[128,640]{1,0:T(8,128)(2,1)S(1)} %copy-done.27), channel_id=1, source_target_pairs={{0,24},{8,0},{16,8},{24,16},{1,25},{9,1},{17,9},{25,17},{2,26},{10... | collective-permute-start | bytes 491528 | tf_op jit(solution)/shard_map/ppermute | solution.py:407
  254.9 32.3 %collective-permute-start.44 = (bf16[4,144,768]{2,1,0:T(8,128)(2,1)S(1)}, bf16[4,144,768]{2,1,0:T(8,128)(2,1)}, u32[]{:S(2)}, u32[]{:S(2)}) collective-permute-start(bf16[4,144,768]{2,1,0:T(8,128)(2,1)S(1)} %pad_maximum_fusion.1.refs_0_), channel_id=1, source_target_pairs={{0,2},{2,0},{1,3},{3,1},{4,6},{6,4},{5,7},{7,5},{8,10},{10,8},{9,1... | collective-permute-start | bytes 2654216 | tf_op jit(solution)/shard_map/ppermute | solution.py:407
  255.1 32.1 %collective-permute-start.45 = (bf16[4,144,768]{2,1,0:T(8,128)(2,1)}, bf16[4,144,768]{2,1,0:T(8,128)(2,1)}, u32[]{:S(2)}, u32[]{:S(2)}) collective-permute-start(bf16[4,144,768]{2,1,0:T(8,128)(2,1)} %collective-permute-done.43.refs_1_), channel_id=1, source_target_pairs={{0,2},{2,0},{1,3},{3,1},{4,6},{6,4},{5,7},{7,5},{8,10},{10,8},{9,1... | collective-permute-start | bytes 2654216 | tf_op jit(solution)/shard_map/ppermute | solution.py:407
  255.4 16.5 %collective-permute-start.22 = (bf16[128,640]{1,0:T(8,128)(2,1)}, bf16[128,640]{1,0:T(8,128)(2,1)S(1)}, u32[]{:S(2)}, u32[]{:S(2)}) collective-permute-start(bf16[128,640]{1,0:T(8,128)(2,1)} %get-tuple-element.57), channel_id=1, source_target_pairs={{0,16},{8,24},{16,0},{24,8},{1,17},{9,25},{17,1},{25,9},{2,18},{10... | collective-permute-start | bytes 491528 | tf_op jit(solution)/shard_map/ppermute | solution.py:407
  260.7 11.3 %collective-permute-start.23 = (bf16[128,640]{1,0:T(8,128)(2,1)S(1)}, bf16[128,640]{1,0:T(8,128)(2,1)S(1)}, u32[]{:S(2)}, u32[]{:S(2)}) collective-permute-start(bf16[128,640]{1,0:T(8,128)(2,1)S(1)} %copy-done.26), channel_id=1, source_target_pairs={{0,8},{8,16},{16,24},{24,0},{1,9},{9,17},{17,25},{25,1},{2,10},{10... | collective-permute-start | bytes 491528 | tf_op jit(solution)/shard_map/ppermute | solution.py:407
  (32 other events, 220.2 us)

commit v2 on v1

v2 whole, which is shorter than its diff:
```python
import functools
import math

import jax
import jax.numpy as jnp
from jax import lax
from jax.experimental import pallas as pl
from jax.experimental.pallas import tpu as pltpu
from jax.sharding import Mesh, PartitionSpec as P

D = 768
HEADS = 12
HEAD_DIM = 64
FF = 1152
EPS = 1e-05
THETA = 160000.0

TP = 4
GH = HEADS // TP
GW = GH * HEAD_DIM
WC = 640
CTX = ("zo", "z", "x", "core")
BF = jnp.bfloat16
F32 = jnp.float32
VMEM_LIMIT = 56 * 1024 * 1024

KEY_AT = ((0, 0), (0, 1), (1, 0))
VALUE_AT = ((1, 1), (2, 0), (2, 1))


def dot(a, b):
    return jnp.dot(a, b, preferred_element_type=F32)


def dot_nt(a, b):
    return lax.dot_general(a, b, (((1,), (1,)), ((), ())), preferred_element_type=F32)


def dot_tn(a, b):
    return lax.dot_general(a, b, (((0,), (0,)), ((), ())), preferred_element_type=F32)


def call(body, outs, n_smem, ins, scratch=(), any_ins=(), name=None):
    specs = []
    for i in range(len(ins)):
        if i < n_smem:
            specs.append(pl.BlockSpec(memory_space=pltpu.SMEM))
        elif i in any_ins:
            specs.append(pl.BlockSpec(memory_space=pl.ANY))
        else:
            specs.append(pl.BlockSpec(memory_space=pltpu.VMEM))
    return pl.pallas_call(
        body,
        out_shape=[jax.ShapeDtypeStruct(s, t) for s, t in outs],
        in_specs=specs,
        out_specs=[pl.BlockSpec(memory_space=pltpu.VMEM)] * len(outs),
        scratch_shapes=list(scratch),
        compiler_params=pltpu.CompilerParams(vmem_limit_bytes=VMEM_LIMIT),
        cost_estimate=pl.CostEstimate(
            flops=1, bytes_accessed=1, transcendentals=0
        ),
        name=name,
    )(*ins)


def normalise(values):
    mean = jnp.mean(values, axis=-1, keepdims=True)
    centred = values - mean
    spread = jnp.mean(centred * centred, axis=-1, keepdims=True)
    scale = lax.rsqrt(spread + EPS)
    return centred * scale, scale


def normalise_back(grad_unit, unit, scale):
    return scale * (
        grad_unit
        - jnp.mean(grad_unit, axis=-1, keepdims=True)
        - unit * jnp.mean(grad_unit * unit, axis=-1, keepdims=True)
    )


def turn(tile, cosine, signed_sine, first_half):
    swapped = jnp.where(first_half, pltpu.roll(tile, 96, 1), pltpu.roll(tile, 32, 1))
    return tile * cosine + swapped * signed_sine


def lane_masks(rows):
    lane = lax.broadcasted_iota(jnp.int32, (rows, 128), 1)
    return lax.rem(lane, 64) < 32, lane < 64


def group_kernel(idx, w_ref, own_ref, half_ref):
    height = w_ref.shape[0]
    half = height // 2
    for g in range(TP):

        @pl.when(idx[0] == g)
        def _():
            parts = [w_ref[:, p * D + g * GW : p * D + (g + 1) * GW] for p in (1, 2, 0)]
            parts.append(jnp.zeros((height, WC - 3 * GW), BF))
            own_ref[...] = jnp.concatenate(parts, axis=1)

    half_ref[...] = own_ref[pl.ds(pl.multiple_of(idx[2] * half, half), half), :]


def pack_kernel(idx, out_ref, in_ref, down_ref, pack_ref):
    c = idx[2]
    half = out_ref.shape[0] // 2
    at = pl.ds(pl.multiple_of(c * half, half), half)
    pack_ref[0:half, :] = out_ref[at, :]
    for b in range(3):
        pack_ref[(1 + b) * half : (2 + b) * half, :] = in_ref[at, b * D : (b + 1) * D]
    count, step = down_half(down_ref.shape[0])
    at = pl.ds(pl.multiple_of(c * step, 16), count)
    pack_ref[4 * half :, :] = down_ref[at, :]


def down_half(height):
    count = -(-height // 32) * 16
    return count, height - count


def front_kernel(shards, idx, *refs):
    toks = refs[:TP]
    n_w = 2 * shards - 1
    ws = refs[TP : TP + n_w]
    gain_refs = refs[TP + n_w : TP + n_w + shards]
    cos_ref, sin_ref, q_ref, kv_ref, h_ref, w_ref, gains_ref = refs[TP + n_w + shards :]
    c, y = idx[2], idx[3]
    rows = toks[0].shape[0]
    part = ws[0].shape[0]
    half = part // 2
    gains_ref[...] = jnp.zeros_like(gains_ref)
    for k in range(shards):
        start = lax.rem(y - k + shards, shards) * part
        at = pl.ds(pl.multiple_of(start, part), part)
        if k == 0:
            w_ref[at, :] = ws[0][...]
            continue
        at = pl.ds(pl.multiple_of(start + c * half, half), half)
        w_ref[at, :] = ws[2 * k - 1][...]
        at = pl.ds(pl.multiple_of(start + (1 - c) * half, half), half)
        w_ref[at, :] = ws[2 * k][...]
    for s in range(shards):

        @pl.when(y == s)
        def _():
            for k in range(shards):
                start = (s - k) % shards * part
                gains_ref[0:2, start : start + part] = gain_refs[k][...].astype(F32)

    gain = gains_ref[0:1, :]
    first, low = lane_masks(rows)
    for j in range(TP):
        at = slice(j * rows, (j + 1) * rows)
        unit, _ = normalise(toks[j][...].astype(F32))
        h = (unit * gain).astype(BF)
        h_ref[at, :] = h
        out = dot(h, w_ref[...])
        cosine, sine = cos_ref[at, :], sin_ref[at, :]
        key_a = turn(out[:, 0:128], cosine, sine, first)
        mixed = out[:, 128:256]
        key_b = jnp.where(low, turn(mixed, cosine, sine, first), mixed)
        kv_ref[at, 0:128] = key_a.astype(BF)
        kv_ref[at, 128:256] = key_b.astype(BF)
        kv_ref[at, 256:384] = out[:, 256:384].astype(BF)
        query_a = turn(out[:, 384:512], cosine, sine, first)
        query_b = jnp.where(low, turn(out[:, 512:640], cosine, sine, first), 0.0)
        factor = HEAD_DIM ** (-0.5)
        q_ref[at, 0:128] = (query_a * factor).astype(BF)
        q_ref[at, 128:256] = (query_b * factor).astype(BF)


def half_rows(values_t, head):
    at = head * HEAD_DIM
    rows = values_t[at : at + HEAD_DIM]
    zeros = jnp.zeros_like(rows)
    return jnp.concatenate([rows, zeros] if head % 2 == 0 else [zeros, rows], axis=0)


def forward_kernel(n_kv, q_ref, *refs):
    kvs = refs[:n_kv]
    atts = refs[n_kv : n_kv + TP]
    att_t_ref, lse_ref, kv_s, v_t, q_t = refs[n_kv + TP :]
    rows = kvs[0].shape[0]
    block = math.gcd(rows, 256)
    for i, kv in enumerate(kvs):
        kv_s[i * rows : (i + 1) * rows, :] = kv[...]
        v_t[:, i * rows : (i + 1) * rows] = kv[:, 128:384].T
    q_t[...] = q_ref[...].T
    lse_ref[...] = jnp.zeros_like(lse_ref)
    for i in range(rows // block):
        at = slice(i * block, (i + 1) * block)
        for h in range(GH):
            tile = KEY_AT[h][0]
            keys = kv_s[:, tile * 128 : tile * 128 + 128]
            scores = dot(keys, half_rows(q_t[:, at], h))
            top = jnp.max(scores, axis=0, keepdims=True)
            weights = jnp.exp(scores - top)
            total = jnp.sum(weights, axis=0, keepdims=True)
            tile, half = VALUE_AT[h]
            values_t = v_t[(tile - 1) * 128 : tile * 128, :]
            out = dot(values_t, weights.astype(BF))[half * 64 : half * 64 + 64]
            att_t_ref[h * 64 : h * 64 + 64, at] = out / total
            lse_ref[h : h + 1, at] = top + jnp.log(total)
    small = rows // TP
    for j in range(TP):
        atts[j][...] = att_t_ref[:, j * small : (j + 1) * small].T.astype(BF)


def backward_kernel(n_kv, q_ref, *refs):
    kvs = refs[:n_kv]
    gas = refs[n_kv : n_kv + TP]
    att_t_ref, lse_ref = refs[n_kv + TP : n_kv + TP + 2]
    tables = refs[n_kv + TP + 2 : n_kv + TP + 4]
    keep_ref, send_ref, dq_ref = refs[n_kv + TP + 4 : n_kv + TP + 7]
    kv_s, k_t, q_t, g_t, q_m, g_m, acc, dq_t = refs[n_kv + TP + 7 :]
    rows = kvs[0].shape[0]
    small = gas[0].shape[0]
    block = math.gcd(rows, 256)
    for i, kv in enumerate(kvs):
        kv_s[i * rows : (i + 1) * rows, :] = kv[...]
        k_t[:, i * rows : (i + 1) * rows] = kv[:, 0:256].T
    q_t[...] = q_ref[...].T
    _, low = lane_masks(small)
    for j in range(TP):
        at = slice(j * small, (j + 1) * small)
        g_t[:, at] = gas[j][...].T
        first, second = gas[j][:, 0:128], gas[j][:, 128:256].astype(F32)
        g_m[at, 0:128] = first
        g_m[at, 128:256] = jnp.where(low, second, 0.0).astype(BF)
        g_m[at, 256:384] = jnp.where(low, 0.0, second).astype(BF)
        both = q_ref[at, 0:128].astype(F32)
        q_m[at, 0:128] = jnp.where(low, both, 0.0).astype(BF)
        q_m[at, 128:256] = jnp.where(low, 0.0, both).astype(BF)
        q_m[at, 256:384] = q_ref[at, 128:256]
    dq_t[...] = jnp.zeros_like(dq_t)
    acc[...] = jnp.zeros_like(acc)
    for i in range(rows // block):
        at = slice(i * block, (i + 1) * block)
        for h in range(GH):
            ktile, khalf = KEY_AT[h]
            vtile = VALUE_AT[h][0]
            klanes = slice(ktile * 128, ktile * 128 + 128)
            vlanes = slice(vtile * 128, vtile * 128 + 128)
            scores = dot(kv_s[:, klanes], half_rows(q_t[:, at], h))
            probs = jnp.exp(scores - lse_ref[h : h + 1, at])
            grad_t = half_rows(g_t[:, at], h + 1)
            grad_probs = dot(kv_s[:, vlanes], grad_t)
            own = g_t[(h + 1) * 64 : (h + 2) * 64, at].astype(F32)
            inner = jnp.sum(
                own * att_t_ref[h * 64 : h * 64 + 64, at], axis=0, keepdims=True
            )
            grad_scores = (probs * (grad_probs - inner)).astype(BF)
            lanes = slice(h * 128, h * 128 + 128)
            acc[:, vlanes] += dot(probs.astype(BF), g_m[at, lanes])
            acc[:, klanes] += dot(grad_scores, q_m[at, lanes])
            part = dot(k_t[klanes, :], grad_scores)[khalf * 64 : khalf * 64 + 64]
            dq_t[h * 64 : h * 64 + 64, at] = part * HEAD_DIM ** (-0.5)
    first, low = lane_masks(rows)
    cosine, sine = tables[0][0:rows, :], -tables[1][0:rows, :]
    grad_q = dq_t[...].T
    for t in range(2):
        lanes = slice(t * 128, t * 128 + 128)
        dq_ref[:, lanes] = turn(grad_q[:, lanes], cosine, sine, first).astype(BF)
    for i in range(n_kv):
        at = slice(i * rows, (i + 1) * rows)
        cosine, sine = tables[0][at, :], -tables[1][at, :]
        target = keep_ref if i < n_kv // 2 else send_ref
        block = i % (n_kv // 2)
        grad = acc[at, 0:128]
        target[block, :, 0:128] = turn(grad, cosine, sine, first).astype(BF)
        grad = acc[at, 128:256]
        grad = jnp.where(low, turn(grad, cosine, sine, first), grad)
        target[block, :, 128:256] = grad.astype(BF)
        target[block, :, 256:384] = acc[at, 256:384].astype(BF)


ACT_H, ACT_MIX, ACT_GU, ACT_GB, ACT_ATT, ACT_COT, ACT_ALL = (
    0, D, D + FF, D + 3 * FF, 2 * D + 3 * FF, 3 * D + 3 * FF, 4 * D + 3 * FF
)


def middle_kernel(n_packs, idx, *refs):
    atts = refs[:TP]
    tok_ref, cot_ref, gains_ref, out_own, in_own, down_own = refs[TP : TP + 6]
    packs = refs[TP + 6 : TP + 6 + n_packs]
    rest = refs[TP + 6 + n_packs :]
    result_ref, gmid_ref, act_ref, gain_ref = rest[:4]
    gatts = rest[4 : 4 + TP]
    w_out, w_in, w_down, sems = rest[4 + TP :]
    half = out_own.shape[0] // 2
    count, step = down_half(down_own.shape[0])

    def rows(start, height):
        return pl.ds(pl.multiple_of(start, 16), height)

    z, c, y = idx[0], idx[2], idx[3]
    shards = n_packs // 2 + 1
    own, own_down = y * 2 * half, y * down_own.shape[0]
    outs = [pltpu.make_async_copy(out_own, w_out.at[rows(own, 2 * half), :], sems.at[0])]
    ins = [pltpu.make_async_copy(in_own, w_in.at[rows(own, 2 * half), :], sems.at[1])]
    target = w_down.at[rows(own_down, down_own.shape[0]), :]
    downs = [pltpu.make_async_copy(down_own, target, sems.at[2])]
    for i, pack in enumerate(packs):
        shard = lax.rem(y - (i // 2 + 1) + shards, shards)
        core = 1 - c if i % 2 else c
        at = rows((shard * 2 + core) * half, half)
        source = pack.at[0:half, :]
        outs.append(pltpu.make_async_copy(source, w_out.at[at, :], sems.at[3 + 5 * i]))
        for b in range(3):
            source = pack.at[(1 + b) * half : (2 + b) * half, :]
            target = w_in.at[at, b * D : (b + 1) * D]
            ins.append(pltpu.make_async_copy(source, target, sems.at[4 + 5 * i + b]))
        at = rows(shard * down_own.shape[0] + core * step, count)
        source = pack.at[4 * half : 4 * half + count, :]
        downs.append(pltpu.make_async_copy(source, w_down.at[at, :], sems.at[7 + 5 * i]))
    apart = 2 * count == down_own.shape[0]
    for copy in outs + ins + (downs if apart else downs[:1]):
        copy.start()
    starts = [pl.multiple_of(lax.rem(z + j, TP) * GW, GW) for j in range(TP)]
    for copy in outs:
        copy.wait()
    middle = tok_ref[...].astype(F32)
    for j in range(TP):
        middle += dot(atts[j][...], w_out[pl.ds(starts[j], GW), :])
        act_ref[:, ACT_ATT + j * GW : ACT_ATT + (j + 1) * GW] = atts[j][...]
    gain = gains_ref[1:2, :]
    unit, scale = normalise(middle)
    h = (unit * gain).astype(BF)
    act_ref[:, ACT_H : ACT_H + D] = h
    for copy in ins:
        copy.wait()
    gate = dot(h, w_in[:, :FF])
    up = dot(h, w_in[:, FF:])
    phi = 0.5 * (1.0 + lax.erf(gate * math.sqrt(0.5)))
    active = gate * phi
    mixed = (active * up).astype(BF)
    act_ref[:, ACT_MIX : ACT_MIX + FF] = mixed
    for i, copy in enumerate(downs):
        if i and not apart:
            copy.start()
        copy.wait()
    grad_mixed = dot_nt(cot_ref[...], w_down[...])
    slope = phi + gate * (jnp.exp(-0.5 * gate * gate) * (1.0 / math.sqrt(2.0 * math.pi)))
    grad_gate = (grad_mixed * up * slope).astype(BF)
    grad_up = (grad_mixed * active).astype(BF)
    act_ref[:, ACT_GU : ACT_GU + FF] = grad_gate
    act_ref[:, ACT_GU + FF : ACT_GU + 2 * FF] = grad_up
    grad_h = dot_nt(grad_gate, w_in[:, :FF]) + dot_nt(grad_up, w_in[:, FF:])
    gain_ref[...] = jnp.broadcast_to(
        jnp.sum(grad_h * unit, axis=0, keepdims=True), gain_ref.shape
    )
    grad_middle = cot_ref[...].astype(F32) + normalise_back(grad_h * gain, unit, scale)
    gmid_ref[...] = grad_middle
    gb = grad_middle.astype(BF)
    act_ref[:, ACT_GB : ACT_GB + D] = gb
    act_ref[:, ACT_COT : ACT_COT + D] = cot_ref[...]
    for j in range(TP):
        part = dot_nt(gb, w_out[pl.ds(starts[j], GW), :])
        pad = jnp.zeros((part.shape[0], 256 - GW), F32)
        gatts[j][...] = jnp.concatenate([pad, part], axis=1).astype(BF)
    result_ref[...] = middle + dot(mixed, w_down[...])


def up16(n):
    return -(-n // 16) * 16


def plan(shards):
    rows_d, rows_f = D // (4 * shards), FF // (4 * shards)
    return rows_d, rows_f, up16(rows_d), up16(rows_f)


def ffn_grads_kernel(shards, idx, own, got, gain_ref, *refs):
    ins = refs[:shards]
    others = refs[shards : shards + 2]
    h_t, mixed_t, att_t, right = refs[shards + 2 :]
    z, x, c, y = idx[0], idx[1], idx[2], idx[3]
    rows_d, rows_f, pad_d, pad_f = plan(shards)
    n = own.shape[0]
    pieces, per = 4 * shards, GW // rows_d
    for i, act in enumerate((own, got)):
        at = slice(i * n, (i + 1) * n)
        h = act[:, ACT_H : ACT_H + D].T
        mixed = act[:, ACT_MIX : ACT_MIX + FF].T
        att = act[:, ACT_ATT : ACT_ATT + D].T
        for m in range(pieces):
            h_t[m, 0:rows_d, at] = h[m * rows_d : (m + 1) * rows_d]
            mixed_t[m, 0:rows_f, at] = mixed[m * rows_f : (m + 1) * rows_f]
            att_t[m, 0:rows_d, at] = att[m * rows_d : (m + 1) * rows_d]
        right[at, 0 : 2 * FF] = act[:, ACT_GU : ACT_GU + 2 * FF]
        right[at, 2 * FF : 2 * FF + D] = act[:, ACT_GB : ACT_GB + D]
        right[at, 2 * FF + D :] = act[:, ACT_COT : ACT_COT + D]
    for k in range(shards):
        piece = (lax.rem(y + k, shards) * 2 + c) * 2
        left = h_t[pl.ds(piece, 2)].reshape(2 * pad_d, 2 * n)
        grad = dot(left, right[:, 0 : 2 * FF]).astype(BF)
        for xx in range(2):
            for t in range(2 * FF // 128):
                ins[k][xx, t * pad_d : t * pad_d + rows_d, :] = grad[
                    xx * pad_d : xx * pad_d + rows_d, t * 128 : t * 128 + 128
                ]
    gain = jnp.broadcast_to(gain_ref[0:1, :], (16, D)).astype(BF)
    high = pad_f + pad_d + 16
    for xr in range(2):
        for s in range(shards):
            piece = (s * 2 + c) * 2 + lax.rem(x + xr, 2)
            turned = lax.rem(piece // per - z + TP, TP) * per + lax.rem(piece, per)
            down = dot(mixed_t[piece], right[:, 2 * FF + D :]).astype(BF)
            out = dot(att_t[turned], right[:, 2 * FF : 2 * FF + D]).astype(BF)
            for t in range(D // 128):
                lanes = slice(t * 128, t * 128 + 128)
                base = t * high
                others[xr][s, base : base + pad_f, :] = down[:, lanes]
                base += pad_f
                others[xr][s, base : base + pad_d, :] = out[:, lanes]
                base += pad_d
                others[xr][s, base : base + 16, :] = gain[:, lanes]


def qkv_grads_kernel(shards, n_kv, idx, *refs):
    hs = refs[:n_kv]
    keep_ref, send_ref, dq_ref, w_ref, gains_ref, mine_ref, other_ref = refs[n_kv:]
    c = idx[2]
    total = None
    for i in range(n_kv):
        grads = (keep_ref if i < n_kv // 2 else send_ref)[i % (n_kv // 2)]
        part = dot(grads.T, hs[i][...])
        total = part if total is None else total + part
    grad = jnp.concatenate([total, dot(dq_ref[...].T, hs[0][...])], axis=0).T
    w = w_ref[...].astype(F32)
    gain = gains_ref[...].T[:, 0:1]
    lane = lax.broadcasted_iota(jnp.int32, grad.shape, 1)
    by_gain = jnp.sum(grad * w, axis=1, keepdims=True) / gain
    grad = jnp.where(lane < 3 * GW, grad, by_gain).astype(BF)
    height = plan(shards)[0]
    for s in range(shards):
        for cc in range(2):
            block = (s * 2 + cc) * 2 * height
            for xx in range(2):
                part = grad[block + xx * height : block + (xx + 1) * height]

                @pl.when(c == cc)
                def _():
                    mine_ref[s, xx] = part

                @pl.when(c != cc)
                def _():
                    other_ref[s, xx] = part


def combine_kernel(n_sum, idx, *refs):
    parts = refs[:n_sum]
    dq_ref, w_ref, out_ref = refs[n_sum:]
    rows = out_ref.shape[2]
    for j in range(TP):
        at = slice(j * rows, (j + 1) * rows)
        total = parts[0][at, :].astype(F32)
        for part in parts[1:]:
            total += part[at, :].astype(F32)
        grad = jnp.concatenate([total.astype(BF), dq_ref[at, :]], axis=1)
        owner = lax.rem(idx[0] - j + TP, TP)
        out_ref[owner // 2, lax.rem(owner, 2)] = dot_nt(grad, w_ref[...]).astype(BF)


def tail_kernel(n_sum, *refs):
    tok_ref, gmid_ref, gains_ref, out_ref = refs[n_sum:]
    unit, scale = normalise(tok_ref[...].astype(F32))
    total = refs[0][...].astype(F32)
    for grad in refs[1:n_sum]:
        total += grad[...].astype(F32)
    grad_unit = total * gains_ref[0:1, :]
    out_ref[...] = gmid_ref[...] + normalise_back(grad_unit, unit, scale)


def place_z(z, k):
    return lax.rem(z // 2 + k % 2, 2) * 2 + lax.rem(lax.rem(z, 2) + k // 2, 2)


def in_unpack_kernel(shards, idx, own, got, in_ref, held):
    rows_d, _, pad_d, _ = plan(shards)
    size = held.shape[0] // TP
    z, x, c = idx[0], idx[1], idx[2]
    for cr in range(2):
        for xr in range(2):
            for k in range(TP):
                at = pl.ds(pl.multiple_of(place_z(z, k) * size, size), size)
                held[at, :] = (got if cr else own)[xr, k].astype(F32)
            cc, xx = lax.rem(c + cr, 2), lax.rem(x + xr, 2)
            for t in range(2 * FF // 128):
                base = t * pad_d
                in_ref[cc, xx, :, t * 128 : t * 128 + 128] = held[base : base + rows_d, :]


def rest_unpack_kernel(shards, idx, own, got, out_ref, down_ref, gain_ref, held, gain_all):
    rows_d, rows_f, pad_d, pad_f = plan(shards)
    high = pad_f + pad_d + 16
    size = held.shape[0] // TP
    z, x, c = idx[0], idx[1], idx[2]
    gains = []
    for cr in range(2):
        for xr in range(2):
            for k in range(TP):
                at = pl.ds(pl.multiple_of(place_z(z, k) * size, size), size)
                held[at, :] = (got if cr else own)[xr, k].astype(F32)
            cc, xx = lax.rem(c + cr, 2), lax.rem(x + xr, 2)
            for t in range(D // 128):
                lanes = slice(t * 128, t * 128 + 128)
                base = t * high
                down_ref[cc, xx, :, lanes] = held[base : base + rows_f, :]
                base += pad_f
                out_ref[cc, xx, :, lanes] = held[base : base + rows_d, :]
                base += pad_d
                if xr == 0:
                    gains.append(held[base : base + 8, :])
    for t in range(D // 128):
        gain_all[:, t * 128 : t * 128 + 128] = gains[t] + gains[t + D // 128]
    part = gain_ref.shape[1]
    for s in range(shards):

        @pl.when(idx[3] == s)
        def _():
            gain_ref[...] = gain_all[0:1, s * part : (s + 1) * part]


def qkv_unpack_kernel(idx, own, got, out_ref, gain_ref, gain_s):
    z, x, c = idx[0], idx[1], idx[2]
    for cr in range(2):
        for xr in range(2):
            cc, xx = lax.rem(c + cr, 2), lax.rem(x + xr, 2)
            gain = None
            for g in range(TP):
                k = 2 * lax.rem(g % 2 + z, 2) + lax.rem(g // 2 + z // 2, 2)
                block = (got if cr else own)[xr, k].astype(F32)
                for source, place in ((0, 1), (1, 2), (2, 0)):
                    out_ref[cc, xx, :, place * D + g * GW : place * D + (g + 1) * GW] = block[
                        :, source * GW : (source + 1) * GW
                    ]
                tail = block[:, 512:640]
                gain = tail if gain is None else gain + tail
            height = gain.shape[0]
            at = pl.multiple_of((cc * 2 + xx) * height, height)
            gain_s[pl.ds(at, height), :] = gain
    gain_ref[...] = gain_s[...].T[64:65]


def shift(value, axis, k):
    n = lax.axis_size(axis)
    return lax.ppermute(value, axis, [(i, (i + k) % n) for i in range(n)])


def gather(value, axis):
    return [value] + [shift(value, axis, k) for k in range(1, lax.axis_size(axis))]


def pick(value, index, dim):
    return lax.dynamic_index_in_dim(value, index, dim, keepdims=False)


def reduce_step(order, terms, axis, dim):
    n, i = lax.axis_size(axis), lax.axis_index(axis)
    got = []
    for k in range(1, n):
        got.append(shift(order.add([pick(t, lax.rem(i + k, n), dim) for t in terms]), axis, k))
    return [pick(t, i, dim) for t in terms] + got


def add(terms):
    total = terms[0].astype(F32)
    for term in terms[1:]:
        total = total + term.astype(F32)
    return total.astype(BF)


def swap_z(value, bit):
    return lax.ppermute(value, "z", [(i, i ^ bit) for i in range(TP)])


def reduce_z(order, terms, bit):
    z = lax.axis_index("z")
    i, dim = (z % 2, 1) if bit == 1 else (z // 2, 0)
    got = swap_z(order.add([pick(t, 1 - i, dim) for t in terms]), bit)
    return [pick(t, i, dim) for t in terms] + [got]


def gather_z(value, bit):
    got = swap_z(value, bit)
    return jnp.stack([value, got]) if bit == 2 else jnp.concatenate([value, got])


def sum_over(value, axis):
    return add([value] + [shift(value, axis, k) for k in range(1, lax.axis_size(axis))])


def after(value, *others):
    return lax.optimization_barrier((value, *others))[0]


class Order:
    def __init__(self):
        self.last = None

    def __call__(self, values):
        if self.last is None:
            return values
        return lax.optimization_barrier((values, self.last))[0]

    def add(self, terms):
        total = add(self(terms))
        self.last = total
        return total

    def run(self, body, outs, n_smem, ins, **more):
        got = call(body, outs, n_smem, self(list(ins)), **more)
        self.last = got[0]
        return got


def per_device(tokens, gain_one, w_qkv, w_out, gain_two, w_in, w_down, cotangent):
    tok, cot = tokens[0], cotangent[0]
    rows = tok.shape[0]
    many = TP * rows
    zo, z = lax.axis_index("zo"), lax.axis_index("z")
    x, c, y = lax.axis_index("x"), lax.axis_index("core"), lax.axis_index("shard")
    outer, shards = lax.axis_size("zo"), lax.axis_size("shard")
    part = w_qkv.shape[0]
    n_kv = 4 * outer
    keys = n_kv * many
    rows_d, rows_f, pad_d, pad_f = plan(shards)
    high_in, high = 2 * FF // 128 * pad_d, D // 128 * (pad_f + pad_d + 16)
    i32 = jnp.int32
    idx = jnp.stack([z, x, c, y]).astype(i32)
    order = Order()

    toks = gather(tok, "z")
    w_own, w_mine = order.run(
        group_kernel,
        [((part, WC), BF), ((part // 2, WC), BF)],
        1,
        [idx, w_qkv],
        name="group_columns",
    )
    gains_own = jnp.stack([gain_one, gain_two])
    gain_parts = gather(gains_own, "shard")
    w_slices = [w_own]
    for k in range(1, shards):
        w_slices.append(shift(w_mine, "shard", k))
        w_slices.append(shift(w_slices[-1], "core", 1))
    (pack,) = order.run(
        pack_kernel,
        [((2 * part + down_half(w_down.shape[0])[0], D), BF)],
        1,
        [idx, w_out, w_in, w_down],
        name="pack_weights",
    )
    packs = [shift(pack, "shard", k) for k in range(1, shards)]

    freq = THETA ** (-jnp.arange(HEAD_DIM // 2, dtype=F32) * (2.0 / HEAD_DIM))
    owners = lax.rem(z - jnp.arange(TP, dtype=i32) + TP, TP)
    places = []
    for cr in range(2):
        for xr in range(2):
            for zr in range(outer):
                zz = lax.rem(zo - zr + outer, outer)
                place = ((zz * TP + owners) * 2 + lax.rem(x + xr, 2)) * 2 + lax.rem(c + cr, 2)
                places.append(place)
    places = jnp.concatenate(places) * rows
    places = (places[:, None] + jnp.arange(rows, dtype=i32)).reshape(keys)
    angle = places.astype(F32)[:, None] * jnp.tile(freq, 4)[None, :]
    sign = jnp.where(jnp.arange(128) % 64 < 32, -1.0, 1.0).astype(F32)
    cosine, sine = jnp.cos(angle), jnp.sin(angle) * sign[None, :]

    query, kv, h_one, w_full, gains = order.run(
        functools.partial(front_kernel, shards),
        [
            ((many, 256), BF),
            ((many, 2 * GW), BF),
            ((many, D), BF),
            ((D, WC), BF),
            ((8, D), F32),
        ],
        1,
        [idx, *toks, *w_slices, *gain_parts, cosine, sine],
        name="front",
    )

    near = gather(kv, "zo")
    near = near + [shift(v, "x", 1) for v in near]
    kvs = near + [shift(v, "core", 1) for v in near]
    h_near = gather(after(h_one, near[-1]), "zo")
    h_near = h_near + [shift(v, "x", 1) for v in h_near]
    att = order.run(
        functools.partial(forward_kernel, n_kv),
        [((rows, GW), BF)] * TP + [((GW, many), F32), ((8, many), F32)],
        0,
        [query, *kvs],
        scratch=[
            pltpu.VMEM((keys, 2 * GW), BF),
            pltpu.VMEM((256, keys), BF),
            pltpu.VMEM((256, many), BF),
        ],
        name="attention_forward",
    )
    att_blocks, (attended_t, lse) = att[:TP], att[TP:]
    atts = [att_blocks[0]] + [shift(att_blocks[k], "z", -k) for k in range(1, TP)]

    packs = [after(p, lse) for p in packs]
    both = [v for p in packs for v in (p, shift(p, "core", 1))]
    mid = order.run(
        functools.partial(middle_kernel, len(both)),
        [((rows, D), F32), ((rows, D), F32), ((rows, ACT_ALL), BF), ((8, D), F32)]
        + [((rows, 256), BF)] * TP,
        1,
        [idx, *atts, tok, cot, gains, w_out, w_in, w_down, *both],
        scratch=[
            pltpu.VMEM((D, D), BF),
            pltpu.VMEM((D, 2 * FF), BF),
            pltpu.VMEM((FF, D), BF),
            pltpu.SemaphoreType.DMA((3 + 5 * len(both),)),
        ],
        any_ins=range(1 + TP + 3, 1 + TP + 6 + len(both)),
        name="feed_forward",
    )
    result, grad_middle, act, gain_two_row = mid[:4]
    act = after(act, *h_near)
    gatts = mid[4:]
    gas = [gatts[0]] + [shift(gatts[k], "z", k) for k in range(1, TP)]

    ffn = order.run(
        functools.partial(ffn_grads_kernel, shards),
        [((2, high_in, 128), BF)] * shards + [((shards, high, 128), BF)] * 2,
        1,
        [idx, act, shift(act, "core", 1), gain_two_row],
        scratch=[
            pltpu.VMEM((4 * shards, pad_d, 2 * rows), BF),
            pltpu.VMEM((4 * shards, pad_f, 2 * rows), BF),
            pltpu.VMEM((4 * shards, pad_d, 2 * rows), BF),
            pltpu.VMEM((2 * rows, 2 * FF + 2 * D), BF),
        ],
        name="ffn_weight_grads",
    )
    f_in = [ffn[0]] + [shift(ffn[k], "shard", k) for k in range(1, shards)]
    f_rest = [ffn[shards], shift(ffn[shards + 1], "x", 1)]
    hs = h_near + [shift(after(v, ffn[0]), "core", 1) for v in h_near]

    dkv_keep, dkv_send, dq = order.run(
        functools.partial(backward_kernel, n_kv),
        [((n_kv // 2, many, 2 * GW), BF)] * 2 + [((many, 256), BF)],
        0,
        [query, *kvs, *gas, attended_t, lse, cosine, sine],
        scratch=[
            pltpu.VMEM((keys, 2 * GW), BF),
            pltpu.VMEM((256, keys), BF),
            pltpu.VMEM((256, many), BF),
            pltpu.VMEM((256, many), BF),
            pltpu.VMEM((many, 2 * GW), BF),
            pltpu.VMEM((many, 2 * GW), BF),
            pltpu.VMEM((keys, 2 * GW), F32),
            pltpu.VMEM((256, many), F32),
        ],
        name="attention_backward",
    )
    mine, other = order.run(
        functools.partial(qkv_grads_kernel, shards, n_kv),
        [((shards, 2, rows_d, WC), BF)] * 2,
        1,
        [idx, *hs, dkv_keep, dkv_send, dq, w_full, gains],
        name="qkv_weight_grads",
    )
    terms = [dkv_keep, shift(after(dkv_send, mine), "core", 1)]
    wq = [mine, shift(after(other, *f_in, *f_rest), "core", 1)]
    terms = [t.reshape(2, outer, many, 2 * GW) for t in terms]
    got = shift(order.add([t[1] for t in terms]), "x", 1)
    terms = [t[0] for t in terms] + [got]

    f_in = reduce_step(order, f_in, "x", 0)
    f_rest = reduce_step(order, f_rest, "shard", 0)
    wq = reduce_step(order, wq, "shard", 0)
    wq = reduce_step(order, wq, "x", 0)

    if outer > 1:
        total = order.add(terms)
        sums = [total[0]] + [shift(total[k], "zo", -k) for k in range(1, outer)]
    else:
        sums = [t[0] for t in terms]
    (gh,) = order.run(
        functools.partial(combine_kernel, len(sums)),
        [((2, 2, rows, D), BF)],
        1,
        [idx, *sums, dq, w_full],
        name="h_one_grads",
    )
    gh = reduce_z(order, [gh], 1)
    f_rest = reduce_z(order, [order.add(f_rest).reshape(2, 2, high // TP, 128)], 1)
    f_in = reduce_z(order, [order.add(f_in).reshape(2, 2, high_in // TP, 128)], 1)
    wq = gather_z(sum_over(order.add(wq), "zo"), 2)
    gh = reduce_z(order, gh, 2)
    wq = gather_z(wq, 1)
    f_rest = reduce_z(order, f_rest, 2)
    f_in = reduce_z(order, f_in, 2)
    wq = jnp.stack(gather(wq, "x"))
    f_rest = gather_z(sum_over(order.add(f_rest), "zo"), 2)
    f_in = gather_z(sum_over(order.add(f_in), "zo"), 2)
    (grad_tokens,) = order.run(
        functools.partial(tail_kernel, len(gh)),
        [((rows, D), F32)],
        0,
        [*gh, tok, grad_middle, gains],
        name="token_grads",
    )
    f_rest = gather_z(after(f_rest, gh[-1]), 1)
    f_in = gather_z(after(f_in, gh[-1]), 1)
    wq_got = shift(wq, "core", 1)
    f_rest = jnp.stack(gather(f_rest, "x"))
    f_in = jnp.stack(gather(f_in, "x"))

    g_qkv, grad_gain_one = order.run(
        qkv_unpack_kernel,
        [((2, 2, rows_d, 3 * D), F32), ((1, part), F32)],
        1,
        [idx, wq, wq_got],
        scratch=[pltpu.VMEM((part, 128), F32)],
        name="qkv_unpack",
    )
    g_out, g_down, grad_gain_two = order.run(
        functools.partial(rest_unpack_kernel, shards),
        [
            ((2, 2, rows_d, D), F32),
            ((2, 2, rows_f, D), F32),
            ((1, part), F32),
        ],
        1,
        [idx, f_rest, shift(f_rest, "core", 1)],
        scratch=[pltpu.VMEM((high, 128), F32), pltpu.VMEM((8, D), F32)],
        name="w_down_w_out_unpack",
    )
    (g_in,) = order.run(
        functools.partial(in_unpack_kernel, shards),
        [((2, 2, rows_d, 2 * FF), F32)],
        1,
        [idx, f_in, shift(f_in, "core", 1)],
        scratch=[pltpu.VMEM((high_in, 128), F32)],
        name="w_in_unpack",
    )

    return (
        result[None],
        grad_tokens[None],
        grad_gain_one.reshape(part),
        g_qkv.reshape(part, 3 * D),
        g_out.reshape(part, D),
        grad_gain_two.reshape(part),
        g_in.reshape(part, 2 * FF),
        g_down.reshape(w_down.shape[0], D),
    )


def solution(mesh):
    blocks = mesh.shape["ctx"]
    fine = Mesh(
        mesh.devices.reshape(blocks // (TP * 4), TP, 2, 2, mesh.shape["shard"]), CTX + ("shard",)
    )
    rows, split = P("shard", CTX, None), P("shard", None)
    return jax.shard_map(
        per_device,
        mesh=fine,
        in_specs=(rows, P("shard"), split, split, P("shard"), split, split, rows),
        out_specs=(rows, rows, P("shard"), split, split, P("shard"), split, split),
        check_vma=False,
    )
```

time: 295 us -> 232 us (0.79)
  waiting for transfers between devices: 125 us -> 91.7 us
  local copies, waits for them, and re-layouts: 42.2 us -> 14.8 us
  starting transfers between devices: 54.3 us -> 43.2 us
  Pallas kernels: 57.9 us -> 68.4 us
    ppermute x46 -> x36, waiting for transfers between devices: 125 us -> 51.4 us  [shift(): return lax.ppermute(value, axis, [(i, (i + k) % n) for i in range(n)])]
    ppermute x0 -> x12, waiting for transfers between devices: none -> 40.2 us  [swap_z(): return lax.ppermute(value, 'z', [(i, i ^ bit) for i in range(TP)])]
    ppermute x46 -> x36, starting transfers between devices: 54.3 us -> 30.2 us  [shift(): return lax.ppermute(value, axis, [(i, (i + k) % n) for i in range(n)])]
    ppermute x0 -> x12, starting transfers between devices: none -> 13 us  [swap_z(): return lax.ppermute(value, 'z', [(i, i ^ bit) for i in range(TP)])]
    pallas_call x9 -> x13, Pallas kernels: 57.9 us -> 68.4 us  [call(): pl.pallas_call(body, out_shape=[jax.ShapeDtypeStruct(s, t) for s, t in ou...]
    convert_element_type x8 -> x13, other arithmetic: 8.88 us -> 2.47 us  [add(): return total.astype(BF)]
    concatenate x3 -> x2, local copies, waits for them, and re-layouts: 5.96 us -> 0.06 us  [gather_z(): jnp.concatenate([value, got])]
    dynamic_slice x5 -> x0, local copies, waits for them, and re-layouts: 4.85 us -> none  [the longest x3 3.23 us: fetch(): mine = lax.dynamic_slice_in_dim(weight, c * half, half, 0)]
  transfers between devices with their start and end apart: 46 -> 48, of which waited for: 20 -> 24; matrix products, arithmetic and copies ran while one was open for 15% -> 6% of each run, Pallas kernels for 13% -> 26%
where the time goes in v2:
time: 232 us; the launch traced here: 231 us
  waiting for transfers between devices  91.7 us (40%)
  Pallas kernels  68.4 us (29%)
  starting transfers between devices  43.2 us (19%)
  local copies, waits for them, and re-layouts  14.8 us (6%)
  other arithmetic  11.8 us (5%)
    pallas_call x13, Pallas kernels, call(): pl.pallas_call(body, out_shape=[jax.ShapeDtypeStruct(s, t) for s, t in ou...  68.4 us
    ppermute x36, waiting for transfers between devices, shift(): return lax.ppermute(value, axis, [(i, (i + k) % n) for i in range(n)])  51.4 us
    ppermute x12, waiting for transfers between devices, swap_z(): return lax.ppermute(value, 'z', [(i, i ^ bit) for i in range(TP)])  40.2 us
    ppermute x36, starting transfers between devices, shift(): return lax.ppermute(value, axis, [(i, (i + k) % n) for i in range(n)])  30.2 us
    ppermute x12, starting transfers between devices, swap_z(): return lax.ppermute(value, 'z', [(i, i ^ bit) for i in range(TP)])  13 us
    unnamed x90, local copies, waits for them, and re-layouts  8.97 us
    mul x1, other arithmetic, per_device(): cosine, sine = (jnp.cos(angle), jnp.sin(angle) * sign[None, :])  5.56 us
  transfers between devices with their start and end apart: 48, of which 24 were waited for; matrix products, arithmetic and copies ran while one was open for 6% of the time, Pallas kernels for 26%

profile of v2, /device:TPU:0, one launch (start us, length us, event | category | flops | bytes accessed | tf_op | source)
XLA Modules:
  0.0 231.0 jit_solution(9573541786491078665)
XLA Ops:
  0.7 3.1 %collective-permute-start = (bf16[128,768]{1,0:T(8,128)(2,1)}, bf16[128,768]{1,0:T(8,128)(2,1)S(1)}, u32[]{:S(2)}, u32[]{:S(2)}) collective-permute-start(bf16[128,768]{1,0:T(8,128)(2,1)} %bitcast.99), channel_id=1, source_target_pairs={{0,8},{8,16},{16,24},{24,0},{1,9},{9,17},{17,25},{25,1},{2,10},{10... | collective-permute-start | bytes 589832 | tf_op jit(solution)/shard_map/ppermute | solution.py:550
  3.7 2.6 %collective-permute-start.1 = (bf16[128,768]{1,0:T(8,128)(2,1)}, bf16[128,768]{1,0:T(8,128)(2,1)S(1)}, u32[]{:S(2)}, u32[]{:S(2)}) collective-permute-start(bf16[128,768]{1,0:T(8,128)(2,1)} %bitcast.100), channel_id=1, source_target_pairs={{0,16},{8,24},{16,0},{24,8},{1,17},{9,25},{17,1},{25,9},{2,18},{10... | collective-permute-start | bytes 589832 | tf_op jit(solution)/shard_map/ppermute | solution.py:550
  7.0 2.5 %group_columns.1 = (bf16[384,640]{1,0:T(8,128)(2,1)}, bf16[192,640]{1,0:T(8,128)(2,1)}) custom-call(s32[4]{0:T(128)} %pad_add_fusion.idx, bf16[384,2304]{1,0:T(8,128)(2,1)} %w_ref.1), custom_call_target="tpu_custom_call" | custom-call | flops 1 | bytes 1 | tf_op jit(solution)/shard_map/group_columns/pallas_call | solution.py:52
  9.5 1.5 collective-permute-start.3
  11.6 3.2 %pack_weights.1 = bf16[1056,768]{1,0:T(8,128)(2,1)} custom-call(s32[4]{0:T(128)} %pad_add_fusion.idx, bf16[384,768]{1,0:T(8,128)(2,1)} %refs_7_, bf16[384,2304]{1,0:T(8,128)(2,1)} %refs_8_, bf16[576,768]{1,0:T(8,128)(2,1)} %refs_9_), custom_call_target="tpu_custom_call" | custom-call | flops 1 | bytes 1 | tf_op jit(solution)/shard_map/pack_weights/pallas_call | solution.py:52
  14.8 1.5 collective-permute-start.12
  18.7 5.6 %fusion = (f32[2048,128]{1,0:T(8,128)}, f32[2048,128]{1,0:T(8,128)}) fusion(f32[128]{0:T(128)S(1)} %compare_select_fusion.2, f32[128]{0:T(128)S(1)} %mul.81, f32[2048]{0:T(1024)S(1)} %convert_bitcast_fusion), kind=kLoop, calls=%fused_computation.2 | loop fusion | flops 524288 | bytes 2106368 | tf_op jit(solution)/shard_map/mul | solution.py:672
  25.2 4.7 %front.1 = (bf16[512,256]{1,0:T(8,128)(2,1)}, bf16[512,384]{1,0:T(8,128)(2,1)}, bf16[512,768]{1,0:T(8,128)(2,1)}, bf16[768,640]{1,0:T(8,128)(2,1)}, f32[8,768]{1,0:T(8,128)}) custom-call(s32[4]{0:T(128)} %pad_add_fusion.idx, bf16[128,768]{1,0:T(8,128)(2,1)} %bitcast.101, bf16[128,768]{1,0:T(8,128)(2,1)} %copy-done.26, bf16[128,768]{1,0:T(8,128)(2,1)} %copy-done.27, ...), custom_call_target="tpu_custom_call" | custom-call | flops 1 | bytes 1 | tf_op jit(solution)/shard_map/front/pallas_call | solution.py:52
  29.8 1.5 collective-permute-start.6
  31.5 10.0 %collective-permute-done.6.refs_1_ = bf16[512,384]{1,0:T(8,128)(2,1)S(1)} collective-permute-done((bf16[512,384]{1,0:T(8,128)(2,1)}, bf16[512,384]{1,0:T(8,128)(2,1)S(1)}, u32[]{:S(2)}, u32[]{:S(2)}) %collective-permute-start.6) | collective-permute-done | bytes 393248 | tf_op jit(solution)/shard_map/ppermute | solution.py:550
  41.6 1.7 collective-permute-done.8.refs_3_
  44.0 9.6 %attention_forward.1 = (bf16[128,192]{1,0:T(8,128)(2,1)}, bf16[128,192]{1,0:T(8,128)(2,1)}, bf16[128,192]{1,0:T(8,128)(2,1)}, bf16[128,192]{1,0:T(8,128)(2,1)}, f32[192,512]{1,0:T(8,128)}, /*index=5*/f32[8,512]{1,0:T(8,128)}) custom-call(bf16[512,256]{1,0:T(8,128)(2,1)} %get-tuple-element.231.q_ref, bf16[512,384]{1,0:T(8,128)(2,1)} %get-tuple-element.232.refs_0_, ...), custom_call_target="tpu_custom_call" | custom-call | flops 1 | bytes 1 | tf_op jit(solution)/shard_map/attention_forward/pallas_call | solution.py:52
  53.8 1.5 collective-permute-start.17
  55.7 1.7 collective-permute-start.10
  57.8 2.5 %collective-permute-done.9.refs_1_ = bf16[128,192]{1,0:T(8,128)(2,1)S(1)} collective-permute-done((bf16[128,192]{1,0:T(8,128)(2,1)}, bf16[128,192]{1,0:T(8,128)(2,1)S(1)}, u32[]{:S(2)}, u32[]{:S(2)}) %collective-permute-start.9) | collective-permute-done | bytes 49184 | tf_op jit(solution)/shard_map/ppermute | solution.py:550
  60.3 3.7 %collective-permute-done.10.refs_2_ = bf16[128,192]{1,0:T(8,128)(2,1)S(1)} collective-permute-done((bf16[128,192]{1,0:T(8,128)(2,1)}, bf16[128,192]{1,0:T(8,128)(2,1)S(1)}, u32[]{:S(2)}, u32[]{:S(2)}) %collective-permute-start.10) | collective-permute-done | bytes 49184 | tf_op jit(solution)/shard_map/ppermute | solution.py:550
  65.3 8.5 %feed_forward.1 = (f32[128,768]{1,0:T(8,128)}, f32[128,768]{1,0:T(8,128)}, bf16[128,6528]{1,0:T(8,128)(2,1)}, f32[8,768]{1,0:T(8,128)}, bf16[128,256]{1,0:T(8,12...) custom-call(s32[4]{0:T(128)} %pad_add_fusion.idx, ...), custom_call_target="tpu_custom_call" | custom-call | flops 1 | bytes 1 | tf_op jit(solution)/shard_map/feed_forward/pallas_call | solution.py:52
  73.9 3.7 %collective-permute-done.18.got = bf16[128,6528]{1,0:T(8,128)(2,1)S(1)} collective-permute-done((bf16[128,6528]{1,0:T(8,128)(2,1)}, bf16[128,6528]{1,0:T(8,128)(2,1)S(1)}, u32[]{:S(2)}, u32[]{:S(2)}) %collective-permute-start.18) | collective-permute-done | bytes 1671200 | tf_op jit(solution)/shard_map/ppermute | solution.py:550
  78.8 4.5 %ffn_weight_grads.1 = (bf16[2,1728,128]{2,1,0:T(8,128)(2,1)}, bf16[2,1728,128]{2,1,0:T(8,128)(2,1)}, bf16[2,1536,128]{2,1,0:T(8,128)(2,1)}, bf16[2,1536,128]{2,1,0:T(8,128)(2,1)}) custom-call(s32[4]{0:T(128)} %pad_add_fusion.idx, bf16[128,6528]{1,0:T(8,128)(2,1)} %get-tuple-element.227.own, bf16[128,6528]{1,0:T(8,128)(2,1)} %copy-done.6, ...), custom_call_target="tpu_custom_call" | custom-call | flops 1 | bytes 1 | tf_op jit(solution)/shard_map/ffn_weight_grads/pallas_call | solution.py:52
  85.2 2.6 %collective-permute-start.16 = (bf16[128,256]{1,0:T(8,128)(2,1)S(1)}, bf16[128,256]{1,0:T(8,128)(2,1)S(1)}, u32[]{:S(2)}, u32[]{:S(2)}) collective-permute-start(bf16[128,256]{1,0:T(8,128)(2,1)S(1)} %copy-done.41), channel_id=1, source_target_pairs={{0,24},{8,0},{16,8},{24,16},{1,25},{9,1},{17,9},{25,17},{2,26},{10... | collective-permute-start | bytes 196616 | tf_op jit(solution)/shard_map/ppermute | solution.py:550
  87.8 2.8 %collective-permute-done.14.refs_5_ = bf16[128,256]{1,0:T(8,128)(2,1)S(1)} collective-permute-done((bf16[128,256]{1,0:T(8,128)(2,1)S(1)}, bf16[128,256]{1,0:T(8,128)(2,1)S(1)}, u32[]{:S(2)}, u32[]{:S(2)}) %collective-permute-start.14) | collective-permute-done | bytes 65568 | tf_op jit(solution)/shard_map/ppermute | solution.py:550
  90.7 1.5 collective-permute-start.23
  92.7 1.5 collective-permute-start.24
  94.3 11.4 %attention_backward.1 = (bf16[2,512,384]{2,1,0:T(8,128)(2,1)}, bf16[2,512,384]{2,1,0:T(8,128)(2,1)}, bf16[512,256]{1,0:T(8,128)(2,1)}) custom-call(bf16[512,256]{1,0:T(8,128)(2,1)} %get-tuple-element.231.q_ref, bf16[512,384]{1,0:T(8,128)(2,1)} %get-tuple-element.232.refs_0_, bf16[512,384]{1,0:T(8,128)(2,1)} %copy-done.9, bf16[512,384]{1,0:T(8,128)(2,1)} %copy-done.10, ...), custom_call_target="tpu_custom_call" | custom-call | flops 1 | bytes 1 | tf_op jit(solution)/shard_map/attention_backward/pallas_call | solution.py:52
  106.9 6.4 %qkv_weight_grads.1 = (bf16[2,2,96,640]{3,2,1,0:T(8,128)(2,1)}, bf16[2,2,96,640]{3,2,1,0:T(8,128)(2,1)}) custom-call(s32[4]{0:T(128)} %pad_add_fusion.idx, bf16[512,768]{1,0:T(8,128)(2,1)} %get-tuple-element.251.refs_0_, bf16[512,768]{1,0:T(8,128)(2,1)} %copy-done.15, bf16[512,768]{1,0:T(8,128)(2,1)} %collective-permute-done.19.refs_2_, ...), custom_call_target="tpu_custom_call" | custom-call | flops 1 | bytes 1 | tf_op jit(solution)/shard_map/qkv_weight_grads/pallas_call | solution.py:52
  115.0 1.5 collective-permute-done.25
  119.2 1.5 collective-permute-start.26
  121.4 1.5 collective-permute-start.29
  123.5 4.9 %collective-permute-done.26 = bf16[2,96,640]{2,1,0:T(8,128)(2,1)} collective-permute-done((bf16[2,96,640]{2,1,0:T(8,128)(2,1)}, bf16[2,96,640]{2,1,0:T(8,128)(2,1)}, u32[]{:S(2)}, u32[]{:S(2)}) %collective-permute-start.26) | collective-permute-done | bytes 245792 | tf_op jit(solution)/shard_map/ppermute | solution.py:550
  130.0 3.0 %collective-permute-done.22 = bf16[1,512,384]{2,1,0:T(8,128)(2,1)S(1)} collective-permute-done((bf16[1,512,384]{2,1,0:T(8,128)(2,1)}, bf16[1,512,384]{2,1,0:T(8,128)(2,1)S(1)}, u32[]{:S(2)}, u32[]{:S(2)}) %collective-permute-start.22) | collective-permute-done | bytes 393248 | tf_op jit(solution)/shard_map/ppermute | solution.py:550
  133.8 3.9 %h_one_grads.1 = bf16[2,2,128,768]{3,2,1,0:T(8,128)(2,1)} custom-call(s32[4]{0:T(128)} %pad_add_fusion.idx, bf16[512,384]{1,0:T(8,128)(2,1)} %get-tuple-element.279.refs_0_, bf16[512,384]{1,0:T(8,128)(2,1)} %get-tuple-element.280.refs_1_, bf16[512,384]{1,0:T(8,128)(2,1)} %bitcast.119, bf16[512,256]{1,0:T(8,128)(2,1)} %get-tuple-element.282.refs_6_.refs_3_, ...), custom_call_target="tpu_custom_call" | custom-call | flops 1 | bytes 1 | tf_op jit(solution)/shard_map/h_one_grads/pallas_call | solution.py:52
  144.7 2.0 collective-permute-start.33
  146.9 5.2 %collective-permute-done.36 = bf16[96,640]{1,0:T(8,128)(2,1)S(1)} collective-permute-done((bf16[96,640]{1,0:T(8,128)(2,1)S(1)}, bf16[96,640]{1,0:T(8,128)(2,1)S(1)}, u32[]{:S(2)}, u32[]{:S(2)}) %collective-permute-start.36) | collective-permute-done | bytes 122912 | tf_op jit(solution)/shard_map/ppermute | solution.py:577
  152.8 3.5 %collective-permute-done.33 = bf16[2,384,128]{2,1,0:T(8,128)(2,1)S(1)} collective-permute-done((bf16[2,384,128]{2,1,0:T(8,128)(2,1)S(1)}, bf16[2,384,128]{2,1,0:T(8,128)(2,1)S(1)}, u32[]{:S(2)}, u32[]{:S(2)}) %collective-permute-start.33) | collective-permute-done | bytes 196640 | tf_op jit(solution)/shard_map/ppermute | solution.py:577
  156.3 4.7 %collective-permute-done.32 = bf16[2,432,128]{2,1,0:T(8,128)(2,1)S(1)} collective-permute-done((bf16[2,432,128]{2,1,0:T(8,128)(2,1)S(1)}, bf16[2,432,128]{2,1,0:T(8,128)(2,1)S(1)}, u32[]{:S(2)}, u32[]{:S(2)}) %collective-permute-start.32) | collective-permute-done | bytes 221216 | tf_op jit(solution)/shard_map/ppermute | solution.py:577
  162.5 2.4 %collective-permute-start.35 = (bf16[384,128]{1,0:T(8,128)(2,1)S(1)}, bf16[384,128]{1,0:T(8,128)(2,1)S(1)}, u32[]{:S(2)}, u32[]{:S(2)}) collective-permute-start(bf16[384,128]{1,0:T(8,128)(2,1)S(1)} %add_convert_fusion.12), channel_id=1, source_target_pairs={{0,16},{8,24},{16,0},{24,8},{1,17},{9,25},{17,1},{25,9},{2,18},{10... | collective-permute-start | bytes 294920 | tf_op jit(solution)/shard_map/ppermute | solution.py:577
  165.6 13.1 %collective-permute-done.35 = bf16[384,128]{1,0:T(8,128)(2,1)S(1)} collective-permute-done((bf16[384,128]{1,0:T(8,128)(2,1)S(1)}, bf16[384,128]{1,0:T(8,128)(2,1)S(1)}, u32[]{:S(2)}, u32[]{:S(2)}) %collective-permute-start.35) | collective-permute-done | bytes 98336 | tf_op jit(solution)/shard_map/ppermute | solution.py:577
  180.8 2.9 %collective-permute-start.40 = (bf16[384,128]{1,0:T(8,128)(2,1)S(1)}, bf16[384,128]{1,0:T(8,128)(2,1)S(1)}, u32[]{:S(2)}, u32[]{:S(2)}) collective-permute-start(bf16[384,128]{1,0:T(8,128)(2,1)S(1)} %add_convert_fusion.11), channel_id=1, source_target_pairs={{0,16},{8,24},{16,0},{24,8},{1,17},{9,25},{17,1},{25,9},{2,18},{10... | collective-permute-start | bytes 294920 | tf_op jit(solution)/shard_map/ppermute | solution.py:577
  183.7 4.5 %collective-permute-done.44 = bf16[432,128]{1,0:T(8,128)(2,1)S(1)} collective-permute-done((bf16[432,128]{1,0:T(8,128)(2,1)S(1)}, bf16[432,128]{1,0:T(8,128)(2,1)S(1)}, u32[]{:S(2)}, u32[]{:S(2)}) %collective-permute-start.44) | collective-permute-done | bytes 110624 | tf_op jit(solution)/shard_map/ppermute | solution.py:577
  189.7 1.6 collective-permute-start.41
  191.4 4.6 %collective-permute-done.45 = bf16[2,432,128]{2,1,0:T(8,128)(2,1)S(1)} collective-permute-done((bf16[2,432,128]{2,1,0:T(8,128)(2,1)S(1)}, bf16[2,432,128]{2,1,0:T(8,128)(2,1)S(1)}, u32[]{:S(2)}, u32[]{:S(2)}) %collective-permute-start.45) | collective-permute-done | bytes 221216 | tf_op jit(solution)/shard_map/ppermute | solution.py:577
  196.1 2.0 collective-permute-done.41
  198.4 9.3 %collective-permute-done.46 = bf16[4,432,128]{2,1,0:T(8,128)(2,1)S(1)} collective-permute-done((bf16[4,432,128]{2,1,0:T(8,128)(2,1)S(1)}, bf16[4,432,128]{2,1,0:T(8,128)(2,1)S(1)}, u32[]{:S(2)}, u32[]{:S(2)}) %collective-permute-start.46) | collective-permute-done | bytes 442400 | tf_op jit(solution)/shard_map/ppermute | solution.py:550
  207.9 4.0 %collective-permute-done.42 = bf16[4,384,128]{2,1,0:T(8,128)(2,1)S(1)} collective-permute-done((bf16[4,384,128]{2,1,0:T(8,128)(2,1)S(1)}, bf16[4,384,128]{2,1,0:T(8,128)(2,1)S(1)}, u32[]{:S(2)}, u32[]{:S(2)}) %collective-permute-start.42) | collective-permute-done | bytes 393248 | tf_op jit(solution)/shard_map/ppermute | solution.py:550
  212.1 2.7 %token_grads.1 = f32[128,768]{1,0:T(8,128)} custom-call(bf16[128,768]{1,0:T(8,128)(2,1)} %get-tuple-element.310.refs_0_, bf16[128,768]{1,0:T(8,128)(2,1)} %get-tuple-element.311.refs_1_, bf16[128,768]{1,0:T(8,128)(2,1)} %copy-done.29, bf16[128,768]{1,0:T(8,128)(2,1)} %bitcast.103, f32[128,768]{1,0:T(8,128)} %get-tuple-element.314.refs_4_, ...), custom_call_target="tpu_custom_call" | custom-call | flops 1 | bytes 1 | tf_op jit(solution)/shard_map/token_grads/pallas_call | solution.py:52
  215.7 3.8 %qkv_unpack.1 = (f32[2,2,96,2304]{3,2,1,0:T(8,128)}, f32[1,384]{1,0:T(1,128)}) custom-call(s32[4]{0:T(128)} %pad_add_fusion.idx, bf16[2,4,96,640]{3,2,1,0:T(8,128)(2,1)} %copy-done, bf16[2,4,96,640]{3,2,1,0:T(8,128)(2,1)} %copy-done.12), custom_call_target="tpu_custom_call" | custom-call | flops 1 | bytes 1 | tf_op jit(solution)/shard_map/qkv_unpack/pallas_call | solution.py:52
  221.7 3.5 %w_down_w_out_unpack.1 = (f32[2,2,96,768]{3,2,1,0:T(8,128)}, f32[2,2,144,768]{3,2,1,0:T(8,128)}, f32[1,384]{1,0:T(1,128)}) custom-call(s32[4]{0:T(128)} %pad_add_fusion.idx, bf16[2,4,384,128]{3,2,1,0:T(8,128)(2,1)} %copy-done.3, bf16[2,4,384,128]{3,2,1,0:T(8,128)(2,1)} %copy-done.17), custom_call_target="tpu_custom_call" | custom-call | flops 1 | bytes 1 | tf_op jit(solution)/shard_map/w_down_w_out_unpack/pallas_call | solution.py:52
  227.3 3.8 %w_in_unpack.1 = f32[2,2,96,2304]{3,2,1,0:T(8,128)} custom-call(s32[4]{0:T(128)} %pad_add_fusion.idx, bf16[2,4,432,128]{3,2,1,0:T(8,128)(2,1)} %copy-done.1, bf16[2,4,432,128]{3,2,1,0:T(8,128)(2,1)} %copy-done.14), custom_call_target="tpu_custom_call" | custom-call | flops 1 | bytes 1 | tf_op jit(solution)/shard_map/w_in_unpack/pallas_call | solution.py:52
  (208 shorter events, 39.8 us)
Async XLA Ops:
  0.7 23.6 %collective-permute-start = (bf16[128,768]{1,0:T(8,128)(2,1)}, bf16[128,768]{1,0:T(8,128)(2,1)S(1)}, u32[]{:S(2)}, u32[]{:S(2)}) collective-permute-start(bf16[128,768]{1,0:T(8,128)(2,1)} %bitcast.99), channel_id=1, source_target_pairs={{0,8},{8,16},{16,24},{24,0},{1,9},{9,17},{17,25},{25,1},{2,10},{10... | collective-permute-start | bytes 589832 | tf_op jit(solution)/shard_map/ppermute | solution.py:550
  3.7 20.5 %collective-permute-start.1 = (bf16[128,768]{1,0:T(8,128)(2,1)}, bf16[128,768]{1,0:T(8,128)(2,1)S(1)}, u32[]{:S(2)}, u32[]{:S(2)}) collective-permute-start(bf16[128,768]{1,0:T(8,128)(2,1)} %bitcast.100), channel_id=1, source_target_pairs={{0,16},{8,24},{16,0},{24,8},{1,17},{9,25},{17,1},{25,9},{2,18},{10... | collective-permute-start | bytes 589832 | tf_op jit(solution)/shard_map/ppermute | solution.py:550
  9.5 9.2 %collective-permute-start.3 = (bf16[192,640]{1,0:T(8,128)(2,1)}, bf16[192,640]{1,0:T(8,128)(2,1)S(1)}, u32[]{:S(2)}, u32[]{:S(2)}) collective-permute-start(bf16[192,640]{1,0:T(8,128)(2,1)} %get-tuple-element.171), channel_id=1, source_target_pairs={{0,1},{1,0},{2,3},{3,2},{4,5},{5,4},{6,7},{7,6},{8,9},{9,8},{10,11... | collective-permute-start | bytes 737288 | tf_op jit(solution)/shard_map/ppermute | solution.py:550
  11.0 6.3 %collective-permute-start.5 = (bf16[2,384]{1,0:T(2,128)(2,1)S(1)}, bf16[2,384]{1,0:T(2,128)(2,1)S(1)}, u32[]{:S(2)}, u32[]{:S(2)}) collective-permute-start(bf16[2,384]{1,0:T(2,128)(2,1)S(1)} %pad_maximum_fusion.7.refs_7_), channel_id=1, source_target_pairs={{0,1},{1,0},{2,3},{3,2},{4,5},{5,4},{6,7},{7,6},{8,9},{9,8},{10,11... | collective-permute-start | bytes 4616 | tf_op jit(solution)/shard_map/ppermute | solution.py:550
  14.8 38.8 %collective-permute-start.12 = (bf16[1056,768]{1,0:T(8,128)(2,1)}, bf16[1056,768]{1,0:T(8,128)(2,1)S(1)}, u32[]{:S(2)}, u32[]{:S(2)}) collective-permute-start(bf16[1056,768]{1,0:T(8,128)(2,1)} %pack_weights.1), channel_id=1, source_target_pairs={{0,1},{1,0},{2,3},{3,2},{4,5},{5,4},{6,7},{7,6},{8,9},{9,8},{10,11... | collective-permute-start | bytes 4866056 | tf_op jit(solution)/shard_map/ppermute | solution.py:550
  17.3 7.0 %collective-permute-start.2 = (bf16[128,768]{1,0:T(8,128)(2,1)S(1)}, bf16[128,768]{1,0:T(8,128)(2,1)S(1)}, u32[]{:S(2)}, u32[]{:S(2)}) collective-permute-start(bf16[128,768]{1,0:T(8,128)(2,1)S(1)} %bitcast.104), channel_id=1, source_target_pairs={{0,24},{8,0},{16,8},{24,16},{1,25},{9,1},{17,9},{25,17},{2,26},{10... | collective-permute-start | bytes 589832 | tf_op jit(solution)/shard_map/ppermute | solution.py:550
  18.7 5.6 %collective-permute-start.4 = (bf16[192,640]{1,0:T(8,128)(2,1)S(1)}, bf16[192,640]{1,0:T(8,128)(2,1)S(1)}, u32[]{:S(2)}, u32[]{:S(2)}) collective-permute-start(bf16[192,640]{1,0:T(8,128)(2,1)S(1)} %collective-permute-done.3.refs_5_), channel_id=1, source_target_pairs={{0,2},{2,0},{1,3},{3,1},{4,6},{6,4},{5,7},{7,5},{8,10},{10,8},{9,1... | collective-permute-start | bytes 737288 | tf_op jit(solution)/shard_map/ppermute | solution.py:550
  29.8 11.7 %collective-permute-start.6 = (bf16[512,384]{1,0:T(8,128)(2,1)}, bf16[512,384]{1,0:T(8,128)(2,1)S(1)}, u32[]{:S(2)}, u32[]{:S(2)}) collective-permute-start(bf16[512,384]{1,0:T(8,128)(2,1)} %get-tuple-element.232.refs_0_), channel_id=1, source_target_pairs={{0,4},{4,0},{1,5},{5,1},{2,6},{6,2},{3,7},{7,3},{8,12},{12,8},{9,1... | collective-permute-start | bytes 1179656 | tf_op jit(solution)/shard_map/ppermute | solution.py:550
  31.3 10.2 %collective-permute-start.7 = (bf16[512,384]{1,0:T(8,128)(2,1)}, bf16[512,384]{1,0:T(8,128)(2,1)S(1)}, u32[]{:S(2)}, u32[]{:S(2)}) collective-permute-start(bf16[512,384]{1,0:T(8,128)(2,1)} %get-tuple-element.232.refs_0_), channel_id=1, source_target_pairs={{0,2},{2,0},{1,3},{3,1},{4,6},{6,4},{5,7},{7,5},{8,10},{10,8},{9,1... | collective-permute-start | bytes 1179656 | tf_op jit(solution)/shard_map/ppermute | solution.py:550
  41.6 1.7 collective-permute-start.8
  53.6 10.5 %collective-permute-start.13 = (bf16[1056,768]{1,0:T(8,128)(2,1)S(1)}, bf16[1056,768]{1,0:T(8,128)(2,1)S(1)}, u32[]{:S(2)}, u32[]{:S(2)}) collective-permute-start(bf16[1056,768]{1,0:T(8,128)(2,1)S(1)} %collective-permute-done.12.refs_10_), channel_id=1, source_target_pairs={{0,2},{2,0},{1,3},{3,1},{4,6},{6,4},{5,7},{7,5},{8,10},{10,8},{9,1... | collective-permute-start | bytes 4866056 | tf_op jit(solution)/shard_map/ppermute | solution.py:550
  53.8 20.0 %collective-permute-start.17 = (bf16[512,768]{1,0:T(8,128)(2,1)}, bf16[512,768]{1,0:T(8,128)(2,1)S(1)}, u32[]{:S(2)}, u32[]{:S(2)}) collective-permute-start(bf16[512,768]{1,0:T(8,128)(2,1)} %get-tuple-element.251.refs_0_), channel_id=1, source_target_pairs={{0,4},{4,0},{1,5},{5,1},{2,6},{6,2},{3,7},{7,3},{8,12},{12,8},{9,1... | collective-permute-start | bytes 2359304 | tf_op jit(solution)/shard_map/ppermute | solution.py:550
  55.3 5.0 %collective-permute-start.9 = (bf16[128,192]{1,0:T(8,128)(2,1)}, bf16[128,192]{1,0:T(8,128)(2,1)S(1)}, u32[]{:S(2)}, u32[]{:S(2)}) collective-permute-start(bf16[128,192]{1,0:T(8,128)(2,1)} %get-tuple-element.196), channel_id=1, source_target_pairs={{0,24},{8,0},{16,8},{24,16},{1,25},{9,1},{17,9},{25,17},{2,26},{10... | collective-permute-start | bytes 147464 | tf_op jit(solution)/shard_map/ppermute | solution.py:550
  55.7 8.4 %collective-permute-start.10 = (bf16[128,192]{1,0:T(8,128)(2,1)}, bf16[128,192]{1,0:T(8,128)(2,1)S(1)}, u32[]{:S(2)}, u32[]{:S(2)}) collective-permute-start(bf16[128,192]{1,0:T(8,128)(2,1)} %get-tuple-element.197), channel_id=1, source_target_pairs={{0,16},{8,24},{16,0},{24,8},{1,17},{9,25},{17,1},{25,9},{2,18},{10... | collective-permute-start | bytes 147464 | tf_op jit(solution)/shard_map/ppermute | solution.py:550
  57.4 6.7 %collective-permute-start.11 = (bf16[128,192]{1,0:T(8,128)(2,1)}, bf16[128,192]{1,0:T(8,128)(2,1)S(1)}, u32[]{:S(2)}, u32[]{:S(2)}) collective-permute-start(bf16[128,192]{1,0:T(8,128)(2,1)} %get-tuple-element.198), channel_id=1, source_target_pairs={{0,8},{8,16},{16,24},{24,0},{1,9},{9,17},{17,25},{25,1},{2,10},{10... | collective-permute-start | bytes 147464 | tf_op jit(solution)/shard_map/ppermute | solution.py:550
  73.8 3.8 %collective-permute-start.18 = (bf16[128,6528]{1,0:T(8,128)(2,1)}, bf16[128,6528]{1,0:T(8,128)(2,1)S(1)}, u32[]{:S(2)}, u32[]{:S(2)}) collective-permute-start(bf16[128,6528]{1,0:T(8,128)(2,1)} %get-tuple-element.227.own), channel_id=1, source_target_pairs={{0,2},{2,0},{1,3},{3,1},{4,6},{6,4},{5,7},{7,5},{8,10},{10,8},{9,1... | collective-permute-start | bytes 5013512 | tf_op jit(solution)/shard_map/ppermute | solution.py:550
  83.4 23.5 %collective-permute-start.19 = (bf16[512,768]{1,0:T(8,128)(2,1)}, bf16[512,768]{1,0:T(8,128)(2,1)}, u32[]{:S(2)}, u32[]{:S(2)}) collective-permute-start(bf16[512,768]{1,0:T(8,128)(2,1)} %get-tuple-element.251.refs_0_), channel_id=1, source_target_pairs={{0,2},{2,0},{1,3},{3,1},{4,6},{6,4},{5,7},{7,5},{8,10},{10,8},{9,1... | collective-permute-start | bytes 2359304 | tf_op jit(solution)/shard_map/ppermute | solution.py:550
  83.5 23.4 %collective-permute-start.20 = (bf16[512,768]{1,0:T(8,128)(2,1)S(1)}, bf16[512,768]{1,0:T(8,128)(2,1)}, u32[]{:S(2)}, u32[]{:S(2)}) collective-permute-start(bf16[512,768]{1,0:T(8,128)(2,1)S(1)} %collective-permute-done.17.refs_1_), channel_id=1, source_target_pairs={{0,2},{2,0},{1,3},{3,1},{4,6},{6,4},{5,7},{7,5},{8,10},{10,8},{9,1... | collective-permute-start | bytes 2359304 | tf_op jit(solution)/shard_map/ppermute | solution.py:550
  83.9 6.8 %collective-permute-start.14 = (bf16[128,256]{1,0:T(8,128)(2,1)S(1)}, bf16[128,256]{1,0:T(8,128)(2,1)S(1)}, u32[]{:S(2)}, u32[]{:S(2)}) collective-permute-start(bf16[128,256]{1,0:T(8,128)(2,1)S(1)} %copy-done.43), channel_id=1, source_target_pairs={{0,8},{8,16},{16,24},{24,0},{1,9},{9,17},{17,25},{25,1},{2,10},{10... | collective-permute-start | bytes 196616 | tf_op jit(solution)/shard_map/ppermute | solution.py:550
  84.5 8.3 %collective-permute-start.15 = (bf16[128,256]{1,0:T(8,128)(2,1)S(1)}, bf16[128,256]{1,0:T(8,128)(2,1)S(1)}, u32[]{:S(2)}, u32[]{:S(2)}) collective-permute-start(bf16[128,256]{1,0:T(8,128)(2,1)S(1)} %copy-done.42), channel_id=1, source_target_pairs={{0,16},{8,24},{16,0},{24,8},{1,17},{9,25},{17,1},{25,9},{2,18},{10... | collective-permute-start | bytes 196616 | tf_op jit(solution)/shard_map/ppermute | solution.py:550
  85.2 7.5 %collective-permute-start.16 = (bf16[128,256]{1,0:T(8,128)(2,1)S(1)}, bf16[128,256]{1,0:T(8,128)(2,1)S(1)}, u32[]{:S(2)}, u32[]{:S(2)}) collective-permute-start(bf16[128,256]{1,0:T(8,128)(2,1)S(1)} %copy-done.41), channel_id=1, source_target_pairs={{0,24},{8,0},{16,8},{24,16},{1,25},{9,1},{17,9},{25,17},{2,26},{10... | collective-permute-start | bytes 196616 | tf_op jit(solution)/shard_map/ppermute | solution.py:550
  90.7 23.7 %collective-permute-start.23 = (bf16[2,1728,128]{2,1,0:T(8,128)(2,1)}, bf16[2,1728,128]{2,1,0:T(8,128)(2,1)S(1)}, u32[]{:S(2)}, u32[]{:S(2)}) collective-permute-start(bf16[2,1728,128]{2,1,0:T(8,128)(2,1)} %get-tuple-element.265), channel_id=1, source_target_pairs={{0,1},{1,0},{2,3},{3,2},{4,5},{5,4},{6,7},{7,6},{8,9},{9,8},{10,11... | collective-permute-start | bytes 2654216 | tf_op jit(solution)/shard_map/ppermute | solution.py:550
  92.7 21.6 %collective-permute-start.24 = (bf16[2,1536,128]{2,1,0:T(8,128)(2,1)}, bf16[2,1536,128]{2,1,0:T(8,128)(2,1)S(1)}, u32[]{:S(2)}, u32[]{:S(2)}) collective-permute-start(bf16[2,1536,128]{2,1,0:T(8,128)(2,1)} %get-tuple-element.267), channel_id=1, source_target_pairs={{0,4},{4,0},{1,5},{5,1},{2,6},{6,2},{3,7},{7,3},{8,12},{12,8},{9,1... | collective-permute-start | bytes 2359304 | tf_op jit(solution)/shard_map/ppermute | solution.py:550
  113.3 3.2 %collective-permute-start.21 = (bf16[2,512,384]{2,1,0:T(8,128)(2,1)S(1)}, bf16[2,512,384]{2,1,0:T(8,128)(2,1)S(1)}, u32[]{:S(2)}, u32[]{:S(2)}) collective-permute-start(bf16[2,512,384]{2,1,0:T(8,128)(2,1)S(1)} %copy-done.16), channel_id=1, source_target_pairs={{0,2},{2,0},{1,3},{3,1},{4,6},{6,4},{5,7},{7,5},{8,10},{10,8},{9,1... | collective-permute-start | bytes 2359304 | tf_op jit(solution)/shard_map/ppermute | solution.py:550
  114.6 1.9 collective-permute-start.25
  119.2 9.1 %collective-permute-start.26 = (bf16[2,96,640]{2,1,0:T(8,128)(2,1)}, bf16[2,96,640]{2,1,0:T(8,128)(2,1)}, u32[]{:S(2)}, u32[]{:S(2)}) collective-permute-start(bf16[2,96,640]{2,1,0:T(8,128)(2,1)} %add_convert_fusion.5), channel_id=1, source_target_pairs={{0,1},{1,0},{2,3},{3,2},{4,5},{5,4},{6,7},{7,6},{8,9},{9,8},{10,11... | collective-permute-start | bytes 737288 | tf_op jit(solution)/shard_map/ppermute | solution.py:550
  120.8 12.3 %collective-permute-start.22 = (bf16[1,512,384]{2,1,0:T(8,128)(2,1)}, bf16[1,512,384]{2,1,0:T(8,128)(2,1)S(1)}, u32[]{:S(2)}, u32[]{:S(2)}) collective-permute-start(bf16[1,512,384]{2,1,0:T(8,128)(2,1)} %add_convert_fusion.4), channel_id=1, source_target_pairs={{0,4},{4,0},{1,5},{5,1},{2,6},{6,2},{3,7},{7,3},{8,12},{12,8},{9,1... | collective-permute-start | bytes 1179656 | tf_op jit(solution)/shard_map/ppermute | solution.py:550
  121.4 21.1 %collective-permute-start.29 = (bf16[1728,128]{1,0:T(8,128)(2,1)S(1)}, bf16[1728,128]{1,0:T(8,128)(2,1)S(1)}, u32[]{:S(2)}, u32[]{:S(2)}) collective-permute-start(bf16[1728,128]{1,0:T(8,128)(2,1)S(1)} %add_convert_fusion.1), channel_id=1, source_target_pairs={{0,4},{4,0},{1,5},{5,1},{2,6},{6,2},{3,7},{7,3},{8,12},{12,8},{9,1... | collective-permute-start | bytes 1327112 | tf_op jit(solution)/shard_map/ppermute | solution.py:550
  123.0 17.2 %collective-permute-start.30 = (bf16[1536,128]{1,0:T(8,128)(2,1)S(1)}, bf16[1536,128]{1,0:T(8,128)(2,1)S(1)}, u32[]{:S(2)}, u32[]{:S(2)}) collective-permute-start(bf16[1536,128]{1,0:T(8,128)(2,1)S(1)} %add_convert_fusion.3), channel_id=1, source_target_pairs={{0,1},{1,0},{2,3},{3,2},{4,5},{5,4},{6,7},{7,6},{8,9},{9,8},{10,11... | collective-permute-start | bytes 1179656 | tf_op jit(solution)/shard_map/ppermute | solution.py:550
  129.4 14.7 %collective-permute-start.28 = (bf16[96,640]{1,0:T(8,128)(2,1)S(1)}, bf16[96,640]{1,0:T(8,128)(2,1)S(1)}, u32[]{:S(2)}, u32[]{:S(2)}) collective-permute-start(bf16[96,640]{1,0:T(8,128)(2,1)S(1)} %add_convert_fusion.8), channel_id=1, source_target_pairs={{0,4},{4,0},{1,5},{5,1},{2,6},{6,2},{3,7},{7,3},{8,12},{12,8},{9,1... | collective-permute-start | bytes 368648 | tf_op jit(solution)/shard_map/ppermute | solution.py:550
  138.8 22.2 %collective-permute-start.27 = (bf16[2,128,768]{2,1,0:T(8,128)(2,1)S(1)}, bf16[2,128,768]{2,1,0:T(8,128)(2,1)S(1)}, u32[]{:S(2)}, u32[]{:S(2)}) collective-permute-start(bf16[2,128,768]{2,1,0:T(8,128)(2,1)S(1)} %dynamic-slice_bitcast_fusion.6), channel_id=1, source_target_pairs={{0,8},{8,0},{16,24},{24,16},{1,9},{9,1},{17,25},{25,17},{2,10},{10... | collective-permute-start | bytes 1179656 | tf_op jit(solution)/shard_map/ppermute | solution.py:577
  144.2 7.9 %collective-permute-start.36 = (bf16[96,640]{1,0:T(8,128)(2,1)S(1)}, bf16[96,640]{1,0:T(8,128)(2,1)S(1)}, u32[]{:S(2)}, u32[]{:S(2)}) collective-permute-start(bf16[96,640]{1,0:T(8,128)(2,1)S(1)} %add_convert_fusion.7), channel_id=1, source_target_pairs={{0,16},{8,24},{16,0},{24,8},{1,17},{9,25},{17,1},{25,9},{2,18},{10... | collective-permute-start | bytes 368648 | tf_op jit(solution)/shard_map/ppermute | solution.py:577
  144.7 11.6 %collective-permute-start.33 = (bf16[2,384,128]{2,1,0:T(8,128)(2,1)S(1)}, bf16[2,384,128]{2,1,0:T(8,128)(2,1)S(1)}, u32[]{:S(2)}, u32[]{:S(2)}) collective-permute-start(bf16[2,384,128]{2,1,0:T(8,128)(2,1)S(1)} %dynamic-slice_bitcast_fusion.12), channel_id=1, source_target_pairs={{0,8},{8,0},{16,24},{24,16},{1,9},{9,1},{17,25},{25,17},{2,10},{10... | collective-permute-start | bytes 589832 | tf_op jit(solution)/shard_map/ppermute | solution.py:577
  146.8 14.2 %collective-permute-start.32 = (bf16[2,432,128]{2,1,0:T(8,128)(2,1)S(1)}, bf16[2,432,128]{2,1,0:T(8,128)(2,1)S(1)}, u32[]{:S(2)}, u32[]{:S(2)}) collective-permute-start(bf16[2,432,128]{2,1,0:T(8,128)(2,1)S(1)} %dynamic-slice_bitcast_fusion.11), channel_id=1, source_target_pairs={{0,8},{8,0},{16,24},{24,16},{1,9},{9,1},{17,25},{25,17},{2,10},{10... | collective-permute-start | bytes 663560 | tf_op jit(solution)/shard_map/ppermute | solution.py:577
  152.1 27.9 %collective-permute-start.37 = (bf16[2,96,640]{2,1,0:T(8,128)(2,1)S(1)}, bf16[2,96,640]{2,1,0:T(8,128)(2,1)S(1)}, u32[]{:S(2)}, u32[]{:S(2)}) collective-permute-start(bf16[2,96,640]{2,1,0:T(8,128)(2,1)S(1)} %pad_maximum_fusion.4), channel_id=1, source_target_pairs={{0,8},{8,0},{16,24},{24,16},{1,9},{9,1},{17,25},{25,17},{2,10},{10... | collective-permute-start | bytes 737288 | tf_op jit(solution)/shard_map/ppermute | solution.py:577
  161.8 26.4 %collective-permute-start.31 = (bf16[128,768]{1,0:T(8,128)(2,1)S(1)}, bf16[128,768]{1,0:T(8,128)(2,1)S(1)}, u32[]{:S(2)}, u32[]{:S(2)}) collective-permute-start(bf16[128,768]{1,0:T(8,128)(2,1)S(1)} %add_convert_fusion.6), channel_id=1, source_target_pairs={{0,16},{8,24},{16,0},{24,8},{1,17},{9,25},{17,1},{25,9},{2,18},{10... | collective-permute-start | bytes 589832 | tf_op jit(solution)/shard_map/ppermute | solution.py:577
  162.5 16.2 %collective-permute-start.35 = (bf16[384,128]{1,0:T(8,128)(2,1)S(1)}, bf16[384,128]{1,0:T(8,128)(2,1)S(1)}, u32[]{:S(2)}, u32[]{:S(2)}) collective-permute-start(bf16[384,128]{1,0:T(8,128)(2,1)S(1)} %add_convert_fusion.12), channel_id=1, source_target_pairs={{0,16},{8,24},{16,0},{24,8},{1,17},{9,25},{17,1},{25,9},{2,18},{10... | collective-permute-start | bytes 294920 | tf_op jit(solution)/shard_map/ppermute | solution.py:577
  164.9 15.0 %collective-permute-start.34 = (bf16[432,128]{1,0:T(8,128)(2,1)S(1)}, bf16[432,128]{1,0:T(8,128)(2,1)S(1)}, u32[]{:S(2)}, u32[]{:S(2)}) collective-permute-start(bf16[432,128]{1,0:T(8,128)(2,1)S(1)} %add_convert_fusion.10), channel_id=1, source_target_pairs={{0,16},{8,24},{16,0},{24,8},{1,17},{9,25},{17,1},{25,9},{2,18},{10... | collective-permute-start | bytes 331784 | tf_op jit(solution)/shard_map/ppermute | solution.py:577
  180.0 8.2 %collective-permute-start.44 = (bf16[432,128]{1,0:T(8,128)(2,1)S(1)}, bf16[432,128]{1,0:T(8,128)(2,1)S(1)}, u32[]{:S(2)}, u32[]{:S(2)}) collective-permute-start(bf16[432,128]{1,0:T(8,128)(2,1)S(1)} %add_convert_fusion.9), channel_id=1, source_target_pairs={{0,16},{8,24},{16,0},{24,8},{1,17},{9,25},{17,1},{25,9},{2,18},{10... | collective-permute-start | bytes 331784 | tf_op jit(solution)/shard_map/ppermute | solution.py:577
  180.2 18.1 %collective-permute-start.38 = (bf16[4,96,640]{2,1,0:T(8,128)(2,1)S(1)}, bf16[4,96,640]{2,1,0:T(8,128)(2,1)S(1)}, u32[]{:S(2)}, u32[]{:S(2)}) collective-permute-start(bf16[4,96,640]{2,1,0:T(8,128)(2,1)S(1)} %get-tuple-element.347), channel_id=1, source_target_pairs={{0,4},{4,0},{1,5},{5,1},{2,6},{6,2},{3,7},{7,3},{8,12},{12,8},{9,1... | collective-permute-start | bytes 1474568 | tf_op jit(solution)/shard_map/ppermute | solution.py:550
  180.8 8.9 %collective-permute-start.40 = (bf16[384,128]{1,0:T(8,128)(2,1)S(1)}, bf16[384,128]{1,0:T(8,128)(2,1)S(1)}, u32[]{:S(2)}, u32[]{:S(2)}) collective-permute-start(bf16[384,128]{1,0:T(8,128)(2,1)S(1)} %add_convert_fusion.11), channel_id=1, source_target_pairs={{0,16},{8,24},{16,0},{24,8},{1,17},{9,25},{17,1},{25,9},{2,18},{10... | collective-permute-start | bytes 294920 | tf_op jit(solution)/shard_map/ppermute | solution.py:577
  188.2 7.8 %collective-permute-start.45 = (bf16[2,432,128]{2,1,0:T(8,128)(2,1)S(1)}, bf16[2,432,128]{2,1,0:T(8,128)(2,1)S(1)}, u32[]{:S(2)}, u32[]{:S(2)}) collective-permute-start(bf16[2,432,128]{2,1,0:T(8,128)(2,1)S(1)} %pad_maximum_fusion.5), channel_id=1, source_target_pairs={{0,8},{8,0},{16,24},{24,16},{1,9},{9,1},{17,25},{25,17},{2,10},{10... | collective-permute-start | bytes 663560 | tf_op jit(solution)/shard_map/ppermute | solution.py:577
  189.7 8.3 %collective-permute-start.41 = (bf16[2,384,128]{2,1,0:T(8,128)(2,1)S(1)}, bf16[2,384,128]{2,1,0:T(8,128)(2,1)S(1)}, u32[]{:S(2)}, u32[]{:S(2)}) collective-permute-start(bf16[2,384,128]{2,1,0:T(8,128)(2,1)S(1)} %pad_maximum_fusion.6), channel_id=1, source_target_pairs={{0,8},{8,0},{16,24},{24,16},{1,9},{9,1},{17,25},{25,17},{2,10},{10... | collective-permute-start | bytes 589832 | tf_op jit(solution)/shard_map/ppermute | solution.py:577
  196.0 11.7 %collective-permute-start.46 = (bf16[4,432,128]{2,1,0:T(8,128)(2,1)S(1)}, bf16[4,432,128]{2,1,0:T(8,128)(2,1)S(1)}, u32[]{:S(2)}, u32[]{:S(2)}) collective-permute-start(bf16[4,432,128]{2,1,0:T(8,128)(2,1)S(1)} %constant_dynamic-update-slice_fusion.2), channel_id=1, source_target_pairs={{0,4},{4,0},{1,5},{5,1},{2,6},{6,2},{3,7},{7,3},{8,12},{12,8},{9,1... | collective-permute-start | bytes 1327112 | tf_op jit(solution)/shard_map/ppermute | solution.py:550
  198.1 13.8 %collective-permute-start.42 = (bf16[4,384,128]{2,1,0:T(8,128)(2,1)S(1)}, bf16[4,384,128]{2,1,0:T(8,128)(2,1)S(1)}, u32[]{:S(2)}, u32[]{:S(2)}) collective-permute-start(bf16[4,384,128]{2,1,0:T(8,128)(2,1)S(1)} %constant_dynamic-update-slice_fusion), channel_id=1, source_target_pairs={{0,4},{4,0},{1,5},{5,1},{2,6},{6,2},{3,7},{7,3},{8,12},{12,8},{9,1... | collective-permute-start | bytes 1179656 | tf_op jit(solution)/shard_map/ppermute | solution.py:550
  198.4 16.4 %collective-permute-start.39 = (bf16[2,4,96,640]{3,2,1,0:T(8,128)(2,1)S(1)}, bf16[2,4,96,640]{3,2,1,0:T(8,128)(2,1)S(1)}, u32[]{:S(2)}, u32[]{:S(2)}) collective-permute-start(bf16[2,4,96,640]{3,2,1,0:T(8,128)(2,1)S(1)} %pad_maximum_fusion.own), channel_id=1, source_target_pairs={{0,2},{2,0},{1,3},{3,1},{4,6},{6,4},{5,7},{7,5},{8,10},{10,8},{9,1... | collective-permute-start | bytes 2949128 | tf_op jit(solution)/shard_map/ppermute | solution.py:550
  207.8 18.6 %collective-permute-start.47 = (bf16[2,4,432,128]{3,2,1,0:T(8,128)(2,1)S(1)}, bf16[2,4,432,128]{3,2,1,0:T(8,128)(2,1)S(1)}, u32[]{:S(2)}, u32[]{:S(2)}) collective-permute-start(bf16[2,4,432,128]{3,2,1,0:T(8,128)(2,1)S(1)} %pad_maximum_fusion.1.own), channel_id=1, source_target_pairs={{0,2},{2,0},{1,3},{3,1},{4,6},{6,4},{5,7},{7,5},{8,10},{10,8},{9,1... | collective-permute-start | bytes 2654216 | tf_op jit(solution)/shard_map/ppermute | solution.py:550
  212.0 8.8 %collective-permute-start.43 = (bf16[2,4,384,128]{3,2,1,0:T(8,128)(2,1)S(1)}, bf16[2,4,384,128]{3,2,1,0:T(8,128)(2,1)S(1)}, u32[]{:S(2)}, u32[]{:S(2)}) collective-permute-start(bf16[2,4,384,128]{3,2,1,0:T(8,128)(2,1)S(1)} %pad_maximum_fusion.2.own), channel_id=1, source_target_pairs={{0,2},{2,0},{1,3},{3,1},{4,6},{6,4},{5,7},{7,5},{8,10},{10,8},{9,1... | collective-permute-start | bytes 2359304 | tf_op jit(solution)/shard_map/ppermute | solution.py:550
  (44 other events, 210.7 us)

commit v3 on v2

--- a/solution.py
+++ b/solution.py
@@ -89,7 +89,7 @@
     return lax.rem(lane, 64) < 32, lane < 64
 
 
-def group_kernel(idx, w_ref, own_ref, half_ref):
+def group_kernel(idx, w_ref, one_ref, two_ref, own_ref, half_ref):
     height = w_ref.shape[0]
     half = height // 2
     for g in range(TP):
@@ -100,7 +100,10 @@
             parts.append(jnp.zeros((height, WC - 3 * GW), BF))
             own_ref[...] = jnp.concatenate(parts, axis=1)
 
-    half_ref[...] = own_ref[pl.ds(pl.multiple_of(idx[2] * half, half), half), :]
+    half_ref[0:half, :] = own_ref[pl.ds(pl.multiple_of(idx[2] * half, half), half), :]
+    half_ref[half:, :] = jnp.zeros((16, WC), BF)
+    half_ref[half : half + 1, 0:height] = one_ref[...].reshape(1, height)
+    half_ref[half + 1 : half + 2, 0:height] = two_ref[...].reshape(1, height)
 
 
 def pack_kernel(idx, out_ref, in_ref, down_ref, pack_ref):
@@ -124,8 +127,7 @@
     toks = refs[:TP]
     n_w = 2 * shards - 1
     ws = refs[TP : TP + n_w]
-    gain_refs = refs[TP + n_w : TP + n_w + shards]
-    cos_ref, sin_ref, q_ref, kv_ref, h_ref, w_ref, gains_ref = refs[TP + n_w + shards :]
+    mine, cos_ref, sin_ref, q_ref, kv_ref, h_ref, w_ref, gains_ref = refs[TP + n_w :]
     c, y = idx[2], idx[3]
     rows = toks[0].shape[0]
     part = ws[0].shape[0]
@@ -138,16 +140,17 @@
             w_ref[at, :] = ws[0][...]
             continue
         at = pl.ds(pl.multiple_of(start + c * half, half), half)
-        w_ref[at, :] = ws[2 * k - 1][...]
+        w_ref[at, :] = ws[2 * k - 1][0:half]
         at = pl.ds(pl.multiple_of(start + (1 - c) * half, half), half)
-        w_ref[at, :] = ws[2 * k][...]
+        w_ref[at, :] = ws[2 * k][0:half]
     for s in range(shards):
 
         @pl.when(y == s)
         def _():
             for k in range(shards):
                 start = (s - k) % shards * part
-                gains_ref[0:2, start : start + part] = gain_refs[k][...].astype(F32)
+                gains = (ws[2 * k - 1] if k else mine)[half : half + 2, 0:part]
+                gains_ref[0:2, start : start + part] = gains.astype(F32)
 
     gain = gains_ref[0:1, :]
     first, low = lane_masks(rows)
@@ -178,10 +181,12 @@
     return jnp.concatenate([rows, zeros] if head % 2 == 0 else [zeros, rows], axis=0)
 
 
-def forward_kernel(n_kv, q_ref, *refs):
+def forward_kernel(n_kv, last, q_ref, *refs):
     kvs = refs[:n_kv]
-    atts = refs[n_kv : n_kv + TP]
-    att_t_ref, lse_ref, kv_s, v_t, q_t = refs[n_kv + TP :]
+    if last:
+        before_ref, before_lse = refs[n_kv : n_kv + 2]
+        atts = refs[n_kv + 2 : n_kv + 2 + TP]
+    att_t_ref, lse_ref, kv_s, v_t, q_t = refs[-5:]
     rows = kvs[0].shape[0]
     block = math.gcd(rows, 256)
     for i, kv in enumerate(kvs):
@@ -201,11 +206,20 @@
             tile, half = VALUE_AT[h]
             values_t = v_t[(tile - 1) * 128 : tile * 128, :]
             out = dot(values_t, weights.astype(BF))[half * 64 : half * 64 + 64]
-            att_t_ref[h * 64 : h * 64 + 64, at] = out / total
+            head = slice(h * 64, h * 64 + 64)
+            if last:
+                old = before_lse[h : h + 1, at]
+                high = jnp.maximum(old, top)
+                share, own = jnp.exp(old - high), jnp.exp(top - high)
+                total = total * own + share
+                out = out * own + before_ref[head, at] * share
+                top = high
+            att_t_ref[head, at] = out / total
             lse_ref[h : h + 1, at] = top + jnp.log(total)
-    small = rows // TP
-    for j in range(TP):
-        atts[j][...] = att_t_ref[:, j * small : (j + 1) * small].T.astype(BF)
+    if last:
+        small = rows // TP
+        for j in range(TP):
+            atts[j][...] = att_t_ref[:, j * small : (j + 1) * small].T.astype(BF)
 
 
 def backward_kernel(n_kv, q_ref, *refs):
@@ -374,7 +388,7 @@
 
 def ffn_grads_kernel(shards, idx, own, got, gain_ref, *refs):
     ins = refs[:shards]
-    others = refs[shards : shards + 2]
+    mine_ref, other_ref = refs[shards : shards + 2]
     h_t, mixed_t, att_t, right = refs[shards + 2 :]
     z, x, c, y = idx[0], idx[1], idx[2], idx[3]
     rows_d, rows_f, pad_d, pad_f = plan(shards)
@@ -401,22 +415,25 @@
                 ins[k][xx, t * pad_d : t * pad_d + rows_d, :] = grad[
                     xx * pad_d : xx * pad_d + rows_d, t * 128 : t * 128 + 128
                 ]
-    gain = jnp.broadcast_to(gain_ref[0:1, :], (16, D)).astype(BF)
-    high = pad_f + pad_d + 16
-    for xr in range(2):
+    high = mine_ref.shape[3] * TP
+    gain = jnp.broadcast_to(gain_ref[0:1, :], (high - pad_f - pad_d, D)).astype(BF)
+    for xx in range(2):
         for s in range(shards):
-            piece = (s * 2 + c) * 2 + lax.rem(x + xr, 2)
+            piece = (s * 2 + c) * 2 + xx
             turned = lax.rem(piece // per - z + TP, TP) * per + lax.rem(piece, per)
             down = dot(mixed_t[piece], right[:, 2 * FF + D :]).astype(BF)
             out = dot(att_t[turned], right[:, 2 * FF : 2 * FF + D]).astype(BF)
-            for t in range(D // 128):
-                lanes = slice(t * 128, t * 128 + 128)
-                base = t * high
-                others[xr][s, base : base + pad_f, :] = down[:, lanes]
-                base += pad_f
-                others[xr][s, base : base + pad_d, :] = out[:, lanes]
-                base += pad_d
-                others[xr][s, base : base + 16, :] = gain[:, lanes]
+            both = jnp.concatenate([down, out, gain], axis=0)
+            for q in range(TP):
+                chunk = both[q * (high // TP) : (q + 1) * (high // TP)]
+
+                @pl.when(lax.rem(z, 2) == q % 2)
+                def _():
+                    mine_ref[q // 2, s, xx] = chunk
+
+                @pl.when(lax.rem(z, 2) != q % 2)
+                def _():
+                    other_ref[q // 2, s, xx] = chunk
 
 
 def qkv_grads_kernel(shards, n_kv, idx, *refs):
@@ -429,10 +446,9 @@
         part = dot(grads.T, hs[i][...])
         total = part if total is None else total + part
     grad = jnp.concatenate([total, dot(dq_ref[...].T, hs[0][...])], axis=0).T
-    w = w_ref[...].astype(F32)
     gain = gains_ref[...].T[:, 0:1]
     lane = lax.broadcasted_iota(jnp.int32, grad.shape, 1)
-    by_gain = jnp.sum(grad * w, axis=1, keepdims=True) / gain
+    by_gain = jnp.sum(grad * w_ref[...].astype(F32), axis=1, keepdims=True) / gain
     grad = jnp.where(lane < 3 * GW, grad, by_gain).astype(BF)
     height = plan(shards)[0]
     for s in range(shards):
@@ -450,26 +466,28 @@
                     other_ref[s, xx] = part
 
 
-def combine_kernel(n_sum, idx, *refs):
+def h_one_grads_kernel(n_sum, idx, *refs):
     parts = refs[:n_sum]
-    dq_ref, w_ref, out_ref = refs[n_sum:]
-    rows = out_ref.shape[2]
+    dq_ref, w_ref, gh_mine, gh_other = refs[n_sum:]
+    rows = gh_mine.shape[1]
     for j in range(TP):
         at = slice(j * rows, (j + 1) * rows)
-        total = parts[0][at, :].astype(F32)
+        total = parts[0][0, at, :].astype(F32)
         for part in parts[1:]:
-            total += part[at, :].astype(F32)
+            total += part[0, at, :].astype(F32)
         grad = jnp.concatenate([total.astype(BF), dq_ref[at, :]], axis=1)
         owner = lax.rem(idx[0] - j + TP, TP)
-        out_ref[owner // 2, lax.rem(owner, 2)] = dot_nt(grad, w_ref[...]).astype(BF)
-
-
-def tail_kernel(n_sum, *refs):
+        target = gh_other if j % 2 else gh_mine
+        target[owner // 2] = dot_nt(grad, w_ref[...]).astype(BF)
+
+
+def tail_kernel(n_sum, idx, *refs):
     tok_ref, gmid_ref, gains_ref, out_ref = refs[n_sum:]
     unit, scale = normalise(tok_ref[...].astype(F32))
-    total = refs[0][...].astype(F32)
-    for grad in refs[1:n_sum]:
-        total += grad[...].astype(F32)
+    total = 0.0
+    for grad in refs[:n_sum]:
+        grad = grad[idx[0] // 2] if len(grad.shape) == 3 else grad[...]
+        total += grad.astype(F32)
     grad_unit = total * gains_ref[0:1, :]
     out_ref[...] = gmid_ref[...] + normalise_back(grad_unit, unit, scale)
 
@@ -493,35 +511,28 @@
                 in_ref[cc, xx, :, t * 128 : t * 128 + 128] = held[base : base + rows_d, :]
 
 
-def rest_unpack_kernel(shards, idx, own, got, out_ref, down_ref, gain_ref, held, gain_all):
+def rest_unpack_kernel(shards, idx, own, got, out_ref, down_ref, gain_ref, held):
     rows_d, rows_f, pad_d, pad_f = plan(shards)
-    high = pad_f + pad_d + 16
     size = held.shape[0] // TP
     z, x, c = idx[0], idx[1], idx[2]
-    gains = []
+    gain = None
     for cr in range(2):
         for xr in range(2):
             for k in range(TP):
                 at = pl.ds(pl.multiple_of(place_z(z, k) * size, size), size)
                 held[at, :] = (got if cr else own)[xr, k].astype(F32)
             cc, xx = lax.rem(c + cr, 2), lax.rem(x + xr, 2)
-            for t in range(D // 128):
-                lanes = slice(t * 128, t * 128 + 128)
-                base = t * high
-                down_ref[cc, xx, :, lanes] = held[base : base + rows_f, :]
-                base += pad_f
-                out_ref[cc, xx, :, lanes] = held[base : base + rows_d, :]
-                base += pad_d
-                if xr == 0:
-                    gains.append(held[base : base + 8, :])
-    for t in range(D // 128):
-        gain_all[:, t * 128 : t * 128 + 128] = gains[t] + gains[t + D // 128]
-    part = gain_ref.shape[1]
+            down_ref[cc, xx] = held[0:rows_f, :]
+            out_ref[cc, xx] = held[pad_f : pad_f + rows_d, :]
+            if xr == 0:
+                row = held[pad_f + pad_d : pad_f + pad_d + 8, :]
+                gain = row if gain is None else gain + row
+    part = gain_ref.shape[0]
     for s in range(shards):
 
         @pl.when(idx[3] == s)
         def _():
-            gain_ref[...] = gain_all[0:1, s * part : (s + 1) * part]
+            gain_ref[...] = gain[0:1, s * part : (s + 1) * part].reshape(part)
 
 
 def qkv_unpack_kernel(idx, own, got, out_ref, gain_ref, gain_s):
@@ -542,7 +553,7 @@
             height = gain.shape[0]
             at = pl.multiple_of((cc * 2 + xx) * height, height)
             gain_s[pl.ds(at, height), :] = gain
-    gain_ref[...] = gain_s[...].T[64:65]
+    gain_ref[...] = gain_s[...].T[64:65].reshape(gain_ref.shape)
 
 
 def shift(value, axis, k):
@@ -556,20 +567,37 @@
 
 def pick(value, index, dim):
     return lax.dynamic_index_in_dim(value, index, dim, keepdims=False)
+
+
+def term(value, *views):
+    return (value, views)
+
+
+def take(index, dim):
+    return lambda value: pick(value, index, dim)
+
+
+def reshaped(*shape):
+    return lambda value: value.reshape(shape)
+
+
+def viewed(terms, view):
+    return [(value, views + (view,)) for value, views in terms]
 
 
 def reduce_step(order, terms, axis, dim):
     n, i = lax.axis_size(axis), lax.axis_index(axis)
     got = []
     for k in range(1, n):
-        got.append(shift(order.add([pick(t, lax.rem(i + k, n), dim) for t in terms]), axis, k))
-    return [pick(t, i, dim) for t in terms] + got
-
-
-def add(terms):
-    total = terms[0].astype(F32)
-    for term in terms[1:]:
-        total = total + term.astype(F32)
+        part = order.add(viewed(terms, take(lax.rem(i + k, n), dim)))
+        got.append(term(shift(part, axis, k)))
+    return viewed(terms, take(i, dim)) + got
+
+
+def add(values):
+    total = values[0].astype(F32)
+    for value in values[1:]:
+        total = total + value.astype(F32)
     return total.astype(BF)
 
 
@@ -580,11 +608,12 @@
 def reduce_z(order, terms, bit):
     z = lax.axis_index("z")
     i, dim = (z % 2, 1) if bit == 1 else (z // 2, 0)
-    got = swap_z(order.add([pick(t, 1 - i, dim) for t in terms]), bit)
-    return [pick(t, i, dim) for t in terms] + [got]
-
-
-def gather_z(value, bit):
+    part = order.add(viewed(terms, take(1 - i, dim)))
+    return viewed(terms, take(i, dim)) + [term(swap_z(part, bit))]
+
+
+def gather_z(order, value, bit):
+    value = order.step(value)
     got = swap_z(value, bit)
     return jnp.stack([value, got]) if bit == 2 else jnp.concatenate([value, got])
 
@@ -606,10 +635,18 @@
             return values
         return lax.optimization_barrier((values, self.last))[0]
 
+    def step(self, value):
+        self.last = self(value)
+        return self.last
+
     def add(self, terms):
-        total = add(self(terms))
-        self.last = total
-        return total
+        values = []
+        for value, (_, views) in zip(self([t[0] for t in terms]), terms):
+            for view in views:
+                value = view(value)
+            values.append(value)
+        self.last = add(values)
+        return self.last
 
     def run(self, body, outs, n_smem, ins, **more):
         got = call(body, outs, n_smem, self(list(ins)), **more)
@@ -628,7 +665,7 @@
     n_kv = 4 * outer
     keys = n_kv * many
     rows_d, rows_f, pad_d, pad_f = plan(shards)
-    high_in, high = 2 * FF // 128 * pad_d, D // 128 * (pad_f + pad_d + 16)
+    high_in, high = 2 * FF // 128 * pad_d, -(-(pad_f + pad_d + 16) // 64) * 64
     i32 = jnp.int32
     idx = jnp.stack([z, x, c, y]).astype(i32)
     order = Order()
@@ -636,13 +673,11 @@
     toks = gather(tok, "z")
     w_own, w_mine = order.run(
         group_kernel,
-        [((part, WC), BF), ((part // 2, WC), BF)],
-        1,
-        [idx, w_qkv],
+        [((part, WC), BF), ((part // 2 + 16, WC), BF)],
+        1,
+        [idx, w_qkv, gain_one, gain_two],
         name="group_columns",
     )
-    gains_own = jnp.stack([gain_one, gain_two])
-    gain_parts = gather(gains_own, "shard")
     w_slices = [w_own]
     for k in range(1, shards):
         w_slices.append(shift(w_mine, "shard", k))
@@ -665,11 +700,15 @@
                 zz = lax.rem(zo - zr + outer, outer)
                 place = ((zz * TP + owners) * 2 + lax.rem(x + xr, 2)) * 2 + lax.rem(c + cr, 2)
                 places.append(place)
-    places = jnp.concatenate(places) * rows
-    places = (places[:, None] + jnp.arange(rows, dtype=i32)).reshape(keys)
-    angle = places.astype(F32)[:, None] * jnp.tile(freq, 4)[None, :]
+    first_place = jnp.concatenate(places) * rows
+    freq = jnp.tile(freq, 4)[None, :]
     sign = jnp.where(jnp.arange(128) % 64 < 32, -1.0, 1.0).astype(F32)
-    cosine, sine = jnp.cos(angle), jnp.sin(angle) * sign[None, :]
+    start = first_place.astype(F32)[:, None] * freq
+    step = jnp.arange(rows, dtype=i32).astype(F32)[:, None] * freq
+    cos_a, sin_a = jnp.cos(start)[:, None], jnp.sin(start)[:, None]
+    cos_b, sin_b = jnp.cos(step)[None], jnp.sin(step)[None]
+    cosine = (cos_a * cos_b - sin_a * sin_b).reshape(keys, 128)
+    sine = ((sin_a * cos_b + cos_a * sin_b) * sign).reshape(keys, 128)
 
     query, kv, h_one, w_full, gains = order.run(
         functools.partial(front_kernel, shards),
@@ -681,28 +720,41 @@
             ((8, D), F32),
         ],
         1,
-        [idx, *toks, *w_slices, *gain_parts, cosine, sine],
+        [idx, *toks, *w_slices, w_mine, cosine, sine],
         name="front",
     )
 
     near = gather(kv, "zo")
     near = near + [shift(v, "x", 1) for v in near]
-    kvs = near + [shift(v, "core", 1) for v in near]
-    h_near = gather(after(h_one, near[-1]), "zo")
-    h_near = h_near + [shift(v, "x", 1) for v in h_near]
+    kv_core = shift(kv, "core", 1)
+    close = (0, n_kv // 2)
+    far = [i for i in range(n_kv) if i not in close]
+    scratch = lambda count: [
+        pltpu.VMEM((count * many, 2 * GW), BF),
+        pltpu.VMEM((256, count * many), BF),
+        pltpu.VMEM((256, many), BF),
+    ]
+    first = order.run(
+        functools.partial(forward_kernel, 2, False),
+        [((GW, many), F32), ((8, many), F32)],
+        0,
+        [query, kv, kv_core],
+        scratch=scratch(2),
+        name="attention_forward_near",
+    )
+    kvs = near + [kv_core] + [shift(after(v, *first), "core", 1) for v in near[1:]]
     att = order.run(
-        functools.partial(forward_kernel, n_kv),
+        functools.partial(forward_kernel, len(far), True),
         [((rows, GW), BF)] * TP + [((GW, many), F32), ((8, many), F32)],
         0,
-        [query, *kvs],
-        scratch=[
-            pltpu.VMEM((keys, 2 * GW), BF),
-            pltpu.VMEM((256, keys), BF),
-            pltpu.VMEM((256, many), BF),
-        ],
-        name="attention_forward",
+        [query, *[kvs[i] for i in far], *first],
+        scratch=scratch(len(far)),
+        name="attention_forward_far",
     )
     att_blocks, (attended_t, lse) = att[:TP], att[TP:]
+    h_near = gather(after(h_one, lse), "zo")
+    h_near = h_near + [shift(v, "x", 1) for v in h_near]
+    h_core = shift(after(h_one, lse), "core", 1)
     atts = [att_blocks[0]] + [shift(att_blocks[k], "z", -k) for k in range(1, TP)]
 
     packs = [after(p, lse) for p in packs]
@@ -712,7 +764,7 @@
         [((rows, D), F32), ((rows, D), F32), ((rows, ACT_ALL), BF), ((8, D), F32)]
         + [((rows, 256), BF)] * TP,
         1,
-        [idx, *atts, tok, cot, gains, w_out, w_in, w_down, *both],
+        [idx, *atts, tok, cot, after(gains, h_core), w_out, w_in, w_down, *both],
         scratch=[
             pltpu.VMEM((D, D), BF),
             pltpu.VMEM((D, 2 * FF), BF),
@@ -727,9 +779,12 @@
     gatts = mid[4:]
     gas = [gatts[0]] + [shift(gatts[k], "z", k) for k in range(1, TP)]
 
+    hs = h_near + [h_core] + [shift(after(v, result), "core", 1) for v in h_near[1:]]
+    gain_two_row = after(gain_two_row, *hs)
     ffn = order.run(
         functools.partial(ffn_grads_kernel, shards),
-        [((2, high_in, 128), BF)] * shards + [((shards, high, 128), BF)] * 2,
+        [((2, high_in, 128), BF)] * shards
+        + [((2, shards, 2, high // TP, D), BF)] * 2,
         1,
         [idx, act, shift(act, "core", 1), gain_two_row],
         scratch=[
@@ -740,9 +795,9 @@
         ],
         name="ffn_weight_grads",
     )
-    f_in = [ffn[0]] + [shift(ffn[k], "shard", k) for k in range(1, shards)]
-    f_rest = [ffn[shards], shift(ffn[shards + 1], "x", 1)]
-    hs = h_near + [shift(after(v, ffn[0]), "core", 1) for v in h_near]
+    f_in = [term(ffn[0])]
+    f_in += [term(shift(after(ffn[k], *gas), "shard", k)) for k in range(1, shards)]
+    f_rest = [term(ffn[shards]), term(swap_z(after(ffn[shards + 1], *gas), 1))]
 
     dkv_keep, dkv_send, dq = order.run(
         functools.partial(backward_kernel, n_kv),
@@ -768,56 +823,73 @@
         [idx, *hs, dkv_keep, dkv_send, dq, w_full, gains],
         name="qkv_weight_grads",
     )
-    terms = [dkv_keep, shift(after(dkv_send, mine), "core", 1)]
-    wq = [mine, shift(after(other, *f_in, *f_rest), "core", 1)]
-    terms = [t.reshape(2, outer, many, 2 * GW) for t in terms]
-    got = shift(order.add([t[1] for t in terms]), "x", 1)
-    terms = [t[0] for t in terms] + [got]
+    first_got = [t[0] for t in f_in[1:] + f_rest[1:]]
+    mine, other, *_ = lax.optimization_barrier((mine, other, *first_got))
+    order.last = mine
+    terms = [term(dkv_keep), term(shift(after(dkv_send, mine), "core", 1))]
+    terms = viewed(terms, reshaped(2, outer, many, 2 * GW))
+    wq = [term(mine), term(shift(other, "core", 1))]
+
+    def pair(value):
+        return jnp.stack([value, shift(order.step(value), "x", 1)])
 
     f_in = reduce_step(order, f_in, "x", 0)
-    f_rest = reduce_step(order, f_rest, "shard", 0)
+    f_rest = reduce_z(order, f_rest, 2)
     wq = reduce_step(order, wq, "shard", 0)
+    got = shift(order.add(viewed(terms, take(1, 0))), "x", 1)
+    terms = viewed(terms, take(0, 0)) + [term(got)]
     wq = reduce_step(order, wq, "x", 0)
-
     if outer > 1:
         total = order.add(terms)
-        sums = [total[0]] + [shift(total[k], "zo", -k) for k in range(1, outer)]
+        sums = [total[0:1]] + [shift(total[k : k + 1], "zo", -k) for k in range(1, outer)]
     else:
-        sums = [t[0] for t in terms]
-    (gh,) = order.run(
-        functools.partial(combine_kernel, len(sums)),
-        [((2, 2, rows, D), BF)],
+        sums = [
+            dkv_keep.reshape(2, many, 2 * GW),
+            terms[1][0].reshape(2, many, 2 * GW),
+            got.reshape(1, many, 2 * GW),
+        ]
+    gh, gh_other = order.run(
+        functools.partial(h_one_grads_kernel, len(sums)),
+        [((2, rows, D), BF)] * 2,
         1,
         [idx, *sums, dq, w_full],
         name="h_one_grads",
     )
-    gh = reduce_z(order, [gh], 1)
-    f_rest = reduce_z(order, [order.add(f_rest).reshape(2, 2, high // TP, 128)], 1)
-    f_in = reduce_z(order, [order.add(f_in).reshape(2, 2, high_in // TP, 128)], 1)
-    wq = gather_z(sum_over(order.add(wq), "zo"), 2)
+    gh = [term(gh), term(swap_z(gh_other, 1))]
+    f_in = reduce_z(order, viewed(f_in, reshaped(2, 2, high_in // TP, 128)), 1)
+    f_rest = reduce_step(order, f_rest, "shard", 0)
+    wq = gather_z(order, sum_over(order.add(wq), "zo"), 2)
+
+    f_in = reduce_z(order, f_in, 2)
+    f_rest = reduce_step(order, f_rest, "x", 0)
+    wq = gather_z(order, wq, 1)
     gh = reduce_z(order, gh, 2)
-    wq = gather_z(wq, 1)
-    f_rest = reduce_z(order, f_rest, 2)
-    f_in = reduce_z(order, f_in, 2)
-    wq = jnp.stack(gather(wq, "x"))
-    f_rest = gather_z(sum_over(order.add(f_rest), "zo"), 2)
-    f_in = gather_z(sum_over(order.add(f_in), "zo"), 2)
+
+    f_in = gather_z(order, sum_over(order.add(f_in), "zo"), 2)
+    f_rest = gather_z(order, sum_over(order.add(f_rest), "zo"), 2)
+    wq = pair(wq)
+
+    f_rest = gather_z(order, f_rest, 1)
+    f_in = gather_z(order, f_in, 1)
     (grad_tokens,) = order.run(
         functools.partial(tail_kernel, len(gh)),
         [((rows, D), F32)],
-        0,
-        [*gh, tok, grad_middle, gains],
+        1,
+        [idx, *[t[0] for t in gh], tok, grad_middle, gains],
         name="token_grads",
     )
-    f_rest = gather_z(after(f_rest, gh[-1]), 1)
-    f_in = gather_z(after(f_in, gh[-1]), 1)
+    wq = order.step(wq)
     wq_got = shift(wq, "core", 1)
-    f_rest = jnp.stack(gather(f_rest, "x"))
-    f_in = jnp.stack(gather(f_in, "x"))
-
+
+    f_rest = pair(f_rest)
+    f_in = pair(f_in)
+    f_rest = order.step(f_rest)
+    f_rest_got = shift(f_rest, "core", 1)
+    f_in = order.step(f_in)
+    f_in_got = shift(f_in, "core", 1)
     g_qkv, grad_gain_one = order.run(
         qkv_unpack_kernel,
-        [((2, 2, rows_d, 3 * D), F32), ((1, part), F32)],
+        [((2, 2, rows_d, 3 * D), F32), ((part,), F32)],
         1,
         [idx, wq, wq_got],
         scratch=[pltpu.VMEM((part, 128), F32)],
@@ -828,18 +900,18 @@
         [
             ((2, 2, rows_d, D), F32),
             ((2, 2, rows_f, D), F32),
-            ((1, part), F32),
+            ((part,), F32),
         ],
         1,
-        [idx, f_rest, shift(f_rest, "core", 1)],
-        scratch=[pltpu.VMEM((high, 128), F32), pltpu.VMEM((8, D), F32)],
+        [idx, f_rest, f_rest_got],
+        scratch=[pltpu.VMEM((high, D), F32)],
         name="w_down_w_out_unpack",
     )
     (g_in,) = order.run(
         functools.partial(in_unpack_kernel, shards),
         [((2, 2, rows_d, 2 * FF), F32)],
         1,
-        [idx, f_in, shift(f_in, "core", 1)],
+        [idx, f_in, f_in_got],
         scratch=[pltpu.VMEM((high_in, 128), F32)],
         name="w_in_unpack",
     )
@@ -847,10 +919,10 @@
     return (
         result[None],
         grad_tokens[None],
-        grad_gain_one.reshape(part),
+        grad_gain_one,
         g_qkv.reshape(part, 3 * D),
         g_out.reshape(part, D),
-        grad_gain_two.reshape(part),
+        grad_gain_two,
         g_in.reshape(part, 2 * FF),
         g_down.reshape(w_down.shape[0], D),
     )

time: 232 us -> 217 us (0.935)
  waiting for transfers between devices: 91.7 us -> 69.2 us
  local copies, waits for them, and re-layouts: 14.8 us -> 9.24 us
  other arithmetic: 11.8 us -> 17.3 us
  starting transfers between devices: 43.2 us -> 47.6 us
  Pallas kernels: 68.4 us -> 72.3 us
    ppermute x12, waiting for transfers between devices: 40.2 us -> 27 us  [swap_z(): return lax.ppermute(value, 'z', [(i, i ^ bit) for i in range(TP)])]
    convert_element_type x13, other arithmetic: 2.47 us -> 12.5 us  [add(): return total.astype(BF)]
    ppermute x36 -> x35, waiting for transfers between devices: 51.4 us -> 42.2 us  [shift(): return lax.ppermute(value, axis, [(i, (i + k) % n) for i in range(n)])]
    ppermute x36 -> x35, starting transfers between devices: 30.2 us -> 35.8 us  [shift(): return lax.ppermute(value, axis, [(i, (i + k) % n) for i in range(n)])]
    mul x2 -> x1, other arithmetic: 5.64 us -> 1.05 us  [per_device(): sine = ((sin_a * cos_b + cos_a * sin_b) * sign).reshape(keys, 128)]
    pallas_call x13 -> x14, Pallas kernels: 68.4 us -> 72.3 us  [call(): pl.pallas_call(body, out_shape=[jax.ShapeDtypeStruct(s, t) for s, t in ou...]
    squeeze x18 -> x0, local copies, waits for them, and re-layouts: 3.95 us -> none  [pick(): return lax.dynamic_index_in_dim(value, index, dim, keepdims=False)]
    pallas_call x2 -> x0, other arithmetic: 2.48 us -> none  [call(): pl.pallas_call(body, out_shape=[jax.ShapeDtypeStruct(s, t) for s, t in ou...]
  transfers between devices with their start and end apart: 48 -> 47, of which waited for: 24 -> 24; matrix products, arithmetic and copies ran while one was open for 6% -> 8% of each run, Pallas kernels for 26% -> 32%
where the time goes in v3:
time: 217 us
  Pallas kernels  72.3 us (33%)
  waiting for transfers between devices  69.2 us (32%)
  starting transfers between devices  47.6 us (22%)
  other arithmetic  17.3 us (8%)
  local copies, waits for them, and re-layouts  9.24 us (4%)
    pallas_call x14, Pallas kernels, call(): pl.pallas_call(body, out_shape=[jax.ShapeDtypeStruct(s, t) for s, t in ou...  72.3 us
    ppermute x35, waiting for transfers between devices, shift(): return lax.ppermute(value, axis, [(i, (i + k) % n) for i in range(n)])  42.2 us
    ppermute x35, starting transfers between devices, shift(): return lax.ppermute(value, axis, [(i, (i + k) % n) for i in range(n)])  35.8 us
    ppermute x12, waiting for transfers between devices, swap_z(): return lax.ppermute(value, 'z', [(i, i ^ bit) for i in range(TP)])  27 us
    convert_element_type x13, other arithmetic, add(): return total.astype(BF)  12.5 us
    ppermute x12, starting transfers between devices, swap_z(): return lax.ppermute(value, 'z', [(i, i ^ bit) for i in range(TP)])  11.7 us
    unnamed x87, local copies, waits for them, and re-layouts  8.86 us
  transfers between devices with their start and end apart: 47, of which 24 were waited for; matrix products, arithmetic and copies ran while one was open for 8% of the time, Pallas kernels for 32%

profile of v3, /device:TPU:0, one launch (start us, length us, event | category | flops | bytes accessed | tf_op | source)
XLA Modules:
  0.0 216.8 jit_solution(7624830316560224111)
XLA Ops:
  0.6 3.1 %collective-permute-start = (bf16[128,768]{1,0:T(8,128)(2,1)}, bf16[128,768]{1,0:T(8,128)(2,1)S(1)}, u32[]{:S(2)}, u32[]{:S(2)}) collective-permute-start(bf16[128,768]{1,0:T(8,128)(2,1)} %bitcast.96), channel_id=1, source_target_pairs={{0,8},{8,16},{16,24},{24,0},{1,9},{9,17},{17,25},{25,1},{2,10},{10... | collective-permute-start | bytes 589832 | tf_op jit(solution)/shard_map/ppermute | solution.py:561
  3.7 2.6 %collective-permute-start.1 = (bf16[128,768]{1,0:T(8,128)(2,1)}, bf16[128,768]{1,0:T(8,128)(2,1)S(1)}, u32[]{:S(2)}, u32[]{:S(2)}) collective-permute-start(bf16[128,768]{1,0:T(8,128)(2,1)} %bitcast.97), channel_id=1, source_target_pairs={{0,16},{8,24},{16,0},{24,8},{1,17},{9,25},{17,1},{25,9},{2,18},{10... | collective-permute-start | bytes 589832 | tf_op jit(solution)/shard_map/ppermute | solution.py:561
  8.3 2.5 %group_columns.1 = (bf16[384,640]{1,0:T(8,128)(2,1)}, bf16[208,640]{1,0:T(8,128)(2,1)}) custom-call(s32[4]{0:T(128)} %pad_add_fusion.idx, bf16[384,2304]{1,0:T(8,128)(2,1)} %w_ref.1, bf16[384]{0:T(512)(128)(2,1)} %one_ref.1, bf16[384]{0:T(512)(128)(2,1)} %two_ref.1), custom_call_target="tpu_custom_call" | custom-call | flops 1 | bytes 1 | tf_op jit(solution)/shard_map/group_columns/pallas_call | solution.py:52
  10.8 1.5 collective-permute-start.3
  12.3 3.2 %pack_weights.1 = bf16[1056,768]{1,0:T(8,128)(2,1)} custom-call(s32[4]{0:T(128)} %pad_add_fusion.idx, bf16[384,768]{1,0:T(8,128)(2,1)} %refs_7_, bf16[384,2304]{1,0:T(8,128)(2,1)} %refs_8_, bf16[576,768]{1,0:T(8,128)(2,1)} %refs_9_), custom_call_target="tpu_custom_call" | custom-call | flops 1 | bytes 1 | tf_op jit(solution)/shard_map/pack_weights/pallas_call | solution.py:52
  17.9 1.6 collective-permute-done.3.refs_5_
  21.8 4.7 %front.1 = (bf16[512,256]{1,0:T(8,128)(2,1)}, bf16[512,384]{1,0:T(8,128)(2,1)}, bf16[512,768]{1,0:T(8,128)(2,1)}, bf16[768,640]{1,0:T(8,128)(2,1)}, f32[8,768]{1,0:T(8,128)}) custom-call(s32[4]{0:T(128)} %pad_add_fusion.idx, bf16[128,768]{1,0:T(8,128)(2,1)} %bitcast.99, bf16[128,768]{1,0:T(8,128)(2,1)} %copy-done.32, bf16[128,768]{1,0:T(8,128)(2,1)} %copy-done.33, ...), custom_call_target="tpu_custom_call" | custom-call | flops 1 | bytes 1 | tf_op jit(solution)/shard_map/front/pallas_call | solution.py:52
  29.2 6.1 %attention_forward_near.1 = (f32[192,512]{1,0:T(8,128)}, f32[8,512]{1,0:T(8,128)}) custom-call(bf16[512,256]{1,0:T(8,128)(2,1)} %get-tuple-element.263.q_ref, bf16[512,384]{1,0:T(8,128)(2,1)} %get-tuple-element.264.refs_0_, bf16[512,384]{1,0:T(8,128)(2,1)} %copy-done.9), custom_call_target="tpu_custom_call" | custom-call | flops 1 | bytes 1 | tf_op jit(solution)/shard_map/attention_forward_near/pallas_call | solution.py:52
  35.4 2.9 %collective-permute-done.5.refs_0_.refs_1_ = bf16[512,384]{1,0:T(8,128)(2,1)S(1)} collective-permute-done((bf16[512,384]{1,0:T(8,128)(2,1)}, bf16[512,384]{1,0:T(8,128)(2,1)S(1)}, u32[]{:S(2)}, u32[]{:S(2)}) %collective-permute-start.5) | collective-permute-done | bytes 393248 | tf_op jit(solution)/shard_map/ppermute | solution.py:561
  38.3 1.7 collective-permute-done.7.refs_1_.refs_3_
  40.8 6.4 %attention_forward_far.1 = (bf16[128,192]{1,0:T(8,128)(2,1)}, bf16[128,192]{1,0:T(8,128)(2,1)}, bf16[128,192]{1,0:T(8,128)(2,1)}, bf16[128,192]{1,0:T(8,128)(2,1...) custom-call(bf16[512,256]{1,0:T(8,128)(2,1)} %get-tuple-element.263.q_ref, bf16[512,384]{1,0:T(8,128)(2,1)} %copy-done.10, ...), custom_call_target="tpu_custom_call" | custom-call | flops 1 | bytes 1 | tf_op jit(solution)/shard_map/attention_forward_far/pallas_call | solution.py:52
  47.2 5.9 %collective-permute-done.12.refs_10_ = bf16[1056,768]{1,0:T(8,128)(2,1)S(1)} collective-permute-done((bf16[1056,768]{1,0:T(8,128)(2,1)}, bf16[1056,768]{1,0:T(8,128)(2,1)S(1)}, u32[]{:S(2)}, u32[]{:S(2)}) %collective-permute-start.12) | collective-permute-done | bytes 1622048 | tf_op jit(solution)/shard_map/ppermute | solution.py:561
  55.6 1.7 collective-permute-start.9
  58.4 1.7 collective-permute-done.8.refs_1_
  60.2 2.2 collective-permute-done.9.refs_2_
  62.3 1.6 collective-permute-done.10.refs_3_
  65.1 8.5 %feed_forward.1 = (f32[128,768]{1,0:T(8,128)}, f32[128,768]{1,0:T(8,128)}, bf16[128,6528]{1,0:T(8,128)(2,1)}, f32[8,768]{1,0:T(8,128)}, bf16[128,256]{1,0:T(8,12...) custom-call(s32[4]{0:T(128)} %pad_add_fusion.idx, ...), custom_call_target="tpu_custom_call" | custom-call | flops 1 | bytes 1 | tf_op jit(solution)/shard_map/feed_forward/pallas_call | solution.py:52
  75.6 2.5 %collective-permute-start.16 = (bf16[128,256]{1,0:T(8,128)(2,1)}, bf16[128,256]{1,0:T(8,128)(2,1)S(1)}, u32[]{:S(2)}, u32[]{:S(2)}) collective-permute-start(bf16[128,256]{1,0:T(8,128)(2,1)} %get-tuple-element.251), channel_id=1, source_target_pairs={{0,24},{8,0},{16,8},{24,16},{1,25},{9,1},{17,9},{25,17},{2,26},{10... | collective-permute-start | bytes 196616 | tf_op jit(solution)/shard_map/ppermute | solution.py:561
  79.8 5.6 %ffn_weight_grads.1 = (bf16[2,1728,128]{2,1,0:T(8,128)(2,1)}, bf16[2,1728,128]{2,1,0:T(8,128)(2,1)}, bf16[2,2,2,64,768]{4,3,2,1,0:T(8,128)(2,1)}, bf16[2,2,2,64,768]{4,3,2,1,0:T(8,128)(2,1)}) custom-call(s32[4]{0:T(128)} %pad_add_fusion.idx, bf16[128,6528]{1,0:T(8,128)(2,1)} %get-tuple-element.259.own, bf16[128,6528]{1,0:T(8,128)(2,1)} %copy-done.6, ...), custom_call_target="tpu_custom_call" | custom-call | flops 1 | bytes 1 | tf_op jit(solution)/shard_map/ffn_weight_grads/pallas_call | solution.py:52
  85.4 1.6 collective-permute-start.20
  87.2 11.4 %attention_backward.1 = (bf16[2,512,384]{2,1,0:T(8,128)(2,1)}, bf16[2,512,384]{2,1,0:T(8,128)(2,1)}, bf16[512,256]{1,0:T(8,128)(2,1)}) custom-call(bf16[512,256]{1,0:T(8,128)(2,1)} %get-tuple-element.263.q_ref, bf16[512,384]{1,0:T(8,128)(2,1)} %get-tuple-element.264.refs_0_, bf16[512,384]{1,0:T(8,128)(2,1)} %copy-done.10, bf16[512,384]{1,0:T(8,128)(2,1)} %copy-done.9, ...), custom_call_target="tpu_custom_call" | custom-call | flops 1 | bytes 1 | tf_op jit(solution)/shard_map/attention_backward/pallas_call | solution.py:52
  98.6 6.4 %qkv_weight_grads.1 = (bf16[2,2,96,640]{3,2,1,0:T(8,128)(2,1)}, bf16[2,2,96,640]{3,2,1,0:T(8,128)(2,1)}) custom-call(s32[4]{0:T(128)} %pad_add_fusion.idx, bf16[512,768]{1,0:T(8,128)(2,1)} %get-tuple-element.281.refs_0_, bf16[512,768]{1,0:T(8,128)(2,1)} %copy-done.18, bf16[512,768]{1,0:T(8,128)(2,1)} %copy-done.17, bf16[512,768]{1,0:T(8,128)(2,1)} %copy-done.19, ...), custom_call_target="tpu_custom_call" | custom-call | flops 1 | bytes 1 | tf_op jit(solution)/shard_map/qkv_weight_grads/pallas_call | solution.py:52
  105.0 1.5 collective-permute-done.21
  110.3 2.0 fusion.1
  112.3 1.7 fusion.3
  115.5 1.5 collective-permute-start.25
  117.9 5.2 %collective-permute-done.25 = bf16[2,96,640]{2,1,0:T(8,128)(2,1)S(1)} collective-permute-done((bf16[2,96,640]{2,1,0:T(8,128)(2,1)}, bf16[2,96,640]{2,1,0:T(8,128)(2,1)S(1)}, u32[]{:S(2)}, u32[]{:S(2)}) %collective-permute-start.25) | collective-permute-done | bytes 245792 | tf_op jit(solution)/shard_map/ppermute | solution.py:561
  124.1 1.5 collective-permute-start.27
  125.7 4.8 %collective-permute-done.24.refs_2_ = bf16[1,512,384]{2,1,0:T(8,128)(2,1)S(1)} collective-permute-done((bf16[1,512,384]{2,1,0:T(8,128)(2,1)}, bf16[1,512,384]{2,1,0:T(8,128)(2,1)S(1)}, u32[]{:S(2)}, u32[]{:S(2)}) %collective-permute-start.24) | collective-permute-done | bytes 393248 | tf_op jit(solution)/shard_map/ppermute | solution.py:561
  131.2 4.0 %h_one_grads.1 = (bf16[2,128,768]{2,1,0:T(8,128)(2,1)}, bf16[2,128,768]{2,1,0:T(8,128)(2,1)}) custom-call(s32[4]{0:T(128)} %pad_add_fusion.idx, bf16[2,512,384]{2,1,0:T(8,128)(2,1)} %get-tuple-element.312.refs_4_.refs_0_, bf16[2,512,384]{2,1,0:T(8,128)(2,1)} %copy-done.5, bf16[1,512,384]{2,1,0:T(8,128)(2,1)} %copy-done.27, ...), custom_call_target="tpu_custom_call" | custom-call | flops 1 | bytes 1 | tf_op jit(solution)/shard_map/h_one_grads/pallas_call | solution.py:52
  135.4 1.8 fusion.7
  143.5 2.7 %collective-permute-done.30 = bf16[96,640]{1,0:T(8,128)(2,1)} collective-permute-done((bf16[96,640]{1,0:T(8,128)(2,1)S(1)}, bf16[96,640]{1,0:T(8,128)(2,1)}, u32[]{:S(2)}, u32[]{:S(2)}) %collective-permute-start.30) | collective-permute-done | bytes 122912 | tf_op jit(solution)/shard_map/ppermute | solution.py:605
  147.2 2.7 %collective-permute-done.32 = bf16[2,432,128]{2,1,0:T(8,128)(2,1)} collective-permute-done((bf16[2,432,128]{2,1,0:T(8,128)(2,1)}, bf16[2,432,128]{2,1,0:T(8,128)(2,1)}, u32[]{:S(2)}, u32[]{:S(2)}) %collective-permute-start.32) | collective-permute-done | bytes 221216 | tf_op jit(solution)/shard_map/ppermute | solution.py:605
  151.0 1.6 collective-permute-start.34
  152.6 1.5 collective-permute-start.36
  154.7 5.9 %collective-permute-done.26.refs_1_ = bf16[2,128,768]{2,1,0:T(8,128)(2,1)S(1)} collective-permute-done((bf16[2,128,768]{2,1,0:T(8,128)(2,1)}, bf16[2,128,768]{2,1,0:T(8,128)(2,1)S(1)}, u32[]{:S(2)}, u32[]{:S(2)}) %collective-permute-start.26) | collective-permute-done | bytes 393248 | tf_op jit(solution)/shard_map/ppermute | solution.py:605
  161.9 3.0 %collective-permute-start.35 = (bf16[432,128]{1,0:T(8,128)(2,1)S(1)}, bf16[432,128]{1,0:T(8,128)(2,1)S(1)}, u32[]{:S(2)}, u32[]{:S(2)}) collective-permute-start(bf16[432,128]{1,0:T(8,128)(2,1)S(1)} %fusion.9), channel_id=1, source_target_pairs={{0,16},{8,24},{16,0},{24,8},{1,17},{9,25},{17,1},{25,9},{2,18},{10... | collective-permute-start | bytes 331784 | tf_op jit(solution)/shard_map/ppermute | solution.py:605
  165.0 3.1 %collective-permute-done.38 = bf16[2,96,640]{2,1,0:T(8,128)(2,1)S(1)} collective-permute-done((bf16[2,96,640]{2,1,0:T(8,128)(2,1)S(1)}, bf16[2,96,640]{2,1,0:T(8,128)(2,1)S(1)}, u32[]{:S(2)}, u32[]{:S(2)}) %collective-permute-start.38) | collective-permute-done | bytes 245792 | tf_op jit(solution)/shard_map/ppermute | solution.py:605
  169.6 9.6 %collective-permute-done.37 = bf16[64,768]{1,0:T(8,128)(2,1)S(1)} collective-permute-done((bf16[64,768]{1,0:T(8,128)(2,1)S(1)}, bf16[64,768]{1,0:T(8,128)(2,1)S(1)}, u32[]{:S(2)}, u32[]{:S(2)}) %collective-permute-start.37) | collective-permute-done | bytes 98336 | tf_op jit(solution)/shard_map/ppermute | solution.py:605
  179.3 2.1 collective-permute-start.41
  182.1 2.5 %token_grads.1 = f32[128,768]{1,0:T(8,128)} custom-call(s32[4]{0:T(128)} %pad_add_fusion.idx, bf16[2,128,768]{2,1,0:T(8,128)(2,1)} %get-tuple-element.355.refs_0_, bf16[2,128,768]{2,1,0:T(8,128)(2,1)} %copy-done.14, bf16[128,768]{1,0:T(8,128)(2,1)} %copy-done.35, bf16[128,768]{1,0:T(8,128)(2,1)} %bitcast.101, f32[128,768]{1,0:T(8,128)} %get-tuple-element.359.refs_4_, ...), custom_call_target="tpu_custom_call" | custom-call | flops 1 | bytes 1 | tf_op jit(solution)/shard_map/token_grads/pallas_call | solution.py:52
  185.9 2.0 collective-permute-start.44
  188.2 2.0 collective-permute-start.43
  190.1 7.4 %collective-permute-done.44 = bf16[4,64,768]{2,1,0:T(8,128)(2,1)S(1)} collective-permute-done((bf16[4,64,768]{2,1,0:T(8,128)(2,1)S(1)}, bf16[4,64,768]{2,1,0:T(8,128)(2,1)S(1)}, u32[]{:S(2)}, u32[]{:S(2)}) %collective-permute-start.44) | collective-permute-done | bytes 393248 | tf_op jit(solution)/shard_map/ppermute | solution.py:561
  197.6 4.7 %collective-permute-done.43 = bf16[4,432,128]{2,1,0:T(8,128)(2,1)S(1)} collective-permute-done((bf16[4,432,128]{2,1,0:T(8,128)(2,1)S(1)}, bf16[4,432,128]{2,1,0:T(8,128)(2,1)S(1)}, u32[]{:S(2)}, u32[]{:S(2)}) %collective-permute-start.43) | collective-permute-done | bytes 442400 | tf_op jit(solution)/shard_map/ppermute | solution.py:561
  203.9 3.8 %qkv_unpack.1 = (f32[2,2,96,2304]{3,2,1,0:T(8,128)}, f32[384]{0:T(512)}) custom-call(s32[4]{0:T(128)} %pad_add_fusion.idx, bf16[2,4,96,640]{3,2,1,0:T(8,128)(2,1)} %copy-done.1, bf16[2,4,96,640]{3,2,1,0:T(8,128)(2,1)} %copy-done.12), custom_call_target="tpu_custom_call" | custom-call | flops 1 | bytes 1 | tf_op jit(solution)/shard_map/qkv_unpack/pallas_call | solution.py:52
  208.6 3.4 %w_down_w_out_unpack.1 = (f32[2,2,96,768]{3,2,1,0:T(8,128)}, f32[2,2,144,768]{3,2,1,0:T(8,128)}, f32[384]{0:T(512)}) custom-call(s32[4]{0:T(128)} %pad_add_fusion.idx, bf16[2,4,64,768]{3,2,1,0:T(8,128)(2,1)} %copy-done.4, bf16[2,4,64,768]{3,2,1,0:T(8,128)(2,1)} %copy-done.20), custom_call_target="tpu_custom_call" | custom-call | flops 1 | bytes 1 | tf_op jit(solution)/shard_map/w_down_w_out_unpack/pallas_call | solution.py:52
  213.0 3.8 %w_in_unpack.1 = f32[2,2,96,2304]{3,2,1,0:T(8,128)} custom-call(s32[4]{0:T(128)} %pad_add_fusion.idx, bf16[2,4,432,128]{3,2,1,0:T(8,128)(2,1)} %copy-done.3, bf16[2,4,432,128]{3,2,1,0:T(8,128)(2,1)} %copy-done.15), custom_call_target="tpu_custom_call" | custom-call | flops 1 | bytes 1 | tf_op jit(solution)/shard_map/w_in_unpack/pallas_call | solution.py:52
  (188 shorter events, 44.4 us)
Async XLA Ops:
  0.6 20.0 %collective-permute-start = (bf16[128,768]{1,0:T(8,128)(2,1)}, bf16[128,768]{1,0:T(8,128)(2,1)S(1)}, u32[]{:S(2)}, u32[]{:S(2)}) collective-permute-start(bf16[128,768]{1,0:T(8,128)(2,1)} %bitcast.96), channel_id=1, source_target_pairs={{0,8},{8,16},{16,24},{24,0},{1,9},{9,17},{17,25},{25,1},{2,10},{10... | collective-permute-start | bytes 589832 | tf_op jit(solution)/shard_map/ppermute | solution.py:561
  3.7 16.9 %collective-permute-start.1 = (bf16[128,768]{1,0:T(8,128)(2,1)}, bf16[128,768]{1,0:T(8,128)(2,1)S(1)}, u32[]{:S(2)}, u32[]{:S(2)}) collective-permute-start(bf16[128,768]{1,0:T(8,128)(2,1)} %bitcast.97), channel_id=1, source_target_pairs={{0,16},{8,24},{16,0},{24,8},{1,17},{9,25},{17,1},{25,9},{2,18},{10... | collective-permute-start | bytes 589832 | tf_op jit(solution)/shard_map/ppermute | solution.py:561
  6.3 14.3 %collective-permute-start.2 = (bf16[128,768]{1,0:T(8,128)(2,1)}, bf16[128,768]{1,0:T(8,128)(2,1)S(1)}, u32[]{:S(2)}, u32[]{:S(2)}) collective-permute-start(bf16[128,768]{1,0:T(8,128)(2,1)} %bitcast.98), channel_id=1, source_target_pairs={{0,24},{8,0},{16,8},{24,16},{1,25},{9,1},{17,9},{25,17},{2,26},{10... | collective-permute-start | bytes 589832 | tf_op jit(solution)/shard_map/ppermute | solution.py:561
  10.8 8.7 %collective-permute-start.3 = (bf16[208,640]{1,0:T(8,128)(2,1)}, bf16[208,640]{1,0:T(8,128)(2,1)S(1)}, u32[]{:S(2)}, u32[]{:S(2)}) collective-permute-start(bf16[208,640]{1,0:T(8,128)(2,1)} %get-tuple-element.208.refs_7_), channel_id=1, source_target_pairs={{0,1},{1,0},{2,3},{3,2},{4,5},{5,4},{6,7},{7,6},{8,9},{9,8},{10,11... | collective-permute-start | bytes 798728 | tf_op jit(solution)/shard_map/ppermute | solution.py:561
  15.5 37.6 %collective-permute-start.12 = (bf16[1056,768]{1,0:T(8,128)(2,1)}, bf16[1056,768]{1,0:T(8,128)(2,1)S(1)}, u32[]{:S(2)}, u32[]{:S(2)}) collective-permute-start(bf16[1056,768]{1,0:T(8,128)(2,1)} %pack_weights.1), channel_id=1, source_target_pairs={{0,1},{1,0},{2,3},{3,2},{4,5},{5,4},{6,7},{7,6},{8,9},{9,8},{10,11... | collective-permute-start | bytes 4866056 | tf_op jit(solution)/shard_map/ppermute | solution.py:561
  19.6 1.5 collective-permute-start.4
  26.5 2.0 collective-permute-start.6
  26.8 11.5 %collective-permute-start.5 = (bf16[512,384]{1,0:T(8,128)(2,1)}, bf16[512,384]{1,0:T(8,128)(2,1)S(1)}, u32[]{:S(2)}, u32[]{:S(2)}) collective-permute-start(bf16[512,384]{1,0:T(8,128)(2,1)} %get-tuple-element.264.refs_0_), channel_id=1, source_target_pairs={{0,4},{4,0},{1,5},{5,1},{2,6},{6,2},{3,7},{7,3},{8,12},{12,8},{9,1... | collective-permute-start | bytes 1179656 | tf_op jit(solution)/shard_map/ppermute | solution.py:561
  38.3 1.7 collective-permute-start.7
  53.1 10.9 %collective-permute-start.13 = (bf16[1056,768]{1,0:T(8,128)(2,1)S(1)}, bf16[1056,768]{1,0:T(8,128)(2,1)S(1)}, u32[]{:S(2)}, u32[]{:S(2)}) collective-permute-start(bf16[1056,768]{1,0:T(8,128)(2,1)S(1)} %collective-permute-done.12.refs_10_), channel_id=1, source_target_pairs={{0,2},{2,0},{1,3},{3,1},{4,6},{6,4},{5,7},{7,5},{8,10},{10,8},{9,1... | collective-permute-start | bytes 4866056 | tf_op jit(solution)/shard_map/ppermute | solution.py:561
  53.1 4.6 %collective-permute-start.11 = (bf16[512,768]{1,0:T(8,128)(2,1)S(1)}, bf16[512,768]{1,0:T(8,128)(2,1)S(1)}, u32[]{:S(2)}, u32[]{:S(2)}) collective-permute-start(bf16[512,768]{1,0:T(8,128)(2,1)S(1)} %copy-done.16), channel_id=1, source_target_pairs={{0,2},{2,0},{1,3},{3,1},{4,6},{6,4},{5,7},{7,5},{8,10},{10,8},{9,1... | collective-permute-start | bytes 2359304 | tf_op jit(solution)/shard_map/ppermute | solution.py:561
  53.6 20.1 %collective-permute-start.17 = (bf16[512,768]{1,0:T(8,128)(2,1)S(1)}, bf16[512,768]{1,0:T(8,128)(2,1)S(1)}, u32[]{:S(2)}, u32[]{:S(2)}) collective-permute-start(bf16[512,768]{1,0:T(8,128)(2,1)S(1)} %copy-done.16), channel_id=1, source_target_pairs={{0,4},{4,0},{1,5},{5,1},{2,6},{6,2},{3,7},{7,3},{8,12},{12,8},{9,1... | collective-permute-start | bytes 2359304 | tf_op jit(solution)/shard_map/ppermute | solution.py:561
  55.1 5.1 %collective-permute-start.8 = (bf16[128,192]{1,0:T(8,128)(2,1)}, bf16[128,192]{1,0:T(8,128)(2,1)S(1)}, u32[]{:S(2)}, u32[]{:S(2)}) collective-permute-start(bf16[128,192]{1,0:T(8,128)(2,1)} %get-tuple-element.225), channel_id=1, source_target_pairs={{0,24},{8,0},{16,8},{24,16},{1,25},{9,1},{17,9},{25,17},{2,26},{10... | collective-permute-start | bytes 147464 | tf_op jit(solution)/shard_map/ppermute | solution.py:561
  55.6 6.7 %collective-permute-start.9 = (bf16[128,192]{1,0:T(8,128)(2,1)}, bf16[128,192]{1,0:T(8,128)(2,1)S(1)}, u32[]{:S(2)}, u32[]{:S(2)}) collective-permute-start(bf16[128,192]{1,0:T(8,128)(2,1)} %get-tuple-element.226), channel_id=1, source_target_pairs={{0,16},{8,24},{16,0},{24,8},{1,17},{9,25},{17,1},{25,9},{2,18},{10... | collective-permute-start | bytes 147464 | tf_op jit(solution)/shard_map/ppermute | solution.py:561
  57.7 27.7 %copy-start.17 = (bf16[512,768]{1,0:T(8,128)(2,1)}, bf16[512,768]{1,0:T(8,128)(2,1)S(1)}, u32[]{:S(2)}) copy-start(bf16[512,768]{1,0:T(8,128)(2,1)S(1)} %collective-permute-done.11.refs_2_) | copy-start | bytes 2359300
  57.7 6.3 %collective-permute-start.10 = (bf16[128,192]{1,0:T(8,128)(2,1)}, bf16[128,192]{1,0:T(8,128)(2,1)S(1)}, u32[]{:S(2)}, u32[]{:S(2)}) collective-permute-start(bf16[128,192]{1,0:T(8,128)(2,1)} %get-tuple-element.227), channel_id=1, source_target_pairs={{0,8},{8,16},{16,24},{24,0},{1,9},{9,17},{17,25},{25,1},{2,10},{10... | collective-permute-start | bytes 147464 | tf_op jit(solution)/shard_map/ppermute | solution.py:561
  73.7 5.0 %collective-permute-start.18 = (bf16[128,6528]{1,0:T(8,128)(2,1)}, bf16[128,6528]{1,0:T(8,128)(2,1)S(1)}, u32[]{:S(2)}, u32[]{:S(2)}) collective-permute-start(bf16[128,6528]{1,0:T(8,128)(2,1)} %get-tuple-element.259.own), channel_id=1, source_target_pairs={{0,2},{2,0},{1,3},{3,1},{4,6},{6,4},{5,7},{7,5},{8,10},{10,8},{9,1... | collective-permute-start | bytes 5013512 | tf_op jit(solution)/shard_map/ppermute | solution.py:561
  73.8 4.3 %collective-permute-start.19 = (bf16[512,768]{1,0:T(8,128)(2,1)S(1)}, bf16[512,768]{1,0:T(8,128)(2,1)S(1)}, u32[]{:S(2)}, u32[]{:S(2)}) collective-permute-start(bf16[512,768]{1,0:T(8,128)(2,1)S(1)} %collective-permute-done.17.refs_1_), channel_id=1, source_target_pairs={{0,2},{2,0},{1,3},{3,1},{4,6},{6,4},{5,7},{7,5},{8,10},{10,8},{9,1... | collective-permute-start | bytes 2359304 | tf_op jit(solution)/shard_map/ppermute | solution.py:561
  74.3 11.1 %collective-permute-start.14 = (bf16[128,256]{1,0:T(8,128)(2,1)}, bf16[128,256]{1,0:T(8,128)(2,1)S(1)}, u32[]{:S(2)}, u32[]{:S(2)}) collective-permute-start(bf16[128,256]{1,0:T(8,128)(2,1)} %get-tuple-element.249), channel_id=1, source_target_pairs={{0,8},{8,16},{16,24},{24,0},{1,9},{9,17},{17,25},{25,1},{2,10},{10... | collective-permute-start | bytes 196616 | tf_op jit(solution)/shard_map/ppermute | solution.py:561
  74.4 11.0 %collective-permute-start.15 = (bf16[128,256]{1,0:T(8,128)(2,1)}, bf16[128,256]{1,0:T(8,128)(2,1)S(1)}, u32[]{:S(2)}, u32[]{:S(2)}) collective-permute-start(bf16[128,256]{1,0:T(8,128)(2,1)} %get-tuple-element.250), channel_id=1, source_target_pairs={{0,16},{8,24},{16,0},{24,8},{1,17},{9,25},{17,1},{25,9},{2,18},{10... | collective-permute-start | bytes 196616 | tf_op jit(solution)/shard_map/ppermute | solution.py:561
  75.6 9.8 %collective-permute-start.16 = (bf16[128,256]{1,0:T(8,128)(2,1)}, bf16[128,256]{1,0:T(8,128)(2,1)S(1)}, u32[]{:S(2)}, u32[]{:S(2)}) collective-permute-start(bf16[128,256]{1,0:T(8,128)(2,1)} %get-tuple-element.251), channel_id=1, source_target_pairs={{0,24},{8,0},{16,8},{24,16},{1,25},{9,1},{17,9},{25,17},{2,26},{10... | collective-permute-start | bytes 196616 | tf_op jit(solution)/shard_map/ppermute | solution.py:561
  85.4 22.0 %collective-permute-start.20 = (bf16[2,1728,128]{2,1,0:T(8,128)(2,1)}, bf16[2,1728,128]{2,1,0:T(8,128)(2,1)S(1)}, u32[]{:S(2)}, u32[]{:S(2)}) collective-permute-start(bf16[2,1728,128]{2,1,0:T(8,128)(2,1)} %get-tuple-element.293), channel_id=1, source_target_pairs={{0,1},{1,0},{2,3},{3,2},{4,5},{5,4},{6,7},{7,6},{8,9},{9,8},{10,11... | collective-permute-start | bytes 2654216 | tf_op jit(solution)/shard_map/ppermute | solution.py:561
  87.0 19.5 %collective-permute-start.21 = (bf16[2,2,2,64,768]{4,3,2,1,0:T(8,128)(2,1)}, bf16[2,2,2,64,768]{4,3,2,1,0:T(8,128)(2,1)S(1)}, u32[]{:S(2)}, u32[]{:S(2)}) collective-permute-start(bf16[2,2,2,64,768]{4,3,2,1,0:T(8,128)(2,1)} %get-tuple-element.295), channel_id=1, source_target_pairs={{0,8},{8,0},{16,24},{24,16},{1,9},{9,1},{17,25},{25,17},{2,10},{10... | collective-permute-start | bytes 2359304 | tf_op jit(solution)/shard_map/ppermute | solution.py:605
  107.4 6.6 %collective-permute-start.22 = (bf16[2,512,384]{2,1,0:T(8,128)(2,1)}, bf16[2,512,384]{2,1,0:T(8,128)(2,1)S(1)}, u32[]{:S(2)}, u32[]{:S(2)}) collective-permute-start(bf16[2,512,384]{2,1,0:T(8,128)(2,1)} %get-tuple-element.297.refs_5_), channel_id=1, source_target_pairs={{0,2},{2,0},{1,3},{3,1},{4,6},{6,4},{5,7},{7,5},{8,10},{10,8},{9,1... | collective-permute-start | bytes 2359304 | tf_op jit(solution)/shard_map/ppermute | solution.py:561
  107.4 4.9 %collective-permute-start.23 = (bf16[2,2,96,640]{3,2,1,0:T(8,128)(2,1)}, bf16[2,2,96,640]{3,2,1,0:T(8,128)(2,1)}, u32[]{:S(2)}, u32[]{:S(2)}) collective-permute-start(bf16[2,2,96,640]{3,2,1,0:T(8,128)(2,1)} %get-tuple-element.298), channel_id=1, source_target_pairs={{0,2},{2,0},{1,3},{3,1},{4,6},{6,4},{5,7},{7,5},{8,10},{10,8},{9,1... | collective-permute-start | bytes 1474568 | tf_op jit(solution)/shard_map/ppermute | solution.py:561
  108.8 26.5 %collective-permute-start.29 = (bf16[1728,128]{1,0:T(8,128)(2,1)}, bf16[1728,128]{1,0:T(8,128)(2,1)}, u32[]{:S(2)}, u32[]{:S(2)}) collective-permute-start(bf16[1728,128]{1,0:T(8,128)(2,1)} %fusion), channel_id=1, source_target_pairs={{0,4},{4,0},{1,5},{5,1},{2,6},{6,2},{3,7},{7,3},{8,12},{12,8},{9,1... | collective-permute-start | bytes 1327112 | tf_op jit(solution)/shard_map/ppermute | solution.py:561
  115.0 15.5 %collective-permute-start.24 = (bf16[1,512,384]{2,1,0:T(8,128)(2,1)}, bf16[1,512,384]{2,1,0:T(8,128)(2,1)S(1)}, u32[]{:S(2)}, u32[]{:S(2)}) collective-permute-start(bf16[1,512,384]{2,1,0:T(8,128)(2,1)} %add_convert_fusion.1), channel_id=1, source_target_pairs={{0,4},{4,0},{1,5},{5,1},{2,6},{6,2},{3,7},{7,3},{8,12},{12,8},{9,1... | collective-permute-start | bytes 1179656 | tf_op jit(solution)/shard_map/ppermute | solution.py:561
  115.5 7.5 %collective-permute-start.25 = (bf16[2,96,640]{2,1,0:T(8,128)(2,1)}, bf16[2,96,640]{2,1,0:T(8,128)(2,1)S(1)}, u32[]{:S(2)}, u32[]{:S(2)}) collective-permute-start(bf16[2,96,640]{2,1,0:T(8,128)(2,1)} %fusion.3), channel_id=1, source_target_pairs={{0,1},{1,0},{2,3},{3,2},{4,5},{5,4},{6,7},{7,6},{8,9},{9,8},{10,11... | collective-permute-start | bytes 737288 | tf_op jit(solution)/shard_map/ppermute | solution.py:561
  117.0 20.2 %collective-permute-start.28 = (bf16[2,2,64,768]{3,2,1,0:T(8,128)(2,1)}, bf16[2,2,64,768]{3,2,1,0:T(8,128)(2,1)S(1)}, u32[]{:S(2)}, u32[]{:S(2)}) collective-permute-start(bf16[2,2,64,768]{3,2,1,0:T(8,128)(2,1)} %fusion.1), channel_id=1, source_target_pairs={{0,16},{8,24},{16,0},{24,8},{1,17},{9,25},{17,1},{25,9},{2,18},{10... | collective-permute-start | bytes 1179656 | tf_op jit(solution)/shard_map/ppermute | solution.py:605
  124.1 13.9 %collective-permute-start.27 = (bf16[96,640]{1,0:T(8,128)(2,1)S(1)}, bf16[96,640]{1,0:T(8,128)(2,1)S(1)}, u32[]{:S(2)}, u32[]{:S(2)}) collective-permute-start(bf16[96,640]{1,0:T(8,128)(2,1)S(1)} %fusion.6), channel_id=1, source_target_pairs={{0,4},{4,0},{1,5},{5,1},{2,6},{6,2},{3,7},{7,3},{8,12},{12,8},{9,1... | collective-permute-start | bytes 368648 | tf_op jit(solution)/shard_map/ppermute | solution.py:561
  139.1 7.2 %collective-permute-start.30 = (bf16[96,640]{1,0:T(8,128)(2,1)S(1)}, bf16[96,640]{1,0:T(8,128)(2,1)}, u32[]{:S(2)}, u32[]{:S(2)}) collective-permute-start(bf16[96,640]{1,0:T(8,128)(2,1)S(1)} %fusion.5), channel_id=1, source_target_pairs={{0,16},{8,24},{16,0},{24,8},{1,17},{9,25},{17,1},{25,9},{2,18},{10... | collective-permute-start | bytes 368648 | tf_op jit(solution)/shard_map/ppermute | solution.py:605
  140.0 9.9 %collective-permute-start.32 = (bf16[2,432,128]{2,1,0:T(8,128)(2,1)}, bf16[2,432,128]{2,1,0:T(8,128)(2,1)}, u32[]{:S(2)}, u32[]{:S(2)}) collective-permute-start(bf16[2,432,128]{2,1,0:T(8,128)(2,1)} %fusion.7), channel_id=1, source_target_pairs={{0,8},{8,0},{16,24},{24,16},{1,9},{9,1},{17,25},{25,17},{2,10},{10... | collective-permute-start | bytes 663560 | tf_op jit(solution)/shard_map/ppermute | solution.py:605
  141.0 11.6 %collective-permute-start.31 = (bf16[2,64,768]{2,1,0:T(8,128)(2,1)}, bf16[2,64,768]{2,1,0:T(8,128)(2,1)S(1)}, u32[]{:S(2)}, u32[]{:S(2)}) collective-permute-start(bf16[2,64,768]{2,1,0:T(8,128)(2,1)} %fusion.2), channel_id=1, source_target_pairs={{0,1},{1,0},{2,3},{3,2},{4,5},{5,4},{6,7},{7,6},{8,9},{9,8},{10,11... | collective-permute-start | bytes 589832 | tf_op jit(solution)/shard_map/ppermute | solution.py:561
  142.0 18.6 %collective-permute-start.26 = (bf16[2,128,768]{2,1,0:T(8,128)(2,1)}, bf16[2,128,768]{2,1,0:T(8,128)(2,1)S(1)}, u32[]{:S(2)}, u32[]{:S(2)}) collective-permute-start(bf16[2,128,768]{2,1,0:T(8,128)(2,1)} %get-tuple-element.318), channel_id=1, source_target_pairs={{0,8},{8,0},{16,24},{24,16},{1,9},{9,1},{17,25},{25,17},{2,10},{10... | collective-permute-start | bytes 1179656 | tf_op jit(solution)/shard_map/ppermute | solution.py:605
  151.0 9.7 %collective-permute-start.34 = (bf16[432,128]{1,0:T(8,128)(2,1)S(1)}, bf16[432,128]{1,0:T(8,128)(2,1)S(1)}, u32[]{:S(2)}, u32[]{:S(2)}) collective-permute-start(bf16[432,128]{1,0:T(8,128)(2,1)S(1)} %fusion.10), channel_id=1, source_target_pairs={{0,16},{8,24},{16,0},{24,8},{1,17},{9,25},{17,1},{25,9},{2,18},{10... | collective-permute-start | bytes 331784 | tf_op jit(solution)/shard_map/ppermute | solution.py:605
  152.6 12.2 %collective-permute-start.36 = (bf16[64,768]{1,0:T(8,128)(2,1)S(1)}, bf16[64,768]{1,0:T(8,128)(2,1)S(1)}, u32[]{:S(2)}, u32[]{:S(2)}) collective-permute-start(bf16[64,768]{1,0:T(8,128)(2,1)S(1)} %fusion.14), channel_id=1, source_target_pairs={{0,4},{4,0},{1,5},{5,1},{2,6},{6,2},{3,7},{7,3},{8,12},{12,8},{9,1... | collective-permute-start | bytes 294920 | tf_op jit(solution)/shard_map/ppermute | solution.py:561
  154.2 14.0 %collective-permute-start.38 = (bf16[2,96,640]{2,1,0:T(8,128)(2,1)S(1)}, bf16[2,96,640]{2,1,0:T(8,128)(2,1)S(1)}, u32[]{:S(2)}, u32[]{:S(2)}) collective-permute-start(bf16[2,96,640]{2,1,0:T(8,128)(2,1)S(1)} %pad_maximum_fusion.3), channel_id=1, source_target_pairs={{0,8},{8,0},{16,24},{24,16},{1,9},{9,1},{17,25},{25,17},{2,10},{10... | collective-permute-start | bytes 737288 | tf_op jit(solution)/shard_map/ppermute | solution.py:605
  160.6 20.8 %collective-permute-start.33 = (bf16[128,768]{1,0:T(8,128)(2,1)S(1)}, bf16[128,768]{1,0:T(8,128)(2,1)S(1)}, u32[]{:S(2)}, u32[]{:S(2)}) collective-permute-start(bf16[128,768]{1,0:T(8,128)(2,1)S(1)} %fusion.11), channel_id=1, source_target_pairs={{0,16},{8,24},{16,0},{24,8},{1,17},{9,25},{17,1},{25,9},{2,18},{10... | collective-permute-start | bytes 589832 | tf_op jit(solution)/shard_map/ppermute | solution.py:605
  161.9 17.4 %collective-permute-start.35 = (bf16[432,128]{1,0:T(8,128)(2,1)S(1)}, bf16[432,128]{1,0:T(8,128)(2,1)S(1)}, u32[]{:S(2)}, u32[]{:S(2)}) collective-permute-start(bf16[432,128]{1,0:T(8,128)(2,1)S(1)} %fusion.9), channel_id=1, source_target_pairs={{0,16},{8,24},{16,0},{24,8},{1,17},{9,25},{17,1},{25,9},{2,18},{10... | collective-permute-start | bytes 331784 | tf_op jit(solution)/shard_map/ppermute | solution.py:605
  164.9 14.2 %collective-permute-start.37 = (bf16[64,768]{1,0:T(8,128)(2,1)S(1)}, bf16[64,768]{1,0:T(8,128)(2,1)S(1)}, u32[]{:S(2)}, u32[]{:S(2)}) collective-permute-start(bf16[64,768]{1,0:T(8,128)(2,1)S(1)} %fusion.13), channel_id=1, source_target_pairs={{0,16},{8,24},{16,0},{24,8},{1,17},{9,25},{17,1},{25,9},{2,18},{10... | collective-permute-start | bytes 294920 | tf_op jit(solution)/shard_map/ppermute | solution.py:605
  168.2 17.6 %collective-permute-start.39 = (bf16[4,96,640]{2,1,0:T(8,128)(2,1)S(1)}, bf16[4,96,640]{2,1,0:T(8,128)(2,1)S(1)}, u32[]{:S(2)}, u32[]{:S(2)}) collective-permute-start(bf16[4,96,640]{2,1,0:T(8,128)(2,1)S(1)} %constant_dynamic-update-slice_fusion), channel_id=1, source_target_pairs={{0,4},{4,0},{1,5},{5,1},{2,6},{6,2},{3,7},{7,3},{8,12},{12,8},{9,1... | collective-permute-start | bytes 1474568 | tf_op jit(solution)/shard_map/ppermute | solution.py:561
  179.2 6.6 %collective-permute-start.42 = (bf16[2,64,768]{2,1,0:T(8,128)(2,1)S(1)}, bf16[2,64,768]{2,1,0:T(8,128)(2,1)S(1)}, u32[]{:S(2)}, u32[]{:S(2)}) collective-permute-start(bf16[2,64,768]{2,1,0:T(8,128)(2,1)S(1)} %pad_maximum_fusion.5), channel_id=1, source_target_pairs={{0,8},{8,0},{16,24},{24,16},{1,9},{9,1},{17,25},{25,17},{2,10},{10... | collective-permute-start | bytes 589832 | tf_op jit(solution)/shard_map/ppermute | solution.py:605
  179.3 8.8 %collective-permute-start.41 = (bf16[2,432,128]{2,1,0:T(8,128)(2,1)S(1)}, bf16[2,432,128]{2,1,0:T(8,128)(2,1)S(1)}, u32[]{:S(2)}, u32[]{:S(2)}) collective-permute-start(bf16[2,432,128]{2,1,0:T(8,128)(2,1)S(1)} %pad_maximum_fusion.4), channel_id=1, source_target_pairs={{0,8},{8,0},{16,24},{24,16},{1,9},{9,1},{17,25},{25,17},{2,10},{10... | collective-permute-start | bytes 663560 | tf_op jit(solution)/shard_map/ppermute | solution.py:605
  185.9 11.6 %collective-permute-start.44 = (bf16[4,64,768]{2,1,0:T(8,128)(2,1)S(1)}, bf16[4,64,768]{2,1,0:T(8,128)(2,1)S(1)}, u32[]{:S(2)}, u32[]{:S(2)}) collective-permute-start(bf16[4,64,768]{2,1,0:T(8,128)(2,1)S(1)} %constant_dynamic-update-slice_fusion.4), channel_id=1, source_target_pairs={{0,4},{4,0},{1,5},{5,1},{2,6},{6,2},{3,7},{7,3},{8,12},{12,8},{9,1... | collective-permute-start | bytes 1179656 | tf_op jit(solution)/shard_map/ppermute | solution.py:561
  188.2 14.1 %collective-permute-start.43 = (bf16[4,432,128]{2,1,0:T(8,128)(2,1)S(1)}, bf16[4,432,128]{2,1,0:T(8,128)(2,1)S(1)}, u32[]{:S(2)}, u32[]{:S(2)}) collective-permute-start(bf16[4,432,128]{2,1,0:T(8,128)(2,1)S(1)} %constant_dynamic-update-slice_fusion.2), channel_id=1, source_target_pairs={{0,4},{4,0},{1,5},{5,1},{2,6},{6,2},{3,7},{7,3},{8,12},{12,8},{9,1... | collective-permute-start | bytes 1327112 | tf_op jit(solution)/shard_map/ppermute | solution.py:561
  190.1 12.8 %collective-permute-start.40 = (bf16[2,4,96,640]{3,2,1,0:T(8,128)(2,1)S(1)}, bf16[2,4,96,640]{3,2,1,0:T(8,128)(2,1)S(1)}, u32[]{:S(2)}, u32[]{:S(2)}) collective-permute-start(bf16[2,4,96,640]{3,2,1,0:T(8,128)(2,1)S(1)} %pad_maximum_fusion.own), channel_id=1, source_target_pairs={{0,2},{2,0},{1,3},{3,1},{4,6},{6,4},{5,7},{7,5},{8,10},{10,8},{9,1... | collective-permute-start | bytes 2949128 | tf_op jit(solution)/shard_map/ppermute | solution.py:561
  202.4 9.7 %collective-permute-start.46 = (bf16[2,4,432,128]{3,2,1,0:T(8,128)(2,1)S(1)}, bf16[2,4,432,128]{3,2,1,0:T(8,128)(2,1)S(1)}, u32[]{:S(2)}, u32[]{:S(2)}) collective-permute-start(bf16[2,4,432,128]{3,2,1,0:T(8,128)(2,1)S(1)} %pad_maximum_fusion.1.own), channel_id=1, source_target_pairs={{0,2},{2,0},{1,3},{3,1},{4,6},{6,4},{5,7},{7,5},{8,10},{10,8},{9,1... | collective-permute-start | bytes 2654216 | tf_op jit(solution)/shard_map/ppermute | solution.py:561
  202.5 5.3 %collective-permute-start.45 = (bf16[2,4,64,768]{3,2,1,0:T(8,128)(2,1)S(1)}, bf16[2,4,64,768]{3,2,1,0:T(8,128)(2,1)S(1)}, u32[]{:S(2)}, u32[]{:S(2)}) collective-permute-start(bf16[2,4,64,768]{3,2,1,0:T(8,128)(2,1)S(1)} %pad_maximum_fusion.2.own), channel_id=1, source_target_pairs={{0,2},{2,0},{1,3},{3,1},{4,6},{6,4},{5,7},{7,5},{8,10},{10,8},{9,1... | collective-permute-start | bytes 2359304 | tf_op jit(solution)/shard_map/ppermute | solution.py:561
  (41 other events, 229.3 us)

commit v4 on v3

--- a/solution.py
+++ b/solution.py
@@ -22,7 +22,7 @@
 CTX = ("zo", "z", "x", "core")
 BF = jnp.bfloat16
 F32 = jnp.float32
-VMEM_LIMIT = 56 * 1024 * 1024
+VMEM_LIMIT = 32 * 1024 * 1024
 
 KEY_AT = ((0, 0), (0, 1), (1, 0))
 VALUE_AT = ((1, 1), (2, 0), (2, 1))
@@ -40,27 +40,27 @@
     return lax.dot_general(a, b, (((0,), (0,)), ((), ())), preferred_element_type=F32)
 
 
-def call(body, outs, n_smem, ins, scratch=(), any_ins=(), name=None):
-    specs = []
-    for i in range(len(ins)):
-        if i < n_smem:
-            specs.append(pl.BlockSpec(memory_space=pltpu.SMEM))
-        elif i in any_ins:
-            specs.append(pl.BlockSpec(memory_space=pl.ANY))
-        else:
-            specs.append(pl.BlockSpec(memory_space=pltpu.VMEM))
+def call(body, outs, n_smem, ins, scratch=(), any_ins=(), hbm_ins=(), hbm_outs=(), name=None):
+    specs, values = [], []
+    for i, value in enumerate(ins):
+        space = pltpu.SMEM if i < n_smem else (pl.ANY if i in any_ins else pltpu.VMEM)
+        if i in hbm_ins:
+            value = pltpu.with_memory_space_constraint(value, pltpu.HBM)
+        specs.append(pl.BlockSpec(memory_space=space))
+        values.append(value)
+    shapes = []
+    for i, (shape, kind) in enumerate(outs):
+        shapes.append(pltpu.HBM(shape, kind) if i in hbm_outs else jax.ShapeDtypeStruct(shape, kind))
     return pl.pallas_call(
         body,
-        out_shape=[jax.ShapeDtypeStruct(s, t) for s, t in outs],
+        out_shape=shapes,
         in_specs=specs,
         out_specs=[pl.BlockSpec(memory_space=pltpu.VMEM)] * len(outs),
         scratch_shapes=list(scratch),
         compiler_params=pltpu.CompilerParams(vmem_limit_bytes=VMEM_LIMIT),
-        cost_estimate=pl.CostEstimate(
-            flops=1, bytes_accessed=1, transcendentals=0
-        ),
+        cost_estimate=pl.CostEstimate(flops=1, bytes_accessed=1, transcendentals=0),
         name=name,
-    )(*ins)
+    )(*values)
 
 
 def normalise(values):
@@ -106,7 +106,7 @@
     half_ref[half + 1 : half + 2, 0:height] = two_ref[...].reshape(1, height)
 
 
-def pack_kernel(idx, out_ref, in_ref, down_ref, pack_ref):
+def pack_kernel(idx, out_ref, in_ref, down_ref, pack_ref, pack_down):
     c = idx[2]
     half = out_ref.shape[0] // 2
     at = pl.ds(pl.multiple_of(c * half, half), half)
@@ -114,8 +114,9 @@
     for b in range(3):
         pack_ref[(1 + b) * half : (2 + b) * half, :] = in_ref[at, b * D : (b + 1) * D]
     count, step = down_half(down_ref.shape[0])
-    at = pl.ds(pl.multiple_of(c * step, 16), count)
-    pack_ref[4 * half :, :] = down_ref[at, :]
+    quarter, hop = down_half(count)
+    at = pl.multiple_of(c * step + lax.rem(idx[0], 2) * hop, 16)
+    pack_down[...] = down_ref[pl.ds(at, quarter), :]
 
 
 def down_half(height):
@@ -299,7 +300,8 @@
     atts = refs[:TP]
     tok_ref, cot_ref, gains_ref, out_own, in_own, down_own = refs[TP : TP + 6]
     packs = refs[TP + 6 : TP + 6 + n_packs]
-    rest = refs[TP + 6 + n_packs :]
+    down_packs = refs[TP + 6 + n_packs : TP + 6 + 2 * n_packs]
+    rest = refs[TP + 6 + 2 * n_packs :]
     result_ref, gmid_ref, act_ref, gain_ref = rest[:4]
     gatts = rest[4 : 4 + TP]
     w_out, w_in, w_down, sems = rest[4 + TP :]
@@ -321,15 +323,18 @@
         core = 1 - c if i % 2 else c
         at = rows((shard * 2 + core) * half, half)
         source = pack.at[0:half, :]
-        outs.append(pltpu.make_async_copy(source, w_out.at[at, :], sems.at[3 + 5 * i]))
+        outs.append(pltpu.make_async_copy(source, w_out.at[at, :], sems.at[3 + 6 * i]))
         for b in range(3):
             source = pack.at[(1 + b) * half : (2 + b) * half, :]
             target = w_in.at[at, b * D : (b + 1) * D]
-            ins.append(pltpu.make_async_copy(source, target, sems.at[4 + 5 * i + b]))
-        at = rows(shard * down_own.shape[0] + core * step, count)
-        source = pack.at[4 * half : 4 * half + count, :]
-        downs.append(pltpu.make_async_copy(source, w_down.at[at, :], sems.at[7 + 5 * i]))
-    apart = 2 * count == down_own.shape[0]
+            ins.append(pltpu.make_async_copy(source, target, sems.at[4 + 6 * i + b]))
+        quarter, hop = down_half(count)
+        for b in range(2):
+            parity = lax.rem(z + b, 2)
+            at = rows(shard * down_own.shape[0] + core * step + parity * hop, quarter)
+            source = down_packs[i].at[b]
+            downs.append(pltpu.make_async_copy(source, w_down.at[at, :], sems.at[7 + 6 * i + b]))
+    apart = 4 * down_half(count)[0] == down_own.shape[0]
     for copy in outs + ins + (downs if apart else downs[:1]):
         copy.start()
     starts = [pl.multiple_of(lax.rem(z + j, TP) * GW, GW) for j in range(TP)]
@@ -415,7 +420,7 @@
                 ins[k][xx, t * pad_d : t * pad_d + rows_d, :] = grad[
                     xx * pad_d : xx * pad_d + rows_d, t * 128 : t * 128 + 128
                 ]
-    high = mine_ref.shape[3] * TP
+    high = mine_ref.shape[1]
     gain = jnp.broadcast_to(gain_ref[0:1, :], (high - pad_f - pad_d, D)).astype(BF)
     for xx in range(2):
         for s in range(shards):
@@ -424,16 +429,14 @@
             down = dot(mixed_t[piece], right[:, 2 * FF + D :]).astype(BF)
             out = dot(att_t[turned], right[:, 2 * FF : 2 * FF + D]).astype(BF)
             both = jnp.concatenate([down, out, gain], axis=0)
-            for q in range(TP):
-                chunk = both[q * (high // TP) : (q + 1) * (high // TP)]
-
-                @pl.when(lax.rem(z, 2) == q % 2)
-                def _():
-                    mine_ref[q // 2, s, xx] = chunk
-
-                @pl.when(lax.rem(z, 2) != q % 2)
-                def _():
-                    other_ref[q // 2, s, xx] = chunk
+
+            @pl.when(x == xx)
+            def _():
+                mine_ref[s] = both
+
+            @pl.when(x != xx)
+            def _():
+                other_ref[s] = both
 
 
 def qkv_grads_kernel(shards, n_kv, idx, *refs):
@@ -587,11 +590,9 @@
 
 def reduce_step(order, terms, axis, dim):
     n, i = lax.axis_size(axis), lax.axis_index(axis)
-    got = []
-    for k in range(1, n):
-        part = order.add(viewed(terms, take(lax.rem(i + k, n), dim)))
-        got.append(term(shift(part, axis, k)))
-    return viewed(terms, take(i, dim)) + got
+    total = order.add(terms)
+    got = [term(shift(pick(total, lax.rem(i + k, n), dim), axis, k)) for k in range(1, n)]
+    return [term(pick(total, i, dim))] + got
 
 
 def add(values):
@@ -608,8 +609,8 @@
 def reduce_z(order, terms, bit):
     z = lax.axis_index("z")
     i, dim = (z % 2, 1) if bit == 1 else (z // 2, 0)
-    part = order.add(viewed(terms, take(1 - i, dim)))
-    return viewed(terms, take(i, dim)) + [term(swap_z(part, bit))]
+    total = order.add(terms)
+    return [term(pick(total, i, dim)), term(swap_z(pick(total, 1 - i, dim), bit))]
 
 
 def gather_z(order, value, bit):
@@ -676,19 +677,22 @@
         [((part, WC), BF), ((part // 2 + 16, WC), BF)],
         1,
         [idx, w_qkv, gain_one, gain_two],
+        hbm_ins=(1, 2, 3),
         name="group_columns",
     )
     w_slices = [w_own]
     for k in range(1, shards):
         w_slices.append(shift(w_mine, "shard", k))
         w_slices.append(shift(w_slices[-1], "core", 1))
-    (pack,) = order.run(
+    pack, pack_down = order.run(
         pack_kernel,
-        [((2 * part + down_half(w_down.shape[0])[0], D), BF)],
+        [((2 * part, D), BF), ((down_half(down_half(w_down.shape[0])[0])[0], D), BF)],
         1,
         [idx, w_out, w_in, w_down],
+        hbm_ins=(1, 2, 3),
         name="pack_weights",
     )
+    downs = [shift(pack_down, "shard", k) for k in range(1, shards)]
     packs = [shift(pack, "shard", k) for k in range(1, shards)]
 
     freq = THETA ** (-jnp.arange(HEAD_DIM // 2, dtype=F32) * (2.0 / HEAD_DIM))
@@ -721,6 +725,8 @@
         ],
         1,
         [idx, *toks, *w_slices, w_mine, cosine, sine],
+        hbm_ins=range(1, 1 + TP + len(w_slices) + 3),
+        hbm_outs=(2, 3, 4),
         name="front",
     )
 
@@ -743,12 +749,16 @@
         name="attention_forward_near",
     )
     kvs = near + [kv_core] + [shift(after(v, *first), "core", 1) for v in near[1:]]
+    downs = [jnp.stack([v, swap_z(v, 1)]) for v in downs]
+    both_down = [v for p in downs for v in (p, shift(p, "core", 1))]
+    first = [first[0], after(first[1], *both_down)]
     att = order.run(
         functools.partial(forward_kernel, len(far), True),
         [((rows, GW), BF)] * TP + [((GW, many), F32), ((8, many), F32)],
         0,
         [query, *[kvs[i] for i in far], *first],
         scratch=scratch(len(far)),
+        hbm_outs=(TP, TP + 1),
         name="attention_forward_far",
     )
     att_blocks, (attended_t, lse) = att[:TP], att[TP:]
@@ -764,14 +774,16 @@
         [((rows, D), F32), ((rows, D), F32), ((rows, ACT_ALL), BF), ((8, D), F32)]
         + [((rows, 256), BF)] * TP,
         1,
-        [idx, *atts, tok, cot, after(gains, h_core), w_out, w_in, w_down, *both],
+        [idx, *atts, tok, cot, after(gains, h_core), w_out, w_in, w_down, *both, *both_down],
         scratch=[
             pltpu.VMEM((D, D), BF),
             pltpu.VMEM((D, 2 * FF), BF),
             pltpu.VMEM((FF, D), BF),
-            pltpu.SemaphoreType.DMA((3 + 5 * len(both),)),
+            pltpu.SemaphoreType.DMA((3 + 6 * len(both),)),
         ],
-        any_ins=range(1 + TP + 3, 1 + TP + 6 + len(both)),
+        any_ins=range(1 + TP + 3, 1 + TP + 6 + 2 * len(both)),
+        hbm_ins=(1 + TP, 2 + TP, 3 + TP),
+        hbm_outs=(0, 1, 3),
         name="feed_forward",
     )
     result, grad_middle, act, gain_two_row = mid[:4]
@@ -784,7 +796,7 @@
     ffn = order.run(
         functools.partial(ffn_grads_kernel, shards),
         [((2, high_in, 128), BF)] * shards
-        + [((2, shards, 2, high // TP, D), BF)] * 2,
+        + [((shards, high, D), BF)] * 2,
         1,
         [idx, act, shift(act, "core", 1), gain_two_row],
         scratch=[
@@ -793,11 +805,12 @@
             pltpu.VMEM((4 * shards, pad_d, 2 * rows), BF),
             pltpu.VMEM((2 * rows, 2 * FF + 2 * D), BF),
         ],
+        hbm_outs=range(shards + 2),
         name="ffn_weight_grads",
     )
     f_in = [term(ffn[0])]
     f_in += [term(shift(after(ffn[k], *gas), "shard", k)) for k in range(1, shards)]
-    f_rest = [term(ffn[shards]), term(swap_z(after(ffn[shards + 1], *gas), 1))]
+    f_rest = [term(ffn[shards]), term(shift(after(ffn[shards + 1], *gas), "x", 1))]
 
     dkv_keep, dkv_send, dq = order.run(
         functools.partial(backward_kernel, n_kv),
@@ -814,6 +827,7 @@
             pltpu.VMEM((keys, 2 * GW), F32),
             pltpu.VMEM((256, many), F32),
         ],
+        hbm_ins=range(0, 1 + n_kv + TP + 4),
         name="attention_backward",
     )
     mine, other = order.run(
@@ -821,6 +835,7 @@
         [((shards, 2, rows_d, WC), BF)] * 2,
         1,
         [idx, *hs, dkv_keep, dkv_send, dq, w_full, gains],
+        hbm_ins=range(1, 1 + n_kv),
         name="qkv_weight_grads",
     )
     first_got = [t[0] for t in f_in[1:] + f_rest[1:]]
@@ -834,11 +849,19 @@
         return jnp.stack([value, shift(order.step(value), "x", 1)])
 
     f_in = reduce_step(order, f_in, "x", 0)
-    f_rest = reduce_z(order, f_rest, 2)
+    f_rest = reduce_step(order, f_rest, "shard", 0)
     wq = reduce_step(order, wq, "shard", 0)
+    f_in = reduce_z(order, viewed(f_in, reshaped(2, 2, high_in // TP, 128)), 1)
+    f_rest = reduce_z(order, viewed(f_rest, reshaped(2, 2, high // TP, D)), 1)
     got = shift(order.add(viewed(terms, take(1, 0))), "x", 1)
     terms = viewed(terms, take(0, 0)) + [term(got)]
     wq = reduce_step(order, wq, "x", 0)
+    f_in = reduce_z(order, f_in, 2)
+    f_rest = reduce_z(order, f_rest, 2)
+    wq = gather_z(order, sum_over(order.add(wq), "zo"), 2)
+    f_in = gather_z(order, sum_over(order.add(f_in), "zo"), 2)
+    f_rest = gather_z(order, sum_over(order.add(f_rest), "zo"), 2)
+
     if outer > 1:
         total = order.add(terms)
         sums = [total[0:1]] + [shift(total[k : k + 1], "zo", -k) for k in range(1, outer)]
@@ -855,38 +878,15 @@
         [idx, *sums, dq, w_full],
         name="h_one_grads",
     )
-    gh = [term(gh), term(swap_z(gh_other, 1))]
-    f_in = reduce_z(order, viewed(f_in, reshaped(2, 2, high_in // TP, 128)), 1)
-    f_rest = reduce_step(order, f_rest, "shard", 0)
-    wq = gather_z(order, sum_over(order.add(wq), "zo"), 2)
-
-    f_in = reduce_z(order, f_in, 2)
-    f_rest = reduce_step(order, f_rest, "x", 0)
     wq = gather_z(order, wq, 1)
-    gh = reduce_z(order, gh, 2)
-
-    f_in = gather_z(order, sum_over(order.add(f_in), "zo"), 2)
-    f_rest = gather_z(order, sum_over(order.add(f_rest), "zo"), 2)
+    f_in = gather_z(order, f_in, 1)
+    f_rest = gather_z(order, f_rest, 1)
     wq = pair(wq)
-
-    f_rest = gather_z(order, f_rest, 1)
-    f_in = gather_z(order, f_in, 1)
-    (grad_tokens,) = order.run(
-        functools.partial(tail_kernel, len(gh)),
-        [((rows, D), F32)],
-        1,
-        [idx, *[t[0] for t in gh], tok, grad_middle, gains],
-        name="token_grads",
-    )
+    f_in = pair(f_in)
+    gh = [term(gh), term(swap_z(order(gh_other), 1))]
     wq = order.step(wq)
     wq_got = shift(wq, "core", 1)
-
     f_rest = pair(f_rest)
-    f_in = pair(f_in)
-    f_rest = order.step(f_rest)
-    f_rest_got = shift(f_rest, "core", 1)
-    f_in = order.step(f_in)
-    f_in_got = shift(f_in, "core", 1)
     g_qkv, grad_gain_one = order.run(
         qkv_unpack_kernel,
         [((2, 2, rows_d, 3 * D), F32), ((part,), F32)],
@@ -894,6 +894,19 @@
         [idx, wq, wq_got],
         scratch=[pltpu.VMEM((part, 128), F32)],
         name="qkv_unpack",
+    )
+    gh = reduce_z(order, gh, 2)
+    f_in = order.step(f_in)
+    f_in_got = shift(f_in, "core", 1)
+    f_rest = order.step(f_rest)
+    f_rest_got = shift(f_rest, "core", 1)
+    (g_in,) = order.run(
+        functools.partial(in_unpack_kernel, shards),
+        [((2, 2, rows_d, 2 * FF), F32)],
+        1,
+        [idx, f_in, f_in_got],
+        scratch=[pltpu.VMEM((high_in, 128), F32)],
+        name="w_in_unpack",
     )
     g_out, g_down, grad_gain_two = order.run(
         functools.partial(rest_unpack_kernel, shards),
@@ -907,13 +920,12 @@
         scratch=[pltpu.VMEM((high, D), F32)],
         name="w_down_w_out_unpack",
     )
-    (g_in,) = order.run(
-        functools.partial(in_unpack_kernel, shards),
-        [((2, 2, rows_d, 2 * FF), F32)],
-        1,
-        [idx, f_in, f_in_got],
-        scratch=[pltpu.VMEM((high_in, 128), F32)],
-        name="w_in_unpack",
+    (grad_tokens,) = order.run(
+        functools.partial(tail_kernel, len(gh)),
+        [((rows, D), F32)],
+        1,
+        [idx, *[t[0] for t in gh], tok, grad_middle, gains],
+        name="token_grads",
     )
 
     return (

time: 217 us -> 200 us (0.922)
  Pallas kernels: 72.3 us -> 56.7 us
  other arithmetic: 17.3 us -> 4.47 us
  waiting for transfers between devices: 69.2 us -> 80.5 us
  starting transfers between devices: 47.6 us -> 54.2 us
  local copies, waits for them, and re-layouts: 9.24 us -> 2.9 us
    pallas_call x14, Pallas kernels: 72.3 us -> 56.7 us  [call(): pl.pallas_call(body, out_shape=shapes, in_specs=specs, out_specs=[pl.Bloc...]
    ppermute x12 -> x13, waiting for transfers between devices: 27 us -> 40 us  [swap_z(): return lax.ppermute(value, 'z', [(i, i ^ bit) for i in range(TP)])]
    convert_element_type x13, other arithmetic: 12.5 us -> 1.23 us  [add(): return total.astype(BF)]
    unnamed x87 -> x61, local copies, waits for them, and re-layouts: 8.86 us -> 2.38 us
    ppermute x12 -> x13, starting transfers between devices: 11.7 us -> 17.9 us  [swap_z(): return lax.ppermute(value, 'z', [(i, i ^ bit) for i in range(TP)])]
    ppermute x35 -> x37, waiting for transfers between devices: 42.2 us -> 40.5 us  [shift(): return lax.ppermute(value, axis, [(i, (i + k) % n) for i in range(n)])]
    ppermute x35 -> x37, starting transfers between devices: 35.8 us -> 36.3 us  [shift(): return lax.ppermute(value, axis, [(i, (i + k) % n) for i in range(n)])]
  transfers between devices with their start and end apart: 47 -> 50, of which waited for: 24 -> 26; matrix products, arithmetic and copies ran while one was open for 8% -> 2% of each run, Pallas kernels for 32% -> 28%
where the time goes in v4:
time: 200 us
  waiting for transfers between devices  80.5 us (40%)
  Pallas kernels  56.7 us (28%)
  starting transfers between devices  54.2 us (27%)
  other arithmetic  4.47 us (2%)
  local copies, waits for them, and re-layouts  2.9 us (1%)
    pallas_call x14, Pallas kernels, call(): pl.pallas_call(body, out_shape=shapes, in_specs=specs, out_specs=[pl.Bloc...  56.7 us
    ppermute x37, waiting for transfers between devices, shift(): return lax.ppermute(value, axis, [(i, (i + k) % n) for i in range(n)])  40.5 us
    ppermute x13, waiting for transfers between devices, swap_z(): return lax.ppermute(value, 'z', [(i, i ^ bit) for i in range(TP)])  40 us
    ppermute x37, starting transfers between devices, shift(): return lax.ppermute(value, axis, [(i, (i + k) % n) for i in range(n)])  36.3 us
    ppermute x13, starting transfers between devices, swap_z(): return lax.ppermute(value, 'z', [(i, i ^ bit) for i in range(TP)])  17.9 us
  transfers between devices with their start and end apart: 50, of which 26 were waited for; matrix products, arithmetic and copies ran while one was open for 2% of the time, Pallas kernels for 28%

profile of v4, /device:TPU:0, one launch (start us, length us, event | category | flops | bytes accessed | tf_op | source)
XLA Modules:
  0.0 200.0 jit_solution(150115790955767699)
XLA Ops:
  0.6 3.1 %collective-permute-start = (bf16[128,768]{1,0:T(8,128)(2,1)}, bf16[128,768]{1,0:T(8,128)(2,1)S(1)}, u32[]{:S(2)}, u32[]{:S(2)}) collective-permute-start(bf16[128,768]{1,0:T(8,128)(2,1)} %bitcast.67), channel_id=1, source_target_pairs={{0,8},{8,16},{16,24},{24,0},{1,9},{9,17},{17,25},{25,1},{2,10},{10... | collective-permute-start | bytes 589832 | tf_op jit(solution)/shard_map/ppermute | solution.py:564
  3.7 2.6 %collective-permute-start.1 = (bf16[128,768]{1,0:T(8,128)(2,1)}, bf16[128,768]{1,0:T(8,128)(2,1)S(1)}, u32[]{:S(2)}, u32[]{:S(2)}) collective-permute-start(bf16[128,768]{1,0:T(8,128)(2,1)} %bitcast.68), channel_id=1, source_target_pairs={{0,16},{8,24},{16,0},{24,8},{1,17},{9,25},{17,1},{25,9},{2,18},{10... | collective-permute-start | bytes 589832 | tf_op jit(solution)/shard_map/ppermute | solution.py:564
  7.7 1.7 group_columns.1
  10.2 1.5 collective-permute-start.3
  11.7 2.0 pack_weights.1
  16.1 1.5 collective-permute-start.15
  17.7 1.9 collective-permute-done.3.refs_5_
  21.8 4.0 %front.1 = (bf16[512,256]{1,0:T(8,128)(2,1)S(1)}, bf16[512,384]{1,0:T(8,128)(2,1)S(1)}, bf16[512,768]{1,0:T(8,128)(2,1)}, bf16[768,640]{1,0:T(8,128)(2,1)}, f32[8,768]{1,0:T(8,128)}) custom-call(s32[4]{0:T(128)S(1)} %pad_add_fusion.idx, bf16[128,768]{1,0:T(8,128)(2,1)} %bitcast.70, bf16[128,768]{1,0:T(8,128)(2,1)} %copy-done.23, ...), custom_call_target="tpu_custom_call" | custom-call | flops 1 | bytes 1 | tf_op jit(solution)/shard_map/front/pallas_call | solution.py:54
  26.0 3.0 %collective-permute-start.9 = (bf16[144,768]{1,0:T(8,128)(2,1)S(1)}, bf16[144,768]{1,0:T(8,128)(2,1)S(1)}, u32[]{:S(2)}, u32[]{:S(2)}) collective-permute-start(bf16[144,768]{1,0:T(8,128)(2,1)S(1)} %collective-permute-done.8), channel_id=1, source_target_pairs={{0,8},{8,0},{16,24},{24,16},{1,9},{9,1},{17,25},{25,17},{2,10},{10... | collective-permute-start | bytes 663560 | tf_op jit(solution)/shard_map/ppermute | solution.py:606
  30.5 4.6 %collective-permute-done.9 = bf16[144,768]{1,0:T(8,128)(2,1)S(1)} collective-permute-done((bf16[144,768]{1,0:T(8,128)(2,1)S(1)}, bf16[144,768]{1,0:T(8,128)(2,1)S(1)}, u32[]{:S(2)}, u32[]{:S(2)}) %collective-permute-start.9) | collective-permute-done | bytes 221216 | tf_op jit(solution)/shard_map/ppermute | solution.py:606
  35.2 4.4 %attention_forward_near.1 = (f32[192,512]{1,0:T(8,128)S(1)}, f32[8,512]{1,0:T(8,128)S(1)}) custom-call(bf16[512,256]{1,0:T(8,128)(2,1)S(1)} %get-tuple-element.258.q_ref, bf16[512,384]{1,0:T(8,128)(2,1)S(1)} %get-tuple-element.259.refs_0_, bf16[512,384]{1,0:T(8,128)(2,1)S(1)} %collective-permute-done.6.refs_1_.refs_2_), custom_call_target="tpu_custom_call" | custom-call | flops 1 | bytes 1 | tf_op jit(solution)/shard_map/attention_forward_near/pallas_call | solution.py:54
  40.2 1.7 collective-permute-done.7.refs_1_.refs_3_
  42.0 5.0 %attention_forward_far.1 = (bf16[128,192]{1,0:T(8,128)(2,1)S(1)}, bf16[128,192]{1,0:T(8,128)(2,1)S(1)}, bf16[128,192]{1,0:T(8,128)(2,1)S(1)}, bf16[128,192]{1,0:...) custom-call(bf16[512,256]{1,0:T(8,128)(2,1)S(1)} %get-tuple-element.258.q_ref, ...), custom_call_target="tpu_custom_call" | custom-call | flops 1 | bytes 1 | tf_op jit(solution)/shard_map/attention_forward_far/pallas_call | solution.py:54
  49.5 2.0 collective-permute-start.11
  53.9 4.6 %collective-permute-done.12.refs_2_ = bf16[128,192]{1,0:T(8,128)(2,1)S(1)} collective-permute-done((bf16[128,192]{1,0:T(8,128)(2,1)S(1)}, bf16[128,192]{1,0:T(8,128)(2,1)S(1)}, u32[]{:S(2)}, u32[]{:S(2)}) %collective-permute-start.12) | collective-permute-done | bytes 49184 | tf_op jit(solution)/shard_map/ppermute | solution.py:564
  58.6 8.5 %feed_forward.1 = (f32[128,768]{1,0:T(8,128)}, f32[128,768]{1,0:T(8,128)}, bf16[128,6528]{1,0:T(8,128)(2,1)S(1)}, f32[8,768]{1,0:T(8,128)}, bf16[128,256]{1,0:T(...) custom-call(s32[4]{0:T(128)S(1)} %pad_add_fusion.idx, ...), custom_call_target="tpu_custom_call" | custom-call | flops 1 | bytes 1 | tf_op jit(solution)/shard_map/feed_forward/pallas_call | solution.py:54
  69.4 1.7 collective-permute-start.18
  73.2 4.1 %ffn_weight_grads.1 = (bf16[2,1728,128]{2,1,0:T(8,128)(2,1)}, bf16[2,1728,128]{2,1,0:T(8,128)(2,1)}, bf16[2,256,768]{2,1,0:T(8,128)(2,1)}, bf16[2,256,768]{2,1,0:T(8,128)(2,1)}) custom-call(s32[4]{0:T(128)S(1)} %pad_add_fusion.idx, bf16[128,6528]{1,0:T(8,128)(2,1)S(1)} %get-tuple-element.254.own, bf16[128,6528]{1,0:T(8,128)(2,1)S(1)} %collective-permute-done.21.got, ...), custom_call_target="tpu_custom_call" | custom-call | flops 1 | bytes 1 | tf_op jit(solution)/shard_map/ffn_weight_grads/pallas_call | solution.py:54
  77.4 1.6 collective-permute-start.23
  79.0 1.5 collective-permute-start.24
  80.5 10.5 %attention_backward.1 = (bf16[2,512,384]{2,1,0:T(8,128)(2,1)S(1)}, bf16[2,512,384]{2,1,0:T(8,128)(2,1)S(1)}, bf16[512,256]{1,0:T(8,128)(2,1)S(1)}) custom-call(bf16[512,256]{1,0:T(8,128)(2,1)} %copy-done.4, bf16[512,384]{1,0:T(8,128)(2,1)} %copy-done.6, bf16[512,384]{1,0:T(8,128)(2,1)} %copy-done.8, bf16[512,384]{1,0:T(8,128)(2,1)} %copy-done.7, ...), custom_call_target="tpu_custom_call" | custom-call | flops 1 | bytes 1 | tf_op jit(solution)/shard_map/attention_backward/pallas_call | solution.py:54
  91.0 4.6 %qkv_weight_grads.1 = (bf16[2,2,96,640]{3,2,1,0:T(8,128)(2,1)S(1)}, bf16[2,2,96,640]{3,2,1,0:T(8,128)(2,1)S(1)}) custom-call(s32[4]{0:T(128)S(1)} %pad_add_fusion.idx, bf16[512,768]{1,0:T(8,128)(2,1)} %get-tuple-element.276.refs_0_, bf16[512,768]{1,0:T(8,128)(2,1)} %copy-done.18, bf16[512,768]{1,0:T(8,128)(2,1)} %copy-done.17, bf16[512,768]{1,0:T(8,128)(2,1)} %copy-done.19, ...), custom_call_target="tpu_custom_call" | custom-call | flops 1 | bytes 1 | tf_op jit(solution)/shard_map/qkv_weight_grads/pallas_call | solution.py:54
  95.7 2.8 %collective-permute-done.24 = bf16[2,256,768]{2,1,0:T(8,128)(2,1)S(1)} collective-permute-done((bf16[2,256,768]{2,1,0:T(8,128)(2,1)}, bf16[2,256,768]{2,1,0:T(8,128)(2,1)S(1)}, u32[]{:S(2)}, u32[]{:S(2)}) %collective-permute-start.24) | collective-permute-done | bytes 786464 | tf_op jit(solution)/shard_map/ppermute | solution.py:564
  100.1 1.6 collective-permute-start.27
  102.0 1.6 collective-permute-start.26
  103.7 8.6 %collective-permute-done.27 = bf16[1728,128]{1,0:T(8,128)(2,1)S(1)} collective-permute-done((bf16[1728,128]{1,0:T(8,128)(2,1)S(1)}, bf16[1728,128]{1,0:T(8,128)(2,1)S(1)}, u32[]{:S(2)}, u32[]{:S(2)}) %collective-permute-start.27) | collective-permute-done | bytes 442400 | tf_op jit(solution)/shard_map/ppermute | solution.py:564
  115.2 1.6 collective-permute-start.32
  118.1 3.4 %collective-permute-done.32 = bf16[2,96,640]{2,1,0:T(8,128)(2,1)S(1)} collective-permute-done((bf16[2,96,640]{2,1,0:T(8,128)(2,1)S(1)}, bf16[2,96,640]{2,1,0:T(8,128)(2,1)S(1)}, u32[]{:S(2)}, u32[]{:S(2)}) %collective-permute-start.32) | collective-permute-done | bytes 245792 | tf_op jit(solution)/shard_map/ppermute | solution.py:564
  121.5 1.8 collective-permute-done.31
  123.4 1.5 collective-permute-start.35
  126.4 1.7 collective-permute-start.34
  130.0 9.3 %collective-permute-done.34 = bf16[432,128]{1,0:T(8,128)(2,1)S(1)} collective-permute-done((bf16[432,128]{1,0:T(8,128)(2,1)S(1)}, bf16[432,128]{1,0:T(8,128)(2,1)S(1)}, u32[]{:S(2)}, u32[]{:S(2)}) %collective-permute-start.34) | collective-permute-done | bytes 110624 | tf_op jit(solution)/shard_map/ppermute | solution.py:606
  139.4 3.0 %collective-permute-start.40 = (bf16[64,768]{1,0:T(8,128)(2,1)S(1)}, bf16[64,768]{1,0:T(8,128)(2,1)S(1)}, u32[]{:S(2)}, u32[]{:S(2)}) collective-permute-start(bf16[64,768]{1,0:T(8,128)(2,1)S(1)} %add_convert_fusion.12), channel_id=1, source_target_pairs={{0,16},{8,24},{16,0},{24,8},{1,17},{9,25},{17,1},{25,9},{2,18},{10... | collective-permute-start | bytes 294920 | tf_op jit(solution)/shard_map/ppermute | solution.py:606
  142.4 1.9 h_one_grads.1
  144.4 1.9 collective-permute-start.39
  146.3 3.5 %collective-permute-done.40 = bf16[64,768]{1,0:T(8,128)(2,1)S(1)} collective-permute-done((bf16[64,768]{1,0:T(8,128)(2,1)S(1)}, bf16[64,768]{1,0:T(8,128)(2,1)S(1)}, u32[]{:S(2)}, u32[]{:S(2)}) %collective-permute-start.40) | collective-permute-done | bytes 98336 | tf_op jit(solution)/shard_map/ppermute | solution.py:606
  149.9 3.2 %collective-permute-done.39 = bf16[2,96,640]{2,1,0:T(8,128)(2,1)S(1)} collective-permute-done((bf16[2,96,640]{2,1,0:T(8,128)(2,1)S(1)}, bf16[2,96,640]{2,1,0:T(8,128)(2,1)S(1)}, u32[]{:S(2)}, u32[]{:S(2)}) %collective-permute-start.39) | collective-permute-done | bytes 245792 | tf_op jit(solution)/shard_map/ppermute | solution.py:606
  153.7 5.9 %collective-permute-done.38 = bf16[2,432,128]{2,1,0:T(8,128)(2,1)S(1)} collective-permute-done((bf16[2,432,128]{2,1,0:T(8,128)(2,1)S(1)}, bf16[2,432,128]{2,1,0:T(8,128)(2,1)S(1)}, u32[]{:S(2)}, u32[]{:S(2)}) %collective-permute-start.38) | collective-permute-done | bytes 221216 | tf_op jit(solution)/shard_map/ppermute | solution.py:606
  159.7 4.8 %collective-permute-done.42 = bf16[4,96,640]{2,1,0:T(8,128)(2,1)S(1)} collective-permute-done((bf16[4,96,640]{2,1,0:T(8,128)(2,1)S(1)}, bf16[4,96,640]{2,1,0:T(8,128)(2,1)S(1)}, u32[]{:S(2)}, u32[]{:S(2)}) %collective-permute-start.42) | collective-permute-done | bytes 491552 | tf_op jit(solution)/shard_map/ppermute | solution.py:564
  165.6 2.0 %collective-permute-start.41 = (bf16[2,128,768]{2,1,0:T(8,128)(2,1)S(1)}, bf16[2,128,768]{2,1,0:T(8,128)(2,1)S(1)}, u32[]{:S(2)}, u32[]{:S(2)}) collective-permute-start(bf16[2,128,768]{2,1,0:T(8,128)(2,1)S(1)} %get-tuple-element.332), channel_id=1, source_target_pairs={{0,8},{8,0},{16,24},{24,16},{1,9},{9,1},{17,25},{25,17},{2,10},{10... | collective-permute-start | bytes 1179656 | tf_op jit(solution)/shard_map/ppermute | solution.py:606
  167.6 5.7 %collective-permute-done.44 = bf16[2,64,768]{2,1,0:T(8,128)(2,1)S(1)} collective-permute-done((bf16[2,64,768]{2,1,0:T(8,128)(2,1)S(1)}, bf16[2,64,768]{2,1,0:T(8,128)(2,1)S(1)}, u32[]{:S(2)}, u32[]{:S(2)}) %collective-permute-start.44) | collective-permute-done | bytes 196640 | tf_op jit(solution)/shard_map/ppermute | solution.py:606
  174.6 3.1 %collective-permute-done.47 = bf16[4,432,128]{2,1,0:T(8,128)(2,1)S(1)} collective-permute-done((bf16[4,432,128]{2,1,0:T(8,128)(2,1)S(1)}, bf16[4,432,128]{2,1,0:T(8,128)(2,1)S(1)}, u32[]{:S(2)}, u32[]{:S(2)}) %collective-permute-start.47) | collective-permute-done | bytes 442400 | tf_op jit(solution)/shard_map/ppermute | solution.py:564
  177.8 2.8 %qkv_unpack.1 = (f32[2,2,96,2304]{3,2,1,0:T(8,128)}, f32[384]{0:T(512)}) custom-call(s32[4]{0:T(128)S(1)} %pad_add_fusion.idx, bf16[2,4,96,640]{3,2,1,0:T(8,128)(2,1)S(1)} %pad_maximum_fusion.own, bf16[2,4,96,640]{3,2,1,0:T(8,128)(2,1)S(1)} %collective-permute-done.43.got), custom_call_target="tpu_custom_call" | custom-call | flops 1 | bytes 1 | tf_op jit(solution)/shard_map/qkv_unpack/pallas_call | solution.py:54
  181.2 4.5 %collective-permute-done.46 = bf16[4,64,768]{2,1,0:T(8,128)(2,1)S(1)} collective-permute-done((bf16[4,64,768]{2,1,0:T(8,128)(2,1)S(1)}, bf16[4,64,768]{2,1,0:T(8,128)(2,1)S(1)}, u32[]{:S(2)}, u32[]{:S(2)}) %collective-permute-start.46) | collective-permute-done | bytes 393248 | tf_op jit(solution)/shard_map/ppermute | solution.py:564
  187.2 2.9 %w_in_unpack.1 = f32[2,2,96,2304]{3,2,1,0:T(8,128)} custom-call(s32[4]{0:T(128)S(1)} %pad_add_fusion.idx, bf16[2,4,432,128]{3,2,1,0:T(8,128)(2,1)S(1)} %pad_maximum_fusion.1.own, bf16[2,4,432,128]{3,2,1,0:T(8,128)(2,1)S(1)} %collective-permute-done.49.got), custom_call_target="tpu_custom_call" | custom-call | flops 1 | bytes 1 | tf_op jit(solution)/shard_map/w_in_unpack/pallas_call | solution.py:54
  190.1 2.6 %w_down_w_out_unpack.1 = (f32[2,2,96,768]{3,2,1,0:T(8,128)}, f32[2,2,144,768]{3,2,1,0:T(8,128)}, f32[384]{0:T(512)}) custom-call(s32[4]{0:T(128)S(1)} %pad_add_fusion.idx, bf16[2,4,64,768]{3,2,1,0:T(8,128)(2,1)S(1)} %pad_maximum_fusion.2.own, bf16[2,4,64,768]{3,2,1,0:T(8,128)(2,1)S(1)} %collective-permute-done.48.got), custom_call_target="tpu_custom_call" | custom-call | flops 1 | bytes 1 | tf_op jit(solution)/shard_map/w_down_w_out_unpack/pallas_call | solution.py:54
  192.7 5.6 %collective-permute-done.45.refs_1_ = bf16[128,768]{1,0:T(8,128)(2,1)S(1)} collective-permute-done((bf16[128,768]{1,0:T(8,128)(2,1)S(1)}, bf16[128,768]{1,0:T(8,128)(2,1)S(1)}, u32[]{:S(2)}, u32[]{:S(2)}) %collective-permute-start.45) | collective-permute-done | bytes 196640 | tf_op jit(solution)/shard_map/ppermute | solution.py:606
  198.3 1.6 token_grads.1
  (172 shorter events, 33.9 us)
Async XLA Ops:
  0.6 15.5 %collective-permute-start = (bf16[128,768]{1,0:T(8,128)(2,1)}, bf16[128,768]{1,0:T(8,128)(2,1)S(1)}, u32[]{:S(2)}, u32[]{:S(2)}) collective-permute-start(bf16[128,768]{1,0:T(8,128)(2,1)} %bitcast.67), channel_id=1, source_target_pairs={{0,8},{8,16},{16,24},{24,0},{1,9},{9,17},{17,25},{25,1},{2,10},{10... | collective-permute-start | bytes 589832 | tf_op jit(solution)/shard_map/ppermute | solution.py:564
  3.7 16.9 %collective-permute-start.1 = (bf16[128,768]{1,0:T(8,128)(2,1)}, bf16[128,768]{1,0:T(8,128)(2,1)S(1)}, u32[]{:S(2)}, u32[]{:S(2)}) collective-permute-start(bf16[128,768]{1,0:T(8,128)(2,1)} %bitcast.68), channel_id=1, source_target_pairs={{0,16},{8,24},{16,0},{24,8},{1,17},{9,25},{17,1},{25,9},{2,18},{10... | collective-permute-start | bytes 589832 | tf_op jit(solution)/shard_map/ppermute | solution.py:564
  6.3 14.3 %collective-permute-start.2 = (bf16[128,768]{1,0:T(8,128)(2,1)}, bf16[128,768]{1,0:T(8,128)(2,1)S(1)}, u32[]{:S(2)}, u32[]{:S(2)}) collective-permute-start(bf16[128,768]{1,0:T(8,128)(2,1)} %bitcast.69), channel_id=1, source_target_pairs={{0,24},{8,0},{16,8},{24,16},{1,25},{9,1},{17,9},{25,17},{2,26},{10... | collective-permute-start | bytes 589832 | tf_op jit(solution)/shard_map/ppermute | solution.py:564
  10.2 9.3 %collective-permute-start.3 = (bf16[208,640]{1,0:T(8,128)(2,1)S(1)}, bf16[208,640]{1,0:T(8,128)(2,1)S(1)}, u32[]{:S(2)}, u32[]{:S(2)}) collective-permute-start(bf16[208,640]{1,0:T(8,128)(2,1)S(1)} %get-tuple-element.199.refs_7_), channel_id=1, source_target_pairs={{0,1},{1,0},{2,3},{3,2},{4,5},{5,4},{6,7},{7,6},{8,9},{9,8},{10,11... | collective-permute-start | bytes 798728 | tf_op jit(solution)/shard_map/ppermute | solution.py:564
  13.7 12.3 %collective-permute-start.8 = (bf16[144,768]{1,0:T(8,128)(2,1)S(1)}, bf16[144,768]{1,0:T(8,128)(2,1)S(1)}, u32[]{:S(2)}, u32[]{:S(2)}) collective-permute-start(bf16[144,768]{1,0:T(8,128)(2,1)S(1)} %get-tuple-element.210), channel_id=1, source_target_pairs={{0,1},{1,0},{2,3},{3,2},{4,5},{5,4},{6,7},{7,6},{8,9},{9,8},{10,11... | collective-permute-start | bytes 663560 | tf_op jit(solution)/shard_map/ppermute | solution.py:564
  16.1 31.4 %collective-permute-start.15 = (bf16[768,768]{1,0:T(8,128)(2,1)S(1)}, bf16[768,768]{1,0:T(8,128)(2,1)S(1)}, u32[]{:S(2)}, u32[]{:S(2)}) collective-permute-start(bf16[768,768]{1,0:T(8,128)(2,1)S(1)} %get-tuple-element.190), channel_id=1, source_target_pairs={{0,1},{1,0},{2,3},{3,2},{4,5},{5,4},{6,7},{7,6},{8,9},{9,8},{10,11... | collective-permute-start | bytes 3538952 | tf_op jit(solution)/shard_map/ppermute | solution.py:564
  25.8 9.4 %collective-permute-start.6 = (bf16[512,384]{1,0:T(8,128)(2,1)S(1)}, bf16[512,384]{1,0:T(8,128)(2,1)S(1)}, u32[]{:S(2)}, u32[]{:S(2)}) collective-permute-start(bf16[512,384]{1,0:T(8,128)(2,1)S(1)} %get-tuple-element.259.refs_0_), channel_id=1, source_target_pairs={{0,2},{2,0},{1,3},{3,1},{4,6},{6,4},{5,7},{7,5},{8,10},{10,8},{9,1... | collective-permute-start | bytes 1179656 | tf_op jit(solution)/shard_map/ppermute | solution.py:564
  26.0 9.0 %collective-permute-start.9 = (bf16[144,768]{1,0:T(8,128)(2,1)S(1)}, bf16[144,768]{1,0:T(8,128)(2,1)S(1)}, u32[]{:S(2)}, u32[]{:S(2)}) collective-permute-start(bf16[144,768]{1,0:T(8,128)(2,1)S(1)} %collective-permute-done.8), channel_id=1, source_target_pairs={{0,8},{8,0},{16,24},{24,16},{1,9},{9,1},{17,25},{25,17},{2,10},{10... | collective-permute-start | bytes 663560 | tf_op jit(solution)/shard_map/ppermute | solution.py:606
  29.1 11.2 %collective-permute-start.5 = (bf16[512,384]{1,0:T(8,128)(2,1)S(1)}, bf16[512,384]{1,0:T(8,128)(2,1)S(1)}, u32[]{:S(2)}, u32[]{:S(2)}) collective-permute-start(bf16[512,384]{1,0:T(8,128)(2,1)S(1)} %get-tuple-element.259.refs_0_), channel_id=1, source_target_pairs={{0,4},{4,0},{1,5},{5,1},{2,6},{6,2},{3,7},{7,3},{8,12},{12,8},{9,1... | collective-permute-start | bytes 1179656 | tf_op jit(solution)/shard_map/ppermute | solution.py:564
  35.1 5.1 %collective-permute-start.10 = (bf16[2,144,768]{2,1,0:T(8,128)(2,1)S(1)}, bf16[2,144,768]{2,1,0:T(8,128)(2,1)S(1)}, u32[]{:S(2)}, u32[]{:S(2)}) collective-permute-start(bf16[2,144,768]{2,1,0:T(8,128)(2,1)S(1)} %pad_maximum_fusion.3.refs_12_), channel_id=1, source_target_pairs={{0,2},{2,0},{1,3},{3,1},{4,6},{6,4},{5,7},{7,5},{8,10},{10,8},{9,1... | collective-permute-start | bytes 1327112 | tf_op jit(solution)/shard_map/ppermute | solution.py:564
  47.5 11.1 %collective-permute-start.16 = (bf16[768,768]{1,0:T(8,128)(2,1)S(1)}, bf16[768,768]{1,0:T(8,128)(2,1)S(1)}, u32[]{:S(2)}, u32[]{:S(2)}) collective-permute-start(bf16[768,768]{1,0:T(8,128)(2,1)S(1)} %collective-permute-done.15.refs_10_), channel_id=1, source_target_pairs={{0,2},{2,0},{1,3},{3,1},{4,6},{6,4},{5,7},{7,5},{8,10},{10,8},{9,1... | collective-permute-start | bytes 3538952 | tf_op jit(solution)/shard_map/ppermute | solution.py:564
  47.5 4.3 %collective-permute-start.14 = (bf16[512,768]{1,0:T(8,128)(2,1)}, bf16[512,768]{1,0:T(8,128)(2,1)S(1)}, u32[]{:S(2)}, u32[]{:S(2)}) collective-permute-start(bf16[512,768]{1,0:T(8,128)(2,1)} %get-tuple-element.276.refs_0_), channel_id=1, source_target_pairs={{0,2},{2,0},{1,3},{3,1},{4,6},{6,4},{5,7},{7,5},{8,10},{10,8},{9,1... | collective-permute-start | bytes 2359304 | tf_op jit(solution)/shard_map/ppermute | solution.py:564
  48.0 19.7 %collective-permute-start.20 = (bf16[512,768]{1,0:T(8,128)(2,1)}, bf16[512,768]{1,0:T(8,128)(2,1)S(1)}, u32[]{:S(2)}, u32[]{:S(2)}) collective-permute-start(bf16[512,768]{1,0:T(8,128)(2,1)} %get-tuple-element.276.refs_0_), channel_id=1, source_target_pairs={{0,4},{4,0},{1,5},{5,1},{2,6},{6,2},{3,7},{7,3},{8,12},{12,8},{9,1... | collective-permute-start | bytes 2359304 | tf_op jit(solution)/shard_map/ppermute | solution.py:564
  49.5 4.4 %collective-permute-start.11 = (bf16[128,192]{1,0:T(8,128)(2,1)S(1)}, bf16[128,192]{1,0:T(8,128)(2,1)S(1)}, u32[]{:S(2)}, u32[]{:S(2)}) collective-permute-start(bf16[128,192]{1,0:T(8,128)(2,1)S(1)} %get-tuple-element.218), channel_id=1, source_target_pairs={{0,24},{8,0},{16,8},{24,16},{1,25},{9,1},{17,9},{25,17},{2,26},{10... | collective-permute-start | bytes 147464 | tf_op jit(solution)/shard_map/ppermute | solution.py:564
  51.5 7.1 %collective-permute-start.12 = (bf16[128,192]{1,0:T(8,128)(2,1)S(1)}, bf16[128,192]{1,0:T(8,128)(2,1)S(1)}, u32[]{:S(2)}, u32[]{:S(2)}) collective-permute-start(bf16[128,192]{1,0:T(8,128)(2,1)S(1)} %get-tuple-element.219), channel_id=1, source_target_pairs={{0,16},{8,24},{16,0},{24,8},{1,17},{9,25},{17,1},{25,9},{2,18},{10... | collective-permute-start | bytes 147464 | tf_op jit(solution)/shard_map/ppermute | solution.py:564
  51.8 6.7 %collective-permute-start.13 = (bf16[128,192]{1,0:T(8,128)(2,1)S(1)}, bf16[128,192]{1,0:T(8,128)(2,1)S(1)}, u32[]{:S(2)}, u32[]{:S(2)}) collective-permute-start(bf16[128,192]{1,0:T(8,128)(2,1)S(1)} %get-tuple-element.220), channel_id=1, source_target_pairs={{0,8},{8,16},{16,24},{24,0},{1,9},{9,17},{17,25},{25,1},{2,10},{10... | collective-permute-start | bytes 147464 | tf_op jit(solution)/shard_map/ppermute | solution.py:564
  67.7 4.7 %collective-permute-start.21 = (bf16[128,6528]{1,0:T(8,128)(2,1)S(1)}, bf16[128,6528]{1,0:T(8,128)(2,1)S(1)}, u32[]{:S(2)}, u32[]{:S(2)}) collective-permute-start(bf16[128,6528]{1,0:T(8,128)(2,1)S(1)} %get-tuple-element.254.own), channel_id=1, source_target_pairs={{0,2},{2,0},{1,3},{3,1},{4,6},{6,4},{5,7},{7,5},{8,10},{10,8},{9,1... | collective-permute-start | bytes 5013512 | tf_op jit(solution)/shard_map/ppermute | solution.py:564
  67.7 4.7 %collective-permute-start.22 = (bf16[512,768]{1,0:T(8,128)(2,1)S(1)}, bf16[512,768]{1,0:T(8,128)(2,1)S(1)}, u32[]{:S(2)}, u32[]{:S(2)}) collective-permute-start(bf16[512,768]{1,0:T(8,128)(2,1)S(1)} %collective-permute-done.20.refs_1_), channel_id=1, source_target_pairs={{0,2},{2,0},{1,3},{3,1},{4,6},{6,4},{5,7},{7,5},{8,10},{10,8},{9,1... | collective-permute-start | bytes 2359304 | tf_op jit(solution)/shard_map/ppermute | solution.py:564
  68.2 9.1 %collective-permute-start.17 = (bf16[128,256]{1,0:T(8,128)(2,1)S(1)}, bf16[128,256]{1,0:T(8,128)(2,1)S(1)}, u32[]{:S(2)}, u32[]{:S(2)}) collective-permute-start(bf16[128,256]{1,0:T(8,128)(2,1)S(1)} %get-tuple-element.244), channel_id=1, source_target_pairs={{0,8},{8,16},{16,24},{24,0},{1,9},{9,17},{17,25},{25,1},{2,10},{10... | collective-permute-start | bytes 196616 | tf_op jit(solution)/shard_map/ppermute | solution.py:564
  69.4 7.9 %collective-permute-start.18 = (bf16[128,256]{1,0:T(8,128)(2,1)S(1)}, bf16[128,256]{1,0:T(8,128)(2,1)S(1)}, u32[]{:S(2)}, u32[]{:S(2)}) collective-permute-start(bf16[128,256]{1,0:T(8,128)(2,1)S(1)} %get-tuple-element.245), channel_id=1, source_target_pairs={{0,16},{8,24},{16,0},{24,8},{1,17},{9,25},{17,1},{25,9},{2,18},{10... | collective-permute-start | bytes 196616 | tf_op jit(solution)/shard_map/ppermute | solution.py:564
  71.1 6.3 %collective-permute-start.19 = (bf16[128,256]{1,0:T(8,128)(2,1)S(1)}, bf16[128,256]{1,0:T(8,128)(2,1)S(1)}, u32[]{:S(2)}, u32[]{:S(2)}) collective-permute-start(bf16[128,256]{1,0:T(8,128)(2,1)S(1)} %get-tuple-element.246), channel_id=1, source_target_pairs={{0,24},{8,0},{16,8},{24,16},{1,25},{9,1},{17,9},{25,17},{2,26},{10... | collective-permute-start | bytes 196616 | tf_op jit(solution)/shard_map/ppermute | solution.py:564
  77.4 21.9 %collective-permute-start.23 = (bf16[2,1728,128]{2,1,0:T(8,128)(2,1)}, bf16[2,1728,128]{2,1,0:T(8,128)(2,1)S(1)}, u32[]{:S(2)}, u32[]{:S(2)}) collective-permute-start(bf16[2,1728,128]{2,1,0:T(8,128)(2,1)} %get-tuple-element.288), channel_id=1, source_target_pairs={{0,1},{1,0},{2,3},{3,2},{4,5},{5,4},{6,7},{7,6},{8,9},{9,8},{10,11... | collective-permute-start | bytes 2654216 | tf_op jit(solution)/shard_map/ppermute | solution.py:564
  79.0 19.5 %collective-permute-start.24 = (bf16[2,256,768]{2,1,0:T(8,128)(2,1)}, bf16[2,256,768]{2,1,0:T(8,128)(2,1)S(1)}, u32[]{:S(2)}, u32[]{:S(2)}) collective-permute-start(bf16[2,256,768]{2,1,0:T(8,128)(2,1)} %get-tuple-element.290), channel_id=1, source_target_pairs={{0,4},{4,0},{1,5},{5,1},{2,6},{6,2},{3,7},{7,3},{8,12},{12,8},{9,1... | collective-permute-start | bytes 2359304 | tf_op jit(solution)/shard_map/ppermute | solution.py:564
  99.3 17.5 %collective-permute-start.25 = (bf16[2,512,384]{2,1,0:T(8,128)(2,1)S(1)}, bf16[2,512,384]{2,1,0:T(8,128)(2,1)S(1)}, u32[]{:S(2)}, u32[]{:S(2)}) collective-permute-start(bf16[2,512,384]{2,1,0:T(8,128)(2,1)S(1)} %get-tuple-element.292.refs_5_), channel_id=1, source_target_pairs={{0,2},{2,0},{1,3},{3,1},{4,6},{6,4},{5,7},{7,5},{8,10},{10,8},{9,1... | collective-permute-start | bytes 2359304 | tf_op jit(solution)/shard_map/ppermute | solution.py:564
  99.3 4.3 %collective-permute-start.28 = (bf16[2,2,96,640]{3,2,1,0:T(8,128)(2,1)S(1)}, bf16[2,2,96,640]{3,2,1,0:T(8,128)(2,1)S(1)}, u32[]{:S(2)}, u32[]{:S(2)}) collective-permute-start(bf16[2,2,96,640]{3,2,1,0:T(8,128)(2,1)S(1)} %get-tuple-element.298), channel_id=1, source_target_pairs={{0,2},{2,0},{1,3},{3,1},{4,6},{6,4},{5,7},{7,5},{8,10},{10,8},{9,1... | collective-permute-start | bytes 1474568 | tf_op jit(solution)/shard_map/ppermute | solution.py:564
  100.1 12.1 %collective-permute-start.27 = (bf16[1728,128]{1,0:T(8,128)(2,1)S(1)}, bf16[1728,128]{1,0:T(8,128)(2,1)S(1)}, u32[]{:S(2)}, u32[]{:S(2)}) collective-permute-start(bf16[1728,128]{1,0:T(8,128)(2,1)S(1)} %get-tuple-element.360), channel_id=1, source_target_pairs={{0,4},{4,0},{1,5},{5,1},{2,6},{6,2},{3,7},{7,3},{8,12},{12,8},{9,1... | collective-permute-start | bytes 1327112 | tf_op jit(solution)/shard_map/ppermute | solution.py:564
  102.0 10.8 %collective-permute-start.26 = (bf16[256,768]{1,0:T(8,128)(2,1)S(1)}, bf16[256,768]{1,0:T(8,128)(2,1)S(1)}, u32[]{:S(2)}, u32[]{:S(2)}) collective-permute-start(bf16[256,768]{1,0:T(8,128)(2,1)S(1)} %get-tuple-element.362), channel_id=1, source_target_pairs={{0,1},{1,0},{2,3},{3,2},{4,5},{5,4},{6,7},{7,6},{8,9},{9,8},{10,11... | collective-permute-start | bytes 1179656 | tf_op jit(solution)/shard_map/ppermute | solution.py:564
  112.9 10.5 %collective-permute-start.30 = (bf16[2,64,768]{2,1,0:T(8,128)(2,1)S(1)}, bf16[2,64,768]{2,1,0:T(8,128)(2,1)S(1)}, u32[]{:S(2)}, u32[]{:S(2)}) collective-permute-start(bf16[2,64,768]{2,1,0:T(8,128)(2,1)S(1)} %get-tuple-element.370), channel_id=1, source_target_pairs={{0,8},{8,0},{16,24},{24,16},{1,9},{9,1},{17,25},{25,17},{2,10},{10... | collective-permute-start | bytes 589832 | tf_op jit(solution)/shard_map/ppermute | solution.py:606
  114.3 9.1 %collective-permute-start.31 = (bf16[2,432,128]{2,1,0:T(8,128)(2,1)S(1)}, bf16[2,432,128]{2,1,0:T(8,128)(2,1)S(1)}, u32[]{:S(2)}, u32[]{:S(2)}) collective-permute-start(bf16[2,432,128]{2,1,0:T(8,128)(2,1)S(1)} %get-tuple-element.366), channel_id=1, source_target_pairs={{0,8},{8,0},{16,24},{24,16},{1,9},{9,1},{17,25},{25,17},{2,10},{10... | collective-permute-start | bytes 663560 | tf_op jit(solution)/shard_map/ppermute | solution.py:606
  115.2 6.3 %collective-permute-start.32 = (bf16[2,96,640]{2,1,0:T(8,128)(2,1)S(1)}, bf16[2,96,640]{2,1,0:T(8,128)(2,1)S(1)}, u32[]{:S(2)}, u32[]{:S(2)}) collective-permute-start(bf16[2,96,640]{2,1,0:T(8,128)(2,1)S(1)} %get-tuple-element.364), channel_id=1, source_target_pairs={{0,1},{1,0},{2,3},{3,2},{4,5},{5,4},{6,7},{7,6},{8,9},{9,8},{10,11... | collective-permute-start | bytes 737288 | tf_op jit(solution)/shard_map/ppermute | solution.py:564
  116.9 25.6 %collective-permute-start.29 = (bf16[1,512,384]{2,1,0:T(8,128)(2,1)S(1)}, bf16[1,512,384]{2,1,0:T(8,128)(2,1)S(1)}, u32[]{:S(2)}, u32[]{:S(2)}) collective-permute-start(bf16[1,512,384]{2,1,0:T(8,128)(2,1)S(1)} %add_convert_fusion.5), channel_id=1, source_target_pairs={{0,4},{4,0},{1,5},{5,1},{2,6},{6,2},{3,7},{7,3},{8,12},{12,8},{9,1... | collective-permute-start | bytes 1179656 | tf_op jit(solution)/shard_map/ppermute | solution.py:564
  123.4 5.1 %collective-permute-start.35 = (bf16[96,640]{1,0:T(8,128)(2,1)S(1)}, bf16[96,640]{1,0:T(8,128)(2,1)S(1)}, u32[]{:S(2)}, u32[]{:S(2)}) collective-permute-start(bf16[96,640]{1,0:T(8,128)(2,1)S(1)} %get-tuple-element.372), channel_id=1, source_target_pairs={{0,4},{4,0},{1,5},{5,1},{2,6},{6,2},{3,7},{7,3},{8,12},{12,8},{9,1... | collective-permute-start | bytes 368648 | tf_op jit(solution)/shard_map/ppermute | solution.py:564
  125.0 14.4 %collective-permute-start.33 = (bf16[64,768]{1,0:T(8,128)(2,1)S(1)}, bf16[64,768]{1,0:T(8,128)(2,1)S(1)}, u32[]{:S(2)}, u32[]{:S(2)}) collective-permute-start(bf16[64,768]{1,0:T(8,128)(2,1)S(1)} %get-tuple-element.376), channel_id=1, source_target_pairs={{0,16},{8,24},{16,0},{24,8},{1,17},{9,25},{17,1},{25,9},{2,18},{10... | collective-permute-start | bytes 294920 | tf_op jit(solution)/shard_map/ppermute | solution.py:606
  126.4 12.8 %collective-permute-start.34 = (bf16[432,128]{1,0:T(8,128)(2,1)S(1)}, bf16[432,128]{1,0:T(8,128)(2,1)S(1)}, u32[]{:S(2)}, u32[]{:S(2)}) collective-permute-start(bf16[432,128]{1,0:T(8,128)(2,1)S(1)} %get-tuple-element.374), channel_id=1, source_target_pairs={{0,16},{8,24},{16,0},{24,8},{1,17},{9,25},{17,1},{25,9},{2,18},{10... | collective-permute-start | bytes 331784 | tf_op jit(solution)/shard_map/ppermute | solution.py:606
  128.6 13.8 %collective-permute-start.37 = (bf16[96,640]{1,0:T(8,128)(2,1)S(1)}, bf16[96,640]{1,0:T(8,128)(2,1)S(1)}, u32[]{:S(2)}, u32[]{:S(2)}) collective-permute-start(bf16[96,640]{1,0:T(8,128)(2,1)S(1)} %add_convert_fusion.10), channel_id=1, source_target_pairs={{0,16},{8,24},{16,0},{24,8},{1,17},{9,25},{17,1},{25,9},{2,18},{10... | collective-permute-start | bytes 368648 | tf_op jit(solution)/shard_map/ppermute | solution.py:606
  139.3 10.5 %collective-permute-start.36 = (bf16[432,128]{1,0:T(8,128)(2,1)S(1)}, bf16[432,128]{1,0:T(8,128)(2,1)S(1)}, u32[]{:S(2)}, u32[]{:S(2)}) collective-permute-start(bf16[432,128]{1,0:T(8,128)(2,1)S(1)} %add_convert_fusion.11), channel_id=1, source_target_pairs={{0,16},{8,24},{16,0},{24,8},{1,17},{9,25},{17,1},{25,9},{2,18},{10... | collective-permute-start | bytes 331784 | tf_op jit(solution)/shard_map/ppermute | solution.py:606
  139.4 10.3 %collective-permute-start.40 = (bf16[64,768]{1,0:T(8,128)(2,1)S(1)}, bf16[64,768]{1,0:T(8,128)(2,1)S(1)}, u32[]{:S(2)}, u32[]{:S(2)}) collective-permute-start(bf16[64,768]{1,0:T(8,128)(2,1)S(1)} %add_convert_fusion.12), channel_id=1, source_target_pairs={{0,16},{8,24},{16,0},{24,8},{1,17},{9,25},{17,1},{25,9},{2,18},{10... | collective-permute-start | bytes 294920 | tf_op jit(solution)/shard_map/ppermute | solution.py:606
  144.4 8.7 %collective-permute-start.39 = (bf16[2,96,640]{2,1,0:T(8,128)(2,1)S(1)}, bf16[2,96,640]{2,1,0:T(8,128)(2,1)S(1)}, u32[]{:S(2)}, u32[]{:S(2)}) collective-permute-start(bf16[2,96,640]{2,1,0:T(8,128)(2,1)S(1)} %pad_maximum_fusion.4), channel_id=1, source_target_pairs={{0,8},{8,0},{16,24},{24,16},{1,9},{9,1},{17,25},{25,17},{2,10},{10... | collective-permute-start | bytes 737288 | tf_op jit(solution)/shard_map/ppermute | solution.py:606
  153.1 11.3 %collective-permute-start.42 = (bf16[4,96,640]{2,1,0:T(8,128)(2,1)S(1)}, bf16[4,96,640]{2,1,0:T(8,128)(2,1)S(1)}, u32[]{:S(2)}, u32[]{:S(2)}) collective-permute-start(bf16[4,96,640]{2,1,0:T(8,128)(2,1)S(1)} %constant_dynamic-update-slice_fusion.2), channel_id=1, source_target_pairs={{0,4},{4,0},{1,5},{5,1},{2,6},{6,2},{3,7},{7,3},{8,12},{12,8},{9,1... | collective-permute-start | bytes 1474568 | tf_op jit(solution)/shard_map/ppermute | solution.py:564
  153.7 5.9 %collective-permute-start.38 = (bf16[2,432,128]{2,1,0:T(8,128)(2,1)S(1)}, bf16[2,432,128]{2,1,0:T(8,128)(2,1)S(1)}, u32[]{:S(2)}, u32[]{:S(2)}) collective-permute-start(bf16[2,432,128]{2,1,0:T(8,128)(2,1)S(1)} %pad_maximum_fusion.5), channel_id=1, source_target_pairs={{0,8},{8,0},{16,24},{24,16},{1,9},{9,1},{17,25},{25,17},{2,10},{10... | collective-permute-start | bytes 663560 | tf_op jit(solution)/shard_map/ppermute | solution.py:606
  164.6 13.2 %collective-permute-start.43 = (bf16[2,4,96,640]{3,2,1,0:T(8,128)(2,1)S(1)}, bf16[2,4,96,640]{3,2,1,0:T(8,128)(2,1)S(1)}, u32[]{:S(2)}, u32[]{:S(2)}) collective-permute-start(bf16[2,4,96,640]{3,2,1,0:T(8,128)(2,1)S(1)} %pad_maximum_fusion.own), channel_id=1, source_target_pairs={{0,2},{2,0},{1,3},{3,1},{4,6},{6,4},{5,7},{7,5},{8,10},{10,8},{9,1... | collective-permute-start | bytes 2949128 | tf_op jit(solution)/shard_map/ppermute | solution.py:564
  164.7 13.0 %collective-permute-start.47 = (bf16[4,432,128]{2,1,0:T(8,128)(2,1)S(1)}, bf16[4,432,128]{2,1,0:T(8,128)(2,1)S(1)}, u32[]{:S(2)}, u32[]{:S(2)}) collective-permute-start(bf16[4,432,128]{2,1,0:T(8,128)(2,1)S(1)} %constant_dynamic-update-slice_fusion), channel_id=1, source_target_pairs={{0,4},{4,0},{1,5},{5,1},{2,6},{6,2},{3,7},{7,3},{8,12},{12,8},{9,1... | collective-permute-start | bytes 1327112 | tf_op jit(solution)/shard_map/ppermute | solution.py:564
  165.6 7.7 %collective-permute-start.44 = (bf16[2,64,768]{2,1,0:T(8,128)(2,1)S(1)}, bf16[2,64,768]{2,1,0:T(8,128)(2,1)S(1)}, u32[]{:S(2)}, u32[]{:S(2)}) collective-permute-start(bf16[2,64,768]{2,1,0:T(8,128)(2,1)S(1)} %pad_maximum_fusion.6), channel_id=1, source_target_pairs={{0,8},{8,0},{16,24},{24,16},{1,9},{9,1},{17,25},{25,17},{2,10},{10... | collective-permute-start | bytes 589832 | tf_op jit(solution)/shard_map/ppermute | solution.py:606
  165.6 15.4 %collective-permute-start.41 = (bf16[2,128,768]{2,1,0:T(8,128)(2,1)S(1)}, bf16[2,128,768]{2,1,0:T(8,128)(2,1)S(1)}, u32[]{:S(2)}, u32[]{:S(2)}) collective-permute-start(bf16[2,128,768]{2,1,0:T(8,128)(2,1)S(1)} %get-tuple-element.332), channel_id=1, source_target_pairs={{0,8},{8,0},{16,24},{24,16},{1,9},{9,1},{17,25},{25,17},{2,10},{10... | collective-permute-start | bytes 1179656 | tf_op jit(solution)/shard_map/ppermute | solution.py:606
  173.4 12.3 %collective-permute-start.46 = (bf16[4,64,768]{2,1,0:T(8,128)(2,1)S(1)}, bf16[4,64,768]{2,1,0:T(8,128)(2,1)S(1)}, u32[]{:S(2)}, u32[]{:S(2)}) collective-permute-start(bf16[4,64,768]{2,1,0:T(8,128)(2,1)S(1)} %constant_dynamic-update-slice_fusion.4), channel_id=1, source_target_pairs={{0,4},{4,0},{1,5},{5,1},{2,6},{6,2},{3,7},{7,3},{8,12},{12,8},{9,1... | collective-permute-start | bytes 1179656 | tf_op jit(solution)/shard_map/ppermute | solution.py:564
  181.1 6.1 %collective-permute-start.49 = (bf16[2,4,432,128]{3,2,1,0:T(8,128)(2,1)S(1)}, bf16[2,4,432,128]{3,2,1,0:T(8,128)(2,1)S(1)}, u32[]{:S(2)}, u32[]{:S(2)}) collective-permute-start(bf16[2,4,432,128]{3,2,1,0:T(8,128)(2,1)S(1)} %pad_maximum_fusion.1.own), channel_id=1, source_target_pairs={{0,2},{2,0},{1,3},{3,1},{4,6},{6,4},{5,7},{7,5},{8,10},{10,8},{9,1... | collective-permute-start | bytes 2654216 | tf_op jit(solution)/shard_map/ppermute | solution.py:564
  185.7 4.4 %collective-permute-start.48 = (bf16[2,4,64,768]{3,2,1,0:T(8,128)(2,1)S(1)}, bf16[2,4,64,768]{3,2,1,0:T(8,128)(2,1)S(1)}, u32[]{:S(2)}, u32[]{:S(2)}) collective-permute-start(bf16[2,4,64,768]{3,2,1,0:T(8,128)(2,1)S(1)} %pad_maximum_fusion.2.own), channel_id=1, source_target_pairs={{0,2},{2,0},{1,3},{3,1},{4,6},{6,4},{5,7},{7,5},{8,10},{10,8},{9,1... | collective-permute-start | bytes 2359304 | tf_op jit(solution)/shard_map/ppermute | solution.py:564
  185.9 12.5 %collective-permute-start.45 = (bf16[128,768]{1,0:T(8,128)(2,1)S(1)}, bf16[128,768]{1,0:T(8,128)(2,1)S(1)}, u32[]{:S(2)}, u32[]{:S(2)}) collective-permute-start(bf16[128,768]{1,0:T(8,128)(2,1)S(1)} %get-tuple-element.368), channel_id=1, source_target_pairs={{0,16},{8,24},{16,0},{24,8},{1,17},{9,25},{17,1},{25,9},{2,18},{10... | collective-permute-start | bytes 589832 | tf_op jit(solution)/shard_map/ppermute | solution.py:606
  (31 other events, 313.0 us)

commit v5 on v4

--- a/solution.py
+++ b/solution.py
@@ -862,6 +862,9 @@
     f_in = gather_z(order, sum_over(order.add(f_in), "zo"), 2)
     f_rest = gather_z(order, sum_over(order.add(f_rest), "zo"), 2)
 
+    wq = gather_z(order, wq, 1)
+    f_in = gather_z(order, f_in, 1)
+    f_rest = gather_z(order, f_rest, 1)
     if outer > 1:
         total = order.add(terms)
         sums = [total[0:1]] + [shift(total[k : k + 1], "zo", -k) for k in range(1, outer)]
@@ -878,15 +881,13 @@
         [idx, *sums, dq, w_full],
         name="h_one_grads",
     )
-    wq = gather_z(order, wq, 1)
-    f_in = gather_z(order, f_in, 1)
-    f_rest = gather_z(order, f_rest, 1)
     wq = pair(wq)
-    f_in = pair(f_in)
+    f_in = pair(after(f_in, f_rest))
     gh = [term(gh), term(swap_z(order(gh_other), 1))]
     wq = order.step(wq)
     wq_got = shift(wq, "core", 1)
     f_rest = pair(f_rest)
+    gh = reduce_z(order, gh, 2)
     g_qkv, grad_gain_one = order.run(
         qkv_unpack_kernel,
         [((2, 2, rows_d, 3 * D), F32), ((part,), F32)],
@@ -895,10 +896,9 @@
         scratch=[pltpu.VMEM((part, 128), F32)],
         name="qkv_unpack",
     )
-    gh = reduce_z(order, gh, 2)
     f_in = order.step(f_in)
     f_in_got = shift(f_in, "core", 1)
-    f_rest = order.step(f_rest)
+    f_rest = order.step(after(f_rest, gh[1][0]))
     f_rest_got = shift(f_rest, "core", 1)
     (g_in,) = order.run(
         functools.partial(in_unpack_kernel, shards),
@@ -908,6 +908,14 @@
         scratch=[pltpu.VMEM((high_in, 128), F32)],
         name="w_in_unpack",
     )
+    (grad_tokens,) = order.run(
+        functools.partial(tail_kernel, len(gh)),
+        [((rows, D), F32)],
+        1,
+        [idx, *[t[0] for t in gh], tok, grad_middle, gains],
+        name="token_grads",
+    )
+
     g_out, g_down, grad_gain_two = order.run(
         functools.partial(rest_unpack_kernel, shards),
         [
@@ -920,14 +928,6 @@
         scratch=[pltpu.VMEM((high, D), F32)],
         name="w_down_w_out_unpack",
     )
-    (grad_tokens,) = order.run(
-        functools.partial(tail_kernel, len(gh)),
-        [((rows, D), F32)],
-        1,
-        [idx, *[t[0] for t in gh], tok, grad_middle, gains],
-        name="token_grads",
-    )
-
     return (
         result[None],
         grad_tokens[None],

time: 200 us -> 195 us (0.975)
  waiting for transfers between devices: 80.5 us -> 75 us
    ppermute x37, waiting for transfers between devices: 40.5 us -> 33.8 us  [shift(): return lax.ppermute(value, axis, [(i, (i + k) % n) for i in range(n)])]
  transfers between devices with their start and end apart: 50 -> 50, of which waited for: 26 -> 24; matrix products, arithmetic and copies ran while one was open for 2% -> 3% of each run, Pallas kernels for 28% -> 28%
where the time goes in v5:
time: 195 us
  waiting for transfers between devices  75 us (38%)
  Pallas kernels  56.7 us (29%)
  starting transfers between devices  54.4 us (28%)
  other arithmetic  4.51 us (2%)
  local copies, waits for them, and re-layouts  2.86 us (1%)
    pallas_call x14, Pallas kernels, call(): pl.pallas_call(body, out_shape=shapes, in_specs=specs, out_specs=[pl.Bloc...  56.7 us
    ppermute x13, waiting for transfers between devices, swap_z(): return lax.ppermute(value, 'z', [(i, i ^ bit) for i in range(TP)])  41.3 us
    ppermute x37, starting transfers between devices, shift(): return lax.ppermute(value, axis, [(i, (i + k) % n) for i in range(n)])  35.9 us
    ppermute x37, waiting for transfers between devices, shift(): return lax.ppermute(value, axis, [(i, (i + k) % n) for i in range(n)])  33.8 us
    ppermute x13, starting transfers between devices, swap_z(): return lax.ppermute(value, 'z', [(i, i ^ bit) for i in range(TP)])  18.5 us
  transfers between devices with their start and end apart: 50, of which 24 were waited for; matrix products, arithmetic and copies ran while one was open for 3% of the time, Pallas kernels for 28%

profile of v5, /device:TPU:0, one launch (start us, length us, event | category | flops | bytes accessed | tf_op | source)
XLA Modules:
  0.0 194.7 jit_solution(7289876624301451007)
XLA Ops:
  0.6 3.1 %collective-permute-start = (bf16[128,768]{1,0:T(8,128)(2,1)}, bf16[128,768]{1,0:T(8,128)(2,1)S(1)}, u32[]{:S(2)}, u32[]{:S(2)}) collective-permute-start(bf16[128,768]{1,0:T(8,128)(2,1)} %bitcast.67), channel_id=1, source_target_pairs={{0,8},{8,16},{16,24},{24,0},{1,9},{9,17},{17,25},{25,1},{2,10},{10... | collective-permute-start | bytes 589832 | tf_op jit(solution)/shard_map/ppermute | solution.py:564
  3.7 2.6 %collective-permute-start.1 = (bf16[128,768]{1,0:T(8,128)(2,1)}, bf16[128,768]{1,0:T(8,128)(2,1)S(1)}, u32[]{:S(2)}, u32[]{:S(2)}) collective-permute-start(bf16[128,768]{1,0:T(8,128)(2,1)} %bitcast.68), channel_id=1, source_target_pairs={{0,16},{8,24},{16,0},{24,8},{1,17},{9,25},{17,1},{25,9},{2,18},{10... | collective-permute-start | bytes 589832 | tf_op jit(solution)/shard_map/ppermute | solution.py:564
  7.7 1.7 group_columns.1
  10.2 1.5 collective-permute-start.3
  11.7 2.0 %pack_weights.1 = (bf16[768,768]{1,0:T(8,128)(2,1)S(1)}, bf16[144,768]{1,0:T(8,128)(2,1)S(1)}) custom-call(s32[4]{0:T(128)S(1)} %pad_add_fusion.idx, bf16[384,768]{1,0:T(8,128)(2,1)} %refs_7_, bf16[384,2304]{1,0:T(8,128)(2,1)} %refs_8_, bf16[576,768]{1,0:T(8,128)(2,1)} %refs_9_), custom_call_target="tpu_custom_call" | custom-call | flops 1 | bytes 1 | tf_op jit(solution)/shard_map/pack_weights/pallas_call | solution.py:54
  16.1 1.5 collective-permute-start.15
  17.7 1.9 collective-permute-done.3.refs_5_
  21.8 4.0 %front.1 = (bf16[512,256]{1,0:T(8,128)(2,1)S(1)}, bf16[512,384]{1,0:T(8,128)(2,1)S(1)}, bf16[512,768]{1,0:T(8,128)(2,1)}, bf16[768,640]{1,0:T(8,128)(2,1)}, f32[8,768]{1,0:T(8,128)}) custom-call(s32[4]{0:T(128)S(1)} %pad_add_fusion.idx, bf16[128,768]{1,0:T(8,128)(2,1)} %bitcast.70, bf16[128,768]{1,0:T(8,128)(2,1)} %copy-done.23, ...), custom_call_target="tpu_custom_call" | custom-call | flops 1 | bytes 1 | tf_op jit(solution)/shard_map/front/pallas_call | solution.py:54
  26.0 3.0 %collective-permute-start.9 = (bf16[144,768]{1,0:T(8,128)(2,1)S(1)}, bf16[144,768]{1,0:T(8,128)(2,1)S(1)}, u32[]{:S(2)}, u32[]{:S(2)}) collective-permute-start(bf16[144,768]{1,0:T(8,128)(2,1)S(1)} %collective-permute-done.8), channel_id=1, source_target_pairs={{0,8},{8,0},{16,24},{24,16},{1,9},{9,1},{17,25},{25,17},{2,10},{10... | collective-permute-start | bytes 663560 | tf_op jit(solution)/shard_map/ppermute | solution.py:606
  30.5 4.6 %collective-permute-done.9 = bf16[144,768]{1,0:T(8,128)(2,1)S(1)} collective-permute-done((bf16[144,768]{1,0:T(8,128)(2,1)S(1)}, bf16[144,768]{1,0:T(8,128)(2,1)S(1)}, u32[]{:S(2)}, u32[]{:S(2)}) %collective-permute-start.9) | collective-permute-done | bytes 221216 | tf_op jit(solution)/shard_map/ppermute | solution.py:606
  35.2 4.4 %attention_forward_near.1 = (f32[192,512]{1,0:T(8,128)S(1)}, f32[8,512]{1,0:T(8,128)S(1)}) custom-call(bf16[512,256]{1,0:T(8,128)(2,1)S(1)} %get-tuple-element.260.q_ref, bf16[512,384]{1,0:T(8,128)(2,1)S(1)} %get-tuple-element.261.refs_0_, bf16[512,384]{1,0:T(8,128)(2,1)S(1)} %collective-permute-done.6.refs_1_.refs_2_), custom_call_target="tpu_custom_call" | custom-call | flops 1 | bytes 1 | tf_op jit(solution)/shard_map/attention_forward_near/pallas_call | solution.py:54
  40.2 1.7 collective-permute-done.7.refs_1_.refs_3_
  42.0 5.0 %attention_forward_far.1 = (bf16[128,192]{1,0:T(8,128)(2,1)S(1)}, bf16[128,192]{1,0:T(8,128)(2,1)S(1)}, bf16[128,192]{1,0:T(8,128)(2,1)S(1)}, bf16[128,192]{1,0:...) custom-call(bf16[512,256]{1,0:T(8,128)(2,1)S(1)} %get-tuple-element.260.q_ref, ...), custom_call_target="tpu_custom_call" | custom-call | flops 1 | bytes 1 | tf_op jit(solution)/shard_map/attention_forward_far/pallas_call | solution.py:54
  49.5 2.0 %collective-permute-start.11 = (bf16[128,192]{1,0:T(8,128)(2,1)S(1)}, bf16[128,192]{1,0:T(8,128)(2,1)S(1)}, u32[]{:S(2)}, u32[]{:S(2)}) collective-permute-start(bf16[128,192]{1,0:T(8,128)(2,1)S(1)} %get-tuple-element.220), channel_id=1, source_target_pairs={{0,24},{8,0},{16,8},{24,16},{1,25},{9,1},{17,9},{25,17},{2,26},{10... | collective-permute-start | bytes 147464 | tf_op jit(solution)/shard_map/ppermute | solution.py:564
  53.9 4.6 %collective-permute-done.12.refs_2_ = bf16[128,192]{1,0:T(8,128)(2,1)S(1)} collective-permute-done((bf16[128,192]{1,0:T(8,128)(2,1)S(1)}, bf16[128,192]{1,0:T(8,128)(2,1)S(1)}, u32[]{:S(2)}, u32[]{:S(2)}) %collective-permute-start.12) | collective-permute-done | bytes 49184 | tf_op jit(solution)/shard_map/ppermute | solution.py:564
  58.6 8.5 %feed_forward.1 = (f32[128,768]{1,0:T(8,128)}, f32[128,768]{1,0:T(8,128)}, bf16[128,6528]{1,0:T(8,128)(2,1)S(1)}, f32[8,768]{1,0:T(8,128)}, bf16[128,256]{1,0:T(...) custom-call(s32[4]{0:T(128)S(1)} %pad_add_fusion.idx, ...), custom_call_target="tpu_custom_call" | custom-call | flops 1 | bytes 1 | tf_op jit(solution)/shard_map/feed_forward/pallas_call | solution.py:54
  69.4 1.7 collective-permute-start.18
  73.2 4.1 %ffn_weight_grads.1 = (bf16[2,1728,128]{2,1,0:T(8,128)(2,1)}, bf16[2,1728,128]{2,1,0:T(8,128)(2,1)}, bf16[2,256,768]{2,1,0:T(8,128)(2,1)}, bf16[2,256,768]{2,1,0:T(8,128)(2,1)}) custom-call(s32[4]{0:T(128)S(1)} %pad_add_fusion.idx, bf16[128,6528]{1,0:T(8,128)(2,1)S(1)} %get-tuple-element.256.own, bf16[128,6528]{1,0:T(8,128)(2,1)S(1)} %collective-permute-done.21.got, ...), custom_call_target="tpu_custom_call" | custom-call | flops 1 | bytes 1 | tf_op jit(solution)/shard_map/ffn_weight_grads/pallas_call | solution.py:54
  77.4 1.6 collective-permute-start.23
  79.0 1.5 collective-permute-start.24
  80.5 10.5 %attention_backward.1 = (bf16[2,512,384]{2,1,0:T(8,128)(2,1)S(1)}, bf16[2,512,384]{2,1,0:T(8,128)(2,1)S(1)}, bf16[512,256]{1,0:T(8,128)(2,1)S(1)}) custom-call(bf16[512,256]{1,0:T(8,128)(2,1)} %copy-done.4, bf16[512,384]{1,0:T(8,128)(2,1)} %copy-done.6, bf16[512,384]{1,0:T(8,128)(2,1)} %copy-done.8, bf16[512,384]{1,0:T(8,128)(2,1)} %copy-done.7, ...), custom_call_target="tpu_custom_call" | custom-call | flops 1 | bytes 1 | tf_op jit(solution)/shard_map/attention_backward/pallas_call | solution.py:54
  91.0 4.6 %qkv_weight_grads.1 = (bf16[2,2,96,640]{3,2,1,0:T(8,128)(2,1)S(1)}, bf16[2,2,96,640]{3,2,1,0:T(8,128)(2,1)S(1)}) custom-call(s32[4]{0:T(128)S(1)} %pad_add_fusion.idx, bf16[512,768]{1,0:T(8,128)(2,1)} %get-tuple-element.278.refs_0_, bf16[512,768]{1,0:T(8,128)(2,1)} %copy-done.18, bf16[512,768]{1,0:T(8,128)(2,1)} %copy-done.17, bf16[512,768]{1,0:T(8,128)(2,1)} %copy-done.19, ...), custom_call_target="tpu_custom_call" | custom-call | flops 1 | bytes 1 | tf_op jit(solution)/shard_map/qkv_weight_grads/pallas_call | solution.py:54
  95.7 2.8 %collective-permute-done.24 = bf16[2,256,768]{2,1,0:T(8,128)(2,1)S(1)} collective-permute-done((bf16[2,256,768]{2,1,0:T(8,128)(2,1)}, bf16[2,256,768]{2,1,0:T(8,128)(2,1)S(1)}, u32[]{:S(2)}, u32[]{:S(2)}) %collective-permute-start.24) | collective-permute-done | bytes 786464 | tf_op jit(solution)/shard_map/ppermute | solution.py:564
  100.1 1.6 collective-permute-start.27
  102.0 1.6 collective-permute-start.26
  103.7 8.6 %collective-permute-done.27 = bf16[1728,128]{1,0:T(8,128)(2,1)S(1)} collective-permute-done((bf16[1728,128]{1,0:T(8,128)(2,1)S(1)}, bf16[1728,128]{1,0:T(8,128)(2,1)S(1)}, u32[]{:S(2)}, u32[]{:S(2)}) %collective-permute-start.27) | collective-permute-done | bytes 442400 | tf_op jit(solution)/shard_map/ppermute | solution.py:564
  115.2 1.6 collective-permute-start.32
  118.1 3.4 %collective-permute-done.32 = bf16[2,96,640]{2,1,0:T(8,128)(2,1)S(1)} collective-permute-done((bf16[2,96,640]{2,1,0:T(8,128)(2,1)S(1)}, bf16[2,96,640]{2,1,0:T(8,128)(2,1)S(1)}, u32[]{:S(2)}, u32[]{:S(2)}) %collective-permute-start.32) | collective-permute-done | bytes 245792 | tf_op jit(solution)/shard_map/ppermute | solution.py:564
  121.5 1.8 collective-permute-done.31
  123.4 1.5 collective-permute-start.35
  126.4 1.7 collective-permute-start.34
  130.0 9.3 %collective-permute-done.34 = bf16[432,128]{1,0:T(8,128)(2,1)S(1)} collective-permute-done((bf16[432,128]{1,0:T(8,128)(2,1)S(1)}, bf16[432,128]{1,0:T(8,128)(2,1)S(1)}, u32[]{:S(2)}, u32[]{:S(2)}) %collective-permute-start.34) | collective-permute-done | bytes 110624 | tf_op jit(solution)/shard_map/ppermute | solution.py:606
  139.4 3.0 %collective-permute-start.36 = (bf16[64,768]{1,0:T(8,128)(2,1)S(1)}, bf16[64,768]{1,0:T(8,128)(2,1)S(1)}, u32[]{:S(2)}, u32[]{:S(2)}) collective-permute-start(bf16[64,768]{1,0:T(8,128)(2,1)S(1)} %add_convert_fusion.12), channel_id=1, source_target_pairs={{0,16},{8,24},{16,0},{24,8},{1,17},{9,25},{17,1},{25,9},{2,18},{10... | collective-permute-start | bytes 294920 | tf_op jit(solution)/shard_map/ppermute | solution.py:606
  142.4 1.7 collective-permute-start.41
  144.2 5.6 %collective-permute-done.36 = bf16[64,768]{1,0:T(8,128)(2,1)S(1)} collective-permute-done((bf16[64,768]{1,0:T(8,128)(2,1)S(1)}, bf16[64,768]{1,0:T(8,128)(2,1)S(1)}, u32[]{:S(2)}, u32[]{:S(2)}) %collective-permute-start.36) | collective-permute-done | bytes 98336 | tf_op jit(solution)/shard_map/ppermute | solution.py:606
  149.9 1.9 h_one_grads.1
  152.2 2.0 %collective-permute-start.39 = (bf16[2,432,128]{2,1,0:T(8,128)(2,1)S(1)}, bf16[2,432,128]{2,1,0:T(8,128)(2,1)S(1)}, u32[]{:S(2)}, u32[]{:S(2)}) collective-permute-start(bf16[2,432,128]{2,1,0:T(8,128)(2,1)S(1)} %pad_maximum_fusion.6), channel_id=1, source_target_pairs={{0,8},{8,0},{16,24},{24,16},{1,9},{9,1},{17,25},{25,17},{2,10},{10... | collective-permute-start | bytes 663560 | tf_op jit(solution)/shard_map/ppermute | solution.py:606
  154.2 5.8 %collective-permute-done.40 = bf16[2,64,768]{2,1,0:T(8,128)(2,1)S(1)} collective-permute-done((bf16[2,64,768]{2,1,0:T(8,128)(2,1)S(1)}, bf16[2,64,768]{2,1,0:T(8,128)(2,1)S(1)}, u32[]{:S(2)}, u32[]{:S(2)}) %collective-permute-start.40) | collective-permute-done | bytes 196640 | tf_op jit(solution)/shard_map/ppermute | solution.py:606
  160.1 2.6 %collective-permute-done.39 = bf16[2,432,128]{2,1,0:T(8,128)(2,1)S(1)} collective-permute-done((bf16[2,432,128]{2,1,0:T(8,128)(2,1)S(1)}, bf16[2,432,128]{2,1,0:T(8,128)(2,1)S(1)}, u32[]{:S(2)}, u32[]{:S(2)}) %collective-permute-start.39) | collective-permute-done | bytes 221216 | tf_op jit(solution)/shard_map/ppermute | solution.py:606
  164.9 1.5 collective-permute-start.48
  166.4 9.4 %collective-permute-done.42 = bf16[2,128,768]{2,1,0:T(8,128)(2,1)S(1)} collective-permute-done((bf16[2,128,768]{2,1,0:T(8,128)(2,1)S(1)}, bf16[2,128,768]{2,1,0:T(8,128)(2,1)S(1)}, u32[]{:S(2)}, u32[]{:S(2)}) %collective-permute-start.42) | collective-permute-done | bytes 393248 | tf_op jit(solution)/shard_map/ppermute | solution.py:606
  175.9 2.0 %collective-permute-start.44 = (bf16[128,768]{1,0:T(8,128)(2,1)S(1)}, bf16[128,768]{1,0:T(8,128)(2,1)S(1)}, u32[]{:S(2)}, u32[]{:S(2)}) collective-permute-start(bf16[128,768]{1,0:T(8,128)(2,1)S(1)} %get-tuple-element.372), channel_id=1, source_target_pairs={{0,16},{8,24},{16,0},{24,8},{1,17},{9,25},{17,1},{25,9},{2,18},{10... | collective-permute-start | bytes 589832 | tf_op jit(solution)/shard_map/ppermute | solution.py:606
  178.0 2.8 %qkv_unpack.1 = (f32[2,2,96,2304]{3,2,1,0:T(8,128)}, f32[384]{0:T(512)}) custom-call(s32[4]{0:T(128)S(1)} %pad_add_fusion.idx, bf16[2,4,96,640]{3,2,1,0:T(8,128)(2,1)S(1)} %pad_maximum_fusion.own, bf16[2,4,96,640]{3,2,1,0:T(8,128)(2,1)S(1)} %collective-permute-done.46.got), custom_call_target="tpu_custom_call" | custom-call | flops 1 | bytes 1 | tf_op jit(solution)/shard_map/qkv_unpack/pallas_call | solution.py:54
  180.9 4.4 %collective-permute-done.48 = bf16[4,64,768]{2,1,0:T(8,128)(2,1)S(1)} collective-permute-done((bf16[4,64,768]{2,1,0:T(8,128)(2,1)S(1)}, bf16[4,64,768]{2,1,0:T(8,128)(2,1)S(1)}, u32[]{:S(2)}, u32[]{:S(2)}) %collective-permute-start.48) | collective-permute-done | bytes 393248 | tf_op jit(solution)/shard_map/ppermute | solution.py:564
  185.3 2.2 %collective-permute-done.44.refs_1_ = bf16[128,768]{1,0:T(8,128)(2,1)S(1)} collective-permute-done((bf16[128,768]{1,0:T(8,128)(2,1)S(1)}, bf16[128,768]{1,0:T(8,128)(2,1)S(1)}, u32[]{:S(2)}, u32[]{:S(2)}) %collective-permute-start.44) | collective-permute-done | bytes 196640 | tf_op jit(solution)/shard_map/ppermute | solution.py:606
  187.6 2.9 %w_in_unpack.1 = f32[2,2,96,2304]{3,2,1,0:T(8,128)} custom-call(s32[4]{0:T(128)S(1)} %pad_add_fusion.idx, bf16[2,4,432,128]{3,2,1,0:T(8,128)(2,1)S(1)} %pad_maximum_fusion.1.own, bf16[2,4,432,128]{3,2,1,0:T(8,128)(2,1)S(1)} %collective-permute-done.47.got), custom_call_target="tpu_custom_call" | custom-call | flops 1 | bytes 1 | tf_op jit(solution)/shard_map/w_in_unpack/pallas_call | solution.py:54
  190.4 1.6 token_grads.1
  192.1 2.6 %w_down_w_out_unpack.1 = (f32[2,2,96,768]{3,2,1,0:T(8,128)}, f32[2,2,144,768]{3,2,1,0:T(8,128)}, f32[384]{0:T(512)}) custom-call(s32[4]{0:T(128)S(1)} %pad_add_fusion.idx, bf16[2,4,64,768]{3,2,1,0:T(8,128)(2,1)S(1)} %pad_maximum_fusion.2.own, bf16[2,4,64,768]{3,2,1,0:T(8,128)(2,1)S(1)} %collective-permute-done.49.got), custom_call_target="tpu_custom_call" | custom-call | flops 1 | bytes 1 | tf_op jit(solution)/shard_map/w_down_w_out_unpack/pallas_call | solution.py:54
  (171 shorter events, 31.6 us)
Async XLA Ops:
  0.6 15.5 %collective-permute-start = (bf16[128,768]{1,0:T(8,128)(2,1)}, bf16[128,768]{1,0:T(8,128)(2,1)S(1)}, u32[]{:S(2)}, u32[]{:S(2)}) collective-permute-start(bf16[128,768]{1,0:T(8,128)(2,1)} %bitcast.67), channel_id=1, source_target_pairs={{0,8},{8,16},{16,24},{24,0},{1,9},{9,17},{17,25},{25,1},{2,10},{10... | collective-permute-start | bytes 589832 | tf_op jit(solution)/shard_map/ppermute | solution.py:564
  3.7 16.9 %collective-permute-start.1 = (bf16[128,768]{1,0:T(8,128)(2,1)}, bf16[128,768]{1,0:T(8,128)(2,1)S(1)}, u32[]{:S(2)}, u32[]{:S(2)}) collective-permute-start(bf16[128,768]{1,0:T(8,128)(2,1)} %bitcast.68), channel_id=1, source_target_pairs={{0,16},{8,24},{16,0},{24,8},{1,17},{9,25},{17,1},{25,9},{2,18},{10... | collective-permute-start | bytes 589832 | tf_op jit(solution)/shard_map/ppermute | solution.py:564
  6.3 14.3 %collective-permute-start.2 = (bf16[128,768]{1,0:T(8,128)(2,1)}, bf16[128,768]{1,0:T(8,128)(2,1)S(1)}, u32[]{:S(2)}, u32[]{:S(2)}) collective-permute-start(bf16[128,768]{1,0:T(8,128)(2,1)} %bitcast.69), channel_id=1, source_target_pairs={{0,24},{8,0},{16,8},{24,16},{1,25},{9,1},{17,9},{25,17},{2,26},{10... | collective-permute-start | bytes 589832 | tf_op jit(solution)/shard_map/ppermute | solution.py:564
  10.2 9.3 %collective-permute-start.3 = (bf16[208,640]{1,0:T(8,128)(2,1)S(1)}, bf16[208,640]{1,0:T(8,128)(2,1)S(1)}, u32[]{:S(2)}, u32[]{:S(2)}) collective-permute-start(bf16[208,640]{1,0:T(8,128)(2,1)S(1)} %get-tuple-element.201.refs_7_), channel_id=1, source_target_pairs={{0,1},{1,0},{2,3},{3,2},{4,5},{5,4},{6,7},{7,6},{8,9},{9,8},{10,11... | collective-permute-start | bytes 798728 | tf_op jit(solution)/shard_map/ppermute | solution.py:564
  13.7 12.3 %collective-permute-start.8 = (bf16[144,768]{1,0:T(8,128)(2,1)S(1)}, bf16[144,768]{1,0:T(8,128)(2,1)S(1)}, u32[]{:S(2)}, u32[]{:S(2)}) collective-permute-start(bf16[144,768]{1,0:T(8,128)(2,1)S(1)} %get-tuple-element.212), channel_id=1, source_target_pairs={{0,1},{1,0},{2,3},{3,2},{4,5},{5,4},{6,7},{7,6},{8,9},{9,8},{10,11... | collective-permute-start | bytes 663560 | tf_op jit(solution)/shard_map/ppermute | solution.py:564
  16.1 31.4 %collective-permute-start.15 = (bf16[768,768]{1,0:T(8,128)(2,1)S(1)}, bf16[768,768]{1,0:T(8,128)(2,1)S(1)}, u32[]{:S(2)}, u32[]{:S(2)}) collective-permute-start(bf16[768,768]{1,0:T(8,128)(2,1)S(1)} %get-tuple-element.192), channel_id=1, source_target_pairs={{0,1},{1,0},{2,3},{3,2},{4,5},{5,4},{6,7},{7,6},{8,9},{9,8},{10,11... | collective-permute-start | bytes 3538952 | tf_op jit(solution)/shard_map/ppermute | solution.py:564
  25.8 9.4 %collective-permute-start.6 = (bf16[512,384]{1,0:T(8,128)(2,1)S(1)}, bf16[512,384]{1,0:T(8,128)(2,1)S(1)}, u32[]{:S(2)}, u32[]{:S(2)}) collective-permute-start(bf16[512,384]{1,0:T(8,128)(2,1)S(1)} %get-tuple-element.261.refs_0_), channel_id=1, source_target_pairs={{0,2},{2,0},{1,3},{3,1},{4,6},{6,4},{5,7},{7,5},{8,10},{10,8},{9,1... | collective-permute-start | bytes 1179656 | tf_op jit(solution)/shard_map/ppermute | solution.py:564
  26.0 9.0 %collective-permute-start.9 = (bf16[144,768]{1,0:T(8,128)(2,1)S(1)}, bf16[144,768]{1,0:T(8,128)(2,1)S(1)}, u32[]{:S(2)}, u32[]{:S(2)}) collective-permute-start(bf16[144,768]{1,0:T(8,128)(2,1)S(1)} %collective-permute-done.8), channel_id=1, source_target_pairs={{0,8},{8,0},{16,24},{24,16},{1,9},{9,1},{17,25},{25,17},{2,10},{10... | collective-permute-start | bytes 663560 | tf_op jit(solution)/shard_map/ppermute | solution.py:606
  29.1 11.2 %collective-permute-start.5 = (bf16[512,384]{1,0:T(8,128)(2,1)S(1)}, bf16[512,384]{1,0:T(8,128)(2,1)S(1)}, u32[]{:S(2)}, u32[]{:S(2)}) collective-permute-start(bf16[512,384]{1,0:T(8,128)(2,1)S(1)} %get-tuple-element.261.refs_0_), channel_id=1, source_target_pairs={{0,4},{4,0},{1,5},{5,1},{2,6},{6,2},{3,7},{7,3},{8,12},{12,8},{9,1... | collective-permute-start | bytes 1179656 | tf_op jit(solution)/shard_map/ppermute | solution.py:564
  35.1 5.1 %collective-permute-start.10 = (bf16[2,144,768]{2,1,0:T(8,128)(2,1)S(1)}, bf16[2,144,768]{2,1,0:T(8,128)(2,1)S(1)}, u32[]{:S(2)}, u32[]{:S(2)}) collective-permute-start(bf16[2,144,768]{2,1,0:T(8,128)(2,1)S(1)} %pad_maximum_fusion.3.refs_12_), channel_id=1, source_target_pairs={{0,2},{2,0},{1,3},{3,1},{4,6},{6,4},{5,7},{7,5},{8,10},{10,8},{9,1... | collective-permute-start | bytes 1327112 | tf_op jit(solution)/shard_map/ppermute | solution.py:564
  47.5 11.1 %collective-permute-start.16 = (bf16[768,768]{1,0:T(8,128)(2,1)S(1)}, bf16[768,768]{1,0:T(8,128)(2,1)S(1)}, u32[]{:S(2)}, u32[]{:S(2)}) collective-permute-start(bf16[768,768]{1,0:T(8,128)(2,1)S(1)} %collective-permute-done.15.refs_10_), channel_id=1, source_target_pairs={{0,2},{2,0},{1,3},{3,1},{4,6},{6,4},{5,7},{7,5},{8,10},{10,8},{9,1... | collective-permute-start | bytes 3538952 | tf_op jit(solution)/shard_map/ppermute | solution.py:564
  47.5 4.3 %collective-permute-start.14 = (bf16[512,768]{1,0:T(8,128)(2,1)}, bf16[512,768]{1,0:T(8,128)(2,1)S(1)}, u32[]{:S(2)}, u32[]{:S(2)}) collective-permute-start(bf16[512,768]{1,0:T(8,128)(2,1)} %get-tuple-element.278.refs_0_), channel_id=1, source_target_pairs={{0,2},{2,0},{1,3},{3,1},{4,6},{6,4},{5,7},{7,5},{8,10},{10,8},{9,1... | collective-permute-start | bytes 2359304 | tf_op jit(solution)/shard_map/ppermute | solution.py:564
  48.0 19.7 %collective-permute-start.20 = (bf16[512,768]{1,0:T(8,128)(2,1)}, bf16[512,768]{1,0:T(8,128)(2,1)S(1)}, u32[]{:S(2)}, u32[]{:S(2)}) collective-permute-start(bf16[512,768]{1,0:T(8,128)(2,1)} %get-tuple-element.278.refs_0_), channel_id=1, source_target_pairs={{0,4},{4,0},{1,5},{5,1},{2,6},{6,2},{3,7},{7,3},{8,12},{12,8},{9,1... | collective-permute-start | bytes 2359304 | tf_op jit(solution)/shard_map/ppermute | solution.py:564
  49.5 4.4 %collective-permute-start.11 = (bf16[128,192]{1,0:T(8,128)(2,1)S(1)}, bf16[128,192]{1,0:T(8,128)(2,1)S(1)}, u32[]{:S(2)}, u32[]{:S(2)}) collective-permute-start(bf16[128,192]{1,0:T(8,128)(2,1)S(1)} %get-tuple-element.220), channel_id=1, source_target_pairs={{0,24},{8,0},{16,8},{24,16},{1,25},{9,1},{17,9},{25,17},{2,26},{10... | collective-permute-start | bytes 147464 | tf_op jit(solution)/shard_map/ppermute | solution.py:564
  51.5 7.1 %collective-permute-start.12 = (bf16[128,192]{1,0:T(8,128)(2,1)S(1)}, bf16[128,192]{1,0:T(8,128)(2,1)S(1)}, u32[]{:S(2)}, u32[]{:S(2)}) collective-permute-start(bf16[128,192]{1,0:T(8,128)(2,1)S(1)} %get-tuple-element.221), channel_id=1, source_target_pairs={{0,16},{8,24},{16,0},{24,8},{1,17},{9,25},{17,1},{25,9},{2,18},{10... | collective-permute-start | bytes 147464 | tf_op jit(solution)/shard_map/ppermute | solution.py:564
  51.8 6.7 %collective-permute-start.13 = (bf16[128,192]{1,0:T(8,128)(2,1)S(1)}, bf16[128,192]{1,0:T(8,128)(2,1)S(1)}, u32[]{:S(2)}, u32[]{:S(2)}) collective-permute-start(bf16[128,192]{1,0:T(8,128)(2,1)S(1)} %get-tuple-element.222), channel_id=1, source_target_pairs={{0,8},{8,16},{16,24},{24,0},{1,9},{9,17},{17,25},{25,1},{2,10},{10... | collective-permute-start | bytes 147464 | tf_op jit(solution)/shard_map/ppermute | solution.py:564
  67.7 4.7 %collective-permute-start.21 = (bf16[128,6528]{1,0:T(8,128)(2,1)S(1)}, bf16[128,6528]{1,0:T(8,128)(2,1)S(1)}, u32[]{:S(2)}, u32[]{:S(2)}) collective-permute-start(bf16[128,6528]{1,0:T(8,128)(2,1)S(1)} %get-tuple-element.256.own), channel_id=1, source_target_pairs={{0,2},{2,0},{1,3},{3,1},{4,6},{6,4},{5,7},{7,5},{8,10},{10,8},{9,1... | collective-permute-start | bytes 5013512 | tf_op jit(solution)/shard_map/ppermute | solution.py:564
  67.7 4.7 %collective-permute-start.22 = (bf16[512,768]{1,0:T(8,128)(2,1)S(1)}, bf16[512,768]{1,0:T(8,128)(2,1)S(1)}, u32[]{:S(2)}, u32[]{:S(2)}) collective-permute-start(bf16[512,768]{1,0:T(8,128)(2,1)S(1)} %collective-permute-done.20.refs_1_), channel_id=1, source_target_pairs={{0,2},{2,0},{1,3},{3,1},{4,6},{6,4},{5,7},{7,5},{8,10},{10,8},{9,1... | collective-permute-start | bytes 2359304 | tf_op jit(solution)/shard_map/ppermute | solution.py:564
  68.2 9.1 %collective-permute-start.17 = (bf16[128,256]{1,0:T(8,128)(2,1)S(1)}, bf16[128,256]{1,0:T(8,128)(2,1)S(1)}, u32[]{:S(2)}, u32[]{:S(2)}) collective-permute-start(bf16[128,256]{1,0:T(8,128)(2,1)S(1)} %get-tuple-element.246), channel_id=1, source_target_pairs={{0,8},{8,16},{16,24},{24,0},{1,9},{9,17},{17,25},{25,1},{2,10},{10... | collective-permute-start | bytes 196616 | tf_op jit(solution)/shard_map/ppermute | solution.py:564
  69.4 7.9 %collective-permute-start.18 = (bf16[128,256]{1,0:T(8,128)(2,1)S(1)}, bf16[128,256]{1,0:T(8,128)(2,1)S(1)}, u32[]{:S(2)}, u32[]{:S(2)}) collective-permute-start(bf16[128,256]{1,0:T(8,128)(2,1)S(1)} %get-tuple-element.247), channel_id=1, source_target_pairs={{0,16},{8,24},{16,0},{24,8},{1,17},{9,25},{17,1},{25,9},{2,18},{10... | collective-permute-start | bytes 196616 | tf_op jit(solution)/shard_map/ppermute | solution.py:564
  71.1 6.3 %collective-permute-start.19 = (bf16[128,256]{1,0:T(8,128)(2,1)S(1)}, bf16[128,256]{1,0:T(8,128)(2,1)S(1)}, u32[]{:S(2)}, u32[]{:S(2)}) collective-permute-start(bf16[128,256]{1,0:T(8,128)(2,1)S(1)} %get-tuple-element.248), channel_id=1, source_target_pairs={{0,24},{8,0},{16,8},{24,16},{1,25},{9,1},{17,9},{25,17},{2,26},{10... | collective-permute-start | bytes 196616 | tf_op jit(solution)/shard_map/ppermute | solution.py:564
  77.4 21.9 %collective-permute-start.23 = (bf16[2,1728,128]{2,1,0:T(8,128)(2,1)}, bf16[2,1728,128]{2,1,0:T(8,128)(2,1)S(1)}, u32[]{:S(2)}, u32[]{:S(2)}) collective-permute-start(bf16[2,1728,128]{2,1,0:T(8,128)(2,1)} %get-tuple-element.290), channel_id=1, source_target_pairs={{0,1},{1,0},{2,3},{3,2},{4,5},{5,4},{6,7},{7,6},{8,9},{9,8},{10,11... | collective-permute-start | bytes 2654216 | tf_op jit(solution)/shard_map/ppermute | solution.py:564
  79.0 19.5 %collective-permute-start.24 = (bf16[2,256,768]{2,1,0:T(8,128)(2,1)}, bf16[2,256,768]{2,1,0:T(8,128)(2,1)S(1)}, u32[]{:S(2)}, u32[]{:S(2)}) collective-permute-start(bf16[2,256,768]{2,1,0:T(8,128)(2,1)} %get-tuple-element.292), channel_id=1, source_target_pairs={{0,4},{4,0},{1,5},{5,1},{2,6},{6,2},{3,7},{7,3},{8,12},{12,8},{9,1... | collective-permute-start | bytes 2359304 | tf_op jit(solution)/shard_map/ppermute | solution.py:564
  99.3 17.5 %collective-permute-start.25 = (bf16[2,512,384]{2,1,0:T(8,128)(2,1)S(1)}, bf16[2,512,384]{2,1,0:T(8,128)(2,1)S(1)}, u32[]{:S(2)}, u32[]{:S(2)}) collective-permute-start(bf16[2,512,384]{2,1,0:T(8,128)(2,1)S(1)} %get-tuple-element.294.refs_5_), channel_id=1, source_target_pairs={{0,2},{2,0},{1,3},{3,1},{4,6},{6,4},{5,7},{7,5},{8,10},{10,8},{9,1... | collective-permute-start | bytes 2359304 | tf_op jit(solution)/shard_map/ppermute | solution.py:564
  99.3 4.3 %collective-permute-start.28 = (bf16[2,2,96,640]{3,2,1,0:T(8,128)(2,1)S(1)}, bf16[2,2,96,640]{3,2,1,0:T(8,128)(2,1)S(1)}, u32[]{:S(2)}, u32[]{:S(2)}) collective-permute-start(bf16[2,2,96,640]{3,2,1,0:T(8,128)(2,1)S(1)} %get-tuple-element.300), channel_id=1, source_target_pairs={{0,2},{2,0},{1,3},{3,1},{4,6},{6,4},{5,7},{7,5},{8,10},{10,8},{9,1... | collective-permute-start | bytes 1474568 | tf_op jit(solution)/shard_map/ppermute | solution.py:564
  100.1 12.1 %collective-permute-start.27 = (bf16[1728,128]{1,0:T(8,128)(2,1)S(1)}, bf16[1728,128]{1,0:T(8,128)(2,1)S(1)}, u32[]{:S(2)}, u32[]{:S(2)}) collective-permute-start(bf16[1728,128]{1,0:T(8,128)(2,1)S(1)} %get-tuple-element.364), channel_id=1, source_target_pairs={{0,4},{4,0},{1,5},{5,1},{2,6},{6,2},{3,7},{7,3},{8,12},{12,8},{9,1... | collective-permute-start | bytes 1327112 | tf_op jit(solution)/shard_map/ppermute | solution.py:564
  102.0 10.8 %collective-permute-start.26 = (bf16[256,768]{1,0:T(8,128)(2,1)S(1)}, bf16[256,768]{1,0:T(8,128)(2,1)S(1)}, u32[]{:S(2)}, u32[]{:S(2)}) collective-permute-start(bf16[256,768]{1,0:T(8,128)(2,1)S(1)} %get-tuple-element.366), channel_id=1, source_target_pairs={{0,1},{1,0},{2,3},{3,2},{4,5},{5,4},{6,7},{7,6},{8,9},{9,8},{10,11... | collective-permute-start | bytes 1179656 | tf_op jit(solution)/shard_map/ppermute | solution.py:564
  112.9 10.5 %collective-permute-start.30 = (bf16[2,64,768]{2,1,0:T(8,128)(2,1)S(1)}, bf16[2,64,768]{2,1,0:T(8,128)(2,1)S(1)}, u32[]{:S(2)}, u32[]{:S(2)}) collective-permute-start(bf16[2,64,768]{2,1,0:T(8,128)(2,1)S(1)} %get-tuple-element.374), channel_id=1, source_target_pairs={{0,8},{8,0},{16,24},{24,16},{1,9},{9,1},{17,25},{25,17},{2,10},{10... | collective-permute-start | bytes 589832 | tf_op jit(solution)/shard_map/ppermute | solution.py:606
  114.3 9.1 %collective-permute-start.31 = (bf16[2,432,128]{2,1,0:T(8,128)(2,1)S(1)}, bf16[2,432,128]{2,1,0:T(8,128)(2,1)S(1)}, u32[]{:S(2)}, u32[]{:S(2)}) collective-permute-start(bf16[2,432,128]{2,1,0:T(8,128)(2,1)S(1)} %get-tuple-element.370), channel_id=1, source_target_pairs={{0,8},{8,0},{16,24},{24,16},{1,9},{9,1},{17,25},{25,17},{2,10},{10... | collective-permute-start | bytes 663560 | tf_op jit(solution)/shard_map/ppermute | solution.py:606
  115.2 6.3 %collective-permute-start.32 = (bf16[2,96,640]{2,1,0:T(8,128)(2,1)S(1)}, bf16[2,96,640]{2,1,0:T(8,128)(2,1)S(1)}, u32[]{:S(2)}, u32[]{:S(2)}) collective-permute-start(bf16[2,96,640]{2,1,0:T(8,128)(2,1)S(1)} %get-tuple-element.368), channel_id=1, source_target_pairs={{0,1},{1,0},{2,3},{3,2},{4,5},{5,4},{6,7},{7,6},{8,9},{9,8},{10,11... | collective-permute-start | bytes 737288 | tf_op jit(solution)/shard_map/ppermute | solution.py:564
  116.9 33.0 %collective-permute-start.29 = (bf16[1,512,384]{2,1,0:T(8,128)(2,1)S(1)}, bf16[1,512,384]{2,1,0:T(8,128)(2,1)S(1)}, u32[]{:S(2)}, u32[]{:S(2)}) collective-permute-start(bf16[1,512,384]{2,1,0:T(8,128)(2,1)S(1)} %add_convert_fusion.5), channel_id=1, source_target_pairs={{0,4},{4,0},{1,5},{5,1},{2,6},{6,2},{3,7},{7,3},{8,12},{12,8},{9,1... | collective-permute-start | bytes 1179656 | tf_op jit(solution)/shard_map/ppermute | solution.py:564
  123.4 5.1 %collective-permute-start.35 = (bf16[96,640]{1,0:T(8,128)(2,1)S(1)}, bf16[96,640]{1,0:T(8,128)(2,1)S(1)}, u32[]{:S(2)}, u32[]{:S(2)}) collective-permute-start(bf16[96,640]{1,0:T(8,128)(2,1)S(1)} %get-tuple-element.376), channel_id=1, source_target_pairs={{0,4},{4,0},{1,5},{5,1},{2,6},{6,2},{3,7},{7,3},{8,12},{12,8},{9,1... | collective-permute-start | bytes 368648 | tf_op jit(solution)/shard_map/ppermute | solution.py:564
  125.0 14.4 %collective-permute-start.33 = (bf16[64,768]{1,0:T(8,128)(2,1)S(1)}, bf16[64,768]{1,0:T(8,128)(2,1)S(1)}, u32[]{:S(2)}, u32[]{:S(2)}) collective-permute-start(bf16[64,768]{1,0:T(8,128)(2,1)S(1)} %get-tuple-element.380), channel_id=1, source_target_pairs={{0,16},{8,24},{16,0},{24,8},{1,17},{9,25},{17,1},{25,9},{2,18},{10... | collective-permute-start | bytes 294920 | tf_op jit(solution)/shard_map/ppermute | solution.py:606
  126.4 12.8 %collective-permute-start.34 = (bf16[432,128]{1,0:T(8,128)(2,1)S(1)}, bf16[432,128]{1,0:T(8,128)(2,1)S(1)}, u32[]{:S(2)}, u32[]{:S(2)}) collective-permute-start(bf16[432,128]{1,0:T(8,128)(2,1)S(1)} %get-tuple-element.378), channel_id=1, source_target_pairs={{0,16},{8,24},{16,0},{24,8},{1,17},{9,25},{17,1},{25,9},{2,18},{10... | collective-permute-start | bytes 331784 | tf_op jit(solution)/shard_map/ppermute | solution.py:606
  128.6 13.8 %collective-permute-start.38 = (bf16[96,640]{1,0:T(8,128)(2,1)S(1)}, bf16[96,640]{1,0:T(8,128)(2,1)S(1)}, u32[]{:S(2)}, u32[]{:S(2)}) collective-permute-start(bf16[96,640]{1,0:T(8,128)(2,1)S(1)} %add_convert_fusion.10), channel_id=1, source_target_pairs={{0,16},{8,24},{16,0},{24,8},{1,17},{9,25},{17,1},{25,9},{2,18},{10... | collective-permute-start | bytes 368648 | tf_op jit(solution)/shard_map/ppermute | solution.py:606
  139.3 10.5 %collective-permute-start.37 = (bf16[432,128]{1,0:T(8,128)(2,1)S(1)}, bf16[432,128]{1,0:T(8,128)(2,1)S(1)}, u32[]{:S(2)}, u32[]{:S(2)}) collective-permute-start(bf16[432,128]{1,0:T(8,128)(2,1)S(1)} %add_convert_fusion.11), channel_id=1, source_target_pairs={{0,16},{8,24},{16,0},{24,8},{1,17},{9,25},{17,1},{25,9},{2,18},{10... | collective-permute-start | bytes 331784 | tf_op jit(solution)/shard_map/ppermute | solution.py:606
  139.4 10.3 %collective-permute-start.36 = (bf16[64,768]{1,0:T(8,128)(2,1)S(1)}, bf16[64,768]{1,0:T(8,128)(2,1)S(1)}, u32[]{:S(2)}, u32[]{:S(2)}) collective-permute-start(bf16[64,768]{1,0:T(8,128)(2,1)S(1)} %add_convert_fusion.12), channel_id=1, source_target_pairs={{0,16},{8,24},{16,0},{24,8},{1,17},{9,25},{17,1},{25,9},{2,18},{10... | collective-permute-start | bytes 294920 | tf_op jit(solution)/shard_map/ppermute | solution.py:606
  142.4 9.4 %collective-permute-start.41 = (bf16[2,96,640]{2,1,0:T(8,128)(2,1)S(1)}, bf16[2,96,640]{2,1,0:T(8,128)(2,1)S(1)}, u32[]{:S(2)}, u32[]{:S(2)}) collective-permute-start(bf16[2,96,640]{2,1,0:T(8,128)(2,1)S(1)} %pad_maximum_fusion.5), channel_id=1, source_target_pairs={{0,8},{8,0},{16,24},{24,16},{1,9},{9,1},{17,25},{25,17},{2,10},{10... | collective-permute-start | bytes 737288 | tf_op jit(solution)/shard_map/ppermute | solution.py:606
  151.8 12.2 %collective-permute-start.43 = (bf16[4,96,640]{2,1,0:T(8,128)(2,1)S(1)}, bf16[4,96,640]{2,1,0:T(8,128)(2,1)S(1)}, u32[]{:S(2)}, u32[]{:S(2)}) collective-permute-start(bf16[4,96,640]{2,1,0:T(8,128)(2,1)S(1)} %constant_dynamic-update-slice_fusion.2), channel_id=1, source_target_pairs={{0,4},{4,0},{1,5},{5,1},{2,6},{6,2},{3,7},{7,3},{8,12},{12,8},{9,1... | collective-permute-start | bytes 1474568 | tf_op jit(solution)/shard_map/ppermute | solution.py:564
  152.2 7.8 %collective-permute-start.40 = (bf16[2,64,768]{2,1,0:T(8,128)(2,1)S(1)}, bf16[2,64,768]{2,1,0:T(8,128)(2,1)S(1)}, u32[]{:S(2)}, u32[]{:S(2)}) collective-permute-start(bf16[2,64,768]{2,1,0:T(8,128)(2,1)S(1)} %pad_maximum_fusion.7), channel_id=1, source_target_pairs={{0,8},{8,0},{16,24},{24,16},{1,9},{9,1},{17,25},{25,17},{2,10},{10... | collective-permute-start | bytes 589832 | tf_op jit(solution)/shard_map/ppermute | solution.py:606
  152.2 10.5 %collective-permute-start.39 = (bf16[2,432,128]{2,1,0:T(8,128)(2,1)S(1)}, bf16[2,432,128]{2,1,0:T(8,128)(2,1)S(1)}, u32[]{:S(2)}, u32[]{:S(2)}) collective-permute-start(bf16[2,432,128]{2,1,0:T(8,128)(2,1)S(1)} %pad_maximum_fusion.6), channel_id=1, source_target_pairs={{0,8},{8,0},{16,24},{24,16},{1,9},{9,1},{17,25},{25,17},{2,10},{10... | collective-permute-start | bytes 663560 | tf_op jit(solution)/shard_map/ppermute | solution.py:606
  164.2 13.9 %collective-permute-start.46 = (bf16[2,4,96,640]{3,2,1,0:T(8,128)(2,1)S(1)}, bf16[2,4,96,640]{3,2,1,0:T(8,128)(2,1)S(1)}, u32[]{:S(2)}, u32[]{:S(2)}) collective-permute-start(bf16[2,4,96,640]{3,2,1,0:T(8,128)(2,1)S(1)} %pad_maximum_fusion.own), channel_id=1, source_target_pairs={{0,2},{2,0},{1,3},{3,1},{4,6},{6,4},{5,7},{7,5},{8,10},{10,8},{9,1... | collective-permute-start | bytes 2949128 | tf_op jit(solution)/shard_map/ppermute | solution.py:564
  164.2 11.5 %collective-permute-start.42 = (bf16[2,128,768]{2,1,0:T(8,128)(2,1)S(1)}, bf16[2,128,768]{2,1,0:T(8,128)(2,1)S(1)}, u32[]{:S(2)}, u32[]{:S(2)}) collective-permute-start(bf16[2,128,768]{2,1,0:T(8,128)(2,1)S(1)} %get-tuple-element.335), channel_id=1, source_target_pairs={{0,8},{8,0},{16,24},{24,16},{1,9},{9,1},{17,25},{25,17},{2,10},{10... | collective-permute-start | bytes 1179656 | tf_op jit(solution)/shard_map/ppermute | solution.py:606
  164.3 13.6 %collective-permute-start.45 = (bf16[4,432,128]{2,1,0:T(8,128)(2,1)S(1)}, bf16[4,432,128]{2,1,0:T(8,128)(2,1)S(1)}, u32[]{:S(2)}, u32[]{:S(2)}) collective-permute-start(bf16[4,432,128]{2,1,0:T(8,128)(2,1)S(1)} %pad_maximum_fusion.4), channel_id=1, source_target_pairs={{0,4},{4,0},{1,5},{5,1},{2,6},{6,2},{3,7},{7,3},{8,12},{12,8},{9,1... | collective-permute-start | bytes 1327112 | tf_op jit(solution)/shard_map/ppermute | solution.py:564
  164.9 20.4 %collective-permute-start.48 = (bf16[4,64,768]{2,1,0:T(8,128)(2,1)S(1)}, bf16[4,64,768]{2,1,0:T(8,128)(2,1)S(1)}, u32[]{:S(2)}, u32[]{:S(2)}) collective-permute-start(bf16[4,64,768]{2,1,0:T(8,128)(2,1)S(1)} %constant_dynamic-update-slice_fusion), channel_id=1, source_target_pairs={{0,4},{4,0},{1,5},{5,1},{2,6},{6,2},{3,7},{7,3},{8,12},{12,8},{9,1... | collective-permute-start | bytes 1179656 | tf_op jit(solution)/shard_map/ppermute | solution.py:564
  175.9 11.6 %collective-permute-start.44 = (bf16[128,768]{1,0:T(8,128)(2,1)S(1)}, bf16[128,768]{1,0:T(8,128)(2,1)S(1)}, u32[]{:S(2)}, u32[]{:S(2)}) collective-permute-start(bf16[128,768]{1,0:T(8,128)(2,1)S(1)} %get-tuple-element.372), channel_id=1, source_target_pairs={{0,16},{8,24},{16,0},{24,8},{1,17},{9,25},{17,1},{25,9},{2,18},{10... | collective-permute-start | bytes 589832 | tf_op jit(solution)/shard_map/ppermute | solution.py:606
  180.9 6.7 %collective-permute-start.47 = (bf16[2,4,432,128]{3,2,1,0:T(8,128)(2,1)S(1)}, bf16[2,4,432,128]{3,2,1,0:T(8,128)(2,1)S(1)}, u32[]{:S(2)}, u32[]{:S(2)}) collective-permute-start(bf16[2,4,432,128]{3,2,1,0:T(8,128)(2,1)S(1)} %pad_maximum_fusion.1.own), channel_id=1, source_target_pairs={{0,2},{2,0},{1,3},{3,1},{4,6},{6,4},{5,7},{7,5},{8,10},{10,8},{9,1... | collective-permute-start | bytes 2654216 | tf_op jit(solution)/shard_map/ppermute | solution.py:564
  187.5 4.5 %collective-permute-start.49 = (bf16[2,4,64,768]{3,2,1,0:T(8,128)(2,1)S(1)}, bf16[2,4,64,768]{3,2,1,0:T(8,128)(2,1)S(1)}, u32[]{:S(2)}, u32[]{:S(2)}) collective-permute-start(bf16[2,4,64,768]{3,2,1,0:T(8,128)(2,1)S(1)} %pad_maximum_fusion.2.own), channel_id=1, source_target_pairs={{0,2},{2,0},{1,3},{3,1},{4,6},{6,4},{5,7},{7,5},{8,10},{10,8},{9,1... | collective-permute-start | bytes 2359304 | tf_op jit(solution)/shard_map/ppermute | solution.py:564
  (31 other events, 306.8 us)

commit v6 on v5

--- a/solution.py
+++ b/solution.py
@@ -851,10 +851,10 @@
     f_in = reduce_step(order, f_in, "x", 0)
     f_rest = reduce_step(order, f_rest, "shard", 0)
     wq = reduce_step(order, wq, "shard", 0)
+    got = shift(order.add(viewed(terms, take(1, 0))), "x", 1)
+    terms = viewed(terms, take(0, 0)) + [term(got)]
     f_in = reduce_z(order, viewed(f_in, reshaped(2, 2, high_in // TP, 128)), 1)
     f_rest = reduce_z(order, viewed(f_rest, reshaped(2, 2, high // TP, D)), 1)
-    got = shift(order.add(viewed(terms, take(1, 0))), "x", 1)
-    terms = viewed(terms, take(0, 0)) + [term(got)]
     wq = reduce_step(order, wq, "x", 0)
     f_in = reduce_z(order, f_in, 2)
     f_rest = reduce_z(order, f_rest, 2)

time: 195 us -> 193 us (0.990)
  waiting for transfers between devices: 75 us -> 72.6 us
    ppermute x37, waiting for transfers between devices: 33.8 us -> 28.9 us  [shift(): return lax.ppermute(value, axis, [(i, (i + k) % n) for i in range(n)])]
    ppermute x13, waiting for transfers between devices: 41.3 us -> 43.7 us  [swap_z(): return lax.ppermute(value, 'z', [(i, i ^ bit) for i in range(TP)])]
  transfers between devices with their start and end apart: 50 -> 50, of which waited for: 24 -> 21; matrix products, arithmetic and copies ran while one was open for 3% -> 3% of each run, Pallas kernels for 28% -> 28%
where the time goes in v6:
time: 193 us
  waiting for transfers between devices  72.6 us (38%)
  Pallas kernels  56.7 us (29%)
  starting transfers between devices  55.1 us (29%)
  other arithmetic  4.52 us (2%)
  local copies, waits for them, and re-layouts  2.86 us (1%)
    pallas_call x14, Pallas kernels, call(): pl.pallas_call(body, out_shape=shapes, in_specs=specs, out_specs=[pl.Bloc...  56.7 us
    ppermute x13, waiting for transfers between devices, swap_z(): return lax.ppermute(value, 'z', [(i, i ^ bit) for i in range(TP)])  43.7 us
    ppermute x37, starting transfers between devices, shift(): return lax.ppermute(value, axis, [(i, (i + k) % n) for i in range(n)])  36.3 us
    ppermute x37, waiting for transfers between devices, shift(): return lax.ppermute(value, axis, [(i, (i + k) % n) for i in range(n)])  28.9 us
    ppermute x13, starting transfers between devices, swap_z(): return lax.ppermute(value, 'z', [(i, i ^ bit) for i in range(TP)])  18.9 us
  transfers between devices with their start and end apart: 50, of which 21 were waited for; matrix products, arithmetic and copies ran while one was open for 3% of the time, Pallas kernels for 28%

profile of v6, /device:TPU:0, one launch (start us, length us, event | category | flops | bytes accessed | tf_op | source)
XLA Modules:
  0.0 193.1 jit_solution(17154314256814527087)
XLA Ops:
  0.6 3.1 %collective-permute-start = (bf16[128,768]{1,0:T(8,128)(2,1)}, bf16[128,768]{1,0:T(8,128)(2,1)S(1)}, u32[]{:S(2)}, u32[]{:S(2)}) collective-permute-start(bf16[128,768]{1,0:T(8,128)(2,1)} %bitcast.67), channel_id=1, source_target_pairs={{0,8},{8,16},{16,24},{24,0},{1,9},{9,17},{17,25},{25,1},{2,10},{10... | collective-permute-start | bytes 589832 | tf_op jit(solution)/shard_map/ppermute | solution.py:564
  3.7 2.6 %collective-permute-start.1 = (bf16[128,768]{1,0:T(8,128)(2,1)}, bf16[128,768]{1,0:T(8,128)(2,1)S(1)}, u32[]{:S(2)}, u32[]{:S(2)}) collective-permute-start(bf16[128,768]{1,0:T(8,128)(2,1)} %bitcast.68), channel_id=1, source_target_pairs={{0,16},{8,24},{16,0},{24,8},{1,17},{9,25},{17,1},{25,9},{2,18},{10... | collective-permute-start | bytes 589832 | tf_op jit(solution)/shard_map/ppermute | solution.py:564
  7.7 1.7 group_columns.1
  10.2 1.5 collective-permute-start.3
  11.7 2.0 %pack_weights.1 = (bf16[768,768]{1,0:T(8,128)(2,1)S(1)}, bf16[144,768]{1,0:T(8,128)(2,1)S(1)}) custom-call(s32[4]{0:T(128)S(1)} %pad_add_fusion.idx, bf16[384,768]{1,0:T(8,128)(2,1)} %refs_7_, bf16[384,2304]{1,0:T(8,128)(2,1)} %refs_8_, bf16[576,768]{1,0:T(8,128)(2,1)} %refs_9_), custom_call_target="tpu_custom_call" | custom-call | flops 1 | bytes 1 | tf_op jit(solution)/shard_map/pack_weights/pallas_call | solution.py:54
  16.1 1.5 collective-permute-start.15
  17.7 1.9 collective-permute-done.3.refs_5_
  21.8 4.0 %front.1 = (bf16[512,256]{1,0:T(8,128)(2,1)S(1)}, bf16[512,384]{1,0:T(8,128)(2,1)S(1)}, bf16[512,768]{1,0:T(8,128)(2,1)}, bf16[768,640]{1,0:T(8,128)(2,1)}, f32[8,768]{1,0:T(8,128)}) custom-call(s32[4]{0:T(128)S(1)} %pad_add_fusion.idx, bf16[128,768]{1,0:T(8,128)(2,1)} %bitcast.70, bf16[128,768]{1,0:T(8,128)(2,1)} %copy-done.23, ...), custom_call_target="tpu_custom_call" | custom-call | flops 1 | bytes 1 | tf_op jit(solution)/shard_map/front/pallas_call | solution.py:54
  26.0 3.0 %collective-permute-start.9 = (bf16[144,768]{1,0:T(8,128)(2,1)S(1)}, bf16[144,768]{1,0:T(8,128)(2,1)S(1)}, u32[]{:S(2)}, u32[]{:S(2)}) collective-permute-start(bf16[144,768]{1,0:T(8,128)(2,1)S(1)} %collective-permute-done.8), channel_id=1, source_target_pairs={{0,8},{8,0},{16,24},{24,16},{1,9},{9,1},{17,25},{25,17},{2,10},{10... | collective-permute-start | bytes 663560 | tf_op jit(solution)/shard_map/ppermute | solution.py:606
  30.5 4.6 %collective-permute-done.9 = bf16[144,768]{1,0:T(8,128)(2,1)S(1)} collective-permute-done((bf16[144,768]{1,0:T(8,128)(2,1)S(1)}, bf16[144,768]{1,0:T(8,128)(2,1)S(1)}, u32[]{:S(2)}, u32[]{:S(2)}) %collective-permute-start.9) | collective-permute-done | bytes 221216 | tf_op jit(solution)/shard_map/ppermute | solution.py:606
  35.2 4.4 %attention_forward_near.1 = (f32[192,512]{1,0:T(8,128)S(1)}, f32[8,512]{1,0:T(8,128)S(1)}) custom-call(bf16[512,256]{1,0:T(8,128)(2,1)S(1)} %get-tuple-element.260.q_ref, bf16[512,384]{1,0:T(8,128)(2,1)S(1)} %get-tuple-element.261.refs_0_, bf16[512,384]{1,0:T(8,128)(2,1)S(1)} %collective-permute-done.6.refs_1_.refs_2_), custom_call_target="tpu_custom_call" | custom-call | flops 1 | bytes 1 | tf_op jit(solution)/shard_map/attention_forward_near/pallas_call | solution.py:54
  40.2 1.7 collective-permute-done.7.refs_1_.refs_3_
  42.0 5.0 %attention_forward_far.1 = (bf16[128,192]{1,0:T(8,128)(2,1)S(1)}, bf16[128,192]{1,0:T(8,128)(2,1)S(1)}, bf16[128,192]{1,0:T(8,128)(2,1)S(1)}, bf16[128,192]{1,0:...) custom-call(bf16[512,256]{1,0:T(8,128)(2,1)S(1)} %get-tuple-element.260.q_ref, ...), custom_call_target="tpu_custom_call" | custom-call | flops 1 | bytes 1 | tf_op jit(solution)/shard_map/attention_forward_far/pallas_call | solution.py:54
  48.0 1.5 collective-permute-start.20
  49.5 2.0 %collective-permute-start.11 = (bf16[128,192]{1,0:T(8,128)(2,1)S(1)}, bf16[128,192]{1,0:T(8,128)(2,1)S(1)}, u32[]{:S(2)}, u32[]{:S(2)}) collective-permute-start(bf16[128,192]{1,0:T(8,128)(2,1)S(1)} %get-tuple-element.220), channel_id=1, source_target_pairs={{0,24},{8,0},{16,8},{24,16},{1,25},{9,1},{17,9},{25,17},{2,26},{10... | collective-permute-start | bytes 147464 | tf_op jit(solution)/shard_map/ppermute | solution.py:564
  53.9 4.6 %collective-permute-done.12.refs_2_ = bf16[128,192]{1,0:T(8,128)(2,1)S(1)} collective-permute-done((bf16[128,192]{1,0:T(8,128)(2,1)S(1)}, bf16[128,192]{1,0:T(8,128)(2,1)S(1)}, u32[]{:S(2)}, u32[]{:S(2)}) %collective-permute-start.12) | collective-permute-done | bytes 49184 | tf_op jit(solution)/shard_map/ppermute | solution.py:564
  58.6 8.5 %feed_forward.1 = (f32[128,768]{1,0:T(8,128)}, f32[128,768]{1,0:T(8,128)}, bf16[128,6528]{1,0:T(8,128)(2,1)S(1)}, f32[8,768]{1,0:T(8,128)}, bf16[128,256]{1,0:T(...) custom-call(s32[4]{0:T(128)S(1)} %pad_add_fusion.idx, ...), custom_call_target="tpu_custom_call" | custom-call | flops 1 | bytes 1 | tf_op jit(solution)/shard_map/feed_forward/pallas_call | solution.py:54
  69.4 1.7 collective-permute-start.18
  73.2 4.1 %ffn_weight_grads.1 = (bf16[2,1728,128]{2,1,0:T(8,128)(2,1)}, bf16[2,1728,128]{2,1,0:T(8,128)(2,1)}, bf16[2,256,768]{2,1,0:T(8,128)(2,1)}, bf16[2,256,768]{2,1,0:T(8,128)(2,1)}) custom-call(s32[4]{0:T(128)S(1)} %pad_add_fusion.idx, bf16[128,6528]{1,0:T(8,128)(2,1)S(1)} %get-tuple-element.256.own, bf16[128,6528]{1,0:T(8,128)(2,1)S(1)} %collective-permute-done.21.got, ...), custom_call_target="tpu_custom_call" | custom-call | flops 1 | bytes 1 | tf_op jit(solution)/shard_map/ffn_weight_grads/pallas_call | solution.py:54
  77.4 1.6 collective-permute-start.23
  79.0 1.5 collective-permute-start.24
  80.5 10.5 %attention_backward.1 = (bf16[2,512,384]{2,1,0:T(8,128)(2,1)S(1)}, bf16[2,512,384]{2,1,0:T(8,128)(2,1)S(1)}, bf16[512,256]{1,0:T(8,128)(2,1)S(1)}) custom-call(bf16[512,256]{1,0:T(8,128)(2,1)} %copy-done.4, bf16[512,384]{1,0:T(8,128)(2,1)} %copy-done.6, bf16[512,384]{1,0:T(8,128)(2,1)} %copy-done.8, bf16[512,384]{1,0:T(8,128)(2,1)} %copy-done.7, ...), custom_call_target="tpu_custom_call" | custom-call | flops 1 | bytes 1 | tf_op jit(solution)/shard_map/attention_backward/pallas_call | solution.py:54
  91.0 4.6 %qkv_weight_grads.1 = (bf16[2,2,96,640]{3,2,1,0:T(8,128)(2,1)S(1)}, bf16[2,2,96,640]{3,2,1,0:T(8,128)(2,1)S(1)}) custom-call(s32[4]{0:T(128)S(1)} %pad_add_fusion.idx, bf16[512,768]{1,0:T(8,128)(2,1)} %get-tuple-element.278.refs_0_, bf16[512,768]{1,0:T(8,128)(2,1)} %copy-done.18, bf16[512,768]{1,0:T(8,128)(2,1)} %copy-done.17, bf16[512,768]{1,0:T(8,128)(2,1)} %copy-done.19, ...), custom_call_target="tpu_custom_call" | custom-call | flops 1 | bytes 1 | tf_op jit(solution)/shard_map/qkv_weight_grads/pallas_call | solution.py:54
  95.7 2.8 %collective-permute-done.24 = bf16[2,256,768]{2,1,0:T(8,128)(2,1)S(1)} collective-permute-done((bf16[2,256,768]{2,1,0:T(8,128)(2,1)}, bf16[2,256,768]{2,1,0:T(8,128)(2,1)S(1)}, u32[]{:S(2)}, u32[]{:S(2)}) %collective-permute-start.24) | collective-permute-done | bytes 786464 | tf_op jit(solution)/shard_map/ppermute | solution.py:564
  100.3 1.6 collective-permute-start.28
  102.0 1.6 collective-permute-start.29
  105.7 9.4 %collective-permute-done.29 = bf16[1728,128]{1,0:T(8,128)(2,1)S(1)} collective-permute-done((bf16[1728,128]{1,0:T(8,128)(2,1)S(1)}, bf16[1728,128]{1,0:T(8,128)(2,1)S(1)}, u32[]{:S(2)}, u32[]{:S(2)}) %collective-permute-start.29) | collective-permute-done | bytes 442400 | tf_op jit(solution)/shard_map/ppermute | solution.py:564
  117.7 1.6 collective-permute-start.35
  119.3 5.3 %collective-permute-done.31 = bf16[2,432,128]{2,1,0:T(8,128)(2,1)S(1)} collective-permute-done((bf16[2,432,128]{2,1,0:T(8,128)(2,1)S(1)}, bf16[2,432,128]{2,1,0:T(8,128)(2,1)S(1)}, u32[]{:S(2)}, u32[]{:S(2)}) %collective-permute-start.31) | collective-permute-done | bytes 221216 | tf_op jit(solution)/shard_map/ppermute | solution.py:606
  126.1 1.7 collective-permute-start.34
  129.2 8.4 %collective-permute-done.34 = bf16[432,128]{1,0:T(8,128)(2,1)S(1)} collective-permute-done((bf16[432,128]{1,0:T(8,128)(2,1)S(1)}, bf16[432,128]{1,0:T(8,128)(2,1)S(1)}, u32[]{:S(2)}, u32[]{:S(2)}) %collective-permute-start.34) | collective-permute-done | bytes 110624 | tf_op jit(solution)/shard_map/ppermute | solution.py:606
  137.8 3.0 %collective-permute-start.36 = (bf16[64,768]{1,0:T(8,128)(2,1)S(1)}, bf16[64,768]{1,0:T(8,128)(2,1)S(1)}, u32[]{:S(2)}, u32[]{:S(2)}) collective-permute-start(bf16[64,768]{1,0:T(8,128)(2,1)S(1)} %add_convert_fusion.12), channel_id=1, source_target_pairs={{0,16},{8,24},{16,0},{24,8},{1,17},{9,25},{17,1},{25,9},{2,18},{10... | collective-permute-start | bytes 294920 | tf_op jit(solution)/shard_map/ppermute | solution.py:606
  140.8 1.7 collective-permute-start.41
  142.6 5.6 %collective-permute-done.36 = bf16[64,768]{1,0:T(8,128)(2,1)S(1)} collective-permute-done((bf16[64,768]{1,0:T(8,128)(2,1)S(1)}, bf16[64,768]{1,0:T(8,128)(2,1)S(1)}, u32[]{:S(2)}, u32[]{:S(2)}) %collective-permute-start.36) | collective-permute-done | bytes 98336 | tf_op jit(solution)/shard_map/ppermute | solution.py:606
  148.2 1.9 h_one_grads.1
  150.2 1.6 collective-permute-start.43
  151.8 2.0 %collective-permute-start.39 = (bf16[2,432,128]{2,1,0:T(8,128)(2,1)S(1)}, bf16[2,432,128]{2,1,0:T(8,128)(2,1)S(1)}, u32[]{:S(2)}, u32[]{:S(2)}) collective-permute-start(bf16[2,432,128]{2,1,0:T(8,128)(2,1)S(1)} %pad_maximum_fusion.6), channel_id=1, source_target_pairs={{0,8},{8,0},{16,24},{24,16},{1,9},{9,1},{17,25},{25,17},{2,10},{10... | collective-permute-start | bytes 663560 | tf_op jit(solution)/shard_map/ppermute | solution.py:606
  153.8 5.8 %collective-permute-done.40 = bf16[2,64,768]{2,1,0:T(8,128)(2,1)S(1)} collective-permute-done((bf16[2,64,768]{2,1,0:T(8,128)(2,1)S(1)}, bf16[2,64,768]{2,1,0:T(8,128)(2,1)S(1)}, u32[]{:S(2)}, u32[]{:S(2)}) %collective-permute-start.40) | collective-permute-done | bytes 196640 | tf_op jit(solution)/shard_map/ppermute | solution.py:606
  159.6 2.4 %collective-permute-done.39 = bf16[2,432,128]{2,1,0:T(8,128)(2,1)S(1)} collective-permute-done((bf16[2,432,128]{2,1,0:T(8,128)(2,1)S(1)}, bf16[2,432,128]{2,1,0:T(8,128)(2,1)S(1)}, u32[]{:S(2)}, u32[]{:S(2)}) %collective-permute-start.39) | collective-permute-done | bytes 221216 | tf_op jit(solution)/shard_map/ppermute | solution.py:606
  162.7 1.6 collective-permute-start.45
  164.8 9.4 %collective-permute-done.42 = bf16[2,128,768]{2,1,0:T(8,128)(2,1)S(1)} collective-permute-done((bf16[2,128,768]{2,1,0:T(8,128)(2,1)S(1)}, bf16[2,128,768]{2,1,0:T(8,128)(2,1)S(1)}, u32[]{:S(2)}, u32[]{:S(2)}) %collective-permute-start.42) | collective-permute-done | bytes 393248 | tf_op jit(solution)/shard_map/ppermute | solution.py:606
  174.3 2.4 %collective-permute-start.44 = (bf16[128,768]{1,0:T(8,128)(2,1)S(1)}, bf16[128,768]{1,0:T(8,128)(2,1)S(1)}, u32[]{:S(2)}, u32[]{:S(2)}) collective-permute-start(bf16[128,768]{1,0:T(8,128)(2,1)S(1)} %get-tuple-element.372), channel_id=1, source_target_pairs={{0,16},{8,24},{16,0},{24,8},{1,17},{9,25},{17,1},{25,9},{2,18},{10... | collective-permute-start | bytes 589832 | tf_op jit(solution)/shard_map/ppermute | solution.py:606
  176.8 2.8 %qkv_unpack.1 = (f32[2,2,96,2304]{3,2,1,0:T(8,128)}, f32[384]{0:T(512)}) custom-call(s32[4]{0:T(128)S(1)} %pad_add_fusion.idx, bf16[2,4,96,640]{3,2,1,0:T(8,128)(2,1)S(1)} %pad_maximum_fusion.own, bf16[2,4,96,640]{3,2,1,0:T(8,128)(2,1)S(1)} %collective-permute-done.46.got), custom_call_target="tpu_custom_call" | custom-call | flops 1 | bytes 1 | tf_op jit(solution)/shard_map/qkv_unpack/pallas_call | solution.py:54
  179.7 4.0 %collective-permute-done.48 = bf16[4,64,768]{2,1,0:T(8,128)(2,1)S(1)} collective-permute-done((bf16[4,64,768]{2,1,0:T(8,128)(2,1)S(1)}, bf16[4,64,768]{2,1,0:T(8,128)(2,1)S(1)}, u32[]{:S(2)}, u32[]{:S(2)}) %collective-permute-start.48) | collective-permute-done | bytes 393248 | tf_op jit(solution)/shard_map/ppermute | solution.py:564
  183.7 2.2 %collective-permute-done.44.refs_1_ = bf16[128,768]{1,0:T(8,128)(2,1)S(1)} collective-permute-done((bf16[128,768]{1,0:T(8,128)(2,1)S(1)}, bf16[128,768]{1,0:T(8,128)(2,1)S(1)}, u32[]{:S(2)}, u32[]{:S(2)}) %collective-permute-start.44) | collective-permute-done | bytes 196640 | tf_op jit(solution)/shard_map/ppermute | solution.py:606
  185.9 2.9 %w_in_unpack.1 = f32[2,2,96,2304]{3,2,1,0:T(8,128)} custom-call(s32[4]{0:T(128)S(1)} %pad_add_fusion.idx, bf16[2,4,432,128]{3,2,1,0:T(8,128)(2,1)S(1)} %pad_maximum_fusion.1.own, bf16[2,4,432,128]{3,2,1,0:T(8,128)(2,1)S(1)} %collective-permute-done.47.got), custom_call_target="tpu_custom_call" | custom-call | flops 1 | bytes 1 | tf_op jit(solution)/shard_map/w_in_unpack/pallas_call | solution.py:54
  188.8 1.6 token_grads.1
  190.5 2.6 %w_down_w_out_unpack.1 = (f32[2,2,96,768]{3,2,1,0:T(8,128)}, f32[2,2,144,768]{3,2,1,0:T(8,128)}, f32[384]{0:T(512)}) custom-call(s32[4]{0:T(128)S(1)} %pad_add_fusion.idx, bf16[2,4,64,768]{3,2,1,0:T(8,128)(2,1)S(1)} %pad_maximum_fusion.2.own, bf16[2,4,64,768]{3,2,1,0:T(8,128)(2,1)S(1)} %collective-permute-done.49.got), custom_call_target="tpu_custom_call" | custom-call | flops 1 | bytes 1 | tf_op jit(solution)/shard_map/w_down_w_out_unpack/pallas_call | solution.py:54
  (171 shorter events, 28.6 us)
Async XLA Ops:
  0.6 15.5 %collective-permute-start = (bf16[128,768]{1,0:T(8,128)(2,1)}, bf16[128,768]{1,0:T(8,128)(2,1)S(1)}, u32[]{:S(2)}, u32[]{:S(2)}) collective-permute-start(bf16[128,768]{1,0:T(8,128)(2,1)} %bitcast.67), channel_id=1, source_target_pairs={{0,8},{8,16},{16,24},{24,0},{1,9},{9,17},{17,25},{25,1},{2,10},{10... | collective-permute-start | bytes 589832 | tf_op jit(solution)/shard_map/ppermute | solution.py:564
  3.7 16.9 %collective-permute-start.1 = (bf16[128,768]{1,0:T(8,128)(2,1)}, bf16[128,768]{1,0:T(8,128)(2,1)S(1)}, u32[]{:S(2)}, u32[]{:S(2)}) collective-permute-start(bf16[128,768]{1,0:T(8,128)(2,1)} %bitcast.68), channel_id=1, source_target_pairs={{0,16},{8,24},{16,0},{24,8},{1,17},{9,25},{17,1},{25,9},{2,18},{10... | collective-permute-start | bytes 589832 | tf_op jit(solution)/shard_map/ppermute | solution.py:564
  6.3 14.3 %collective-permute-start.2 = (bf16[128,768]{1,0:T(8,128)(2,1)}, bf16[128,768]{1,0:T(8,128)(2,1)S(1)}, u32[]{:S(2)}, u32[]{:S(2)}) collective-permute-start(bf16[128,768]{1,0:T(8,128)(2,1)} %bitcast.69), channel_id=1, source_target_pairs={{0,24},{8,0},{16,8},{24,16},{1,25},{9,1},{17,9},{25,17},{2,26},{10... | collective-permute-start | bytes 589832 | tf_op jit(solution)/shard_map/ppermute | solution.py:564
  10.2 9.3 %collective-permute-start.3 = (bf16[208,640]{1,0:T(8,128)(2,1)S(1)}, bf16[208,640]{1,0:T(8,128)(2,1)S(1)}, u32[]{:S(2)}, u32[]{:S(2)}) collective-permute-start(bf16[208,640]{1,0:T(8,128)(2,1)S(1)} %get-tuple-element.201.refs_7_), channel_id=1, source_target_pairs={{0,1},{1,0},{2,3},{3,2},{4,5},{5,4},{6,7},{7,6},{8,9},{9,8},{10,11... | collective-permute-start | bytes 798728 | tf_op jit(solution)/shard_map/ppermute | solution.py:564
  13.7 12.3 %collective-permute-start.8 = (bf16[144,768]{1,0:T(8,128)(2,1)S(1)}, bf16[144,768]{1,0:T(8,128)(2,1)S(1)}, u32[]{:S(2)}, u32[]{:S(2)}) collective-permute-start(bf16[144,768]{1,0:T(8,128)(2,1)S(1)} %get-tuple-element.212), channel_id=1, source_target_pairs={{0,1},{1,0},{2,3},{3,2},{4,5},{5,4},{6,7},{7,6},{8,9},{9,8},{10,11... | collective-permute-start | bytes 663560 | tf_op jit(solution)/shard_map/ppermute | solution.py:564
  16.1 31.4 %collective-permute-start.15 = (bf16[768,768]{1,0:T(8,128)(2,1)S(1)}, bf16[768,768]{1,0:T(8,128)(2,1)S(1)}, u32[]{:S(2)}, u32[]{:S(2)}) collective-permute-start(bf16[768,768]{1,0:T(8,128)(2,1)S(1)} %get-tuple-element.192), channel_id=1, source_target_pairs={{0,1},{1,0},{2,3},{3,2},{4,5},{5,4},{6,7},{7,6},{8,9},{9,8},{10,11... | collective-permute-start | bytes 3538952 | tf_op jit(solution)/shard_map/ppermute | solution.py:564
  25.8 9.4 %collective-permute-start.6 = (bf16[512,384]{1,0:T(8,128)(2,1)S(1)}, bf16[512,384]{1,0:T(8,128)(2,1)S(1)}, u32[]{:S(2)}, u32[]{:S(2)}) collective-permute-start(bf16[512,384]{1,0:T(8,128)(2,1)S(1)} %get-tuple-element.261.refs_0_), channel_id=1, source_target_pairs={{0,2},{2,0},{1,3},{3,1},{4,6},{6,4},{5,7},{7,5},{8,10},{10,8},{9,1... | collective-permute-start | bytes 1179656 | tf_op jit(solution)/shard_map/ppermute | solution.py:564
  26.0 9.0 %collective-permute-start.9 = (bf16[144,768]{1,0:T(8,128)(2,1)S(1)}, bf16[144,768]{1,0:T(8,128)(2,1)S(1)}, u32[]{:S(2)}, u32[]{:S(2)}) collective-permute-start(bf16[144,768]{1,0:T(8,128)(2,1)S(1)} %collective-permute-done.8), channel_id=1, source_target_pairs={{0,8},{8,0},{16,24},{24,16},{1,9},{9,1},{17,25},{25,17},{2,10},{10... | collective-permute-start | bytes 663560 | tf_op jit(solution)/shard_map/ppermute | solution.py:606
  29.1 11.2 %collective-permute-start.5 = (bf16[512,384]{1,0:T(8,128)(2,1)S(1)}, bf16[512,384]{1,0:T(8,128)(2,1)S(1)}, u32[]{:S(2)}, u32[]{:S(2)}) collective-permute-start(bf16[512,384]{1,0:T(8,128)(2,1)S(1)} %get-tuple-element.261.refs_0_), channel_id=1, source_target_pairs={{0,4},{4,0},{1,5},{5,1},{2,6},{6,2},{3,7},{7,3},{8,12},{12,8},{9,1... | collective-permute-start | bytes 1179656 | tf_op jit(solution)/shard_map/ppermute | solution.py:564
  35.1 5.1 %collective-permute-start.10 = (bf16[2,144,768]{2,1,0:T(8,128)(2,1)S(1)}, bf16[2,144,768]{2,1,0:T(8,128)(2,1)S(1)}, u32[]{:S(2)}, u32[]{:S(2)}) collective-permute-start(bf16[2,144,768]{2,1,0:T(8,128)(2,1)S(1)} %pad_maximum_fusion.3.refs_12_), channel_id=1, source_target_pairs={{0,2},{2,0},{1,3},{3,1},{4,6},{6,4},{5,7},{7,5},{8,10},{10,8},{9,1... | collective-permute-start | bytes 1327112 | tf_op jit(solution)/shard_map/ppermute | solution.py:564
  47.5 11.1 %collective-permute-start.16 = (bf16[768,768]{1,0:T(8,128)(2,1)S(1)}, bf16[768,768]{1,0:T(8,128)(2,1)S(1)}, u32[]{:S(2)}, u32[]{:S(2)}) collective-permute-start(bf16[768,768]{1,0:T(8,128)(2,1)S(1)} %collective-permute-done.15.refs_10_), channel_id=1, source_target_pairs={{0,2},{2,0},{1,3},{3,1},{4,6},{6,4},{5,7},{7,5},{8,10},{10,8},{9,1... | collective-permute-start | bytes 3538952 | tf_op jit(solution)/shard_map/ppermute | solution.py:564
  47.5 4.3 %collective-permute-start.14 = (bf16[512,768]{1,0:T(8,128)(2,1)}, bf16[512,768]{1,0:T(8,128)(2,1)S(1)}, u32[]{:S(2)}, u32[]{:S(2)}) collective-permute-start(bf16[512,768]{1,0:T(8,128)(2,1)} %get-tuple-element.278.refs_0_), channel_id=1, source_target_pairs={{0,2},{2,0},{1,3},{3,1},{4,6},{6,4},{5,7},{7,5},{8,10},{10,8},{9,1... | collective-permute-start | bytes 2359304 | tf_op jit(solution)/shard_map/ppermute | solution.py:564
  48.0 19.7 %collective-permute-start.20 = (bf16[512,768]{1,0:T(8,128)(2,1)}, bf16[512,768]{1,0:T(8,128)(2,1)S(1)}, u32[]{:S(2)}, u32[]{:S(2)}) collective-permute-start(bf16[512,768]{1,0:T(8,128)(2,1)} %get-tuple-element.278.refs_0_), channel_id=1, source_target_pairs={{0,4},{4,0},{1,5},{5,1},{2,6},{6,2},{3,7},{7,3},{8,12},{12,8},{9,1... | collective-permute-start | bytes 2359304 | tf_op jit(solution)/shard_map/ppermute | solution.py:564
  49.5 4.4 %collective-permute-start.11 = (bf16[128,192]{1,0:T(8,128)(2,1)S(1)}, bf16[128,192]{1,0:T(8,128)(2,1)S(1)}, u32[]{:S(2)}, u32[]{:S(2)}) collective-permute-start(bf16[128,192]{1,0:T(8,128)(2,1)S(1)} %get-tuple-element.220), channel_id=1, source_target_pairs={{0,24},{8,0},{16,8},{24,16},{1,25},{9,1},{17,9},{25,17},{2,26},{10... | collective-permute-start | bytes 147464 | tf_op jit(solution)/shard_map/ppermute | solution.py:564
  51.5 7.1 %collective-permute-start.12 = (bf16[128,192]{1,0:T(8,128)(2,1)S(1)}, bf16[128,192]{1,0:T(8,128)(2,1)S(1)}, u32[]{:S(2)}, u32[]{:S(2)}) collective-permute-start(bf16[128,192]{1,0:T(8,128)(2,1)S(1)} %get-tuple-element.221), channel_id=1, source_target_pairs={{0,16},{8,24},{16,0},{24,8},{1,17},{9,25},{17,1},{25,9},{2,18},{10... | collective-permute-start | bytes 147464 | tf_op jit(solution)/shard_map/ppermute | solution.py:564
  51.8 6.7 %collective-permute-start.13 = (bf16[128,192]{1,0:T(8,128)(2,1)S(1)}, bf16[128,192]{1,0:T(8,128)(2,1)S(1)}, u32[]{:S(2)}, u32[]{:S(2)}) collective-permute-start(bf16[128,192]{1,0:T(8,128)(2,1)S(1)} %get-tuple-element.222), channel_id=1, source_target_pairs={{0,8},{8,16},{16,24},{24,0},{1,9},{9,17},{17,25},{25,1},{2,10},{10... | collective-permute-start | bytes 147464 | tf_op jit(solution)/shard_map/ppermute | solution.py:564
  67.7 4.7 %collective-permute-start.21 = (bf16[128,6528]{1,0:T(8,128)(2,1)S(1)}, bf16[128,6528]{1,0:T(8,128)(2,1)S(1)}, u32[]{:S(2)}, u32[]{:S(2)}) collective-permute-start(bf16[128,6528]{1,0:T(8,128)(2,1)S(1)} %get-tuple-element.256.own), channel_id=1, source_target_pairs={{0,2},{2,0},{1,3},{3,1},{4,6},{6,4},{5,7},{7,5},{8,10},{10,8},{9,1... | collective-permute-start | bytes 5013512 | tf_op jit(solution)/shard_map/ppermute | solution.py:564
  67.7 4.7 %collective-permute-start.22 = (bf16[512,768]{1,0:T(8,128)(2,1)S(1)}, bf16[512,768]{1,0:T(8,128)(2,1)S(1)}, u32[]{:S(2)}, u32[]{:S(2)}) collective-permute-start(bf16[512,768]{1,0:T(8,128)(2,1)S(1)} %collective-permute-done.20.refs_1_), channel_id=1, source_target_pairs={{0,2},{2,0},{1,3},{3,1},{4,6},{6,4},{5,7},{7,5},{8,10},{10,8},{9,1... | collective-permute-start | bytes 2359304 | tf_op jit(solution)/shard_map/ppermute | solution.py:564
  68.2 9.1 %collective-permute-start.17 = (bf16[128,256]{1,0:T(8,128)(2,1)S(1)}, bf16[128,256]{1,0:T(8,128)(2,1)S(1)}, u32[]{:S(2)}, u32[]{:S(2)}) collective-permute-start(bf16[128,256]{1,0:T(8,128)(2,1)S(1)} %get-tuple-element.246), channel_id=1, source_target_pairs={{0,8},{8,16},{16,24},{24,0},{1,9},{9,17},{17,25},{25,1},{2,10},{10... | collective-permute-start | bytes 196616 | tf_op jit(solution)/shard_map/ppermute | solution.py:564
  69.4 7.9 %collective-permute-start.18 = (bf16[128,256]{1,0:T(8,128)(2,1)S(1)}, bf16[128,256]{1,0:T(8,128)(2,1)S(1)}, u32[]{:S(2)}, u32[]{:S(2)}) collective-permute-start(bf16[128,256]{1,0:T(8,128)(2,1)S(1)} %get-tuple-element.247), channel_id=1, source_target_pairs={{0,16},{8,24},{16,0},{24,8},{1,17},{9,25},{17,1},{25,9},{2,18},{10... | collective-permute-start | bytes 196616 | tf_op jit(solution)/shard_map/ppermute | solution.py:564
  71.1 6.3 %collective-permute-start.19 = (bf16[128,256]{1,0:T(8,128)(2,1)S(1)}, bf16[128,256]{1,0:T(8,128)(2,1)S(1)}, u32[]{:S(2)}, u32[]{:S(2)}) collective-permute-start(bf16[128,256]{1,0:T(8,128)(2,1)S(1)} %get-tuple-element.248), channel_id=1, source_target_pairs={{0,24},{8,0},{16,8},{24,16},{1,25},{9,1},{17,9},{25,17},{2,26},{10... | collective-permute-start | bytes 196616 | tf_op jit(solution)/shard_map/ppermute | solution.py:564
  77.4 21.9 %collective-permute-start.23 = (bf16[2,1728,128]{2,1,0:T(8,128)(2,1)}, bf16[2,1728,128]{2,1,0:T(8,128)(2,1)S(1)}, u32[]{:S(2)}, u32[]{:S(2)}) collective-permute-start(bf16[2,1728,128]{2,1,0:T(8,128)(2,1)} %get-tuple-element.290), channel_id=1, source_target_pairs={{0,1},{1,0},{2,3},{3,2},{4,5},{5,4},{6,7},{7,6},{8,9},{9,8},{10,11... | collective-permute-start | bytes 2654216 | tf_op jit(solution)/shard_map/ppermute | solution.py:564
  79.0 19.5 %collective-permute-start.24 = (bf16[2,256,768]{2,1,0:T(8,128)(2,1)}, bf16[2,256,768]{2,1,0:T(8,128)(2,1)S(1)}, u32[]{:S(2)}, u32[]{:S(2)}) collective-permute-start(bf16[2,256,768]{2,1,0:T(8,128)(2,1)} %get-tuple-element.292), channel_id=1, source_target_pairs={{0,4},{4,0},{1,5},{5,1},{2,6},{6,2},{3,7},{7,3},{8,12},{12,8},{9,1... | collective-permute-start | bytes 2359304 | tf_op jit(solution)/shard_map/ppermute | solution.py:564
  99.3 5.0 %collective-permute-start.25 = (bf16[2,512,384]{2,1,0:T(8,128)(2,1)S(1)}, bf16[2,512,384]{2,1,0:T(8,128)(2,1)S(1)}, u32[]{:S(2)}, u32[]{:S(2)}) collective-permute-start(bf16[2,512,384]{2,1,0:T(8,128)(2,1)S(1)} %get-tuple-element.294.refs_5_), channel_id=1, source_target_pairs={{0,2},{2,0},{1,3},{3,1},{4,6},{6,4},{5,7},{7,5},{8,10},{10,8},{9,1... | collective-permute-start | bytes 2359304 | tf_op jit(solution)/shard_map/ppermute | solution.py:564
  99.3 4.3 %collective-permute-start.26 = (bf16[2,2,96,640]{3,2,1,0:T(8,128)(2,1)S(1)}, bf16[2,2,96,640]{3,2,1,0:T(8,128)(2,1)S(1)}, u32[]{:S(2)}, u32[]{:S(2)}) collective-permute-start(bf16[2,2,96,640]{3,2,1,0:T(8,128)(2,1)S(1)} %get-tuple-element.295), channel_id=1, source_target_pairs={{0,2},{2,0},{1,3},{3,1},{4,6},{6,4},{5,7},{7,5},{8,10},{10,8},{9,1... | collective-permute-start | bytes 1474568 | tf_op jit(solution)/shard_map/ppermute | solution.py:564
  100.3 14.9 %collective-permute-start.28 = (bf16[256,768]{1,0:T(8,128)(2,1)S(1)}, bf16[256,768]{1,0:T(8,128)(2,1)S(1)}, u32[]{:S(2)}, u32[]{:S(2)}) collective-permute-start(bf16[256,768]{1,0:T(8,128)(2,1)S(1)} %get-tuple-element.366), channel_id=1, source_target_pairs={{0,1},{1,0},{2,3},{3,2},{4,5},{5,4},{6,7},{7,6},{8,9},{9,8},{10,11... | collective-permute-start | bytes 1179656 | tf_op jit(solution)/shard_map/ppermute | solution.py:564
  102.0 13.1 %collective-permute-start.29 = (bf16[1728,128]{1,0:T(8,128)(2,1)S(1)}, bf16[1728,128]{1,0:T(8,128)(2,1)S(1)}, u32[]{:S(2)}, u32[]{:S(2)}) collective-permute-start(bf16[1728,128]{1,0:T(8,128)(2,1)S(1)} %get-tuple-element.364), channel_id=1, source_target_pairs={{0,4},{4,0},{1,5},{5,1},{2,6},{6,2},{3,7},{7,3},{8,12},{12,8},{9,1... | collective-permute-start | bytes 1327112 | tf_op jit(solution)/shard_map/ppermute | solution.py:564
  103.7 13.9 %collective-permute-start.32 = (bf16[2,96,640]{2,1,0:T(8,128)(2,1)S(1)}, bf16[2,96,640]{2,1,0:T(8,128)(2,1)S(1)}, u32[]{:S(2)}, u32[]{:S(2)}) collective-permute-start(bf16[2,96,640]{2,1,0:T(8,128)(2,1)S(1)} %get-tuple-element.368), channel_id=1, source_target_pairs={{0,1},{1,0},{2,3},{3,2},{4,5},{5,4},{6,7},{7,6},{8,9},{9,8},{10,11... | collective-permute-start | bytes 737288 | tf_op jit(solution)/shard_map/ppermute | solution.py:564
  104.4 43.8 %collective-permute-start.27 = (bf16[1,512,384]{2,1,0:T(8,128)(2,1)S(1)}, bf16[1,512,384]{2,1,0:T(8,128)(2,1)S(1)}, u32[]{:S(2)}, u32[]{:S(2)}) collective-permute-start(bf16[1,512,384]{2,1,0:T(8,128)(2,1)S(1)} %add_convert_fusion.6), channel_id=1, source_target_pairs={{0,4},{4,0},{1,5},{5,1},{2,6},{6,2},{3,7},{7,3},{8,12},{12,8},{9,1... | collective-permute-start | bytes 1179656 | tf_op jit(solution)/shard_map/ppermute | solution.py:564
  115.4 9.2 %collective-permute-start.30 = (bf16[2,64,768]{2,1,0:T(8,128)(2,1)S(1)}, bf16[2,64,768]{2,1,0:T(8,128)(2,1)S(1)}, u32[]{:S(2)}, u32[]{:S(2)}) collective-permute-start(bf16[2,64,768]{2,1,0:T(8,128)(2,1)S(1)} %get-tuple-element.374), channel_id=1, source_target_pairs={{0,8},{8,0},{16,24},{24,16},{1,9},{9,1},{17,25},{25,17},{2,10},{10... | collective-permute-start | bytes 589832 | tf_op jit(solution)/shard_map/ppermute | solution.py:606
  116.7 7.8 %collective-permute-start.31 = (bf16[2,432,128]{2,1,0:T(8,128)(2,1)S(1)}, bf16[2,432,128]{2,1,0:T(8,128)(2,1)S(1)}, u32[]{:S(2)}, u32[]{:S(2)}) collective-permute-start(bf16[2,432,128]{2,1,0:T(8,128)(2,1)S(1)} %get-tuple-element.370), channel_id=1, source_target_pairs={{0,8},{8,0},{16,24},{24,16},{1,9},{9,1},{17,25},{25,17},{2,10},{10... | collective-permute-start | bytes 663560 | tf_op jit(solution)/shard_map/ppermute | solution.py:606
  117.7 10.1 %collective-permute-start.35 = (bf16[96,640]{1,0:T(8,128)(2,1)S(1)}, bf16[96,640]{1,0:T(8,128)(2,1)S(1)}, u32[]{:S(2)}, u32[]{:S(2)}) collective-permute-start(bf16[96,640]{1,0:T(8,128)(2,1)S(1)} %get-tuple-element.376), channel_id=1, source_target_pairs={{0,4},{4,0},{1,5},{5,1},{2,6},{6,2},{3,7},{7,3},{8,12},{12,8},{9,1... | collective-permute-start | bytes 368648 | tf_op jit(solution)/shard_map/ppermute | solution.py:564
  124.7 13.0 %collective-permute-start.33 = (bf16[64,768]{1,0:T(8,128)(2,1)S(1)}, bf16[64,768]{1,0:T(8,128)(2,1)S(1)}, u32[]{:S(2)}, u32[]{:S(2)}) collective-permute-start(bf16[64,768]{1,0:T(8,128)(2,1)S(1)} %get-tuple-element.380), channel_id=1, source_target_pairs={{0,16},{8,24},{16,0},{24,8},{1,17},{9,25},{17,1},{25,9},{2,18},{10... | collective-permute-start | bytes 294920 | tf_op jit(solution)/shard_map/ppermute | solution.py:606
  126.1 11.5 %collective-permute-start.34 = (bf16[432,128]{1,0:T(8,128)(2,1)S(1)}, bf16[432,128]{1,0:T(8,128)(2,1)S(1)}, u32[]{:S(2)}, u32[]{:S(2)}) collective-permute-start(bf16[432,128]{1,0:T(8,128)(2,1)S(1)} %get-tuple-element.378), channel_id=1, source_target_pairs={{0,16},{8,24},{16,0},{24,8},{1,17},{9,25},{17,1},{25,9},{2,18},{10... | collective-permute-start | bytes 331784 | tf_op jit(solution)/shard_map/ppermute | solution.py:606
  127.8 12.9 %collective-permute-start.38 = (bf16[96,640]{1,0:T(8,128)(2,1)S(1)}, bf16[96,640]{1,0:T(8,128)(2,1)S(1)}, u32[]{:S(2)}, u32[]{:S(2)}) collective-permute-start(bf16[96,640]{1,0:T(8,128)(2,1)S(1)} %add_convert_fusion.10), channel_id=1, source_target_pairs={{0,16},{8,24},{16,0},{24,8},{1,17},{9,25},{17,1},{25,9},{2,18},{10... | collective-permute-start | bytes 368648 | tf_op jit(solution)/shard_map/ppermute | solution.py:606
  137.7 10.5 %collective-permute-start.37 = (bf16[432,128]{1,0:T(8,128)(2,1)S(1)}, bf16[432,128]{1,0:T(8,128)(2,1)S(1)}, u32[]{:S(2)}, u32[]{:S(2)}) collective-permute-start(bf16[432,128]{1,0:T(8,128)(2,1)S(1)} %add_convert_fusion.11), channel_id=1, source_target_pairs={{0,16},{8,24},{16,0},{24,8},{1,17},{9,25},{17,1},{25,9},{2,18},{10... | collective-permute-start | bytes 331784 | tf_op jit(solution)/shard_map/ppermute | solution.py:606
  137.8 10.4 %collective-permute-start.36 = (bf16[64,768]{1,0:T(8,128)(2,1)S(1)}, bf16[64,768]{1,0:T(8,128)(2,1)S(1)}, u32[]{:S(2)}, u32[]{:S(2)}) collective-permute-start(bf16[64,768]{1,0:T(8,128)(2,1)S(1)} %add_convert_fusion.12), channel_id=1, source_target_pairs={{0,16},{8,24},{16,0},{24,8},{1,17},{9,25},{17,1},{25,9},{2,18},{10... | collective-permute-start | bytes 294920 | tf_op jit(solution)/shard_map/ppermute | solution.py:606
  140.8 9.3 %collective-permute-start.41 = (bf16[2,96,640]{2,1,0:T(8,128)(2,1)S(1)}, bf16[2,96,640]{2,1,0:T(8,128)(2,1)S(1)}, u32[]{:S(2)}, u32[]{:S(2)}) collective-permute-start(bf16[2,96,640]{2,1,0:T(8,128)(2,1)S(1)} %pad_maximum_fusion.5), channel_id=1, source_target_pairs={{0,8},{8,0},{16,24},{24,16},{1,9},{9,1},{17,25},{25,17},{2,10},{10... | collective-permute-start | bytes 737288 | tf_op jit(solution)/shard_map/ppermute | solution.py:606
  150.2 12.2 %collective-permute-start.43 = (bf16[4,96,640]{2,1,0:T(8,128)(2,1)S(1)}, bf16[4,96,640]{2,1,0:T(8,128)(2,1)S(1)}, u32[]{:S(2)}, u32[]{:S(2)}) collective-permute-start(bf16[4,96,640]{2,1,0:T(8,128)(2,1)S(1)} %constant_dynamic-update-slice_fusion.2), channel_id=1, source_target_pairs={{0,4},{4,0},{1,5},{5,1},{2,6},{6,2},{3,7},{7,3},{8,12},{12,8},{9,1... | collective-permute-start | bytes 1474568 | tf_op jit(solution)/shard_map/ppermute | solution.py:564
  151.8 7.8 %collective-permute-start.40 = (bf16[2,64,768]{2,1,0:T(8,128)(2,1)S(1)}, bf16[2,64,768]{2,1,0:T(8,128)(2,1)S(1)}, u32[]{:S(2)}, u32[]{:S(2)}) collective-permute-start(bf16[2,64,768]{2,1,0:T(8,128)(2,1)S(1)} %pad_maximum_fusion.7), channel_id=1, source_target_pairs={{0,8},{8,0},{16,24},{24,16},{1,9},{9,1},{17,25},{25,17},{2,10},{10... | collective-permute-start | bytes 589832 | tf_op jit(solution)/shard_map/ppermute | solution.py:606
  151.8 10.3 %collective-permute-start.39 = (bf16[2,432,128]{2,1,0:T(8,128)(2,1)S(1)}, bf16[2,432,128]{2,1,0:T(8,128)(2,1)S(1)}, u32[]{:S(2)}, u32[]{:S(2)}) collective-permute-start(bf16[2,432,128]{2,1,0:T(8,128)(2,1)S(1)} %pad_maximum_fusion.6), channel_id=1, source_target_pairs={{0,8},{8,0},{16,24},{24,16},{1,9},{9,1},{17,25},{25,17},{2,10},{10... | collective-permute-start | bytes 663560 | tf_op jit(solution)/shard_map/ppermute | solution.py:606
  162.5 14.3 %collective-permute-start.46 = (bf16[2,4,96,640]{3,2,1,0:T(8,128)(2,1)S(1)}, bf16[2,4,96,640]{3,2,1,0:T(8,128)(2,1)S(1)}, u32[]{:S(2)}, u32[]{:S(2)}) collective-permute-start(bf16[2,4,96,640]{3,2,1,0:T(8,128)(2,1)S(1)} %pad_maximum_fusion.own), channel_id=1, source_target_pairs={{0,2},{2,0},{1,3},{3,1},{4,6},{6,4},{5,7},{7,5},{8,10},{10,8},{9,1... | collective-permute-start | bytes 2949128 | tf_op jit(solution)/shard_map/ppermute | solution.py:564
  162.6 11.5 %collective-permute-start.42 = (bf16[2,128,768]{2,1,0:T(8,128)(2,1)S(1)}, bf16[2,128,768]{2,1,0:T(8,128)(2,1)S(1)}, u32[]{:S(2)}, u32[]{:S(2)}) collective-permute-start(bf16[2,128,768]{2,1,0:T(8,128)(2,1)S(1)} %get-tuple-element.335), channel_id=1, source_target_pairs={{0,8},{8,0},{16,24},{24,16},{1,9},{9,1},{17,25},{25,17},{2,10},{10... | collective-permute-start | bytes 1179656 | tf_op jit(solution)/shard_map/ppermute | solution.py:606
  162.7 14.0 %collective-permute-start.45 = (bf16[4,432,128]{2,1,0:T(8,128)(2,1)S(1)}, bf16[4,432,128]{2,1,0:T(8,128)(2,1)S(1)}, u32[]{:S(2)}, u32[]{:S(2)}) collective-permute-start(bf16[4,432,128]{2,1,0:T(8,128)(2,1)S(1)} %pad_maximum_fusion.4), channel_id=1, source_target_pairs={{0,4},{4,0},{1,5},{5,1},{2,6},{6,2},{3,7},{7,3},{8,12},{12,8},{9,1... | collective-permute-start | bytes 1327112 | tf_op jit(solution)/shard_map/ppermute | solution.py:564
  164.3 19.3 %collective-permute-start.48 = (bf16[4,64,768]{2,1,0:T(8,128)(2,1)S(1)}, bf16[4,64,768]{2,1,0:T(8,128)(2,1)S(1)}, u32[]{:S(2)}, u32[]{:S(2)}) collective-permute-start(bf16[4,64,768]{2,1,0:T(8,128)(2,1)S(1)} %constant_dynamic-update-slice_fusion), channel_id=1, source_target_pairs={{0,4},{4,0},{1,5},{5,1},{2,6},{6,2},{3,7},{7,3},{8,12},{12,8},{9,1... | collective-permute-start | bytes 1179656 | tf_op jit(solution)/shard_map/ppermute | solution.py:564
  174.3 11.6 %collective-permute-start.44 = (bf16[128,768]{1,0:T(8,128)(2,1)S(1)}, bf16[128,768]{1,0:T(8,128)(2,1)S(1)}, u32[]{:S(2)}, u32[]{:S(2)}) collective-permute-start(bf16[128,768]{1,0:T(8,128)(2,1)S(1)} %get-tuple-element.372), channel_id=1, source_target_pairs={{0,16},{8,24},{16,0},{24,8},{1,17},{9,25},{17,1},{25,9},{2,18},{10... | collective-permute-start | bytes 589832 | tf_op jit(solution)/shard_map/ppermute | solution.py:606
  179.7 6.3 %collective-permute-start.47 = (bf16[2,4,432,128]{3,2,1,0:T(8,128)(2,1)S(1)}, bf16[2,4,432,128]{3,2,1,0:T(8,128)(2,1)S(1)}, u32[]{:S(2)}, u32[]{:S(2)}) collective-permute-start(bf16[2,4,432,128]{3,2,1,0:T(8,128)(2,1)S(1)} %pad_maximum_fusion.1.own), channel_id=1, source_target_pairs={{0,2},{2,0},{1,3},{3,1},{4,6},{6,4},{5,7},{7,5},{8,10},{10,8},{9,1... | collective-permute-start | bytes 2654216 | tf_op jit(solution)/shard_map/ppermute | solution.py:564
  185.9 4.5 %collective-permute-start.49 = (bf16[2,4,64,768]{3,2,1,0:T(8,128)(2,1)S(1)}, bf16[2,4,64,768]{3,2,1,0:T(8,128)(2,1)S(1)}, u32[]{:S(2)}, u32[]{:S(2)}) collective-permute-start(bf16[2,4,64,768]{3,2,1,0:T(8,128)(2,1)S(1)} %pad_maximum_fusion.2.own), channel_id=1, source_target_pairs={{0,2},{2,0},{1,3},{3,1},{4,6},{6,4},{5,7},{7,5},{8,10},{10,8},{9,1... | collective-permute-start | bytes 2359304 | tf_op jit(solution)/shard_map/ppermute | solution.py:564
  (31 other events, 308.8 us)

commit v7 on v6

--- a/solution.py
+++ b/solution.py
@@ -180,6 +180,19 @@
     rows = values_t[at : at + HEAD_DIM]
     zeros = jnp.zeros_like(rows)
     return jnp.concatenate([rows, zeros] if head % 2 == 0 else [zeros, rows], axis=0)
+
+
+def fold(values):
+    half = values.shape[0] // 2
+    rest = values[:, 128:192]
+    return jnp.concatenate([values[:, 0:128], jnp.concatenate([rest[:half], rest[half:]], axis=1)])
+
+
+def unfold(values):
+    rows = values.shape[0] * 2 // 3
+    rest = values[rows:]
+    rest = jnp.concatenate([rest[:, 0:64], rest[:, 64:128]])
+    return jnp.concatenate([values[:rows], rest], axis=1)
 
 
 def forward_kernel(n_kv, last, q_ref, *refs):
@@ -220,7 +233,7 @@
     if last:
         small = rows // TP
         for j in range(TP):
-            atts[j][...] = att_t_ref[:, j * small : (j + 1) * small].T.astype(BF)
+            atts[j][...] = fold(att_t_ref[:, j * small : (j + 1) * small].T.astype(BF))
 
 
 def backward_kernel(n_kv, q_ref, *refs):
@@ -342,8 +355,9 @@
         copy.wait()
     middle = tok_ref[...].astype(F32)
     for j in range(TP):
-        middle += dot(atts[j][...], w_out[pl.ds(starts[j], GW), :])
-        act_ref[:, ACT_ATT + j * GW : ACT_ATT + (j + 1) * GW] = atts[j][...]
+        att = unfold(atts[j][...])
+        middle += dot(att, w_out[pl.ds(starts[j], GW), :])
+        act_ref[:, ACT_ATT + j * GW : ACT_ATT + (j + 1) * GW] = att
     gain = gains_ref[1:2, :]
     unit, scale = normalise(middle)
     h = (unit * gain).astype(BF)
@@ -754,7 +768,7 @@
     first = [first[0], after(first[1], *both_down)]
     att = order.run(
         functools.partial(forward_kernel, len(far), True),
-        [((rows, GW), BF)] * TP + [((GW, many), F32), ((8, many), F32)],
+        [((rows * 3 // 2, 128), BF)] * TP + [((GW, many), F32), ((8, many), F32)],
         0,
         [query, *[kvs[i] for i in far], *first],
         scratch=scratch(len(far)),

time: 193 us -> 193 us (level)
  transfers between devices with their start and end apart: 50 -> 50, of which waited for: 21 -> 22; matrix products, arithmetic and copies ran while one was open for 3% -> 3% of each run, Pallas kernels for 28% -> 28%
where the time goes in v7:
time: 193 us
  waiting for transfers between devices  72.5 us (38%)
  Pallas kernels  56.8 us (29%)
  starting transfers between devices  55.1 us (29%)
  other arithmetic  4.52 us (2%)
  local copies, waits for them, and re-layouts  2.86 us (1%)
    pallas_call x14, Pallas kernels, call(): pl.pallas_call(body, out_shape=shapes, in_specs=specs, out_specs=[pl.Bloc...  56.8 us
    ppermute x13, waiting for transfers between devices, swap_z(): return lax.ppermute(value, 'z', [(i, i ^ bit) for i in range(TP)])  43.7 us
    ppermute x37, starting transfers between devices, shift(): return lax.ppermute(value, axis, [(i, (i + k) % n) for i in range(n)])  36.2 us
    ppermute x37, waiting for transfers between devices, shift(): return lax.ppermute(value, axis, [(i, (i + k) % n) for i in range(n)])  28.9 us
    ppermute x13, starting transfers between devices, swap_z(): return lax.ppermute(value, 'z', [(i, i ^ bit) for i in range(TP)])  18.9 us
  transfers between devices with their start and end apart: 50, of which 22 were waited for; matrix products, arithmetic and copies ran while one was open for 3% of the time, Pallas kernels for 28%

profile of v7, /device:TPU:0, one launch (start us, length us, event | category | flops | bytes accessed | tf_op | source)
XLA Modules:
  0.0 193.1 jit_solution(11254217330637662262)
XLA Ops:
  0.6 3.1 %collective-permute-start = (bf16[128,768]{1,0:T(8,128)(2,1)}, bf16[128,768]{1,0:T(8,128)(2,1)S(1)}, u32[]{:S(2)}, u32[]{:S(2)}) collective-permute-start(bf16[128,768]{1,0:T(8,128)(2,1)} %bitcast.67), channel_id=1, source_target_pairs={{0,8},{8,16},{16,24},{24,0},{1,9},{9,17},{17,25},{25,1},{2,10},{10... | collective-permute-start | bytes 589832 | tf_op jit(solution)/shard_map/ppermute | solution.py:578
  3.7 2.6 %collective-permute-start.1 = (bf16[128,768]{1,0:T(8,128)(2,1)}, bf16[128,768]{1,0:T(8,128)(2,1)S(1)}, u32[]{:S(2)}, u32[]{:S(2)}) collective-permute-start(bf16[128,768]{1,0:T(8,128)(2,1)} %bitcast.68), channel_id=1, source_target_pairs={{0,16},{8,24},{16,0},{24,8},{1,17},{9,25},{17,1},{25,9},{2,18},{10... | collective-permute-start | bytes 589832 | tf_op jit(solution)/shard_map/ppermute | solution.py:578
  7.7 1.7 group_columns.1
  10.2 1.5 collective-permute-start.3
  11.7 2.0 %pack_weights.1 = (bf16[768,768]{1,0:T(8,128)(2,1)S(1)}, bf16[144,768]{1,0:T(8,128)(2,1)S(1)}) custom-call(s32[4]{0:T(128)S(1)} %pad_add_fusion.idx, bf16[384,768]{1,0:T(8,128)(2,1)} %refs_7_, bf16[384,2304]{1,0:T(8,128)(2,1)} %refs_8_, bf16[576,768]{1,0:T(8,128)(2,1)} %refs_9_), custom_call_target="tpu_custom_call" | custom-call | flops 1 | bytes 1 | tf_op jit(solution)/shard_map/pack_weights/pallas_call | solution.py:54
  16.1 1.5 collective-permute-start.15
  17.7 1.9 collective-permute-done.3.refs_5_
  21.8 4.0 %front.1 = (bf16[512,256]{1,0:T(8,128)(2,1)S(1)}, bf16[512,384]{1,0:T(8,128)(2,1)S(1)}, bf16[512,768]{1,0:T(8,128)(2,1)}, bf16[768,640]{1,0:T(8,128)(2,1)}, f32[8,768]{1,0:T(8,128)}) custom-call(s32[4]{0:T(128)S(1)} %pad_add_fusion.idx, bf16[128,768]{1,0:T(8,128)(2,1)} %bitcast.70, bf16[128,768]{1,0:T(8,128)(2,1)} %copy-done.23, ...), custom_call_target="tpu_custom_call" | custom-call | flops 1 | bytes 1 | tf_op jit(solution)/shard_map/front/pallas_call | solution.py:54
  26.0 3.0 %collective-permute-start.9 = (bf16[144,768]{1,0:T(8,128)(2,1)S(1)}, bf16[144,768]{1,0:T(8,128)(2,1)S(1)}, u32[]{:S(2)}, u32[]{:S(2)}) collective-permute-start(bf16[144,768]{1,0:T(8,128)(2,1)S(1)} %collective-permute-done.8), channel_id=1, source_target_pairs={{0,8},{8,0},{16,24},{24,16},{1,9},{9,1},{17,25},{25,17},{2,10},{10... | collective-permute-start | bytes 663560 | tf_op jit(solution)/shard_map/ppermute | solution.py:620
  30.5 4.6 %collective-permute-done.9 = bf16[144,768]{1,0:T(8,128)(2,1)S(1)} collective-permute-done((bf16[144,768]{1,0:T(8,128)(2,1)S(1)}, bf16[144,768]{1,0:T(8,128)(2,1)S(1)}, u32[]{:S(2)}, u32[]{:S(2)}) %collective-permute-start.9) | collective-permute-done | bytes 221216 | tf_op jit(solution)/shard_map/ppermute | solution.py:620
  35.2 4.4 %attention_forward_near.1 = (f32[192,512]{1,0:T(8,128)S(1)}, f32[8,512]{1,0:T(8,128)S(1)}) custom-call(bf16[512,256]{1,0:T(8,128)(2,1)S(1)} %get-tuple-element.260.q_ref, bf16[512,384]{1,0:T(8,128)(2,1)S(1)} %get-tuple-element.261.refs_0_, bf16[512,384]{1,0:T(8,128)(2,1)S(1)} %collective-permute-done.6.refs_1_.refs_2_), custom_call_target="tpu_custom_call" | custom-call | flops 1 | bytes 1 | tf_op jit(solution)/shard_map/attention_forward_near/pallas_call | solution.py:54
  40.2 1.7 collective-permute-done.7.refs_1_.refs_3_
  42.0 5.0 %attention_forward_far.1 = (bf16[192,128]{1,0:T(8,128)(2,1)S(1)}, bf16[192,128]{1,0:T(8,128)(2,1)S(1)}, bf16[192,128]{1,0:T(8,128)(2,1)S(1)}, bf16[192,128]{1,0:...) custom-call(bf16[512,256]{1,0:T(8,128)(2,1)S(1)} %get-tuple-element.260.q_ref, ...), custom_call_target="tpu_custom_call" | custom-call | flops 1 | bytes 1 | tf_op jit(solution)/shard_map/attention_forward_far/pallas_call | solution.py:54
  48.0 1.5 collective-permute-start.20
  49.5 2.0 %collective-permute-start.11 = (bf16[192,128]{1,0:T(8,128)(2,1)S(1)}, bf16[192,128]{1,0:T(8,128)(2,1)S(1)}, u32[]{:S(2)}, u32[]{:S(2)}) collective-permute-start(bf16[192,128]{1,0:T(8,128)(2,1)S(1)} %get-tuple-element.220), channel_id=1, source_target_pairs={{0,24},{8,0},{16,8},{24,16},{1,25},{9,1},{17,9},{25,17},{2,26},{10... | collective-permute-start | bytes 147464 | tf_op jit(solution)/shard_map/ppermute | solution.py:578
  53.6 3.4 %collective-permute-done.12.refs_2_ = bf16[192,128]{1,0:T(8,128)(2,1)S(1)} collective-permute-done((bf16[192,128]{1,0:T(8,128)(2,1)S(1)}, bf16[192,128]{1,0:T(8,128)(2,1)S(1)}, u32[]{:S(2)}, u32[]{:S(2)}) %collective-permute-start.12) | collective-permute-done | bytes 49184 | tf_op jit(solution)/shard_map/ppermute | solution.py:578
  57.7 8.5 %feed_forward.1 = (f32[128,768]{1,0:T(8,128)}, f32[128,768]{1,0:T(8,128)}, bf16[128,6528]{1,0:T(8,128)(2,1)S(1)}, f32[8,768]{1,0:T(8,128)}, bf16[128,256]{1,0:T(...) custom-call(s32[4]{0:T(128)S(1)} %pad_add_fusion.idx, ...), custom_call_target="tpu_custom_call" | custom-call | flops 1 | bytes 1 | tf_op jit(solution)/shard_map/feed_forward/pallas_call | solution.py:54
  69.4 1.7 collective-permute-start.18
  73.2 4.1 %ffn_weight_grads.1 = (bf16[2,1728,128]{2,1,0:T(8,128)(2,1)}, bf16[2,1728,128]{2,1,0:T(8,128)(2,1)}, bf16[2,256,768]{2,1,0:T(8,128)(2,1)}, bf16[2,256,768]{2,1,0:T(8,128)(2,1)}) custom-call(s32[4]{0:T(128)S(1)} %pad_add_fusion.idx, bf16[128,6528]{1,0:T(8,128)(2,1)S(1)} %get-tuple-element.256.own, bf16[128,6528]{1,0:T(8,128)(2,1)S(1)} %collective-permute-done.21.got, ...), custom_call_target="tpu_custom_call" | custom-call | flops 1 | bytes 1 | tf_op jit(solution)/shard_map/ffn_weight_grads/pallas_call | solution.py:54
  77.4 1.6 collective-permute-start.23
  79.0 1.5 collective-permute-start.24
  80.5 10.5 %attention_backward.1 = (bf16[2,512,384]{2,1,0:T(8,128)(2,1)S(1)}, bf16[2,512,384]{2,1,0:T(8,128)(2,1)S(1)}, bf16[512,256]{1,0:T(8,128)(2,1)S(1)}) custom-call(bf16[512,256]{1,0:T(8,128)(2,1)} %copy-done.3, bf16[512,384]{1,0:T(8,128)(2,1)} %copy-done.6, bf16[512,384]{1,0:T(8,128)(2,1)} %copy-done.8, bf16[512,384]{1,0:T(8,128)(2,1)} %copy-done.7, ...), custom_call_target="tpu_custom_call" | custom-call | flops 1 | bytes 1 | tf_op jit(solution)/shard_map/attention_backward/pallas_call | solution.py:54
  91.0 4.6 %qkv_weight_grads.1 = (bf16[2,2,96,640]{3,2,1,0:T(8,128)(2,1)S(1)}, bf16[2,2,96,640]{3,2,1,0:T(8,128)(2,1)S(1)}) custom-call(s32[4]{0:T(128)S(1)} %pad_add_fusion.idx, bf16[512,768]{1,0:T(8,128)(2,1)} %get-tuple-element.278.refs_0_, bf16[512,768]{1,0:T(8,128)(2,1)} %copy-done.18, bf16[512,768]{1,0:T(8,128)(2,1)} %copy-done.17, bf16[512,768]{1,0:T(8,128)(2,1)} %copy-done.19, ...), custom_call_target="tpu_custom_call" | custom-call | flops 1 | bytes 1 | tf_op jit(solution)/shard_map/qkv_weight_grads/pallas_call | solution.py:54
  95.7 2.8 %collective-permute-done.24 = bf16[2,256,768]{2,1,0:T(8,128)(2,1)S(1)} collective-permute-done((bf16[2,256,768]{2,1,0:T(8,128)(2,1)}, bf16[2,256,768]{2,1,0:T(8,128)(2,1)S(1)}, u32[]{:S(2)}, u32[]{:S(2)}) %collective-permute-start.24) | collective-permute-done | bytes 786464 | tf_op jit(solution)/shard_map/ppermute | solution.py:578
  100.3 1.6 collective-permute-start.28
  102.0 1.6 collective-permute-start.29
  105.7 9.4 %collective-permute-done.29 = bf16[1728,128]{1,0:T(8,128)(2,1)S(1)} collective-permute-done((bf16[1728,128]{1,0:T(8,128)(2,1)S(1)}, bf16[1728,128]{1,0:T(8,128)(2,1)S(1)}, u32[]{:S(2)}, u32[]{:S(2)}) %collective-permute-start.29) | collective-permute-done | bytes 442400 | tf_op jit(solution)/shard_map/ppermute | solution.py:578
  117.7 1.6 collective-permute-start.35
  119.3 5.3 %collective-permute-done.31 = bf16[2,432,128]{2,1,0:T(8,128)(2,1)S(1)} collective-permute-done((bf16[2,432,128]{2,1,0:T(8,128)(2,1)S(1)}, bf16[2,432,128]{2,1,0:T(8,128)(2,1)S(1)}, u32[]{:S(2)}, u32[]{:S(2)}) %collective-permute-start.31) | collective-permute-done | bytes 221216 | tf_op jit(solution)/shard_map/ppermute | solution.py:620
  126.1 1.7 collective-permute-start.34
  129.2 8.4 %collective-permute-done.34 = bf16[432,128]{1,0:T(8,128)(2,1)S(1)} collective-permute-done((bf16[432,128]{1,0:T(8,128)(2,1)S(1)}, bf16[432,128]{1,0:T(8,128)(2,1)S(1)}, u32[]{:S(2)}, u32[]{:S(2)}) %collective-permute-start.34) | collective-permute-done | bytes 110624 | tf_op jit(solution)/shard_map/ppermute | solution.py:620
  137.8 3.0 %collective-permute-start.36 = (bf16[64,768]{1,0:T(8,128)(2,1)S(1)}, bf16[64,768]{1,0:T(8,128)(2,1)S(1)}, u32[]{:S(2)}, u32[]{:S(2)}) collective-permute-start(bf16[64,768]{1,0:T(8,128)(2,1)S(1)} %add_convert_fusion.12), channel_id=1, source_target_pairs={{0,16},{8,24},{16,0},{24,8},{1,17},{9,25},{17,1},{25,9},{2,18},{10... | collective-permute-start | bytes 294920 | tf_op jit(solution)/shard_map/ppermute | solution.py:620
  140.8 1.7 collective-permute-start.41
  142.6 5.6 %collective-permute-done.36 = bf16[64,768]{1,0:T(8,128)(2,1)S(1)} collective-permute-done((bf16[64,768]{1,0:T(8,128)(2,1)S(1)}, bf16[64,768]{1,0:T(8,128)(2,1)S(1)}, u32[]{:S(2)}, u32[]{:S(2)}) %collective-permute-start.36) | collective-permute-done | bytes 98336 | tf_op jit(solution)/shard_map/ppermute | solution.py:620
  148.2 1.9 h_one_grads.1
  150.2 1.6 collective-permute-start.43
  151.8 2.0 %collective-permute-start.39 = (bf16[2,432,128]{2,1,0:T(8,128)(2,1)S(1)}, bf16[2,432,128]{2,1,0:T(8,128)(2,1)S(1)}, u32[]{:S(2)}, u32[]{:S(2)}) collective-permute-start(bf16[2,432,128]{2,1,0:T(8,128)(2,1)S(1)} %pad_maximum_fusion.6), channel_id=1, source_target_pairs={{0,8},{8,0},{16,24},{24,16},{1,9},{9,1},{17,25},{25,17},{2,10},{10... | collective-permute-start | bytes 663560 | tf_op jit(solution)/shard_map/ppermute | solution.py:620
  153.8 5.8 %collective-permute-done.40 = bf16[2,64,768]{2,1,0:T(8,128)(2,1)S(1)} collective-permute-done((bf16[2,64,768]{2,1,0:T(8,128)(2,1)S(1)}, bf16[2,64,768]{2,1,0:T(8,128)(2,1)S(1)}, u32[]{:S(2)}, u32[]{:S(2)}) %collective-permute-start.40) | collective-permute-done | bytes 196640 | tf_op jit(solution)/shard_map/ppermute | solution.py:620
  159.6 2.4 %collective-permute-done.39 = bf16[2,432,128]{2,1,0:T(8,128)(2,1)S(1)} collective-permute-done((bf16[2,432,128]{2,1,0:T(8,128)(2,1)S(1)}, bf16[2,432,128]{2,1,0:T(8,128)(2,1)S(1)}, u32[]{:S(2)}, u32[]{:S(2)}) %collective-permute-start.39) | collective-permute-done | bytes 221216 | tf_op jit(solution)/shard_map/ppermute | solution.py:620
  162.7 1.6 collective-permute-start.45
  164.8 9.4 %collective-permute-done.42 = bf16[2,128,768]{2,1,0:T(8,128)(2,1)S(1)} collective-permute-done((bf16[2,128,768]{2,1,0:T(8,128)(2,1)S(1)}, bf16[2,128,768]{2,1,0:T(8,128)(2,1)S(1)}, u32[]{:S(2)}, u32[]{:S(2)}) %collective-permute-start.42) | collective-permute-done | bytes 393248 | tf_op jit(solution)/shard_map/ppermute | solution.py:620
  174.3 2.4 %collective-permute-start.44 = (bf16[128,768]{1,0:T(8,128)(2,1)S(1)}, bf16[128,768]{1,0:T(8,128)(2,1)S(1)}, u32[]{:S(2)}, u32[]{:S(2)}) collective-permute-start(bf16[128,768]{1,0:T(8,128)(2,1)S(1)} %get-tuple-element.372), channel_id=1, source_target_pairs={{0,16},{8,24},{16,0},{24,8},{1,17},{9,25},{17,1},{25,9},{2,18},{10... | collective-permute-start | bytes 589832 | tf_op jit(solution)/shard_map/ppermute | solution.py:620
  176.8 2.8 %qkv_unpack.1 = (f32[2,2,96,2304]{3,2,1,0:T(8,128)}, f32[384]{0:T(512)}) custom-call(s32[4]{0:T(128)S(1)} %pad_add_fusion.idx, bf16[2,4,96,640]{3,2,1,0:T(8,128)(2,1)S(1)} %pad_maximum_fusion.own, bf16[2,4,96,640]{3,2,1,0:T(8,128)(2,1)S(1)} %collective-permute-done.46.got), custom_call_target="tpu_custom_call" | custom-call | flops 1 | bytes 1 | tf_op jit(solution)/shard_map/qkv_unpack/pallas_call | solution.py:54
  179.7 3.9 %collective-permute-done.48 = bf16[4,64,768]{2,1,0:T(8,128)(2,1)S(1)} collective-permute-done((bf16[4,64,768]{2,1,0:T(8,128)(2,1)S(1)}, bf16[4,64,768]{2,1,0:T(8,128)(2,1)S(1)}, u32[]{:S(2)}, u32[]{:S(2)}) %collective-permute-start.48) | collective-permute-done | bytes 393248 | tf_op jit(solution)/shard_map/ppermute | solution.py:578
  183.7 2.2 %collective-permute-done.44.refs_1_ = bf16[128,768]{1,0:T(8,128)(2,1)S(1)} collective-permute-done((bf16[128,768]{1,0:T(8,128)(2,1)S(1)}, bf16[128,768]{1,0:T(8,128)(2,1)S(1)}, u32[]{:S(2)}, u32[]{:S(2)}) %collective-permute-start.44) | collective-permute-done | bytes 196640 | tf_op jit(solution)/shard_map/ppermute | solution.py:620
  185.9 2.9 %w_in_unpack.1 = f32[2,2,96,2304]{3,2,1,0:T(8,128)} custom-call(s32[4]{0:T(128)S(1)} %pad_add_fusion.idx, bf16[2,4,432,128]{3,2,1,0:T(8,128)(2,1)S(1)} %pad_maximum_fusion.1.own, bf16[2,4,432,128]{3,2,1,0:T(8,128)(2,1)S(1)} %collective-permute-done.47.got), custom_call_target="tpu_custom_call" | custom-call | flops 1 | bytes 1 | tf_op jit(solution)/shard_map/w_in_unpack/pallas_call | solution.py:54
  188.8 1.6 token_grads.1
  190.5 2.6 %w_down_w_out_unpack.1 = (f32[2,2,96,768]{3,2,1,0:T(8,128)}, f32[2,2,144,768]{3,2,1,0:T(8,128)}, f32[384]{0:T(512)}) custom-call(s32[4]{0:T(128)S(1)} %pad_add_fusion.idx, bf16[2,4,64,768]{3,2,1,0:T(8,128)(2,1)S(1)} %pad_maximum_fusion.2.own, bf16[2,4,64,768]{3,2,1,0:T(8,128)(2,1)S(1)} %collective-permute-done.49.got), custom_call_target="tpu_custom_call" | custom-call | flops 1 | bytes 1 | tf_op jit(solution)/shard_map/w_down_w_out_unpack/pallas_call | solution.py:54
  (171 shorter events, 29.7 us)
Async XLA Ops:
  0.6 15.5 %collective-permute-start = (bf16[128,768]{1,0:T(8,128)(2,1)}, bf16[128,768]{1,0:T(8,128)(2,1)S(1)}, u32[]{:S(2)}, u32[]{:S(2)}) collective-permute-start(bf16[128,768]{1,0:T(8,128)(2,1)} %bitcast.67), channel_id=1, source_target_pairs={{0,8},{8,16},{16,24},{24,0},{1,9},{9,17},{17,25},{25,1},{2,10},{10... | collective-permute-start | bytes 589832 | tf_op jit(solution)/shard_map/ppermute | solution.py:578
  3.7 16.9 %collective-permute-start.1 = (bf16[128,768]{1,0:T(8,128)(2,1)}, bf16[128,768]{1,0:T(8,128)(2,1)S(1)}, u32[]{:S(2)}, u32[]{:S(2)}) collective-permute-start(bf16[128,768]{1,0:T(8,128)(2,1)} %bitcast.68), channel_id=1, source_target_pairs={{0,16},{8,24},{16,0},{24,8},{1,17},{9,25},{17,1},{25,9},{2,18},{10... | collective-permute-start | bytes 589832 | tf_op jit(solution)/shard_map/ppermute | solution.py:578
  6.3 14.3 %collective-permute-start.2 = (bf16[128,768]{1,0:T(8,128)(2,1)}, bf16[128,768]{1,0:T(8,128)(2,1)S(1)}, u32[]{:S(2)}, u32[]{:S(2)}) collective-permute-start(bf16[128,768]{1,0:T(8,128)(2,1)} %bitcast.69), channel_id=1, source_target_pairs={{0,24},{8,0},{16,8},{24,16},{1,25},{9,1},{17,9},{25,17},{2,26},{10... | collective-permute-start | bytes 589832 | tf_op jit(solution)/shard_map/ppermute | solution.py:578
  10.2 9.3 %collective-permute-start.3 = (bf16[208,640]{1,0:T(8,128)(2,1)S(1)}, bf16[208,640]{1,0:T(8,128)(2,1)S(1)}, u32[]{:S(2)}, u32[]{:S(2)}) collective-permute-start(bf16[208,640]{1,0:T(8,128)(2,1)S(1)} %get-tuple-element.201.refs_7_), channel_id=1, source_target_pairs={{0,1},{1,0},{2,3},{3,2},{4,5},{5,4},{6,7},{7,6},{8,9},{9,8},{10,11... | collective-permute-start | bytes 798728 | tf_op jit(solution)/shard_map/ppermute | solution.py:578
  13.7 12.3 %collective-permute-start.8 = (bf16[144,768]{1,0:T(8,128)(2,1)S(1)}, bf16[144,768]{1,0:T(8,128)(2,1)S(1)}, u32[]{:S(2)}, u32[]{:S(2)}) collective-permute-start(bf16[144,768]{1,0:T(8,128)(2,1)S(1)} %get-tuple-element.212), channel_id=1, source_target_pairs={{0,1},{1,0},{2,3},{3,2},{4,5},{5,4},{6,7},{7,6},{8,9},{9,8},{10,11... | collective-permute-start | bytes 663560 | tf_op jit(solution)/shard_map/ppermute | solution.py:578
  16.1 31.4 %collective-permute-start.15 = (bf16[768,768]{1,0:T(8,128)(2,1)S(1)}, bf16[768,768]{1,0:T(8,128)(2,1)S(1)}, u32[]{:S(2)}, u32[]{:S(2)}) collective-permute-start(bf16[768,768]{1,0:T(8,128)(2,1)S(1)} %get-tuple-element.192), channel_id=1, source_target_pairs={{0,1},{1,0},{2,3},{3,2},{4,5},{5,4},{6,7},{7,6},{8,9},{9,8},{10,11... | collective-permute-start | bytes 3538952 | tf_op jit(solution)/shard_map/ppermute | solution.py:578
  25.8 9.4 %collective-permute-start.6 = (bf16[512,384]{1,0:T(8,128)(2,1)S(1)}, bf16[512,384]{1,0:T(8,128)(2,1)S(1)}, u32[]{:S(2)}, u32[]{:S(2)}) collective-permute-start(bf16[512,384]{1,0:T(8,128)(2,1)S(1)} %get-tuple-element.261.refs_0_), channel_id=1, source_target_pairs={{0,2},{2,0},{1,3},{3,1},{4,6},{6,4},{5,7},{7,5},{8,10},{10,8},{9,1... | collective-permute-start | bytes 1179656 | tf_op jit(solution)/shard_map/ppermute | solution.py:578
  26.0 9.0 %collective-permute-start.9 = (bf16[144,768]{1,0:T(8,128)(2,1)S(1)}, bf16[144,768]{1,0:T(8,128)(2,1)S(1)}, u32[]{:S(2)}, u32[]{:S(2)}) collective-permute-start(bf16[144,768]{1,0:T(8,128)(2,1)S(1)} %collective-permute-done.8), channel_id=1, source_target_pairs={{0,8},{8,0},{16,24},{24,16},{1,9},{9,1},{17,25},{25,17},{2,10},{10... | collective-permute-start | bytes 663560 | tf_op jit(solution)/shard_map/ppermute | solution.py:620
  29.1 11.2 %collective-permute-start.5 = (bf16[512,384]{1,0:T(8,128)(2,1)S(1)}, bf16[512,384]{1,0:T(8,128)(2,1)S(1)}, u32[]{:S(2)}, u32[]{:S(2)}) collective-permute-start(bf16[512,384]{1,0:T(8,128)(2,1)S(1)} %get-tuple-element.261.refs_0_), channel_id=1, source_target_pairs={{0,4},{4,0},{1,5},{5,1},{2,6},{6,2},{3,7},{7,3},{8,12},{12,8},{9,1... | collective-permute-start | bytes 1179656 | tf_op jit(solution)/shard_map/ppermute | solution.py:578
  35.1 5.1 %collective-permute-start.10 = (bf16[2,144,768]{2,1,0:T(8,128)(2,1)S(1)}, bf16[2,144,768]{2,1,0:T(8,128)(2,1)S(1)}, u32[]{:S(2)}, u32[]{:S(2)}) collective-permute-start(bf16[2,144,768]{2,1,0:T(8,128)(2,1)S(1)} %pad_maximum_fusion.3.refs_12_), channel_id=1, source_target_pairs={{0,2},{2,0},{1,3},{3,1},{4,6},{6,4},{5,7},{7,5},{8,10},{10,8},{9,1... | collective-permute-start | bytes 1327112 | tf_op jit(solution)/shard_map/ppermute | solution.py:578
  47.5 10.2 %collective-permute-start.16 = (bf16[768,768]{1,0:T(8,128)(2,1)S(1)}, bf16[768,768]{1,0:T(8,128)(2,1)S(1)}, u32[]{:S(2)}, u32[]{:S(2)}) collective-permute-start(bf16[768,768]{1,0:T(8,128)(2,1)S(1)} %collective-permute-done.15.refs_10_), channel_id=1, source_target_pairs={{0,2},{2,0},{1,3},{3,1},{4,6},{6,4},{5,7},{7,5},{8,10},{10,8},{9,1... | collective-permute-start | bytes 3538952 | tf_op jit(solution)/shard_map/ppermute | solution.py:578
  47.5 4.3 %collective-permute-start.14 = (bf16[512,768]{1,0:T(8,128)(2,1)}, bf16[512,768]{1,0:T(8,128)(2,1)S(1)}, u32[]{:S(2)}, u32[]{:S(2)}) collective-permute-start(bf16[512,768]{1,0:T(8,128)(2,1)} %get-tuple-element.278.refs_0_), channel_id=1, source_target_pairs={{0,2},{2,0},{1,3},{3,1},{4,6},{6,4},{5,7},{7,5},{8,10},{10,8},{9,1... | collective-permute-start | bytes 2359304 | tf_op jit(solution)/shard_map/ppermute | solution.py:578
  48.0 19.7 %collective-permute-start.20 = (bf16[512,768]{1,0:T(8,128)(2,1)}, bf16[512,768]{1,0:T(8,128)(2,1)S(1)}, u32[]{:S(2)}, u32[]{:S(2)}) collective-permute-start(bf16[512,768]{1,0:T(8,128)(2,1)} %get-tuple-element.278.refs_0_), channel_id=1, source_target_pairs={{0,4},{4,0},{1,5},{5,1},{2,6},{6,2},{3,7},{7,3},{8,12},{12,8},{9,1... | collective-permute-start | bytes 2359304 | tf_op jit(solution)/shard_map/ppermute | solution.py:578
  49.5 4.1 %collective-permute-start.11 = (bf16[192,128]{1,0:T(8,128)(2,1)S(1)}, bf16[192,128]{1,0:T(8,128)(2,1)S(1)}, u32[]{:S(2)}, u32[]{:S(2)}) collective-permute-start(bf16[192,128]{1,0:T(8,128)(2,1)S(1)} %get-tuple-element.220), channel_id=1, source_target_pairs={{0,24},{8,0},{16,8},{24,16},{1,25},{9,1},{17,9},{25,17},{2,26},{10... | collective-permute-start | bytes 147464 | tf_op jit(solution)/shard_map/ppermute | solution.py:578
  51.5 5.5 %collective-permute-start.12 = (bf16[192,128]{1,0:T(8,128)(2,1)S(1)}, bf16[192,128]{1,0:T(8,128)(2,1)S(1)}, u32[]{:S(2)}, u32[]{:S(2)}) collective-permute-start(bf16[192,128]{1,0:T(8,128)(2,1)S(1)} %get-tuple-element.221), channel_id=1, source_target_pairs={{0,16},{8,24},{16,0},{24,8},{1,17},{9,25},{17,1},{25,9},{2,18},{10... | collective-permute-start | bytes 147464 | tf_op jit(solution)/shard_map/ppermute | solution.py:578
  51.8 5.9 %collective-permute-start.13 = (bf16[192,128]{1,0:T(8,128)(2,1)S(1)}, bf16[192,128]{1,0:T(8,128)(2,1)S(1)}, u32[]{:S(2)}, u32[]{:S(2)}) collective-permute-start(bf16[192,128]{1,0:T(8,128)(2,1)S(1)} %get-tuple-element.222), channel_id=1, source_target_pairs={{0,8},{8,16},{16,24},{24,0},{1,9},{9,17},{17,25},{25,1},{2,10},{10... | collective-permute-start | bytes 147464 | tf_op jit(solution)/shard_map/ppermute | solution.py:578
  67.7 4.8 %collective-permute-start.21 = (bf16[128,6528]{1,0:T(8,128)(2,1)S(1)}, bf16[128,6528]{1,0:T(8,128)(2,1)S(1)}, u32[]{:S(2)}, u32[]{:S(2)}) collective-permute-start(bf16[128,6528]{1,0:T(8,128)(2,1)S(1)} %get-tuple-element.256.own), channel_id=1, source_target_pairs={{0,2},{2,0},{1,3},{3,1},{4,6},{6,4},{5,7},{7,5},{8,10},{10,8},{9,1... | collective-permute-start | bytes 5013512 | tf_op jit(solution)/shard_map/ppermute | solution.py:578
  67.7 4.7 %collective-permute-start.22 = (bf16[512,768]{1,0:T(8,128)(2,1)S(1)}, bf16[512,768]{1,0:T(8,128)(2,1)S(1)}, u32[]{:S(2)}, u32[]{:S(2)}) collective-permute-start(bf16[512,768]{1,0:T(8,128)(2,1)S(1)} %collective-permute-done.20.refs_1_), channel_id=1, source_target_pairs={{0,2},{2,0},{1,3},{3,1},{4,6},{6,4},{5,7},{7,5},{8,10},{10,8},{9,1... | collective-permute-start | bytes 2359304 | tf_op jit(solution)/shard_map/ppermute | solution.py:578
  68.2 9.2 %collective-permute-start.17 = (bf16[128,256]{1,0:T(8,128)(2,1)S(1)}, bf16[128,256]{1,0:T(8,128)(2,1)S(1)}, u32[]{:S(2)}, u32[]{:S(2)}) collective-permute-start(bf16[128,256]{1,0:T(8,128)(2,1)S(1)} %get-tuple-element.246), channel_id=1, source_target_pairs={{0,8},{8,16},{16,24},{24,0},{1,9},{9,17},{17,25},{25,1},{2,10},{10... | collective-permute-start | bytes 196616 | tf_op jit(solution)/shard_map/ppermute | solution.py:578
  69.4 8.0 %collective-permute-start.18 = (bf16[128,256]{1,0:T(8,128)(2,1)S(1)}, bf16[128,256]{1,0:T(8,128)(2,1)S(1)}, u32[]{:S(2)}, u32[]{:S(2)}) collective-permute-start(bf16[128,256]{1,0:T(8,128)(2,1)S(1)} %get-tuple-element.247), channel_id=1, source_target_pairs={{0,16},{8,24},{16,0},{24,8},{1,17},{9,25},{17,1},{25,9},{2,18},{10... | collective-permute-start | bytes 196616 | tf_op jit(solution)/shard_map/ppermute | solution.py:578
  71.1 6.3 %collective-permute-start.19 = (bf16[128,256]{1,0:T(8,128)(2,1)S(1)}, bf16[128,256]{1,0:T(8,128)(2,1)S(1)}, u32[]{:S(2)}, u32[]{:S(2)}) collective-permute-start(bf16[128,256]{1,0:T(8,128)(2,1)S(1)} %get-tuple-element.248), channel_id=1, source_target_pairs={{0,24},{8,0},{16,8},{24,16},{1,25},{9,1},{17,9},{25,17},{2,26},{10... | collective-permute-start | bytes 196616 | tf_op jit(solution)/shard_map/ppermute | solution.py:578
  77.4 21.9 %collective-permute-start.23 = (bf16[2,1728,128]{2,1,0:T(8,128)(2,1)}, bf16[2,1728,128]{2,1,0:T(8,128)(2,1)S(1)}, u32[]{:S(2)}, u32[]{:S(2)}) collective-permute-start(bf16[2,1728,128]{2,1,0:T(8,128)(2,1)} %get-tuple-element.290), channel_id=1, source_target_pairs={{0,1},{1,0},{2,3},{3,2},{4,5},{5,4},{6,7},{7,6},{8,9},{9,8},{10,11... | collective-permute-start | bytes 2654216 | tf_op jit(solution)/shard_map/ppermute | solution.py:578
  79.0 19.4 %collective-permute-start.24 = (bf16[2,256,768]{2,1,0:T(8,128)(2,1)}, bf16[2,256,768]{2,1,0:T(8,128)(2,1)S(1)}, u32[]{:S(2)}, u32[]{:S(2)}) collective-permute-start(bf16[2,256,768]{2,1,0:T(8,128)(2,1)} %get-tuple-element.292), channel_id=1, source_target_pairs={{0,4},{4,0},{1,5},{5,1},{2,6},{6,2},{3,7},{7,3},{8,12},{12,8},{9,1... | collective-permute-start | bytes 2359304 | tf_op jit(solution)/shard_map/ppermute | solution.py:578
  99.3 5.0 %collective-permute-start.25 = (bf16[2,512,384]{2,1,0:T(8,128)(2,1)S(1)}, bf16[2,512,384]{2,1,0:T(8,128)(2,1)S(1)}, u32[]{:S(2)}, u32[]{:S(2)}) collective-permute-start(bf16[2,512,384]{2,1,0:T(8,128)(2,1)S(1)} %get-tuple-element.294.refs_5_), channel_id=1, source_target_pairs={{0,2},{2,0},{1,3},{3,1},{4,6},{6,4},{5,7},{7,5},{8,10},{10,8},{9,1... | collective-permute-start | bytes 2359304 | tf_op jit(solution)/shard_map/ppermute | solution.py:578
  99.3 4.3 %collective-permute-start.26 = (bf16[2,2,96,640]{3,2,1,0:T(8,128)(2,1)S(1)}, bf16[2,2,96,640]{3,2,1,0:T(8,128)(2,1)S(1)}, u32[]{:S(2)}, u32[]{:S(2)}) collective-permute-start(bf16[2,2,96,640]{3,2,1,0:T(8,128)(2,1)S(1)} %get-tuple-element.295), channel_id=1, source_target_pairs={{0,2},{2,0},{1,3},{3,1},{4,6},{6,4},{5,7},{7,5},{8,10},{10,8},{9,1... | collective-permute-start | bytes 1474568 | tf_op jit(solution)/shard_map/ppermute | solution.py:578
  100.3 14.9 %collective-permute-start.28 = (bf16[256,768]{1,0:T(8,128)(2,1)S(1)}, bf16[256,768]{1,0:T(8,128)(2,1)S(1)}, u32[]{:S(2)}, u32[]{:S(2)}) collective-permute-start(bf16[256,768]{1,0:T(8,128)(2,1)S(1)} %get-tuple-element.366), channel_id=1, source_target_pairs={{0,1},{1,0},{2,3},{3,2},{4,5},{5,4},{6,7},{7,6},{8,9},{9,8},{10,11... | collective-permute-start | bytes 1179656 | tf_op jit(solution)/shard_map/ppermute | solution.py:578
  102.0 13.1 %collective-permute-start.29 = (bf16[1728,128]{1,0:T(8,128)(2,1)S(1)}, bf16[1728,128]{1,0:T(8,128)(2,1)S(1)}, u32[]{:S(2)}, u32[]{:S(2)}) collective-permute-start(bf16[1728,128]{1,0:T(8,128)(2,1)S(1)} %get-tuple-element.364), channel_id=1, source_target_pairs={{0,4},{4,0},{1,5},{5,1},{2,6},{6,2},{3,7},{7,3},{8,12},{12,8},{9,1... | collective-permute-start | bytes 1327112 | tf_op jit(solution)/shard_map/ppermute | solution.py:578
  103.7 13.9 %collective-permute-start.32 = (bf16[2,96,640]{2,1,0:T(8,128)(2,1)S(1)}, bf16[2,96,640]{2,1,0:T(8,128)(2,1)S(1)}, u32[]{:S(2)}, u32[]{:S(2)}) collective-permute-start(bf16[2,96,640]{2,1,0:T(8,128)(2,1)S(1)} %get-tuple-element.368), channel_id=1, source_target_pairs={{0,1},{1,0},{2,3},{3,2},{4,5},{5,4},{6,7},{7,6},{8,9},{9,8},{10,11... | collective-permute-start | bytes 737288 | tf_op jit(solution)/shard_map/ppermute | solution.py:578
  104.4 43.8 %collective-permute-start.27 = (bf16[1,512,384]{2,1,0:T(8,128)(2,1)S(1)}, bf16[1,512,384]{2,1,0:T(8,128)(2,1)S(1)}, u32[]{:S(2)}, u32[]{:S(2)}) collective-permute-start(bf16[1,512,384]{2,1,0:T(8,128)(2,1)S(1)} %add_convert_fusion.6), channel_id=1, source_target_pairs={{0,4},{4,0},{1,5},{5,1},{2,6},{6,2},{3,7},{7,3},{8,12},{12,8},{9,1... | collective-permute-start | bytes 1179656 | tf_op jit(solution)/shard_map/ppermute | solution.py:578
  115.4 9.2 %collective-permute-start.30 = (bf16[2,64,768]{2,1,0:T(8,128)(2,1)S(1)}, bf16[2,64,768]{2,1,0:T(8,128)(2,1)S(1)}, u32[]{:S(2)}, u32[]{:S(2)}) collective-permute-start(bf16[2,64,768]{2,1,0:T(8,128)(2,1)S(1)} %get-tuple-element.374), channel_id=1, source_target_pairs={{0,8},{8,0},{16,24},{24,16},{1,9},{9,1},{17,25},{25,17},{2,10},{10... | collective-permute-start | bytes 589832 | tf_op jit(solution)/shard_map/ppermute | solution.py:620
  116.7 7.8 %collective-permute-start.31 = (bf16[2,432,128]{2,1,0:T(8,128)(2,1)S(1)}, bf16[2,432,128]{2,1,0:T(8,128)(2,1)S(1)}, u32[]{:S(2)}, u32[]{:S(2)}) collective-permute-start(bf16[2,432,128]{2,1,0:T(8,128)(2,1)S(1)} %get-tuple-element.370), channel_id=1, source_target_pairs={{0,8},{8,0},{16,24},{24,16},{1,9},{9,1},{17,25},{25,17},{2,10},{10... | collective-permute-start | bytes 663560 | tf_op jit(solution)/shard_map/ppermute | solution.py:620
  117.7 10.1 %collective-permute-start.35 = (bf16[96,640]{1,0:T(8,128)(2,1)S(1)}, bf16[96,640]{1,0:T(8,128)(2,1)S(1)}, u32[]{:S(2)}, u32[]{:S(2)}) collective-permute-start(bf16[96,640]{1,0:T(8,128)(2,1)S(1)} %get-tuple-element.376), channel_id=1, source_target_pairs={{0,4},{4,0},{1,5},{5,1},{2,6},{6,2},{3,7},{7,3},{8,12},{12,8},{9,1... | collective-permute-start | bytes 368648 | tf_op jit(solution)/shard_map/ppermute | solution.py:578
  124.7 13.0 %collective-permute-start.33 = (bf16[64,768]{1,0:T(8,128)(2,1)S(1)}, bf16[64,768]{1,0:T(8,128)(2,1)S(1)}, u32[]{:S(2)}, u32[]{:S(2)}) collective-permute-start(bf16[64,768]{1,0:T(8,128)(2,1)S(1)} %get-tuple-element.380), channel_id=1, source_target_pairs={{0,16},{8,24},{16,0},{24,8},{1,17},{9,25},{17,1},{25,9},{2,18},{10... | collective-permute-start | bytes 294920 | tf_op jit(solution)/shard_map/ppermute | solution.py:620
  126.1 11.5 %collective-permute-start.34 = (bf16[432,128]{1,0:T(8,128)(2,1)S(1)}, bf16[432,128]{1,0:T(8,128)(2,1)S(1)}, u32[]{:S(2)}, u32[]{:S(2)}) collective-permute-start(bf16[432,128]{1,0:T(8,128)(2,1)S(1)} %get-tuple-element.378), channel_id=1, source_target_pairs={{0,16},{8,24},{16,0},{24,8},{1,17},{9,25},{17,1},{25,9},{2,18},{10... | collective-permute-start | bytes 331784 | tf_op jit(solution)/shard_map/ppermute | solution.py:620
  127.8 12.9 %collective-permute-start.38 = (bf16[96,640]{1,0:T(8,128)(2,1)S(1)}, bf16[96,640]{1,0:T(8,128)(2,1)S(1)}, u32[]{:S(2)}, u32[]{:S(2)}) collective-permute-start(bf16[96,640]{1,0:T(8,128)(2,1)S(1)} %add_convert_fusion.10), channel_id=1, source_target_pairs={{0,16},{8,24},{16,0},{24,8},{1,17},{9,25},{17,1},{25,9},{2,18},{10... | collective-permute-start | bytes 368648 | tf_op jit(solution)/shard_map/ppermute | solution.py:620
  137.7 10.5 %collective-permute-start.37 = (bf16[432,128]{1,0:T(8,128)(2,1)S(1)}, bf16[432,128]{1,0:T(8,128)(2,1)S(1)}, u32[]{:S(2)}, u32[]{:S(2)}) collective-permute-start(bf16[432,128]{1,0:T(8,128)(2,1)S(1)} %add_convert_fusion.11), channel_id=1, source_target_pairs={{0,16},{8,24},{16,0},{24,8},{1,17},{9,25},{17,1},{25,9},{2,18},{10... | collective-permute-start | bytes 331784 | tf_op jit(solution)/shard_map/ppermute | solution.py:620
  137.8 10.3 %collective-permute-start.36 = (bf16[64,768]{1,0:T(8,128)(2,1)S(1)}, bf16[64,768]{1,0:T(8,128)(2,1)S(1)}, u32[]{:S(2)}, u32[]{:S(2)}) collective-permute-start(bf16[64,768]{1,0:T(8,128)(2,1)S(1)} %add_convert_fusion.12), channel_id=1, source_target_pairs={{0,16},{8,24},{16,0},{24,8},{1,17},{9,25},{17,1},{25,9},{2,18},{10... | collective-permute-start | bytes 294920 | tf_op jit(solution)/shard_map/ppermute | solution.py:620
  140.8 9.3 %collective-permute-start.41 = (bf16[2,96,640]{2,1,0:T(8,128)(2,1)S(1)}, bf16[2,96,640]{2,1,0:T(8,128)(2,1)S(1)}, u32[]{:S(2)}, u32[]{:S(2)}) collective-permute-start(bf16[2,96,640]{2,1,0:T(8,128)(2,1)S(1)} %pad_maximum_fusion.5), channel_id=1, source_target_pairs={{0,8},{8,0},{16,24},{24,16},{1,9},{9,1},{17,25},{25,17},{2,10},{10... | collective-permute-start | bytes 737288 | tf_op jit(solution)/shard_map/ppermute | solution.py:620
  150.2 12.2 %collective-permute-start.43 = (bf16[4,96,640]{2,1,0:T(8,128)(2,1)S(1)}, bf16[4,96,640]{2,1,0:T(8,128)(2,1)S(1)}, u32[]{:S(2)}, u32[]{:S(2)}) collective-permute-start(bf16[4,96,640]{2,1,0:T(8,128)(2,1)S(1)} %constant_dynamic-update-slice_fusion.2), channel_id=1, source_target_pairs={{0,4},{4,0},{1,5},{5,1},{2,6},{6,2},{3,7},{7,3},{8,12},{12,8},{9,1... | collective-permute-start | bytes 1474568 | tf_op jit(solution)/shard_map/ppermute | solution.py:578
  151.8 7.8 %collective-permute-start.40 = (bf16[2,64,768]{2,1,0:T(8,128)(2,1)S(1)}, bf16[2,64,768]{2,1,0:T(8,128)(2,1)S(1)}, u32[]{:S(2)}, u32[]{:S(2)}) collective-permute-start(bf16[2,64,768]{2,1,0:T(8,128)(2,1)S(1)} %pad_maximum_fusion.7), channel_id=1, source_target_pairs={{0,8},{8,0},{16,24},{24,16},{1,9},{9,1},{17,25},{25,17},{2,10},{10... | collective-permute-start | bytes 589832 | tf_op jit(solution)/shard_map/ppermute | solution.py:620
  151.8 10.3 %collective-permute-start.39 = (bf16[2,432,128]{2,1,0:T(8,128)(2,1)S(1)}, bf16[2,432,128]{2,1,0:T(8,128)(2,1)S(1)}, u32[]{:S(2)}, u32[]{:S(2)}) collective-permute-start(bf16[2,432,128]{2,1,0:T(8,128)(2,1)S(1)} %pad_maximum_fusion.6), channel_id=1, source_target_pairs={{0,8},{8,0},{16,24},{24,16},{1,9},{9,1},{17,25},{25,17},{2,10},{10... | collective-permute-start | bytes 663560 | tf_op jit(solution)/shard_map/ppermute | solution.py:620
  162.5 14.3 %collective-permute-start.46 = (bf16[2,4,96,640]{3,2,1,0:T(8,128)(2,1)S(1)}, bf16[2,4,96,640]{3,2,1,0:T(8,128)(2,1)S(1)}, u32[]{:S(2)}, u32[]{:S(2)}) collective-permute-start(bf16[2,4,96,640]{3,2,1,0:T(8,128)(2,1)S(1)} %pad_maximum_fusion.own), channel_id=1, source_target_pairs={{0,2},{2,0},{1,3},{3,1},{4,6},{6,4},{5,7},{7,5},{8,10},{10,8},{9,1... | collective-permute-start | bytes 2949128 | tf_op jit(solution)/shard_map/ppermute | solution.py:578
  162.6 11.5 %collective-permute-start.42 = (bf16[2,128,768]{2,1,0:T(8,128)(2,1)S(1)}, bf16[2,128,768]{2,1,0:T(8,128)(2,1)S(1)}, u32[]{:S(2)}, u32[]{:S(2)}) collective-permute-start(bf16[2,128,768]{2,1,0:T(8,128)(2,1)S(1)} %get-tuple-element.335), channel_id=1, source_target_pairs={{0,8},{8,0},{16,24},{24,16},{1,9},{9,1},{17,25},{25,17},{2,10},{10... | collective-permute-start | bytes 1179656 | tf_op jit(solution)/shard_map/ppermute | solution.py:620
  162.7 14.0 %collective-permute-start.45 = (bf16[4,432,128]{2,1,0:T(8,128)(2,1)S(1)}, bf16[4,432,128]{2,1,0:T(8,128)(2,1)S(1)}, u32[]{:S(2)}, u32[]{:S(2)}) collective-permute-start(bf16[4,432,128]{2,1,0:T(8,128)(2,1)S(1)} %pad_maximum_fusion.4), channel_id=1, source_target_pairs={{0,4},{4,0},{1,5},{5,1},{2,6},{6,2},{3,7},{7,3},{8,12},{12,8},{9,1... | collective-permute-start | bytes 1327112 | tf_op jit(solution)/shard_map/ppermute | solution.py:578
  164.3 19.3 %collective-permute-start.48 = (bf16[4,64,768]{2,1,0:T(8,128)(2,1)S(1)}, bf16[4,64,768]{2,1,0:T(8,128)(2,1)S(1)}, u32[]{:S(2)}, u32[]{:S(2)}) collective-permute-start(bf16[4,64,768]{2,1,0:T(8,128)(2,1)S(1)} %constant_dynamic-update-slice_fusion), channel_id=1, source_target_pairs={{0,4},{4,0},{1,5},{5,1},{2,6},{6,2},{3,7},{7,3},{8,12},{12,8},{9,1... | collective-permute-start | bytes 1179656 | tf_op jit(solution)/shard_map/ppermute | solution.py:578
  174.3 11.6 %collective-permute-start.44 = (bf16[128,768]{1,0:T(8,128)(2,1)S(1)}, bf16[128,768]{1,0:T(8,128)(2,1)S(1)}, u32[]{:S(2)}, u32[]{:S(2)}) collective-permute-start(bf16[128,768]{1,0:T(8,128)(2,1)S(1)} %get-tuple-element.372), channel_id=1, source_target_pairs={{0,16},{8,24},{16,0},{24,8},{1,17},{9,25},{17,1},{25,9},{2,18},{10... | collective-permute-start | bytes 589832 | tf_op jit(solution)/shard_map/ppermute | solution.py:620
  179.7 6.3 %collective-permute-start.47 = (bf16[2,4,432,128]{3,2,1,0:T(8,128)(2,1)S(1)}, bf16[2,4,432,128]{3,2,1,0:T(8,128)(2,1)S(1)}, u32[]{:S(2)}, u32[]{:S(2)}) collective-permute-start(bf16[2,4,432,128]{3,2,1,0:T(8,128)(2,1)S(1)} %pad_maximum_fusion.1.own), channel_id=1, source_target_pairs={{0,2},{2,0},{1,3},{3,1},{4,6},{6,4},{5,7},{7,5},{8,10},{10,8},{9,1... | collective-permute-start | bytes 2654216 | tf_op jit(solution)/shard_map/ppermute | solution.py:578
  185.9 4.5 %collective-permute-start.49 = (bf16[2,4,64,768]{3,2,1,0:T(8,128)(2,1)S(1)}, bf16[2,4,64,768]{3,2,1,0:T(8,128)(2,1)S(1)}, u32[]{:S(2)}, u32[]{:S(2)}) collective-permute-start(bf16[2,4,64,768]{3,2,1,0:T(8,128)(2,1)S(1)} %pad_maximum_fusion.2.own), channel_id=1, source_target_pairs={{0,2},{2,0},{1,3},{3,1},{4,6},{6,4},{5,7},{7,5},{8,10},{10,8},{9,1... | collective-permute-start | bytes 2359304 | tf_op jit(solution)/shard_map/ppermute | solution.py:578
  (31 other events, 303.8 us)
